TPU v7x, 32 devices: a whole 2x2x4 slice. The times are simulated.
32 devices in a mesh: dp: 2 (over y), expert: 16 (over z, x, core).
Axes of the slice: x: 2, y: 2, z: 4, core: 2. Of those that a mesh axis runs over, the one named last changes fastest.
Arguments:
- tokens: bfloat16 [4096, 2048], P(('dp', 'expert')), may hold values from -6 to 6
- out_grad: bfloat16 [4096, 2048], P(('dp', 'expert')), may hold values from -6 to 6
- expert_ids: int32 [4096, 6], P(('dp', 'expert')), may hold values from 0 to 15, all different within a row; in each aligned block of 128 rows (0 to 127, 128 to 255, ...) at most 56 rows name the same one
- route_weights: bfloat16 [4096, 6], P(('dp', 'expert')), may hold values from 0.019897461 to 0.5
- blocks: bfloat16 [16, 3, 12, 128, 128], P('expert'), may hold values from -0.5 to 0.5
- layout: int32 [16, 3, 12, 2], P('expert'), may hold values from 0 to 15, as said below
- moments: float32 [16, 3, 12, 128, 128], P('expert', None, None, 'dp'), may hold values from -12 to 12
- partner: int32 [16], replicated, may hold values from 0 to 15, as said below
Outputs:
- token_grad: bfloat16 [4096, 2048], P(('dp', 'expert'))
- route_grad: bfloat16 [4096, 6], P(('dp', 'expert'))
- new_blocks: bfloat16 [16, 3, 12, 128, 128], P('expert')
- new_moments: float32 [16, 3, 12, 128, 128], P('expert', None, None, 'dp')
Inputs may be any that keep to these rules, and one draw needn't show every extreme that they name: `layout`: within one expert and matrix the stored blocks are at distinct places; for gate and up an entry is (block of the 2048 features, block of the 1408 hidden units), for down (block of the hidden units, block of the features). partner pairs the experts: partner[partner[e]] == e and partner[e] != e. `expert_ids`: each row names 6 different experts; among the rows of one device no expert is named more than 56 times, a bound that some block reaches.
All inputs are finite; a program needn't handle non-finite values.
Results may differ from a plain program's by a relative error of at most 0.0064.
Values may be sent and summed in bfloat16 or wider, within the bound.
No kernel may reach another device: no remote copies, remote signals or barrier semaphores. Data moves between devices by JAX's collectives and lax.ppermute only.
A program may use at most 128 MiB of HBM per device.

v0:
```python
import jax
import jax.numpy as jnp
from jax import lax
from jax.sharding import PartitionSpec as P

HID = 1408


momentum_decay = 0.9
step_rate = 0.01


def block_product(left, mats, source_idx, target_idx, target_count, flipped):
    row_count = left.shape[0]
    block_size = mats.shape[-1]
    pieces = jnp.take(left.reshape(row_count, -1, block_size), source_idx, axis=1)
    if flipped:
        partial_out = jnp.einsum("rbk,bnk->rbn", pieces, mats, preferred_element_type=jnp.float32)
    else:
        partial_out = jnp.einsum("rbk,bkn->rbn", pieces, mats, preferred_element_type=jnp.float32)
    select = (target_idx[:, None] == jnp.arange(target_count, dtype=jnp.int32)[None, :]).astype(
        jnp.float32
    )
    placed = jnp.einsum("rbn,bc->rcn", partial_out, select, precision=lax.Precision.HIGHEST)
    return placed.reshape(row_count, target_count * block_size)


def block_outer(left, right, left_idx, right_idx, block_size):
    row_count = left.shape[0]
    left_pieces = jnp.take(left.reshape(row_count, -1, block_size), left_idx, axis=1)
    right_pieces = jnp.take(right.reshape(row_count, -1, block_size), right_idx, axis=1)
    return jnp.einsum("rbk,rbn->bkn", left_pieces, right_pieces, preferred_element_type=jnp.float32)


def expert_forward(inputs, matrices, layout_one, hidden_blocks, feat_blocks):
    gate_pre = block_product(
        inputs, matrices[0], layout_one[0, :, 0], layout_one[0, :, 1], hidden_blocks, False
    )
    up_pre = block_product(
        inputs, matrices[1], layout_one[1, :, 0], layout_one[1, :, 1], hidden_blocks, False
    )
    sigmoid_gate = jax.nn.sigmoid(gate_pre)
    activated = gate_pre * sigmoid_gate
    hidden = (activated * up_pre).astype(jnp.bfloat16)
    output = block_product(
        hidden, matrices[2], layout_one[2, :, 0], layout_one[2, :, 1], feat_blocks, False
    )
    return (gate_pre, up_pre, sigmoid_gate, activated, hidden, output)


def expert_backward(
    inputs, upstream, weights_col, matrices, layout_one, hidden_blocks, feat_blocks, saved
):
    gate_pre, up_pre, sigmoid_gate, activated, hidden, output = saved
    score = jnp.sum(output * upstream.astype(jnp.float32), axis=1).astype(jnp.bfloat16)
    scaled = (weights_col.astype(jnp.float32)[:, None] * upstream.astype(jnp.float32)).astype(
        jnp.bfloat16
    )
    hidden_grad = block_product(
        scaled, matrices[2], layout_one[2, :, 1], layout_one[2, :, 0], hidden_blocks, True
    )
    gate_grad = (
        hidden_grad * up_pre * sigmoid_gate * (1.0 + gate_pre * (1.0 - sigmoid_gate))
    ).astype(jnp.bfloat16)
    up_grad = (hidden_grad * activated).astype(jnp.bfloat16)
    input_grad = (
        block_product(
            gate_grad, matrices[0], layout_one[0, :, 1], layout_one[0, :, 0], feat_blocks, True
        )
        + block_product(
            up_grad, matrices[1], layout_one[1, :, 1], layout_one[1, :, 0], feat_blocks, True
        )
    ).astype(jnp.bfloat16)
    block_size = matrices.shape[-1]
    weight_grad = jnp.stack(
        [
            block_outer(inputs, gate_grad, layout_one[0, :, 0], layout_one[0, :, 1], block_size),
            block_outer(inputs, up_grad, layout_one[1, :, 0], layout_one[1, :, 1], block_size),
            block_outer(hidden, scaled, layout_one[2, :, 0], layout_one[2, :, 1], block_size),
        ]
    )
    return (score, input_grad, weight_grad)


def relocate(first_state, second_state, partner, expert_count):
    spread = (
        lax.all_to_all(
            first_state.reshape(expert_count, -1), "expert", split_axis=0, concat_axis=0, tiled=True
        ),
        lax.all_to_all(
            second_state.reshape(expert_count, -1),
            "expert",
            split_axis=0,
            concat_axis=0,
            tiled=True,
        ),
    )
    first_moved = jnp.take(spread[0], partner, axis=0)
    second_moved = jnp.take(spread[1], partner, axis=0)
    collected = (
        lax.all_to_all(first_moved, "expert", split_axis=0, concat_axis=0, tiled=True),
        lax.all_to_all(second_moved, "expert", split_axis=0, concat_axis=0, tiled=True),
    )
    return (collected[0].reshape(first_state.shape), collected[1].reshape(second_state.shape))


def body(tokens, out_grad, expert_ids, route_weights, blocks, layout, moments, partner):
    expert_count = lax.axis_size("expert")
    replica_count = lax.axis_size("dp")
    tok_count, topk_count = expert_ids.shape
    width = tokens.shape[1]
    block_size = blocks.shape[-1]
    capacity = max(2, tok_count * topk_count * 7 // (expert_count * 6))
    pick_count = tok_count * topk_count
    feat_blocks = width // block_size
    hidden_blocks = HID // block_size
    flat_ids = expert_ids.reshape(-1)
    onehot = (flat_ids[:, None] == jnp.arange(expert_count, dtype=jnp.int32)[None, :]).astype(
        jnp.int32
    )
    before = jnp.cumsum(onehot, axis=0) - onehot
    rank_within = jnp.sum(before * onehot, axis=1)
    slot_of = flat_ids * capacity + rank_within
    slot_pick = (
        jnp.full((expert_count * capacity,), pick_count, jnp.int32)
        .at[slot_of]
        .set(jnp.arange(pick_count, dtype=jnp.int32))
    )
    filled = slot_pick < pick_count
    safe_pick = jnp.minimum(slot_pick, pick_count - 1)
    token_of = safe_pick // topk_count
    send_tokens = jnp.where(filled[:, None], tokens[token_of], jnp.zeros((), tokens.dtype))
    send_grads = jnp.where(filled[:, None], out_grad[token_of], jnp.zeros((), out_grad.dtype))
    send_weights = jnp.where(
        filled, route_weights.reshape(-1)[safe_pick], jnp.zeros((), route_weights.dtype)
    )
    matrices = blocks[0]
    layout_one = layout[0]
    recv_tokens = lax.all_to_all(send_tokens, "expert", split_axis=0, concat_axis=0, tiled=True)
    saved = expert_forward(recv_tokens, matrices, layout_one, hidden_blocks, feat_blocks)
    recv_grads, recv_weights = (
        lax.all_to_all(send_grads, "expert", split_axis=0, concat_axis=0, tiled=True),
        lax.all_to_all(send_weights, "expert", split_axis=0, concat_axis=0, tiled=True),
    )
    score, input_grad, weight_grad = expert_backward(
        recv_tokens,
        recv_grads,
        recv_weights,
        matrices,
        layout_one,
        hidden_blocks,
        feat_blocks,
        saved,
    )
    back_grad, back_score = (
        lax.all_to_all(input_grad, "expert", split_axis=0, concat_axis=0, tiled=True),
        lax.all_to_all(score, "expert", split_axis=0, concat_axis=0, tiled=True),
    )
    per_pick = back_grad[slot_of].reshape(tok_count, topk_count, width)
    token_grad = jnp.sum(per_pick.astype(jnp.float32), axis=1).astype(jnp.bfloat16)
    route_grad = back_score[slot_of].reshape(tok_count, topk_count)
    shard_grad = lax.psum_scatter(weight_grad, "dp", scatter_dimension=2, tiled=True)
    row_share = block_size // replica_count
    own_rows = lax.dynamic_slice_in_dim(matrices, lax.axis_index("dp") * row_share, row_share, 2)
    new_moment = momentum_decay * moments[0] + shard_grad
    new_shard = (own_rows.astype(jnp.float32) - step_rate * new_moment).astype(jnp.bfloat16)
    moved_shard, moved_moment = relocate(
        new_shard.astype(jnp.float32), new_moment, partner, expert_count
    )
    outgoing = moved_shard.astype(jnp.bfloat16)
    gathered = lax.all_gather(outgoing, "dp", axis=2, tiled=True)
    return (token_grad, route_grad, gathered[None], moved_moment[None])


def solution(mesh):
    placed = (
        P(("dp", "expert"), None),
        P(("dp", "expert"), None),
        P(("dp", "expert"), None),
        P(("dp", "expert"), None),
        P("expert", None, None, None, None),
        P("expert", None, None, None),
        P("expert", None, None, "dp", None),
        P(),
    )
    return jax.shard_map(
        body,
        mesh=mesh,
        in_specs=placed,
        out_specs=(
            P(("dp", "expert"), None),
            P(("dp", "expert"), None),
            P("expert", None, None, None, None),
            P("expert", None, None, "dp", None),
        ),
        check_vma=False,
    )
```

profile of v0, /device:TPU:0, one launch (start us, length us, event | category | flops | bytes accessed | tf_op | source)
XLA Modules:
  0.0 549.6 jit_solution(11560114462182977256)
XLA Ops:
  15.8 5.8 %gather_fusion = bf16[896]{0:T(1024)(128)(2,1)S(1)} fusion(bf16[768]{0:T(1024)(128)(2,1)S(1)} %reshape.187, s32[1024]{0:T(1024)S(1)} %get-tuple-element.67), kind=kCustom, calls=%fused_computation.8 | custom fusion | bytes 7168 | tf_op jit(solution)/shard_map/gather | solution.py:135
  22.3 7.4 %all-to-all-start = ((bf16[16,56,1]{1,2,0:T(2,128)(2,1)}), bf16[16,56,1]{1,2,0:T(2,128)(2,1)S(1)}, u32[]{:S(2)}, u32[]{:S(2)}) async-start(bf16[16,56,1]{1,2,0:T(2,128)(2,1)} %all_to_all.76), calls=%async_computation | async-start | bytes 16384 | tf_op jit(solution)/shard_map/all_to_all | solution.py:143
  39.8 5.3 broadcast_select_fusion
  45.1 87.1 %all_to_all.87 = bf16[16,56,2048]{2,1,0:T(8,128)(2,1)} all-to-all(bf16[16,56,2048]{2,1,0:T(8,128)(2,1)} %get-tuple-element.65), channel_id=1, replica_groups=mesh['dp'=2,'expert'=16] {'expert'}, dimensions={0} | all-to-all | bytes 7340032 | tf_op jit(solution)/shard_map/all_to_all | solution.py:142
  132.2 5.4 all-to-all-start.2
  146.8 59.3 %all-to-all-done.2 = bf16[16,56,2048]{2,1,0:T(8,128)(2,1)} async-done(((bf16[16,56,2048]{2,1,0:T(8,128)(2,1)}), bf16[16,56,2048]{2,1,0:T(8,128)(2,1)}, u32[]{:S(2)}, u32[]{:S(2)}) %all-to-all-start.2) | async-done | bytes 3670048 | tf_op jit(solution)/shard_map/all_to_all | solution.py:139
  219.9 5.5 %gather_fusion.5 = bf16[12,896,128]{2,1,0:T(8,128)(2,1)} fusion(bf16[896,16,128]{2,0,1:T(8,128)(2,1)} %copy.110, s32[1024]{0:T(1024)S(1)} %get-tuple-element.73), kind=kCustom, calls=%fused_computation.clone | custom fusion | bytes 5505072 | tf_op jit(solution)/shard_map/jit(_take)/gather | solution.py:16
  228.2 7.0 %fusion.12 = f32[11,896,128]{2,0,1:T(8,128)S(1)} fusion(f32[896,12,128]{2,0,1:T(8,128)S(1)} %fusion.47, s32[12]{0:T(128)S(1)} %get-tuple-element.52), kind=kOutput, calls=%fused_computation.28 | convolution fusion | flops 181665920 | bytes 10551344 | tf_op jit(solution)/shard_map/rbn,bc->rcn/dot_general | solution.py:24
  236.1 6.8 %fusion.8 = f32[11,896,128]{2,0,1:T(8,128)S(1)} fusion(f32[896,12,128]{2,0,1:T(8,128)S(1)} %fusion.53, s32[12]{0:T(128)S(1)} %get-tuple-element.49), kind=kOutput, calls=%fused_computation.24 | convolution fusion | flops 181665920 | bytes 10551344 | tf_op jit(solution)/shard_map/rbn,bc->rcn/dot_general | solution.py:24
  243.8 7.2 %fusion.10 = f32[11,896,128]{2,0,1:T(8,128)S(1)} fusion(f32[896,12,128]{2,0,1:T(8,128)S(1)} %fusion.50, s32[12]{0:T(128)S(1)} %get-tuple-element.51), kind=kOutput, calls=%fused_computation.26 | convolution fusion | flops 181665920 | bytes 10551344 | tf_op jit(solution)/shard_map/rbn,bc->rcn/dot_general | solution.py:24
  251.0 6.4 %fusion.21 = (bf16[896,11,128]{2,0,1:T(8,128)(2,1)}, bf16[896,11,128]{2,0,1:T(8,128)(2,1)}, bf16[896,11,128]{2,0,1:T(8,128)(2,1)}) fusion(f32[11,896,128]{2,0,1:T(8,128)S(1)} %fusion.10, f32[11,896,128]{2,0,1:T(8,128)S(1)} %fusion.8, f32[11,896,128]{2,0,1:T(8,128)S(1)} %fusion.12), kind=kLoop, calls=%fused_computation.43 | loop fusion | flops 18923520 | bytes 22708224 | tf_op jit(solution)/shard_map/convert_element_type | solution.py:44
  285.4 16.9 %fusion.1 = bf16[896]{0:T(1024)(128)(2,1)S(1)} fusion(f32[112,8,16,128]{3,2,1,0:T(8,128)S(1)} %bitcast.236, f32[896,12,128]{2,0,1:T(8,128)S(1)} %fusion.62, s32[12]{0:T(128)S(1)} %get-tuple-element.48), kind=kOutput, calls=%fused_computation.17 | convolution fusion | flops 267910464 | bytes 12846896 | tf_op jit(solution)/shard_map/rbn,bc->rcn/dot_general | solution.py:24
  303.0 17.5 %all-to-all-start.4 = ((bf16[16,56,1]{1,2,0:T(2,128)(2,1)}), bf16[16,56,1]{1,2,0:T(2,128)(2,1)S(1)}, u32[]{:S(2)}, u32[]{:S(2)}) async-start(bf16[16,56,1]{1,2,0:T(2,128)(2,1)} %convert_element_type.112), calls=%async_computation.4 | async-start | bytes 16384 | tf_op jit(solution)/shard_map/all_to_all | solution.py:157
  320.5 9.2 %reduce-scatter.2.cloned.1.call-done = f32[3,12,64,128]{3,2,1,0:T(8,128)} async-done(((f32[3,12,128,128]{3,2,1,0:T(8,128)}), f32[3,12,64,128]{3,2,1,0:T(8,128)}) %reduce-scatter.2.cloned.1.call-update) | async-done | bytes 1179664 | tf_op jit(solution)/shard_map/reduce_scatter | solution.py:162
  339.7 22.9 %all_to_all.88 = bf16[16,2,9216]{2,1,0:T(2,128)(2,1)S(1)} all-to-all(bf16[16,2,9216]{2,1,0:T(2,128)(2,1)} %reshape.353), channel_id=1, replica_groups=mesh['dp'=2,'expert'=16] {'expert'}, dimensions={0} | all-to-all | bytes 1179648 | tf_op jit(solution)/shard_map/all_to_all | solution.py:87
  371.2 6.6 %fusion.4 = f32[16,896,128]{2,0,1:T(8,128)S(1)} fusion(f32[896,12,128]{2,0,1:T(8,128)S(1)} %fusion.59, s32[12]{0:T(128)S(1)} %get-tuple-element.50), kind=kOutput, calls=%fused_computation.20 | convolution fusion | flops 264241344 | bytes 12845104 | tf_op jit(solution)/shard_map/rbn,bc->rcn/dot_general | solution.py:24
  377.8 11.9 %fusion.23 = bf16[896,16,128]{2,1,0:T(8,128)(2,1)} fusion(f32[16,896,128]{2,0,1:T(8,128)S(1)} %fusion.4, f32[896,12,128]{2,0,1:T(8,128)S(1)} %fusion.56, s32[12]{0:T(128)S(1)} %get-tuple-element.53), kind=kOutput, calls=%fused_computation.46 | convolution fusion | flops 267911360 | bytes 16515120 | tf_op jit(solution)/shard_map/rbn,bc->rcn/dot_general | solution.py:24
  389.7 6.7 %convert_element_type.100 = bf16[16,56,2048]{2,1,0:T(8,128)(2,1)} reshape(bf16[896,16,128]{2,1,0:T(8,128)(2,1)} %fusion.23) | data formatting | bytes 7340032 | tf_op jit(solution)/shard_map/convert_element_type | solution.py:73
  396.5 6.2 %all-to-all-start.3 = ((bf16[16,56,2048]{2,1,0:T(8,128)(2,1)}), bf16[16,56,2048]{2,1,0:T(8,128)(2,1)}, u32[]{:S(2)}, u32[]{:S(2)}) async-start(bf16[16,56,2048]{2,1,0:T(8,128)(2,1)} %convert_element_type.100), calls=%async_computation.3 | async-start | bytes 7340032 | tf_op jit(solution)/shard_map/all_to_all | solution.py:156
  409.6 61.6 %all-to-all-done.3 = bf16[16,56,2048]{2,1,0:T(8,128)(2,1)} async-done(((bf16[16,56,2048]{2,1,0:T(8,128)(2,1)}), bf16[16,56,2048]{2,1,0:T(8,128)(2,1)}, u32[]{:S(2)}, u32[]{:S(2)}) %all-to-all-start.3) | async-done | bytes 3670048 | tf_op jit(solution)/shard_map/all_to_all | solution.py:156
  471.3 17.5 %all-to-all-start.6 = ((bf16[16,2,9216]{2,1,0:T(2,128)(2,1)}), bf16[16,2,9216]{2,1,0:T(2,128)(2,1)S(1)}, u32[]{:S(2)}, u32[]{:S(2)}) async-start(bf16[16,2,9216]{2,1,0:T(2,128)(2,1)} %reshape.355), calls=%async_computation.7 | async-start | bytes 1179648 | tf_op jit(solution)/shard_map/all_to_all | solution.py:101
  491.2 13.2 %all-to-all-done.6 = bf16[16,2,9216]{2,1,0:T(2,128)(2,1)S(1)} async-done(((bf16[16,2,9216]{2,1,0:T(2,128)(2,1)}), bf16[16,2,9216]{2,1,0:T(2,128)(2,1)S(1)}, u32[]{:S(2)}, u32[]{:S(2)}) %all-to-all-start.6) | async-done | bytes 589856 | tf_op jit(solution)/shard_map/all_to_all | solution.py:101
  520.0 9.1 %gather_fusion.3 = bf16[768,2048]{1,0:T(8,128)(2,1)S(1)} fusion(bf16[896,2048]{1,0:T(8,128)(2,1)} %bitcast.32, s32[1024]{0:T(1024)S(1)} %pad_clamp_fusion.2), kind=kCustom, calls=%fused_computation.11 | custom fusion | bytes 6294528 | tf_op jit(solution)/shard_map/gather | solution.py:159
  532.1 5.7 %reduce_sum.34 = bf16[128,2048]{1,0:T(8,128)(2,1)} reduce(bf16[128,6,2048]{2,1,0:T(8,128)(2,1)} %reshape.189, bf16[]{:T(256)} %constant.21.clone.1), dimensions={1}, to_apply=%region_4.7 | reduce | flops 1310720 | bytes 3670018 | tf_op jit(solution)/shard_map/reduce_sum | solution.py:160
  (127 shorter events, 126.4 us)
Async XLA Ops:
  7.2 22.6 %copy-start = (bf16[128,2048]{1,0:T(8,128)(2,1)S(1)}, bf16[128,2048]{1,0:T(8,128)(2,1)}, u32[]{:S(2)}) copy-start(bf16[128,2048]{1,0:T(8,128)(2,1)} %param.14) | copy-start | bytes 1572868
  22.3 22.8 %all-to-all-start = ((bf16[16,56,1]{1,2,0:T(2,128)(2,1)}), bf16[16,56,1]{1,2,0:T(2,128)(2,1)S(1)}, u32[]{:S(2)}, u32[]{:S(2)}) async-start(bf16[16,56,1]{1,2,0:T(2,128)(2,1)} %all_to_all.76), calls=%async_computation | async-start | bytes 16384 | tf_op jit(solution)/shard_map/all_to_all | solution.py:143
  29.8 5.0 copy-start.2
  132.2 5.5 copy-start.13
  132.2 74.0 %all-to-all-start.2 = ((bf16[16,56,2048]{2,1,0:T(8,128)(2,1)}), bf16[16,56,2048]{2,1,0:T(8,128)(2,1)}, u32[]{:S(2)}, u32[]{:S(2)}) async-start(bf16[16,56,2048]{2,1,0:T(8,128)(2,1)} %get-tuple-element.64), calls=%async_computation.2 | async-start | bytes 7340032 | tf_op jit(solution)/shard_map/all_to_all | solution.py:139
  137.6 192.1 %reduce-scatter.2.cloned.1.call-start = ((), (), s32[]{:S(2)}) async-start(), calls=%async_computation.10 | async-start | bytes 3538944 | tf_op jit(solution)/shard_map/reduce_scatter | solution.py:162
  219.8 23.0 %copy-start.8 = (bf16[12,896,128]{2,1,0:T(8,128)(2,1)}, bf16[12,896,128]{2,1,0:T(8,128)(2,1)S(1)}, u32[]{:S(2)}) copy-start(bf16[12,896,128]{2,1,0:T(8,128)(2,1)S(1)} %gather_fusion.6) | copy-start | bytes 8257540
  228.1 7.0 %copy-start.9 = (bf16[12,896,128]{2,1,0:T(8,128)(2,1)S(1)}, bf16[12,896,128]{2,1,0:T(8,128)(2,1)}, u32[]{:S(2)}) copy-start(bf16[12,896,128]{2,1,0:T(8,128)(2,1)} %gather_fusion.7) | copy-start | bytes 8257540
  228.2 7.0 %copy-start.10 = (bf16[1,3,12,128,128]{4,3,2,1,0:T(8,128)(2,1)S(1)}, bf16[1,3,12,128,128]{4,3,2,1,0:T(8,128)(2,1)}, u32[]{:S(2)}) copy-start(bf16[1,3,12,128,128]{4,3,2,1,0:T(8,128)(2,1)} %param.18) | copy-start | bytes 3538948
  261.7 4.8 copy-start.5
  269.0 4.8 copy-start.4
  276.4 3.9 copy-start.11
  276.4 3.9 copy-start.12
  280.3 4.6 slice-start
  282.0 3.5 slice-start.1
  303.0 36.7 %all-to-all-start.4 = ((bf16[16,56,1]{1,2,0:T(2,128)(2,1)}), bf16[16,56,1]{1,2,0:T(2,128)(2,1)S(1)}, u32[]{:S(2)}, u32[]{:S(2)}) async-start(bf16[16,56,1]{1,2,0:T(2,128)(2,1)} %convert_element_type.112), calls=%async_computation.4 | async-start | bytes 16384 | tf_op jit(solution)/shard_map/all_to_all | solution.py:157
  338.4 28.8 %copy-start.7 = (bf16[12,896,128]{2,1,0:T(8,128)(2,1)S(1)}, bf16[12,896,128]{2,1,0:T(8,128)(2,1)}, u32[]{:S(2)}) copy-start(bf16[12,896,128]{2,1,0:T(8,128)(2,1)} %gather_fusion.9) | copy-start | bytes 8257540
  362.6 33.9 %all-to-all-start.7 = ((f32[16,1,18432]{2,1,0:T(1,128)}), f32[16,1,18432]{2,1,0:T(1,128)}, u32[]{:S(2)}, u32[]{:S(2)}) async-start(f32[16,1,18432]{2,1,0:T(1,128)} %bitcast.242), calls=%async_computation.8 | async-start | bytes 2359296 | tf_op jit(solution)/shard_map/all_to_all | solution.py:90
  396.5 6.3 %copy-start.14 = (s32[16]{0:T(128)S(1)}, s32[16]{0:T(128)}, u32[]{:S(2)}) copy-start(s32[16]{0:T(128)} %param.21) | copy-start | bytes 196
  396.5 74.8 %all-to-all-start.3 = ((bf16[16,56,2048]{2,1,0:T(8,128)(2,1)}), bf16[16,56,2048]{2,1,0:T(8,128)(2,1)}, u32[]{:S(2)}, u32[]{:S(2)}) async-start(bf16[16,56,2048]{2,1,0:T(8,128)(2,1)} %convert_element_type.100), calls=%async_computation.3 | async-start | bytes 7340032 | tf_op jit(solution)/shard_map/all_to_all | solution.py:156
  471.3 33.1 %all-to-all-start.6 = ((bf16[16,2,9216]{2,1,0:T(2,128)(2,1)}), bf16[16,2,9216]{2,1,0:T(2,128)(2,1)S(1)}, u32[]{:S(2)}, u32[]{:S(2)}) async-start(bf16[16,2,9216]{2,1,0:T(2,128)(2,1)} %reshape.355), calls=%async_computation.7 | async-start | bytes 1179648 | tf_op jit(solution)/shard_map/all_to_all | solution.py:101
  504.4 33.4 %all-to-all-start.8 = ((f32[16,1,18432]{2,1,0:T(1,128)}), f32[16,1,18432]{2,1,0:T(1,128)}, u32[]{:S(2)}, u32[]{:S(2)}) async-start(f32[16,1,18432]{2,1,0:T(1,128)} %copy.129), calls=%async_computation.9 | async-start | bytes 2359296 | tf_op jit(solution)/shard_map/all_to_all | solution.py:102
  508.9 28.9 %all-gather.2.cloned.1.call-start = ((), (), s32[]{:S(2)}) async-start(), calls=%async_computation.11 | async-start | bytes 1769472 | tf_op jit(solution)/shard_map/all_gather | solution.py:171
  532.1 10.6 %copy-start.1 = (bf16[128,2048]{1,0:T(8,128)(2,1)S(1)}, bf16[128,2048]{1,0:T(8,128)(2,1)}, u32[]{:S(2)}) copy-start(bf16[128,2048]{1,0:T(8,128)(2,1)} %param.14) | copy-start | bytes 1572868
  (2 other events, 5.1 us)
Sparse Core Ops, SparseCore 0:
  282.1 47.5 reduce-scatter.1
  514.2 23.1 all-gather.1
where the time goes:
time: 557 us; the launch traced here: 550 us
  waiting for transfers between devices  143 us (26%)
  blocking collectives  110 us (20%)
  local copies, waits for them, and re-layouts  102 us (18%)
  matrix products  81.3 us (15%)
  starting transfers between devices  63.2 us (11%)
  other arithmetic  34.4 us (6%)
  between operations  14.9 us (3%)
    all_to_all x1, blocking collectives, body(): lax.all_to_all(send_grads, 'expert', split_axis=0, concat_axis=0, tiled=T...  87.1 us
    all_to_all x1, waiting for transfers between devices, body(): lax.all_to_all(input_grad, 'expert', split_axis=0, concat_axis=0, tiled=T...  61.6 us
    all_to_all x1, waiting for transfers between devices, body(): lax.all_to_all(send_tokens, 'expert', split_axis=0, concat_axis=0, tiled=...  59.3 us
    dot_general x6, matrix products, block_product(): jnp.einsum('rbn,bc->rcn', partial_out, select, precision=lax.Precision.HI...  56.3 us
    all_to_all x1, blocking collectives, relocate(): lax.all_to_all(first_state.reshape(expert_count, -1), 'expert', split_axi...  22.9 us
    gather x6, local copies, waits for them, and re-layouts, block_product(): jnp.take(left.reshape(row_count, -1, block_size), source_idx, axis=1)  22.5 us
    unnamed x48, local copies, waits for them, and re-layouts  20.3 us
    all_to_all x1, starting transfers between devices, relocate(): lax.all_to_all(first_moved, 'expert', split_axis=0, concat_axis=0, tiled=...  17.5 us
  transfers between devices with their start and end apart: 9, of which 4 were waited for; matrix products, arithmetic and copies ran while one was open for 22% of the time, Pallas kernels for 0%

commit v1 on v0

v1 whole, which is shorter than its diff:
```python
import functools

import jax
import jax.numpy as jnp
from jax import lax
from jax.experimental import pallas as pl
from jax.experimental.pallas import tpu as pltpu
from jax.sharding import PartitionSpec as P

HID = 1408
LANES = 128

momentum_decay = 0.9
step_rate = 0.01

NN = (((1,), (0,)), ((), ()))
NT = (((1,), (1,)), ((), ()))
TN = (((0,), (0,)), ((), ()))


def dot(left, right, dims):
    return lax.dot_general(left, right, dims, preferred_element_type=jnp.float32)


def expert_kernel(
    sources,
    slots,
    lay_ref,
    expert_ref,
    x_ref,
    g_ref,
    w_ref,
    t_ref,
    dw_ref,
    xs,
    gs,
    ss,
    gate,
    up,
    hid,
    hgrad,
    ggrad,
    ugrad,
    pgrad,
    pgrad_wide,
    prod,
):
    tok = LANES
    feat = xs.shape[0]
    hidden = gate.shape[0]
    width = feat * LANES
    count = w_ref.shape[0] // 3
    rows = sources * slots
    expert = expert_ref[0]
    token_row = lax.broadcasted_iota(jnp.int32, (tok, tok), 0)
    token_col = lax.broadcasted_iota(jnp.int32, (tok, tok), 1)
    earlier_row = (token_row < token_col).astype(jnp.bfloat16)
    earlier_col = (token_col < token_row).astype(jnp.bfloat16)
    table_lanes = x_ref.shape[1] - width
    lane_tok = lax.broadcasted_iota(jnp.int32, (tok, table_lanes), 1)
    lane_few = lax.broadcasted_iota(jnp.int32, (8, table_lanes), 1)
    own_few = (lane_few == expert).astype(jnp.bfloat16)
    slot_rows = lax.broadcasted_iota(jnp.int32, (slots, tok), 0).astype(jnp.float32)
    slot_cols = lax.broadcasted_iota(jnp.int32, (tok, slots), 1).astype(jnp.float32)

    @pl.when(pl.program_id(0) == 0)
    def _():
        dw_ref[...] = jnp.zeros_like(dw_ref)

    spread = []
    for s in range(sources):
        here = slice(s * tok, (s + 1) * tok)
        there = slice(s * slots, (s + 1) * slots)
        table = x_ref[here, width:]
        weight_row = dot(own_few, table, NT)[0:1]
        picked_row = weight_row > 0.0
        rank_row = dot(
            jnp.broadcast_to(picked_row, (8, tok)).astype(jnp.bfloat16), earlier_row, NN
        )[0:1]
        gather = jnp.where(
            jnp.logical_and(slot_rows == rank_row, picked_row), 1.0, 0.0
        )
        weight = jnp.sum(gather * weight_row, axis=1, keepdims=True)
        picked_col = jnp.max(
            jnp.where(lane_tok == expert, table.astype(jnp.float32), 0.0), axis=1, keepdims=True
        ) > 0.0
        rank_col = dot(
            earlier_col, jnp.broadcast_to(picked_col, (tok, tok)).astype(jnp.bfloat16), NN
        )[:, 0:1]
        spread.append(
            jnp.where(jnp.logical_and(slot_cols == rank_col, picked_col), 1.0, 0.0).astype(
                jnp.bfloat16
            )
        )
        gather = gather.astype(jnp.bfloat16)
        x_rows = dot(gather, x_ref[here, :width], NN).astype(jnp.bfloat16)
        g_rows = dot(gather, g_ref[here, :], NN)
        s_rows = (g_rows * weight).astype(jnp.bfloat16)
        g_rows = g_rows.astype(jnp.bfloat16)
        for c in range(feat):
            cut = slice(c * LANES, (c + 1) * LANES)
            xs[c, there, :] = x_rows[:, cut]
            gs[c, there, :] = g_rows[:, cut]
            ss[c, there, :] = s_rows[:, cut]

    gate[...] = jnp.zeros_like(gate)
    up[...] = jnp.zeros_like(up)
    hgrad[...] = jnp.zeros_like(hgrad)
    pgrad[...] = jnp.zeros_like(pgrad)

    def place(m, b):
        return lay_ref[2 * (m * count + b)], lay_ref[2 * (m * count + b) + 1]

    for b in range(count):
        r, c = place(0, b)
        gate[c] += dot(xs[r], w_ref[b], NN)
        r, c = place(1, b)
        up[c] += dot(xs[r], w_ref[count + b], NN)
        r, c = place(2, b)
        hgrad[r] += dot(ss[c], w_ref[2 * count + b], NT)
    for h in range(hidden):
        gate_pre = gate[h]
        up_pre = up[h]
        sig = jax.nn.sigmoid(gate_pre)
        activated = gate_pre * sig
        hid[h] = (activated * up_pre).astype(jnp.bfloat16)
        hidden_grad = hgrad[h]
        ggrad[h] = (hidden_grad * up_pre * sig * (1.0 + gate_pre * (1.0 - sig))).astype(
            jnp.bfloat16
        )
        ugrad[h] = (hidden_grad * activated).astype(jnp.bfloat16)
    prod[...] = jnp.zeros_like(prod)
    for b in range(count):
        r, c = place(0, b)
        pgrad[r] += dot(ggrad[c], w_ref[b], NT)
        dw_ref[b] += dot(xs[r], ggrad[c], TN)
        r, c = place(1, b)
        pgrad[r] += dot(ugrad[c], w_ref[count + b], NT)
        dw_ref[count + b] += dot(xs[r], ugrad[c], TN)
        r, c = place(2, b)
        prod[...] += dot(hid[r], w_ref[2 * count + b], NN) * gs[c].astype(jnp.float32)
        dw_ref[2 * count + b] += dot(hid[r], ss[c], TN)
    for c in range(feat):
        pgrad_wide[:, c * LANES : (c + 1) * LANES] = pgrad[c].astype(jnp.bfloat16)
    score = jnp.sum(prod[...], axis=1, keepdims=True).astype(jnp.bfloat16)
    own_lane = lax.broadcasted_iota(jnp.int32, (rows, table_lanes), 1) == expert
    pgrad_wide[:, width:] = jnp.where(
        own_lane, jnp.broadcast_to(score.astype(jnp.float32), (rows, table_lanes)), 0.0
    ).astype(jnp.bfloat16)
    for s in range(sources):
        t_ref[s * tok : (s + 1) * tok, :] = dot(
            spread[s], pgrad_wide[s * slots : (s + 1) * slots, :], NN
        ).astype(jnp.bfloat16)


def run_expert(x_all, g_all, mats, layout_one, expert, slots, sources):
    total_rows, table_width = x_all.shape
    width = g_all.shape[1]
    feat = width // LANES
    hidden = HID // LANES
    rows = sources * slots
    steps = total_rows // (sources * LANES)
    block_count = mats.shape[0]
    bf16, f32 = jnp.bfloat16, jnp.float32
    return pl.pallas_call(
        functools.partial(expert_kernel, sources, slots),
        grid=(steps,),
        in_specs=[
            pl.BlockSpec(memory_space=pltpu.SMEM),
            pl.BlockSpec(memory_space=pltpu.SMEM),
            pl.BlockSpec((sources * LANES, table_width), lambda i: (i, 0)),
            pl.BlockSpec((sources * LANES, width), lambda i: (i, 0)),
            pl.BlockSpec((block_count, LANES, LANES), lambda i: (0, 0, 0)),
        ],
        out_specs=[
            pl.BlockSpec((sources * LANES, table_width), lambda i: (i, 0)),
            pl.BlockSpec((block_count, LANES, LANES), lambda i: (0, 0, 0)),
        ],
        out_shape=[
            jax.ShapeDtypeStruct((total_rows, table_width), bf16),
            jax.ShapeDtypeStruct((block_count, LANES, LANES), f32),
        ],
        scratch_shapes=[
            pltpu.VMEM((feat, rows, LANES), bf16),
            pltpu.VMEM((feat, rows, LANES), bf16),
            pltpu.VMEM((feat, rows, LANES), bf16),
            pltpu.VMEM((hidden, rows, LANES), f32),
            pltpu.VMEM((hidden, rows, LANES), f32),
            pltpu.VMEM((hidden, rows, LANES), bf16),
            pltpu.VMEM((hidden, rows, LANES), f32),
            pltpu.VMEM((hidden, rows, LANES), bf16),
            pltpu.VMEM((hidden, rows, LANES), bf16),
            pltpu.VMEM((feat, rows, LANES), f32),
            pltpu.VMEM((rows, table_width), bf16),
            pltpu.VMEM((rows, LANES), f32),
        ],
        compiler_params=pltpu.CompilerParams(vmem_limit_bytes=56 * 1024 * 1024),
    )(layout_one, expert, x_all, g_all, mats)


def exchange(state, partner, expert_count):
    pieces = state.reshape(expert_count, -1, LANES)
    spread = lax.all_to_all(pieces, "expert", split_axis=0, concat_axis=0, tiled=True)
    moved = jnp.take(spread, partner, axis=0)
    collected = lax.all_to_all(moved, "expert", split_axis=0, concat_axis=0, tiled=True)
    return collected.reshape(state.shape)


def body(tokens, out_grad, expert_ids, route_weights, blocks, layout, moments, partner):
    expert_count = lax.axis_size("expert")
    replica_count = lax.axis_size("dp")
    tok_count, topk_count = expert_ids.shape
    width = tokens.shape[1]
    block_size = blocks.shape[-1]
    capacity = max(2, tok_count * topk_count * 7 // (expert_count * 6))
    slots = -(-capacity // 16) * 16
    sources = max(1, min(8, 256 // slots, expert_count))
    table_lanes = -(-expert_count // LANES) * LANES
    bf16, f32 = jnp.bfloat16, jnp.float32

    lane = jnp.arange(table_lanes, dtype=jnp.int32)
    named = expert_ids[:, :, None] == lane[None, None, :]
    table = jnp.sum(
        jnp.where(named, route_weights[:, :, None].astype(f32), 0.0), axis=1
    ).astype(bf16)
    me = lax.axis_index("expert")
    mine = partner[me].astype(jnp.int32)

    x_all = lax.all_gather(
        jnp.concatenate([tokens, table], axis=1), "expert", axis=0, tiled=True
    )
    row_share = block_size // replica_count
    own_rows = lax.dynamic_slice_in_dim(blocks[0], lax.axis_index("dp") * row_share, row_share, 2)
    moved_rows = exchange(own_rows, partner, expert_count)
    mats = lax.all_gather(moved_rows, "dp", axis=2, tiled=True)
    layouts = lax.all_gather(layout.reshape(1, -1), "expert", axis=0, tiled=True)
    layout_one = layouts[mine]
    g_all = lax.all_gather(out_grad, "expert", axis=0, tiled=True)
    moved_moments = exchange(moments[0].astype(bf16), partner, expert_count)

    part, weight_grad = run_expert(
        x_all,
        g_all,
        mats.reshape(-1, block_size, block_size),
        layout_one,
        mine.reshape(1),
        slots,
        sources,
    )
    total = lax.psum_scatter(part, "expert", scatter_dimension=0, tiled=True)
    token_grad = total[:, :width]
    scores = total[:, width:]
    route_grad = jnp.sum(
        jnp.where(named, scores[:, None, :].astype(f32), 0.0), axis=2
    ).astype(bf16)

    shard_grad = lax.psum_scatter(
        weight_grad.astype(bf16).reshape(mats.shape), "dp", scatter_dimension=2, tiled=True
    )
    new_moment = momentum_decay * moved_moments.astype(f32) + shard_grad.astype(f32)
    new_shard = (moved_rows.astype(f32) - step_rate * new_moment).astype(bf16)
    gathered = lax.all_gather(new_shard, "dp", axis=2, tiled=True)
    return (token_grad, route_grad, gathered[None], new_moment[None])


def solution(mesh):
    placed = (
        P(("dp", "expert"), None),
        P(("dp", "expert"), None),
        P(("dp", "expert"), None),
        P(("dp", "expert"), None),
        P("expert", None, None, None, None),
        P("expert", None, None, None),
        P("expert", None, None, "dp", None),
        P(),
    )
    return jax.shard_map(
        body,
        mesh=mesh,
        in_specs=placed,
        out_specs=(
            P(("dp", "expert"), None),
            P(("dp", "expert"), None),
            P("expert", None, None, None, None),
            P("expert", None, None, "dp", None),
        ),
        check_vma=False,
    )
```

time: 557 us -> 454 us (0.82); the launches traced: 550 us -> 454 us
  waiting for transfers between devices: 143 us -> 318 us
  local copies, waits for them, and re-layouts: 102 us -> 8.64 us
  matrix products: 81.3 us -> 0 us
  starting transfers between devices: 63.2 us -> 12 us
  blocking collectives: 110 us -> 60.4 us
  Pallas kernels: 0 us -> 28.8 us
  other arithmetic: 34.4 us -> 9.39 us
    all_gather x1 -> x4, waiting for transfers between devices: 0.01 us -> 175 us  [the longest x1 79.3 us: body(): lax.all_gather(jnp.concatenate([tokens, table], axis=1), 'expert', axis=0...]
    all_to_all x7 -> x2, waiting for transfers between devices: 134 us -> 29.4 us  [exchange(): lax.all_to_all(pieces, 'expert', split_axis=0, concat_axis=0, tiled=True)]
    reduce_scatter x1 -> x2, waiting for transfers between devices: 9.16 us -> 112 us  [the longest x1 112 us: body(): total = lax.psum_scatter(part, 'expert', scatter_dimension=0, tiled=True)]
    dot_general x15 -> x0, matrix products: 81.3 us -> none  [the longest x6 56.3 us: block_product(): jnp.einsum('rbn,bc->rcn', partial_out, select, precision=lax.Precision.HI...]
    all_to_all x2, blocking collectives: 110 us -> 41.8 us  [exchange(): lax.all_to_all(moved, 'expert', split_axis=0, concat_axis=0, tiled=True)]
    gather x13 -> x2, local copies, waits for them, and re-layouts: 54.2 us -> 1.33 us  [exchange(): moved = jnp.take(spread, partner, axis=0)]
    all_to_all x7 -> x2, starting transfers between devices: 63.1 us -> 11.8 us  [exchange(): lax.all_to_all(pieces, 'expert', split_axis=0, concat_axis=0, tiled=True)]
    pallas_call x0 -> x1, Pallas kernels: none -> 28.8 us  [run_expert(): pl.pallas_call(functools.partial(expert_kernel, sources, slots), grid=(st...]
  transfers between devices with their start and end apart: 9 -> 8, of which waited for: 4 -> 6; matrix products, arithmetic and copies ran while one was open for 22% -> 1% of each run, Pallas kernels for 0% -> 0%
where the time goes in v1:
time: 454 us
  waiting for transfers between devices  318 us (70%)
  blocking collectives  60.4 us (13%)
  Pallas kernels  28.8 us (6%)
  between operations  16.3 us (4%)
  starting transfers between devices  12 us (3%)
  other arithmetic  9.39 us (2%)
  local copies, waits for them, and re-layouts  8.64 us (2%)
    reduce_scatter x1, waiting for transfers between devices, body(): total = lax.psum_scatter(part, 'expert', scatter_dimension=0, tiled=True)  112 us
    all_gather x1, waiting for transfers between devices, body(): lax.all_gather(jnp.concatenate([tokens, table], axis=1), 'expert', axis=0...  79.3 us
    all_gather x1, waiting for transfers between devices, body(): g_all = lax.all_gather(out_grad, 'expert', axis=0, tiled=True)  74.4 us
    all_to_all x2, blocking collectives, exchange(): lax.all_to_all(moved, 'expert', split_axis=0, concat_axis=0, tiled=True)  41.8 us
    all_to_all x2, waiting for transfers between devices, exchange(): lax.all_to_all(pieces, 'expert', split_axis=0, concat_axis=0, tiled=True)  29.4 us
    pallas_call x1, Pallas kernels, run_expert(): pl.pallas_call(functools.partial(expert_kernel, sources, slots), grid=(st...  28.8 us
    all_gather x1, waiting for transfers between devices, body(): gathered = lax.all_gather(new_shard, 'dp', axis=2, tiled=True)  21.3 us
    all_gather x1, blocking collectives, body(): lax.all_gather(layout.reshape(1, -1), 'expert', axis=0, tiled=True)  18.6 us
  transfers between devices with their start and end apart: 8, of which 6 were waited for; matrix products, arithmetic and copies ran while one was open for 1% of the time, Pallas kernels for 0%

profile of v1, /device:TPU:0, one launch (start us, length us, event | category | flops | bytes accessed | tf_op | source)
XLA Modules:
  0.0 453.5 jit_solution(7238498459321380643)
XLA Ops:
  7.2 1.3 copy-done
  8.4 0.9 constant_dynamic-slice_fusion
  9.3 7.4 %all-to-all-start = ((bf16[16,144,128]{2,1,0:T(8,128)(2,1)}), bf16[16,144,128]{2,1,0:T(8,128)(2,1)S(1)}, u32[]{:S(2)}, u32[]{:S(2)}) async-start(bf16[16,144,128]{2,1,0:T(8,128)(2,1)} %bitcast.2), calls=%async_computation | async-start | bytes 1179648 | tf_op jit(solution)/shard_map/all_to_all | solution.py:203
  16.7 0.9 convert_element_type.42
  17.6 14.6 %all-to-all-done = bf16[16,144,128]{2,1,0:T(8,128)(2,1)S(1)} async-done(((bf16[16,144,128]{2,1,0:T(8,128)(2,1)}), bf16[16,144,128]{2,1,0:T(8,128)(2,1)S(1)}, u32[]{:S(2)}, u32[]{:S(2)}) %all-to-all-start) | async-done | bytes 589856 | tf_op jit(solution)/shard_map/all_to_all | solution.py:203
  32.2 4.4 all-to-all-start.2
  37.4 14.8 %all-to-all-done.2 = bf16[16,144,128]{2,1,0:T(8,128)(2,1)S(1)} async-done(((bf16[16,144,128]{2,1,0:T(8,128)(2,1)}), bf16[16,144,128]{2,1,0:T(8,128)(2,1)S(1)}, u32[]{:S(2)}, u32[]{:S(2)}) %all-to-all-start.2) | async-done | bytes 589856 | tf_op jit(solution)/shard_map/all_to_all | solution.py:203
  53.1 21.7 %all_to_all.20 = bf16[16,144,128]{2,1,0:T(8,128)(2,1)} all-to-all(bf16[16,144,128]{2,1,0:T(8,128)(2,1)S(1)} %get-tuple-element.12), channel_id=1, replica_groups=mesh['dp'=2,'expert'=16] {'expert'}, dimensions={0} | all-to-all | bytes 1179648 | tf_op jit(solution)/shard_map/all_to_all | solution.py:205
  74.9 0.7 all-gather.8.cloned.1.call-update
  76.0 0.9 pad_maximum_fusion
  79.7 18.6 %all-gather = s32[16,1,72]{2,1,0:T(1,128)S(1)} all-gather(s32[1,1,72]{2,1,0:T(1,128)S(1)} %reshape.65), channel_id=1, replica_groups=mesh['dp'=2,'expert'=16] {'expert'}, dimensions={0}, use_global_device_ids=true | all-gather | bytes 4896 | tf_op jit(solution)/shard_map/all_gather | solution.py:236
  98.8 74.4 %all-gather.8.cloned.1.call-done.g_ref = bf16[2048,2048]{1,0:T(8,128)(2,1)} async-done(((bf16[128,2048]{1,0:T(8,128)(2,1)}), bf16[2048,2048]{1,0:T(8,128)(2,1)}) %all-gather.8.cloned.1.call-update) | async-done | bytes 8388624 | tf_op jit(solution)/shard_map/all_gather | solution.py:238
  173.2 79.3 %all-gather.6.cloned.1.call-done.x_ref = bf16[2048,2176]{1,0:T(8,128)(2,1)} async-done(((bf16[128,2176]{1,0:T(8,128)(2,1)}), bf16[2048,2176]{1,0:T(8,128)(2,1)}) %all-gather.6.cloned.1.call-update) | async-done | bytes 8912912 | tf_op jit(solution)/shard_map/all_gather | solution.py:229
  252.5 28.8 %shard_map.111 = (bf16[2048,2176]{1,0:T(8,128)(2,1)}, f32[36,128,128]{2,1,0:T(8,128)}) custom-call(s32[72]{0:T(128)} %dynamic-slice_bitcast_fusion.lay_ref, s32[1]{0:T(128)} %dynamic_slice.9.expert_ref, bf16[2048,2176]{1,0:T(8,128)(2,1)} %all-gather.6.cloned.1.call-done.x_ref, bf16[2048,2048]{1,0:T(8,128)(2,1)} %all-gather.8.cloned.1.call-done.g_ref, ...), custom_call_target="tpu_custom_call" | custom-call | tf_op jit(solution)/shard_map/pallas_call | solution.py:165
  281.3 2.9 convert_element_type.45
  284.2 20.0 %all_to_all.21 = bf16[16,144,128]{2,1,0:T(8,128)(2,1)S(1)} all-to-all(bf16[16,144,128]{2,1,0:T(8,128)(2,1)S(1)} %get-tuple-element.11), channel_id=1, replica_groups=mesh['dp'=2,'expert'=16] {'expert'}, dimensions={0} | all-to-all | bytes 1179648 | tf_op jit(solution)/shard_map/all_to_all | solution.py:205
  304.4 0.9 copy-done.1
  305.4 2.6 fusion
  308.5 21.3 %all-gather.12.cloned.1.call-done = bf16[3,12,128,128]{3,2,1,0:T(8,128)(2,1)} async-done(((bf16[3,12,64,128]{3,2,1,0:T(8,128)(2,1)}), bf16[3,12,128,128]{3,2,1,0:T(8,128)(2,1)}) %all-gather.12.cloned.1.call-update) | async-done | bytes 1179664 | tf_op jit(solution)/shard_map/all_gather | solution.py:262
  329.8 112.3 %reduce-scatter.3.cloned.1.call-done = bf16[128,2176]{1,0:T(8,128)(2,1)} async-done(((bf16[2048,2176]{1,0:T(8,128)(2,1)}), bf16[128,2176]{1,0:T(8,128)(2,1)}) %reduce-scatter.3.cloned.1.call-update) | async-done | bytes 557072 | tf_op jit(solution)/shard_map/reduce_scatter | solution.py:250
  442.1 0.8 slice_convert_fusion
  442.9 0.9 select_reduce_fusion
  443.8 1.9 slice.12
  445.7 1.0 copy.23
  (42 shorter events, 4.1 us)
Async XLA Ops:
  7.2 1.3 copy-start
  8.4 8.2 %copy-start.2 = (f32[1,3,12,64,128]{4,3,2,1,0:T(8,128)S(1)}, f32[1,3,12,64,128]{4,3,2,1,0:T(8,128)}, u32[]{:S(2)}) copy-start(f32[1,3,12,64,128]{4,3,2,1,0:T(8,128)} %param.16) | copy-start | bytes 3538948
  9.3 22.9 %all-to-all-start = ((bf16[16,144,128]{2,1,0:T(8,128)(2,1)}), bf16[16,144,128]{2,1,0:T(8,128)(2,1)S(1)}, u32[]{:S(2)}, u32[]{:S(2)}) async-start(bf16[16,144,128]{2,1,0:T(8,128)(2,1)} %bitcast.2), calls=%async_computation | async-start | bytes 1179648 | tf_op jit(solution)/shard_map/all_to_all | solution.py:203
  16.7 20.0 %copy-start.8 = (s32[16]{0:T(128)S(1)}, s32[16]{0:T(128)}, u32[]{:S(2)}) copy-start(s32[16]{0:T(128)} %param.17) | copy-start | bytes 196
  32.2 20.0 %all-to-all-start.2 = ((bf16[16,144,128]{2,1,0:T(8,128)(2,1)}), bf16[16,144,128]{2,1,0:T(8,128)(2,1)S(1)}, u32[]{:S(2)}, u32[]{:S(2)}) async-start(bf16[16,144,128]{2,1,0:T(8,128)(2,1)} %bitcast.5), calls=%async_computation.3 | async-start | bytes 1179648 | tf_op jit(solution)/shard_map/all_to_all | solution.py:203
  36.7 62.1 %all-gather.10.cloned.1.call-start = ((), (), s32[]{:S(2)}) async-start(), calls=%async_computation.8 | async-start | bytes 1769472 | tf_op jit(solution)/shard_map/all_gather | solution.py:235
  53.0 22.6 %copy-start.7 = (bf16[128,6]{0,1:T(8,128)(2,1)S(1)}, bf16[128,6]{0,1:T(8,128)(2,1)}, u32[]{:S(2)}) copy-start(bf16[128,6]{0,1:T(8,128)(2,1)} %param.13) | copy-start | bytes 4612
  53.1 22.6 %copy-start.5 = (s32[128,6]{0,1:T(8,128)S(1)}, s32[128,6]{0,1:T(8,128)}, u32[]{:S(2)}) copy-start(s32[128,6]{0,1:T(8,128)} %param.12) | copy-start | bytes 9220
  53.1 22.9 %copy-start.4 = (bf16[128,2048]{1,0:T(8,128)(2,1)S(1)}, bf16[128,2048]{1,0:T(8,128)(2,1)}, u32[]{:S(2)}) copy-start(bf16[128,2048]{1,0:T(8,128)(2,1)} %param.10) | copy-start | bytes 1572868
  74.8 3.9 copy-start.6
  74.9 98.3 %all-gather.8.cloned.1.call-start = ((), (), s32[]{:S(2)}) async-start(), calls=%async_computation.7 | async-start | bytes 8912896 | tf_op jit(solution)/shard_map/all_gather | solution.py:238
  75.6 176.9 %all-gather.6.cloned.1.call-start = ((), (), s32[]{:S(2)}) async-start(), calls=%async_computation.6 | async-start | bytes 9469952 | tf_op jit(solution)/shard_map/all_gather | solution.py:229
  76.8 227.6 %reduce-scatter.5.cloned.1.call-start = ((), (), s32[]{:S(2)}) async-start(), calls=%async_computation.10 | async-start | bytes 1769472 | tf_op jit(solution)/shard_map/reduce_scatter | solution.py:257
  284.2 45.6 %all-gather.12.cloned.1.call-start = ((), (), s32[]{:S(2)}) async-start(), calls=%async_computation.11 | async-start | bytes 1769472 | tf_op jit(solution)/shard_map/all_gather | solution.py:262
  304.3 1.1 copy-start.1
  307.9 134.2 %reduce-scatter.3.cloned.1.call-start = ((), (), s32[]{:S(2)}) async-start(), calls=%async_computation.9 | async-start | bytes 9469952 | tf_op jit(solution)/shard_map/reduce_scatter | solution.py:250
  329.8 115.8 %copy-start.3 = (bf16[3,12,128,128]{3,2,1,0:T(8,128)(2,1)S(1)}, bf16[3,12,128,128]{3,2,1,0:T(8,128)(2,1)}, u32[]{:S(2)}) copy-start(bf16[3,12,128,128]{3,2,1,0:T(8,128)(2,1)} %all-gather.12.cloned.1.call-done) | copy-start | bytes 3538948
Sparse Core Ops, SparseCore 0:
  75.0 21.1 all-gather.9
  98.3 74.8 all-gather.7
  176.1 76.4 all-gather.5
  284.3 19.9 reduce-scatter.4
  308.1 21.7 all-gather.11
  334.3 107.7 reduce-scatter.2

commit v2 on v1

v2 whole, which is shorter than its diff:
```python
import functools

import jax
import jax.numpy as jnp
from jax import lax
from jax.experimental import pallas as pl
from jax.experimental.pallas import tpu as pltpu
from jax.sharding import PartitionSpec as P

HID = 1408
LANES = 128

momentum_decay = 0.9
step_rate = 0.01

NN = (((1,), (0,)), ((), ()))
NT = (((1,), (1,)), ((), ()))
TN = (((0,), (0,)), ((), ()))


def dot(left, right, dims):
    return lax.dot_general(left, right, dims, preferred_element_type=jnp.float32)


def expert_kernel(
    shards,
    slots,
    half,
    lay_ref,
    expert_ref,
    *refs,
):
    x_refs, refs = refs[:shards], refs[shards:]
    g_refs, refs = refs[:shards], refs[shards:]
    w_ref, refs = refs[0], refs[1:]
    low_refs, refs = refs[:shards], refs[shards:]
    high_refs, refs = refs[:shards], refs[shards:]
    (
        dw_ref,
        xs,
        gs,
        ss,
        gate,
        up,
        hid,
        hgrad,
        ggrad,
        ugrad,
        pgrad,
        wide,
        spread,
        prod,
    ) = refs
    tok = LANES
    feat = xs.shape[1]
    hidden = gate.shape[0]
    width = feat * LANES
    count = w_ref.shape[0] // 6
    rows = shards * slots
    table_lanes = x_refs[0].shape[1] - width
    token_row = lax.broadcasted_iota(jnp.int32, (tok, tok), 0)
    token_col = lax.broadcasted_iota(jnp.int32, (tok, tok), 1)
    earlier_row = (token_row < token_col).astype(jnp.bfloat16)
    earlier_col = (token_col < token_row).astype(jnp.bfloat16)
    lane_tok = lax.broadcasted_iota(jnp.int32, (tok, table_lanes), 1)
    lane_few = lax.broadcasted_iota(jnp.int32, (8, table_lanes), 1)
    slot_rows = lax.broadcasted_iota(jnp.int32, (slots, tok), 0).astype(jnp.float32)
    slot_cols = lax.broadcasted_iota(jnp.int32, (tok, slots), 1).astype(jnp.float32)

    for s in range(shards):
        there = slice(s * slots, (s + 1) * slots)
        table = x_refs[s][:, width:]
        gathers, weights = [], []
        for q in range(2):
            expert = expert_ref[q]
            weight_row = dot((lane_few == expert).astype(jnp.bfloat16), table, NT)[0:1]
            picked_row = weight_row > 0.0
            rank_row = dot(
                jnp.broadcast_to(picked_row, (8, tok)).astype(jnp.bfloat16), earlier_row, NN
            )[0:1]
            gather = jnp.where(jnp.logical_and(slot_rows == rank_row, picked_row), 1.0, 0.0)
            gathers.append(gather)
            weights.append(jnp.sum(gather * weight_row, axis=1, keepdims=True))
            picked_col = (
                jnp.max(
                    jnp.where(lane_tok == expert, table.astype(jnp.float32), 0.0),
                    axis=1,
                    keepdims=True,
                )
                > 0.0
            )
            rank_col = dot(
                earlier_col, jnp.broadcast_to(picked_col, (tok, tok)).astype(jnp.bfloat16), NN
            )[:, 0:1]
            spread[s, q] = jnp.where(
                jnp.logical_and(slot_cols == rank_col, picked_col), 1.0, 0.0
            ).astype(jnp.bfloat16)
        gather = jnp.concatenate(gathers, axis=0).astype(jnp.bfloat16)
        weight = jnp.concatenate(weights, axis=0)
        x_rows = dot(gather, x_refs[s][:, :width], NN).astype(jnp.bfloat16)
        g_rows = dot(gather, g_refs[s][...], NN)
        s_rows = (g_rows * weight).astype(jnp.bfloat16)
        g_rows = g_rows.astype(jnp.bfloat16)
        for q in range(2):
            own = slice(q * slots, (q + 1) * slots)
            for c in range(feat):
                cut = slice(c * LANES, (c + 1) * LANES)
                xs[q, c, there, :] = x_rows[own, cut]
                gs[q, c, there, :] = g_rows[own, cut]
                ss[q, c, there, :] = s_rows[own, cut]

    def one_expert(q, carry):
        gate[...] = jnp.zeros_like(gate)
        up[...] = jnp.zeros_like(up)
        hgrad[...] = jnp.zeros_like(hgrad)
        pgrad[...] = jnp.zeros_like(pgrad)
        first = q * (3 * count)

        def place(m, b):
            at = 2 * (first + m * count + b)
            return lay_ref[at], lay_ref[at + 1]

        for b in range(count):
            r, c = place(0, b)
            gate[c] += dot(xs[q, r], w_ref[first + b], NN)
            r, c = place(1, b)
            up[c] += dot(xs[q, r], w_ref[first + count + b], NN)
            r, c = place(2, b)
            hgrad[r] += dot(ss[q, c], w_ref[first + 2 * count + b], NT)
        for h in range(hidden):
            gate_pre = gate[h]
            up_pre = up[h]
            sig = jax.nn.sigmoid(gate_pre)
            activated = gate_pre * sig
            hid[h] = (activated * up_pre).astype(jnp.bfloat16)
            hidden_grad = hgrad[h]
            ggrad[h] = (hidden_grad * up_pre * sig * (1.0 + gate_pre * (1.0 - sig))).astype(
                jnp.bfloat16
            )
            ugrad[h] = (hidden_grad * activated).astype(jnp.bfloat16)
        prod[...] = jnp.zeros_like(prod)
        for b in range(count):
            r, c = place(0, b)
            pgrad[r] += dot(ggrad[c], w_ref[first + b], NT)
            dw_ref[first + b] = dot(xs[q, r], ggrad[c], TN)
            r, c = place(1, b)
            pgrad[r] += dot(ugrad[c], w_ref[first + count + b], NT)
            dw_ref[first + count + b] = dot(xs[q, r], ugrad[c], TN)
            r, c = place(2, b)
            prod[...] += dot(hid[r], w_ref[first + 2 * count + b], NN) * gs[q, c].astype(
                jnp.float32
            )
            dw_ref[first + 2 * count + b] = dot(hid[r], ss[q, c], TN)
        for s in range(shards):
            there = slice(s * slots, (s + 1) * slots)
            for c in range(feat):
                wide[s, q, :, c * LANES : (c + 1) * LANES] = pgrad[c, there, :].astype(
                    jnp.bfloat16
                )
            score = jnp.sum(prod[there, :], axis=1, keepdims=True).astype(jnp.bfloat16)
            own_lane = (
                lax.broadcasted_iota(jnp.int32, (slots, table_lanes), 1) == expert_ref[q]
            )
            wide[s, q, :, width:] = jnp.where(own_lane, score.astype(jnp.float32), 0.0).astype(
                jnp.bfloat16
            )
        return carry

    lax.fori_loop(0, 2, one_expert, 0)
    for s in range(shards):
        total = dot(spread[s, 0], wide[s, 0], NN) + dot(spread[s, 1], wide[s, 1], NN)
        low_refs[s][...] = total[:, :half].astype(jnp.bfloat16)
        high_refs[s][...] = total[:, half:].astype(jnp.bfloat16)


def run_experts(x_list, g_list, mats, layouts, experts, slots):
    shards = len(x_list)
    tok, table_width = x_list[0].shape
    width = g_list[0].shape[1]
    half = width // 2
    feat = width // LANES
    hidden = HID // LANES
    rows = shards * slots
    block_count = mats.shape[0]
    bf16, f32 = jnp.bfloat16, jnp.float32
    smem = pl.BlockSpec(memory_space=pltpu.SMEM)
    vmem = pl.BlockSpec(memory_space=pltpu.VMEM)
    outs = pl.pallas_call(
        functools.partial(expert_kernel, shards, slots, half),
        in_specs=[smem, smem] + [vmem] * (2 * shards + 1),
        out_specs=[vmem] * (2 * shards + 1),
        out_shape=[jax.ShapeDtypeStruct((tok, half), bf16)] * shards
        + [jax.ShapeDtypeStruct((tok, table_width - half), bf16)] * shards
        + [jax.ShapeDtypeStruct((block_count, LANES, LANES), f32)],
        scratch_shapes=[
            pltpu.VMEM((2, feat, rows, LANES), bf16),
            pltpu.VMEM((2, feat, rows, LANES), bf16),
            pltpu.VMEM((2, feat, rows, LANES), bf16),
            pltpu.VMEM((hidden, rows, LANES), f32),
            pltpu.VMEM((hidden, rows, LANES), f32),
            pltpu.VMEM((hidden, rows, LANES), bf16),
            pltpu.VMEM((hidden, rows, LANES), f32),
            pltpu.VMEM((hidden, rows, LANES), bf16),
            pltpu.VMEM((hidden, rows, LANES), bf16),
            pltpu.VMEM((feat, rows, LANES), f32),
            pltpu.VMEM((shards, 2, slots, table_width), bf16),
            pltpu.VMEM((shards, 2, tok, slots), bf16),
            pltpu.VMEM((rows, LANES), f32),
        ],
        compiler_params=pltpu.CompilerParams(vmem_limit_bytes=48 * 1024 * 1024),
        cost_estimate=pl.CostEstimate(
            flops=2 * 2 * 108 * rows * LANES * LANES * 4,
            bytes_accessed=shards * tok * table_width * 6 + block_count * LANES * LANES * 6,
            transcendentals=0,
        ),
    )(layouts, experts, *x_list, *g_list, mats)
    return outs[:shards], outs[shards : 2 * shards], outs[2 * shards]


def chip_ring(chips):
    tall, broad = 4, chips // 4
    walk = []
    for row in range(tall):
        columns = list(range(0 if row == 0 else 1, broad))
        walk += [(row, c) for c in (columns if row % 2 == 0 else columns[::-1])]
    walk += [(row, 0) for row in range(tall - 1, 0, -1)]
    return [row * broad + c for row, c in walk]


def spread_out(state, expert_count):
    pieces = state.reshape(expert_count, -1, LANES)
    return lax.all_to_all(pieces, "expert", split_axis=0, concat_axis=0, tiled=True)


def collect(spread, partner, shape):
    moved = jnp.take(spread, partner, axis=0)
    return lax.all_to_all(moved, "expert", split_axis=0, concat_axis=0, tiled=True).reshape(shape)


def body(tokens, out_grad, expert_ids, route_weights, blocks, layout, moments, partner):
    expert_count = lax.axis_size("expert")
    replica_count = lax.axis_size("dp")
    tok_count, topk_count = expert_ids.shape
    width = tokens.shape[1]
    block_size = blocks.shape[-1]
    capacity = max(2, tok_count * topk_count * 7 // (expert_count * 6))
    slots = -(-capacity // 16) * 16
    table_lanes = -(-expert_count // LANES) * LANES
    bf16, f32 = jnp.bfloat16, jnp.float32
    chips = expert_count // 2
    ring = chip_ring(chips)
    steps = list(zip(ring, ring[1:] + ring[:1]))
    onward = [(2 * a + core, 2 * b + core) for a, b in steps for core in range(2)]
    backward = [(b, a) for a, b in onward]
    sister = [(i, i ^ 1) for i in range(expert_count)]
    row_share = block_size // replica_count
    replica = lax.axis_index("dp")

    def step_on(value):
        return lax.ppermute(value, "expert", onward)

    def step_back(value):
        return lax.ppermute(value, "expert", backward)

    def own_rows(value):
        return lax.dynamic_slice_in_dim(value, replica * row_share, row_share, 2)

    def join_rows(rows):
        if replica_count != 2:
            return lax.all_gather(rows, "dp", axis=2, tiled=True)
        other = lax.ppermute(rows, "dp", [(0, 1), (1, 0)])
        first = replica == 0
        return jnp.concatenate(
            [jnp.where(first, rows, other), jnp.where(first, other, rows)], axis=2
        )

    def sum_rows(value):
        if replica_count != 2:
            return lax.psum_scatter(value, "dp", scatter_dimension=2, tiled=True).astype(f32)
        theirs = lax.dynamic_slice_in_dim(value, (1 - replica) * row_share, row_share, 2)
        other = lax.ppermute(theirs, "dp", [(0, 1), (1, 0)])
        return own_rows(value).astype(f32) + other.astype(f32)

    lane = jnp.arange(table_lanes, dtype=jnp.int32)
    named = expert_ids[:, :, None] == lane[None, None, :]
    table = jnp.sum(jnp.where(named, route_weights[:, :, None].astype(f32), 0.0), axis=1).astype(
        bf16
    )
    me = lax.axis_index("expert")
    slots_here = jnp.stack([me, me ^ 1])
    experts = jnp.take(partner, slots_here).astype(jnp.int32)

    x_at = {0: jnp.concatenate([tokens, table], axis=1)}
    g_at = {0: out_grad}
    most = chips // 2
    for s in range(1, most + 1):
        x_at[-s] = step_on(x_at[1 - s])
        g_at[s] = step_back(g_at[s - 1])
        if s < most:
            x_at[s] = step_back(x_at[s - 1])
            g_at[-s] = step_on(g_at[1 - s])
    x_at[most] = x_at[-most]

    rows_now = own_rows(blocks[0])
    moved_rows = collect(spread_out(rows_now, expert_count), partner, rows_now.shape)
    own_mats = join_rows(moved_rows)
    other_mats = lax.ppermute(own_mats, "expert", sister)
    square = (-1, block_size, block_size)
    mats = jnp.concatenate([own_mats.reshape(square), other_mats.reshape(square)], axis=0)
    layouts = lax.all_gather(layout.reshape(1, -1), "expert", axis=0, tiled=True)
    layouts = jnp.take(layouts, experts, axis=0).reshape(-1)
    moved_moments = collect(
        spread_out(moments[0].astype(bf16), expert_count), partner, rows_now.shape
    )

    near = [0]
    for s in range(1, most):
        near += [s, -s]
    near += [most]
    groups = [near[:-3], near[-3:]] if chips <= 8 else [near[i : i + 8] for i in range(0, chips, 8)]
    parts, weight_grad = {}, None
    for group in groups:
        lows, highs, grads = run_experts(
            [x_at[d] for d in group], [g_at[d] for d in group], mats, layouts, experts, slots
        )
        for d, low, high in zip(group, lows, highs):
            parts[d] = (low, high)
        weight_grad = grads if weight_grad is None else weight_grad + grads

    def add(left, right):
        return (left.astype(f32) + right.astype(f32)).astype(bf16)

    def carry_home(part, direction, move, include):
        held = parts[most][part] if include else parts[direction * (most - 1)][part]
        if include:
            held = move(held)
            held = add(held, parts[direction * (most - 1)][part])
        for s in range(most - 2, 0, -1):
            held = add(move(held), parts[direction * s][part])
        return move(held)

    homes = []
    for part in range(2):
        up_way = carry_home(part, 1, step_on, part == 0)
        down_way = carry_home(part, -1, step_back, part == 1)
        homes.append(
            (
                parts[0][part].astype(f32) + up_way.astype(f32) + down_way.astype(f32)
            ).astype(bf16)
        )
    half = homes[0].shape[1]
    token_grad = jnp.concatenate([homes[0], homes[1][:, : width - half]], axis=1)
    scores = homes[1][:, width - half :]
    route_grad = jnp.sum(jnp.where(named, scores[:, None, :].astype(f32), 0.0), axis=2).astype(bf16)

    own_grad, other_grad = jnp.split(weight_grad.astype(bf16), 2, axis=0)
    from_sister = lax.ppermute(other_grad, "expert", sister)
    chip_grad = add(own_grad, from_sister).reshape(blocks[0].shape)
    shard_grad = sum_rows(chip_grad)
    new_moment = momentum_decay * moved_moments.astype(f32) + shard_grad
    new_shard = (moved_rows.astype(f32) - step_rate * new_moment).astype(bf16)
    return (token_grad, route_grad, join_rows(new_shard)[None], new_moment[None])


def solution(mesh):
    placed = (
        P(("dp", "expert"), None),
        P(("dp", "expert"), None),
        P(("dp", "expert"), None),
        P(("dp", "expert"), None),
        P("expert", None, None, None, None),
        P("expert", None, None, None),
        P("expert", None, None, "dp", None),
        P(),
    )
    return jax.shard_map(
        body,
        mesh=mesh,
        in_specs=placed,
        out_specs=(
            P(("dp", "expert"), None),
            P(("dp", "expert"), None),
            P("expert", None, None, None, None),
            P("expert", None, None, "dp", None),
        ),
        check_vma=False,
    )
```

time: 454 us -> 276 us (0.61)
  waiting for transfers between devices: 318 us -> 128 us
  starting transfers between devices: 12 us -> 53.2 us
  blocking collectives: 60.4 us -> 35 us
  between operations: 16.3 us -> 1 us
  other arithmetic: 9.39 us -> 22.6 us
    all_gather x4 -> x0, waiting for transfers between devices: 175 us -> none  [the longest x1 79.3 us: body(): lax.all_gather(jnp.concatenate([tokens, table], axis=1), 'expert', axis=0...]
    reduce_scatter x2 -> x0, waiting for transfers between devices: 112 us -> none  [the longest x1 112 us: body(): total = lax.psum_scatter(part, 'expert', scatter_dimension=0, tiled=True)]
    ppermute x0 -> x33, waiting for transfers between devices: none -> 83.2 us  [the longest x14 46.6 us: step_back(): return lax.ppermute(value, 'expert', backward)]
    all_to_all x2 -> x0, blocking collectives: 41.8 us -> none  [exchange(): lax.all_to_all(moved, 'expert', split_axis=0, concat_axis=0, tiled=True)]
    ppermute x0 -> x33, starting transfers between devices: none -> 32.1 us  [the longest x14 20.4 us: step_back(): return lax.ppermute(value, 'expert', backward)]
    all_gather x1, blocking collectives: 18.6 us -> 35 us  [body(): lax.all_gather(layout.reshape(1, -1), 'expert', axis=0, tiled=True)]
    all_to_all x2 -> x4, waiting for transfers between devices: 29.4 us -> 44.8 us  [the longest x2 29.5 us: spread_out(): lax.all_to_all(pieces, 'expert', split_axis=0, concat_axis=0, tiled=True)]
    all_to_all x2 -> x4, starting transfers between devices: 11.8 us -> 21.1 us  [the longest x2 11.8 us: spread_out(): lax.all_to_all(pieces, 'expert', split_axis=0, concat_axis=0, tiled=True)]
  transfers between devices with their start and end apart: 8 -> 37, of which waited for: 6 -> 17; matrix products, arithmetic and copies ran while one was open for 1% -> 8% of each run, Pallas kernels for 0% -> 7%
where the time goes in v2:
time: 276 us; the launch traced here: 275 us
  waiting for transfers between devices  128 us (46%)
  starting transfers between devices  53.2 us (19%)
  blocking collectives  35 us (13%)
  Pallas kernels  30.6 us (11%)
  other arithmetic  22.6 us (8%)
  local copies, waits for them, and re-layouts  4.72 us (2%)
    ppermute x14, waiting for transfers between devices, step_back(): return lax.ppermute(value, 'expert', backward)  46.6 us
    all_gather x1, blocking collectives, body(): lax.all_gather(layout.reshape(1, -1), 'expert', axis=0, tiled=True)  35 us
    pallas_call x2, Pallas kernels, run_experts(): pl.pallas_call(functools.partial(expert_kernel, shards, slots, half), in_...  30.6 us
    all_to_all x2, waiting for transfers between devices, spread_out(): lax.all_to_all(pieces, 'expert', split_axis=0, concat_axis=0, tiled=True)  29.5 us
    ppermute x14, waiting for transfers between devices, step_on(): return lax.ppermute(value, 'expert', onward)  22.7 us
    ppermute x14, starting transfers between devices, step_back(): return lax.ppermute(value, 'expert', backward)  20.4 us
    all_to_all x2, waiting for transfers between devices, collect(): lax.all_to_all(moved, 'expert', split_axis=0, concat_axis=0, tiled=True)  15.3 us
    all_to_all x2, starting transfers between devices, spread_out(): lax.all_to_all(pieces, 'expert', split_axis=0, concat_axis=0, tiled=True)  11.8 us
  transfers between devices with their start and end apart: 37, of which 17 were waited for; matrix products, arithmetic and copies ran while one was open for 8% of the time, Pallas kernels for 7%

profile of v2, /device:TPU:0, one launch (start us, length us, event | category | flops | bytes accessed | tf_op | source)
XLA Modules:
  0.0 275.1 jit_solution(5997478382385118306)
XLA Ops:
  2.9 7.4 %all-to-all-start.2 = ((bf16[16,144,128]{2,1,0:T(8,128)(2,1)}), bf16[16,144,128]{2,1,0:T(8,128)(2,1)S(1)}, u32[]{:S(2)}, u32[]{:S(2)}) async-start(bf16[16,144,128]{2,1,0:T(8,128)(2,1)} %bitcast.12), calls=%async_computation.2 | async-start | bytes 1179648 | tf_op jit(solution)/shard_map/all_to_all | solution.py:232
  11.2 14.6 %all-to-all-done.2 = bf16[16,144,128]{2,1,0:T(8,128)(2,1)S(1)} async-done(((bf16[16,144,128]{2,1,0:T(8,128)(2,1)}), bf16[16,144,128]{2,1,0:T(8,128)(2,1)S(1)}, u32[]{:S(2)}, u32[]{:S(2)}) %all-to-all-start.2) | async-done | bytes 589856 | tf_op jit(solution)/shard_map/all_to_all | solution.py:232
  25.8 4.4 %all-to-all-start = ((bf16[16,144,128]{2,1,0:T(8,128)(2,1)}), bf16[16,144,128]{2,1,0:T(8,128)(2,1)S(1)}, u32[]{:S(2)}, u32[]{:S(2)}) async-start(bf16[16,144,128]{2,1,0:T(8,128)(2,1)} %bitcast.8), calls=%async_computation | async-start | bytes 1179648 | tf_op jit(solution)/shard_map/all_to_all | solution.py:232
  31.0 14.8 %all-to-all-done = bf16[16,144,128]{2,1,0:T(8,128)(2,1)S(1)} async-done(((bf16[16,144,128]{2,1,0:T(8,128)(2,1)}), bf16[16,144,128]{2,1,0:T(8,128)(2,1)S(1)}, u32[]{:S(2)}, u32[]{:S(2)}) %all-to-all-start) | async-done | bytes 589856 | tf_op jit(solution)/shard_map/all_to_all | solution.py:232
  47.7 4.6 %all-to-all-start.1 = ((bf16[16,144,128]{2,1,0:T(8,128)(2,1)}), bf16[16,144,128]{2,1,0:T(8,128)(2,1)}, u32[]{:S(2)}, u32[]{:S(2)}) async-start(bf16[16,144,128]{2,1,0:T(8,128)(2,1)} %get-tuple-element.50), calls=%async_computation.1 | async-start | bytes 1179648 | tf_op jit(solution)/shard_map/all_to_all | solution.py:237
  52.6 15.3 %all-to-all-done.1 = bf16[16,144,128]{2,1,0:T(8,128)(2,1)} async-done(((bf16[16,144,128]{2,1,0:T(8,128)(2,1)}), bf16[16,144,128]{2,1,0:T(8,128)(2,1)}, u32[]{:S(2)}, u32[]{:S(2)}) %all-to-all-start.1) | async-done | bytes 589856 | tf_op jit(solution)/shard_map/all_to_all | solution.py:237
  73.6 11.4 %collective-permute-done.4.refs_6_ = bf16[128,2048]{1,0:T(8,128)(2,1)S(1)} collective-permute-done((bf16[128,2048]{1,0:T(8,128)(2,1)S(1)}, bf16[128,2048]{1,0:T(8,128)(2,1)S(1)}, u32[]{:S(2)}, u32[]{:S(2)}) %collective-permute-start.4) | collective-permute-done | bytes 524320 | tf_op jit(solution)/shard_map/ppermute | solution.py:263
  87.2 4.7 %all-to-all-start.3 = ((bf16[16,144,128]{2,1,0:T(8,128)(2,1)}), bf16[16,144,128]{2,1,0:T(8,128)(2,1)}, u32[]{:S(2)}, u32[]{:S(2)}) async-start(bf16[16,144,128]{2,1,0:T(8,128)(2,1)} %get-tuple-element.49), calls=%async_computation.3 | async-start | bytes 1179648 | tf_op jit(solution)/shard_map/all_to_all | solution.py:237
  95.7 35.0 %all-gather = s32[16,1,72]{2,1,0:T(1,128)S(1)} all-gather(s32[1,1,72]{2,1,0:T(1,128)S(1)} %reshape.265), channel_id=1, replica_groups=mesh['dp'=2,'expert'=16] {'expert'}, dimensions={0}, use_global_device_ids=true | all-gather | bytes 4896 | tf_op jit(solution)/shard_map/all_gather | solution.py:310
  136.2 9.3 %collective-permute-done.7.refs_9_ = bf16[128,2048]{1,0:T(8,128)(2,1)} collective-permute-done((bf16[128,2048]{1,0:T(8,128)(2,1)S(1)}, bf16[128,2048]{1,0:T(8,128)(2,1)}, u32[]{:S(2)}, u32[]{:S(2)}) %collective-permute-start.7) | collective-permute-done | bytes 524320 | tf_op jit(solution)/shard_map/ppermute | solution.py:260
  149.3 9.7 %collective-permute-done.13.refs_3_ = bf16[128,2048]{1,0:T(8,128)(2,1)} collective-permute-done((bf16[128,2048]{1,0:T(8,128)(2,1)}, bf16[128,2048]{1,0:T(8,128)(2,1)}, u32[]{:S(2)}, u32[]{:S(2)}) %collective-permute-start.13) | collective-permute-done | bytes 524320 | tf_op jit(solution)/shard_map/ppermute | solution.py:263
  162.4 3.2 %pad_maximum_fusion.refs_10_.refs_6_ = bf16[72,128,128]{2,1,0:T(8,128)(2,1)} fusion(bf16[36,128,128]{2,1,0:T(8,128)(2,1)} %bitcast.11, bf16[36,128,128]{2,1,0:T(8,128)(2,1)} %bitcast.10), kind=kLoop, calls=%fused_computation.5 | loop fusion | flops 1179648 | bytes 4718592 | tf_op jit(solution)/shard_map/concatenate | solution.py:309
  165.6 3.1 %collective-permute-done.14.refs_4_ = bf16[128,2048]{1,0:T(8,128)(2,1)} collective-permute-done((bf16[128,2048]{1,0:T(8,128)(2,1)}, bf16[128,2048]{1,0:T(8,128)(2,1)}, u32[]{:S(2)}, u32[]{:S(2)}) %collective-permute-start.14) | collective-permute-done | bytes 524320 | tf_op jit(solution)/shard_map/ppermute | solution.py:260
  170.8 10.4 %collective-permute-done.15.refs_5_ = bf16[128,2048]{1,0:T(8,128)(2,1)} collective-permute-done((bf16[128,2048]{1,0:T(8,128)(2,1)}, bf16[128,2048]{1,0:T(8,128)(2,1)}, u32[]{:S(2)}, u32[]{:S(2)}) %collective-permute-start.15) | collective-permute-done | bytes 524320 | tf_op jit(solution)/shard_map/ppermute | solution.py:263
  181.2 12.5 %shard_map.112 = (bf16[128,1024]{1,0:T(8,128)(2,1)S(1)}, bf16[128,1024]{1,0:T(8,128)(2,1)S(1)}, bf16[128,1024]{1,0:T(8,128)(2,1)S(1)}, bf16[128,1152]{1,0:T(8,12...) custom-call(s32[144]{0:T(256)S(1)} %select_n.100.lay_ref, ...), custom_call_target="tpu_custom_call" | custom-call | flops 5435817984 | bytes 12091392 | tf_op jit(solution)/shard_map/pallas_call | solution.py:188
  197.8 18.1 %shard_map.111 = (bf16[128,1024]{1,0:T(8,128)(2,1)S(1)}, bf16[128,1024]{1,0:T(8,128)(2,1)S(1)}, bf16[128,1024]{1,0:T(8,128)(2,1)S(1)}, bf16[128,1024]{1,0:T(8,12...) custom-call(s32[144]{0:T(256)S(1)} %select_n.100.lay_ref, ...), custom_call_target="tpu_custom_call" | custom-call | flops 9059696640 | bytes 15433728 | tf_op jit(solution)/shard_map/pallas_call | solution.py:188
  216.0 4.8 %add_convert_fusion = bf16[72,128,128]{2,1,0:T(8,128)(2,1)S(1)} fusion(f32[72,128,128]{2,1,0:T(8,128)} %get-tuple-element.39, f32[72,128,128]{2,1,0:T(8,128)} %get-tuple-element.40), kind=kLoop, calls=%fused_computation.4 | loop fusion | flops 2359296 | bytes 11796480 | tf_op jit(solution)/shard_map/convert_element_type | solution.py:356
  225.6 4.7 %collective-permute-done.21 = bf16[128,1024]{1,0:T(8,128)(2,1)S(1)} collective-permute-done((bf16[128,1024]{1,0:T(8,128)(2,1)S(1)}, bf16[128,1024]{1,0:T(8,128)(2,1)S(1)}, u32[]{:S(2)}, u32[]{:S(2)}) %collective-permute-start.21) | collective-permute-done | bytes 262176 | tf_op jit(solution)/shard_map/ppermute | solution.py:263
  232.5 4.0 %collective-permute-done.27 = bf16[128,1152]{1,0:T(8,128)(2,1)S(1)} collective-permute-done((bf16[128,1152]{1,0:T(8,128)(2,1)S(1)}, bf16[128,1152]{1,0:T(8,128)(2,1)S(1)}, u32[]{:S(2)}, u32[]{:S(2)}) %collective-permute-start.27) | collective-permute-done | bytes 294944 | tf_op jit(solution)/shard_map/ppermute | solution.py:263
  238.9 5.0 %collective-permute-done.18 = bf16[128,1024]{1,0:T(8,128)(2,1)S(1)} collective-permute-done((bf16[128,1024]{1,0:T(8,128)(2,1)S(1)}, bf16[128,1024]{1,0:T(8,128)(2,1)S(1)}, u32[]{:S(2)}, u32[]{:S(2)}) %collective-permute-start.18) | collective-permute-done | bytes 262176 | tf_op jit(solution)/shard_map/ppermute | solution.py:260
  249.7 5.3 %collective-permute-done.19 = bf16[128,1024]{1,0:T(8,128)(2,1)S(1)} collective-permute-done((bf16[128,1024]{1,0:T(8,128)(2,1)S(1)}, bf16[128,1024]{1,0:T(8,128)(2,1)S(1)}, u32[]{:S(2)}, u32[]{:S(2)}) %collective-permute-start.19) | collective-permute-done | bytes 262176 | tf_op jit(solution)/shard_map/ppermute | solution.py:260
  255.2 3.6 %collective-permute-done.31 = bf16[3,12,64,128]{3,2,1,0:T(8,128)(2,1)S(1)} collective-permute-done((bf16[3,12,64,128]{3,2,1,0:T(8,128)(2,1)S(1)}, bf16[3,12,64,128]{3,2,1,0:T(8,128)(2,1)S(1)}, u32[]{:S(2)}, u32[]{:S(2)}) %collective-permute-start.31) | collective-permute-done | bytes 589856 | tf_op jit(solution)/shard_map/ppermute | solution.py:281
  258.8 2.5 fusion
  263.6 10.3 %collective-permute-done.32 = bf16[3,12,64,128]{3,2,1,0:T(8,128)(2,1)S(1)} collective-permute-done((bf16[3,12,64,128]{3,2,1,0:T(8,128)(2,1)S(1)}, bf16[3,12,64,128]{3,2,1,0:T(8,128)(2,1)S(1)}, u32[]{:S(2)}, u32[]{:S(2)}) %collective-permute-start.32) | collective-permute-done | bytes 589856 | tf_op jit(solution)/shard_map/ppermute | solution.py:271
  (126 shorter events, 55.4 us)
Async XLA Ops:
  2.9 22.9 %all-to-all-start.2 = ((bf16[16,144,128]{2,1,0:T(8,128)(2,1)}), bf16[16,144,128]{2,1,0:T(8,128)(2,1)S(1)}, u32[]{:S(2)}, u32[]{:S(2)}) async-start(bf16[16,144,128]{2,1,0:T(8,128)(2,1)} %bitcast.12), calls=%async_computation.2 | async-start | bytes 1179648 | tf_op jit(solution)/shard_map/all_to_all | solution.py:232
  25.8 20.0 %all-to-all-start = ((bf16[16,144,128]{2,1,0:T(8,128)(2,1)}), bf16[16,144,128]{2,1,0:T(8,128)(2,1)S(1)}, u32[]{:S(2)}, u32[]{:S(2)}) async-start(bf16[16,144,128]{2,1,0:T(8,128)(2,1)} %bitcast.8), calls=%async_computation | async-start | bytes 1179648 | tf_op jit(solution)/shard_map/all_to_all | solution.py:232
  47.7 20.2 %all-to-all-start.1 = ((bf16[16,144,128]{2,1,0:T(8,128)(2,1)}), bf16[16,144,128]{2,1,0:T(8,128)(2,1)}, u32[]{:S(2)}, u32[]{:S(2)}) async-start(bf16[16,144,128]{2,1,0:T(8,128)(2,1)} %get-tuple-element.50), calls=%async_computation.1 | async-start | bytes 1179648 | tf_op jit(solution)/shard_map/all_to_all | solution.py:237
  67.9 24.0 %collective-permute-start.8 = (bf16[3,12,64,128]{3,2,1,0:T(8,128)(2,1)}, bf16[3,12,64,128]{3,2,1,0:T(8,128)(2,1)}, u32[]{:S(2)}, u32[]{:S(2)}) collective-permute-start(bf16[3,12,64,128]{3,2,1,0:T(8,128)(2,1)} %bitcast.9), channel_id=1, source_target_pairs={{0,16},{16,0},{1,17},{17,1},{2,18},{18,2},{3,19},{19,3},{4,20},{20... | collective-permute-start | bytes 1769480 | tf_op jit(solution)/shard_map/ppermute | solution.py:271
  69.5 16.9 %collective-permute-start.1 = (bf16[128,2176]{1,0:T(8,128)(2,1)S(1)}, bf16[128,2176]{1,0:T(8,128)(2,1)}, u32[]{:S(2)}, u32[]{:S(2)}) collective-permute-start(bf16[128,2176]{1,0:T(8,128)(2,1)S(1)} %pad_maximum_fusion.2.refs_0_), channel_id=1, source_target_pairs={{0,2},{1,3},{2,6},{3,7},{6,10},{7,11},{10,14},{11,15},{14,12},{15,... | collective-permute-start | bytes 1671176 | tf_op jit(solution)/shard_map/ppermute | solution.py:260
  71.6 60.4 %collective-permute-start = (bf16[128,2176]{1,0:T(8,128)(2,1)S(1)}, bf16[128,2176]{1,0:T(8,128)(2,1)}, u32[]{:S(2)}, u32[]{:S(2)}) collective-permute-start(bf16[128,2176]{1,0:T(8,128)(2,1)S(1)} %pad_maximum_fusion.2.refs_0_), channel_id=1, source_target_pairs={{2,0},{3,1},{6,2},{7,3},{10,6},{11,7},{14,10},{15,11},{12,14},{13,... | collective-permute-start | bytes 1671176 | tf_op jit(solution)/shard_map/ppermute | solution.py:263
  72.9 57.7 %collective-permute-start.5 = (bf16[128,2048]{1,0:T(8,128)(2,1)S(1)}, bf16[128,2048]{1,0:T(8,128)(2,1)S(1)}, u32[]{:S(2)}, u32[]{:S(2)}) collective-permute-start(bf16[128,2048]{1,0:T(8,128)(2,1)S(1)} %copy-done.1), channel_id=1, source_target_pairs={{0,2},{1,3},{2,6},{3,7},{6,10},{7,11},{10,14},{11,15},{14,12},{15,... | collective-permute-start | bytes 1572872 | tf_op jit(solution)/shard_map/ppermute | solution.py:260
  85.0 48.5 %collective-permute-start.6 = (bf16[128,2048]{1,0:T(8,128)(2,1)S(1)}, bf16[128,2048]{1,0:T(8,128)(2,1)}, u32[]{:S(2)}, u32[]{:S(2)}) collective-permute-start(bf16[128,2048]{1,0:T(8,128)(2,1)S(1)} %collective-permute-done.4.refs_6_), channel_id=1, source_target_pairs={{2,0},{3,1},{6,2},{7,3},{10,6},{11,7},{14,10},{15,11},{12,14},{13,... | collective-permute-start | bytes 1572872 | tf_op jit(solution)/shard_map/ppermute | solution.py:263
  86.4 47.9 %collective-permute-start.3 = (bf16[128,2176]{1,0:T(8,128)(2,1)}, bf16[128,2176]{1,0:T(8,128)(2,1)}, u32[]{:S(2)}, u32[]{:S(2)}) collective-permute-start(bf16[128,2176]{1,0:T(8,128)(2,1)} %collective-permute-done.1.refs_2_), channel_id=1, source_target_pairs={{0,2},{1,3},{2,6},{3,7},{6,10},{7,11},{10,14},{11,15},{14,12},{15,... | collective-permute-start | bytes 1671176 | tf_op jit(solution)/shard_map/ppermute | solution.py:260
  87.2 74.0 %all-to-all-start.3 = ((bf16[16,144,128]{2,1,0:T(8,128)(2,1)}), bf16[16,144,128]{2,1,0:T(8,128)(2,1)}, u32[]{:S(2)}, u32[]{:S(2)}) async-start(bf16[16,144,128]{2,1,0:T(8,128)(2,1)} %get-tuple-element.49), calls=%async_computation.3 | async-start | bytes 1179648 | tf_op jit(solution)/shard_map/all_to_all | solution.py:237
  94.4 68.0 %collective-permute-start.9 = (bf16[3,12,128,128]{3,2,1,0:T(8,128)(2,1)}, bf16[3,12,128,128]{3,2,1,0:T(8,128)(2,1)}, u32[]{:S(2)}, u32[]{:S(2)}) collective-permute-start(bf16[3,12,128,128]{3,2,1,0:T(8,128)(2,1)} %pad_maximum_fusion.1), channel_id=1, source_target_pairs={{0,1},{1,0},{2,3},{3,2},{4,5},{5,4},{6,7},{7,6},{8,9},{9,8},{10,11... | collective-permute-start | bytes 3538952 | tf_op jit(solution)/shard_map/ppermute | solution.py:307
  133.5 25.5 %collective-permute-start.13 = (bf16[128,2048]{1,0:T(8,128)(2,1)}, bf16[128,2048]{1,0:T(8,128)(2,1)}, u32[]{:S(2)}, u32[]{:S(2)}) collective-permute-start(bf16[128,2048]{1,0:T(8,128)(2,1)} %collective-permute-done.6.refs_8_), channel_id=1, source_target_pairs={{2,0},{3,1},{6,2},{7,3},{10,6},{11,7},{14,10},{15,11},{12,14},{13,... | collective-permute-start | bytes 1572872 | tf_op jit(solution)/shard_map/ppermute | solution.py:263
  134.2 26.3 %collective-permute-start.11 = (bf16[128,2176]{1,0:T(8,128)(2,1)}, bf16[128,2176]{1,0:T(8,128)(2,1)S(1)}, u32[]{:S(2)}, u32[]{:S(2)}) collective-permute-start(bf16[128,2176]{1,0:T(8,128)(2,1)} %collective-permute-done.3.refs_4_), channel_id=1, source_target_pairs={{0,2},{1,3},{2,6},{3,7},{6,10},{7,11},{10,14},{11,15},{14,12},{15,... | collective-permute-start | bytes 1671176 | tf_op jit(solution)/shard_map/ppermute | solution.py:260
  145.5 23.2 %collective-permute-start.14 = (bf16[128,2048]{1,0:T(8,128)(2,1)}, bf16[128,2048]{1,0:T(8,128)(2,1)}, u32[]{:S(2)}, u32[]{:S(2)}) collective-permute-start(bf16[128,2048]{1,0:T(8,128)(2,1)} %collective-permute-done.7.refs_9_), channel_id=1, source_target_pairs={{0,2},{1,3},{2,6},{3,7},{6,10},{7,11},{10,14},{11,15},{14,12},{15,... | collective-permute-start | bytes 1572872 | tf_op jit(solution)/shard_map/ppermute | solution.py:260
  147.8 23.1 %collective-permute-start.10 = (bf16[128,2176]{1,0:T(8,128)(2,1)}, bf16[128,2176]{1,0:T(8,128)(2,1)S(1)}, u32[]{:S(2)}, u32[]{:S(2)}) collective-permute-start(bf16[128,2176]{1,0:T(8,128)(2,1)} %collective-permute-done.2.refs_3_), channel_id=1, source_target_pairs={{2,0},{3,1},{6,2},{7,3},{10,6},{11,7},{14,10},{15,11},{12,14},{13,... | collective-permute-start | bytes 1671176 | tf_op jit(solution)/shard_map/ppermute | solution.py:263
  159.0 22.2 %collective-permute-start.15 = (bf16[128,2048]{1,0:T(8,128)(2,1)}, bf16[128,2048]{1,0:T(8,128)(2,1)}, u32[]{:S(2)}, u32[]{:S(2)}) collective-permute-start(bf16[128,2048]{1,0:T(8,128)(2,1)} %collective-permute-done.13.refs_3_), channel_id=1, source_target_pairs={{2,0},{3,1},{6,2},{7,3},{10,6},{11,7},{14,10},{15,11},{12,14},{13,... | collective-permute-start | bytes 1572872 | tf_op jit(solution)/shard_map/ppermute | solution.py:263
  160.5 20.7 %collective-permute-start.12 = (bf16[128,2176]{1,0:T(8,128)(2,1)S(1)}, bf16[128,2176]{1,0:T(8,128)(2,1)S(1)}, u32[]{:S(2)}, u32[]{:S(2)}) collective-permute-start(bf16[128,2176]{1,0:T(8,128)(2,1)S(1)} %collective-permute-done.11.refs_1_), channel_id=1, source_target_pairs={{0,2},{1,3},{2,6},{3,7},{6,10},{7,11},{10,14},{11,15},{14,12},{15,... | collective-permute-start | bytes 1671176 | tf_op jit(solution)/shard_map/ppermute | solution.py:260
  193.7 29.5 %collective-permute-start.26 = (bf16[128,1152]{1,0:T(8,128)(2,1)S(1)}, bf16[128,1152]{1,0:T(8,128)(2,1)S(1)}, u32[]{:S(2)}, u32[]{:S(2)}) collective-permute-start(bf16[128,1152]{1,0:T(8,128)(2,1)S(1)} %get-tuple-element.35), channel_id=1, source_target_pairs={{2,0},{3,1},{6,2},{7,3},{10,6},{11,7},{14,10},{15,11},{12,14},{13,... | collective-permute-start | bytes 884744 | tf_op jit(solution)/shard_map/ppermute | solution.py:263
  195.3 29.7 %collective-permute-start.23 = (bf16[128,1152]{1,0:T(8,128)(2,1)S(1)}, bf16[128,1152]{1,0:T(8,128)(2,1)S(1)}, u32[]{:S(2)}, u32[]{:S(2)}) collective-permute-start(bf16[128,1152]{1,0:T(8,128)(2,1)S(1)} %get-tuple-element.32), channel_id=1, source_target_pairs={{0,2},{1,3},{2,6},{3,7},{6,10},{7,11},{10,14},{11,15},{14,12},{15,... | collective-permute-start | bytes 884744 | tf_op jit(solution)/shard_map/ppermute | solution.py:260
  195.8 25.2 %collective-permute-start.20 = (bf16[128,1024]{1,0:T(8,128)(2,1)S(1)}, bf16[128,1024]{1,0:T(8,128)(2,1)S(1)}, u32[]{:S(2)}, u32[]{:S(2)}) collective-permute-start(bf16[128,1024]{1,0:T(8,128)(2,1)S(1)} %get-tuple-element.28), channel_id=1, source_target_pairs={{2,0},{3,1},{6,2},{7,3},{10,6},{11,7},{14,10},{15,11},{12,14},{13,... | collective-permute-start | bytes 786440 | tf_op jit(solution)/shard_map/ppermute | solution.py:263
  197.3 25.3 %collective-permute-start.16 = (bf16[128,1024]{1,0:T(8,128)(2,1)S(1)}, bf16[128,1024]{1,0:T(8,128)(2,1)S(1)}, u32[]{:S(2)}, u32[]{:S(2)}) collective-permute-start(bf16[128,1024]{1,0:T(8,128)(2,1)S(1)} %get-tuple-element.24), channel_id=1, source_target_pairs={{0,2},{1,3},{2,6},{3,7},{6,10},{7,11},{10,14},{11,15},{14,12},{15,... | collective-permute-start | bytes 786440 | tf_op jit(solution)/shard_map/ppermute | solution.py:260
  220.9 23.6 %collective-permute-start.30 = (bf16[36,128,128]{2,1,0:T(8,128)(2,1)S(1)}, bf16[36,128,128]{2,1,0:T(8,128)(2,1)S(1)}, u32[]{:S(2)}, u32[]{:S(2)}) collective-permute-start(bf16[36,128,128]{2,1,0:T(8,128)(2,1)S(1)} %split.9), channel_id=1, source_target_pairs={{0,1},{1,0},{2,3},{3,2},{4,5},{5,4},{6,7},{7,6},{8,9},{9,8},{10,11... | collective-permute-start | bytes 3538952 | tf_op jit(solution)/shard_map/ppermute | solution.py:357
  230.3 19.4 %collective-permute-start.22 = (bf16[128,1024]{1,0:T(8,128)(2,1)S(1)}, bf16[128,1024]{1,0:T(8,128)(2,1)S(1)}, u32[]{:S(2)}, u32[]{:S(2)}) collective-permute-start(bf16[128,1024]{1,0:T(8,128)(2,1)S(1)} %add_convert_fusion.9), channel_id=1, source_target_pairs={{2,0},{3,1},{6,2},{7,3},{10,6},{11,7},{14,10},{15,11},{12,14},{13,... | collective-permute-start | bytes 786440 | tf_op jit(solution)/shard_map/ppermute | solution.py:263
  238.3 23.4 %collective-permute-start.25 = (bf16[128,1152]{1,0:T(8,128)(2,1)S(1)}, bf16[128,1152]{1,0:T(8,128)(2,1)S(1)}, u32[]{:S(2)}, u32[]{:S(2)}) collective-permute-start(bf16[128,1152]{1,0:T(8,128)(2,1)S(1)} %add_convert_fusion.6), channel_id=1, source_target_pairs={{0,2},{1,3},{2,6},{3,7},{6,10},{7,11},{10,14},{11,15},{14,12},{15,... | collective-permute-start | bytes 884744 | tf_op jit(solution)/shard_map/ppermute | solution.py:260
  (25 other events, 308.1 us)

commit v3 on v2

--- a/solution.py
+++ b/solution.py
@@ -26,17 +26,27 @@
     shards,
     slots,
     half,
+    pieces,
+    resumed,
+    final,
     lay_ref,
     expert_ref,
+    place_ref,
     *refs,
 ):
     x_refs, refs = refs[:shards], refs[shards:]
     g_refs, refs = refs[:shards], refs[shards:]
-    w_ref, refs = refs[0], refs[1:]
+    piece_refs, refs = refs[:pieces], refs[pieces:]
+    if resumed:
+        so_far_ref, refs = refs[0], refs[1:]
     low_refs, refs = refs[:shards], refs[shards:]
     high_refs, refs = refs[:shards], refs[shards:]
+    if final:
+        own_ref, other_ref, refs = refs[0], refs[1], refs[2:]
+    else:
+        dw_ref, refs = refs[0], refs[1:]
     (
-        dw_ref,
+        w_ref,
         xs,
         gs,
         ss,
@@ -67,6 +77,12 @@
     slot_rows = lax.broadcasted_iota(jnp.int32, (slots, tok), 0).astype(jnp.float32)
     slot_cols = lax.broadcasted_iota(jnp.int32, (tok, slots), 1).astype(jnp.float32)
 
+    in_expert = pieces // 2
+    for i, piece in enumerate(piece_refs):
+        q, rows_in = i // in_expert, piece.shape[1]
+        first = pl.multiple_of(place_ref[i % in_expert], 16)
+        w_ref[q * 3 * count : (q + 1) * 3 * count, pl.ds(first, rows_in), :] = piece[...]
+
     for s in range(shards):
         there = slice(s * slots, (s + 1) * slots)
         table = x_refs[s][:, width:]
@@ -116,6 +132,21 @@
         pgrad[...] = jnp.zeros_like(pgrad)
         first = q * (3 * count)
 
+        def keep(b, grad):
+            if resumed:
+                grad = grad + so_far_ref[first + b]
+            if not final:
+                dw_ref[first + b] = grad
+                return
+
+            @pl.when(q == 0)
+            def _():
+                own_ref[b] = grad.astype(jnp.bfloat16)
+
+            @pl.when(q == 1)
+            def _():
+                other_ref[b] = grad.astype(jnp.bfloat16)
+
         def place(m, b):
             at = 2 * (first + m * count + b)
             return lay_ref[at], lay_ref[at + 1]
@@ -142,15 +173,15 @@
         for b in range(count):
             r, c = place(0, b)
             pgrad[r] += dot(ggrad[c], w_ref[first + b], NT)
-            dw_ref[first + b] = dot(xs[q, r], ggrad[c], TN)
+            keep(b, dot(xs[q, r], ggrad[c], TN))
             r, c = place(1, b)
             pgrad[r] += dot(ugrad[c], w_ref[first + count + b], NT)
-            dw_ref[first + count + b] = dot(xs[q, r], ugrad[c], TN)
+            keep(count + b, dot(xs[q, r], ugrad[c], TN))
             r, c = place(2, b)
             prod[...] += dot(hid[r], w_ref[first + 2 * count + b], NN) * gs[q, c].astype(
                 jnp.float32
             )
-            dw_ref[first + 2 * count + b] = dot(hid[r], ss[q, c], TN)
+            keep(2 * count + b, dot(hid[r], ss[q, c], TN))
         for s in range(shards):
             there = slice(s * slots, (s + 1) * slots)
             for c in range(feat):
@@ -173,7 +204,7 @@
         high_refs[s][...] = total[:, half:].astype(jnp.bfloat16)
 
 
-def run_experts(x_list, g_list, mats, layouts, experts, slots):
+def run_experts(x_list, g_list, weights, places, layouts, experts, slots, so_far, final):
     shards = len(x_list)
     tok, table_width = x_list[0].shape
     width = g_list[0].shape[1]
@@ -181,18 +212,26 @@
     feat = width // LANES
     hidden = HID // LANES
     rows = shards * slots
-    block_count = mats.shape[0]
+    block_count = 2 * weights[0].shape[0]
+    resumed = so_far is not None
     bf16, f32 = jnp.bfloat16, jnp.float32
     smem = pl.BlockSpec(memory_space=pltpu.SMEM)
     vmem = pl.BlockSpec(memory_space=pltpu.VMEM)
+    grads = jax.ShapeDtypeStruct((block_count, LANES, LANES), f32)
+    one_grads = jax.ShapeDtypeStruct((block_count // 2, LANES, LANES), bf16)
+    grad_out = [one_grads, one_grads] if final else [grads]
+    operands = [*x_list, *g_list, *weights] + ([so_far] if resumed else [])
     outs = pl.pallas_call(
-        functools.partial(expert_kernel, shards, slots, half),
-        in_specs=[smem, smem] + [vmem] * (2 * shards + 1),
-        out_specs=[vmem] * (2 * shards + 1),
+        functools.partial(
+            expert_kernel, shards, slots, half, len(weights), resumed, final
+        ),
+        in_specs=[smem] * 3 + [vmem] * len(operands),
+        out_specs=[vmem] * (2 * shards + len(grad_out)),
         out_shape=[jax.ShapeDtypeStruct((tok, half), bf16)] * shards
         + [jax.ShapeDtypeStruct((tok, table_width - half), bf16)] * shards
-        + [jax.ShapeDtypeStruct((block_count, LANES, LANES), f32)],
+        + grad_out,
         scratch_shapes=[
+            pltpu.VMEM((block_count, LANES, LANES), bf16),
             pltpu.VMEM((2, feat, rows, LANES), bf16),
             pltpu.VMEM((2, feat, rows, LANES), bf16),
             pltpu.VMEM((2, feat, rows, LANES), bf16),
@@ -207,14 +246,14 @@
             pltpu.VMEM((shards, 2, tok, slots), bf16),
             pltpu.VMEM((rows, LANES), f32),
         ],
-        compiler_params=pltpu.CompilerParams(vmem_limit_bytes=48 * 1024 * 1024),
+        compiler_params=pltpu.CompilerParams(vmem_limit_bytes=44 * 1024 * 1024),
         cost_estimate=pl.CostEstimate(
             flops=2 * 2 * 108 * rows * LANES * LANES * 4,
             bytes_accessed=shards * tok * table_width * 6 + block_count * LANES * LANES * 6,
             transcendentals=0,
         ),
-    )(layouts, experts, *x_list, *g_list, mats)
-    return outs[:shards], outs[shards : 2 * shards], outs[2 * shards]
+    )(layouts, experts, places, *operands)
+    return outs[:shards], outs[shards : 2 * shards], outs[2 * shards :]
 
 
 def chip_ring(chips):
@@ -227,14 +266,8 @@
     return [row * broad + c for row, c in walk]
 
 
-def spread_out(state, expert_count):
-    pieces = state.reshape(expert_count, -1, LANES)
+def swap_all(pieces):
     return lax.all_to_all(pieces, "expert", split_axis=0, concat_axis=0, tiled=True)
-
-
-def collect(spread, partner, shape):
-    moved = jnp.take(spread, partner, axis=0)
-    return lax.all_to_all(moved, "expert", split_axis=0, concat_axis=0, tiled=True).reshape(shape)
 
 
 def body(tokens, out_grad, expert_ids, route_weights, blocks, layout, moments, partner):
@@ -265,21 +298,34 @@
     def own_rows(value):
         return lax.dynamic_slice_in_dim(value, replica * row_share, row_share, 2)
 
+    def other_replica(value):
+        return lax.ppermute(value, "dp", [(0, 1), (1, 0)])
+
+    def other_core(value):
+        return lax.ppermute(value, "expert", sister)
+
     def join_rows(rows):
         if replica_count != 2:
             return lax.all_gather(rows, "dp", axis=2, tiled=True)
-        other = lax.ppermute(rows, "dp", [(0, 1), (1, 0)])
-        first = replica == 0
-        return jnp.concatenate(
-            [jnp.where(first, rows, other), jnp.where(first, other, rows)], axis=2
-        )
-
-    def sum_rows(value):
+        mine_here = (jnp.arange(2, dtype=jnp.int32) == replica)[None, None, :, None, None]
+        both = jnp.where(mine_here, rows[:, :, None], other_replica(rows)[:, :, None])
+        return both.reshape(rows.shape[:2] + (block_size,) + rows.shape[3:])
+
+    def sum_rows(one, two):
         if replica_count != 2:
-            return lax.psum_scatter(value, "dp", scatter_dimension=2, tiled=True).astype(f32)
-        theirs = lax.dynamic_slice_in_dim(value, (1 - replica) * row_share, row_share, 2)
-        other = lax.ppermute(theirs, "dp", [(0, 1), (1, 0)])
-        return own_rows(value).astype(f32) + other.astype(f32)
+            return lax.psum_scatter(add(one, two), "dp", scatter_dimension=2, tiled=True).astype(f32)
+
+        def half_of(index):
+            return sum(
+                lax.dynamic_slice_in_dim(value, index * row_share, row_share, 2).astype(f32)
+                for value in (one, two)
+            )
+
+        theirs = other_replica(half_of(1 - replica).astype(bf16))
+        return half_of(replica) + theirs.astype(f32)
+
+    def add(left, right):
+        return (left.astype(f32) + right.astype(f32)).astype(bf16)
 
     lane = jnp.arange(table_lanes, dtype=jnp.int32)
     named = expert_ids[:, :, None] == lane[None, None, :]
@@ -291,44 +337,86 @@
     experts = jnp.take(partner, slots_here).astype(jnp.int32)
 
     x_at = {0: jnp.concatenate([tokens, table], axis=1)}
-    g_at = {0: out_grad}
     most = chips // 2
+    x_at[-1], x_at[1] = step_on(x_at[0]), step_back(x_at[0])
+    rows_now = own_rows(blocks[0])
+    x_at[-1], x_at[1], rows_ready, g_ready = lax.optimization_barrier(
+        (x_at[-1], x_at[1], rows_now, out_grad)
+    )
+
+    note_rows = 16
+    layout_flat = layout.reshape(-1)
+    layout_note = jnp.zeros((note_rows * LANES,), bf16).at[: layout_flat.shape[0]].set(
+        layout_flat.astype(bf16)
+    )
+    pieces = rows_ready.reshape(expert_count, -1, LANES)
+    piece_rows = pieces.shape[1]
+    pieces = jnp.concatenate(
+        [
+            pieces,
+            jnp.broadcast_to(
+                layout_note.reshape(1, note_rows, LANES), (expert_count, note_rows, LANES)
+            ),
+        ],
+        axis=1,
+    )
+    spread = swap_all(pieces)
+    layouts = spread[:, piece_rows:].reshape(expert_count, -1)[:, : layout_flat.shape[0]]
+    layouts = jnp.take(layouts, experts, axis=0).reshape(-1).astype(jnp.int32)
+    moved_rows = swap_all(jnp.take(spread[:, :piece_rows], partner, axis=0)).reshape(
+        rows_now.shape
+    )
+    moved_rows, moments_ready = lax.optimization_barrier((moved_rows, moments))
+    moment_pieces = moments_ready[0].astype(bf16).reshape(expert_count, -1, LANES)
+    moved_moments = swap_all(jnp.take(swap_all(moment_pieces), partner, axis=0)).reshape(
+        rows_now.shape
+    )
+
+    g_at = {0: g_ready}
     for s in range(1, most + 1):
-        x_at[-s] = step_on(x_at[1 - s])
+        if s > 1:
+            x_at[-s] = step_on(x_at[1 - s])
+            if s < most:
+                x_at[s] = step_back(x_at[s - 1])
         g_at[s] = step_back(g_at[s - 1])
         if s < most:
-            x_at[s] = step_back(x_at[s - 1])
             g_at[-s] = step_on(g_at[1 - s])
     x_at[most] = x_at[-most]
 
-    rows_now = own_rows(blocks[0])
-    moved_rows = collect(spread_out(rows_now, expert_count), partner, rows_now.shape)
-    own_mats = join_rows(moved_rows)
-    other_mats = lax.ppermute(own_mats, "expert", sister)
-    square = (-1, block_size, block_size)
-    mats = jnp.concatenate([own_mats.reshape(square), other_mats.reshape(square)], axis=0)
-    layouts = lax.all_gather(layout.reshape(1, -1), "expert", axis=0, tiled=True)
-    layouts = jnp.take(layouts, experts, axis=0).reshape(-1)
-    moved_moments = collect(
-        spread_out(moments[0].astype(bf16), expert_count), partner, rows_now.shape
-    )
+    if replica_count == 2:
+        halves = [moved_rows, other_replica(moved_rows)]
+        places = jnp.stack([replica * row_share, (1 - replica) * row_share]).astype(jnp.int32)
+    else:
+        halves = [join_rows(moved_rows)]
+        places = jnp.zeros((1,), jnp.int32)
+    weights = halves + [other_core(value) for value in halves]
+    weights = [value.reshape(-1, value.shape[2], LANES) for value in weights]
 
     near = [0]
     for s in range(1, most):
         near += [s, -s]
     near += [most]
-    groups = [near[:-3], near[-3:]] if chips <= 8 else [near[i : i + 8] for i in range(0, chips, 8)]
-    parts, weight_grad = {}, None
+    if chips <= 8:
+        groups = [near[:3], near[3:-1], near[-1:]]
+    else:
+        groups = [near[i : i + 8] for i in range(0, chips, 8)]
+    parts, sums = {}, [None]
     for group in groups:
-        lows, highs, grads = run_experts(
-            [x_at[d] for d in group], [g_at[d] for d in group], mats, layouts, experts, slots
+        lows, highs, sums = run_experts(
+            [x_at[d] for d in group],
+            [g_at[d] for d in group],
+            weights,
+            places,
+            layouts,
+            experts,
+            slots,
+            sums[0],
+            group is groups[-1],
         )
         for d, low, high in zip(group, lows, highs):
             parts[d] = (low, high)
-        weight_grad = grads if weight_grad is None else weight_grad + grads
-
-    def add(left, right):
-        return (left.astype(f32) + right.astype(f32)).astype(bf16)
+    own_grad, other_grad = (value.reshape(blocks[0].shape) for value in sums)
+    from_sister = other_core(other_grad)
 
     def carry_home(part, direction, move, include):
         held = parts[most][part] if include else parts[direction * (most - 1)][part]
@@ -353,10 +441,7 @@
     scores = homes[1][:, width - half :]
     route_grad = jnp.sum(jnp.where(named, scores[:, None, :].astype(f32), 0.0), axis=2).astype(bf16)
 
-    own_grad, other_grad = jnp.split(weight_grad.astype(bf16), 2, axis=0)
-    from_sister = lax.ppermute(other_grad, "expert", sister)
-    chip_grad = add(own_grad, from_sister).reshape(blocks[0].shape)
-    shard_grad = sum_rows(chip_grad)
+    shard_grad = sum_rows(own_grad, from_sister)
     new_moment = momentum_decay * moved_moments.astype(f32) + shard_grad
     new_shard = (moved_rows.astype(f32) - step_rate * new_moment).astype(bf16)
     return (token_grad, route_grad, join_rows(new_shard)[None], new_moment[None])

time: 276 us -> 273 us (0.989); the launches traced: 275 us -> 269 us
  blocking collectives: 35 us -> 0 us
  waiting for transfers between devices: 128 us -> 96.1 us
  starting transfers between devices: 53.2 us -> 76.3 us
  Pallas kernels: 30.6 us -> 48.2 us
  local copies, waits for them, and re-layouts: 4.72 us -> 20.9 us
  other arithmetic: 22.6 us -> 26.5 us
    ppermute x14, waiting for transfers between devices: 46.6 us -> 10.6 us  [step_back(): return lax.ppermute(value, 'expert', backward)]
    all_gather x1 -> x0, blocking collectives: 35 us -> none  [body(): lax.all_gather(layout.reshape(1, -1), 'expert', axis=0, tiled=True)]
    ppermute x14, waiting for transfers between devices: 22.7 us -> 44.7 us  [step_on(): return lax.ppermute(value, 'expert', onward)]
    pallas_call x2 -> x3, Pallas kernels: 30.6 us -> 48.2 us  [run_experts(): pl.pallas_call(functools.partial(expert_kernel, shards, slots, half, len(...]
    all_to_all x4, waiting for transfers between devices: 44.8 us -> 28.5 us  [swap_all(): lax.all_to_all(pieces, 'expert', split_axis=0, concat_axis=0, tiled=True)]
    ppermute x14, starting transfers between devices: 20.4 us -> 33.6 us  [step_back(): return lax.ppermute(value, 'expert', backward)]
    unnamed x26 -> x89, local copies, waits for them, and re-layouts: 1.06 us -> 12.1 us
    ppermute x14, starting transfers between devices: 8.69 us -> 16.7 us  [step_on(): return lax.ppermute(value, 'expert', onward)]
  transfers between devices with their start and end apart: 37 -> 38, of which waited for: 17 -> 17; matrix products, arithmetic and copies ran while one was open for 8% -> 10% of each run, Pallas kernels for 7% -> 18%
where the time goes in v3:
time: 273 us; the launch traced here: 269 us
  waiting for transfers between devices  96.1 us (35%)
  starting transfers between devices  76.3 us (28%)
  Pallas kernels  48.2 us (18%)
  other arithmetic  26.5 us (10%)
  local copies, waits for them, and re-layouts  20.9 us (8%)
    pallas_call x3, Pallas kernels, run_experts(): pl.pallas_call(functools.partial(expert_kernel, shards, slots, half, len(...  48.2 us
    ppermute x14, waiting for transfers between devices, step_on(): return lax.ppermute(value, 'expert', onward)  44.7 us
    ppermute x14, starting transfers between devices, step_back(): return lax.ppermute(value, 'expert', backward)  33.6 us
    all_to_all x4, waiting for transfers between devices, swap_all(): lax.all_to_all(pieces, 'expert', split_axis=0, concat_axis=0, tiled=True)  28.5 us
    all_to_all x4, starting transfers between devices, swap_all(): lax.all_to_all(pieces, 'expert', split_axis=0, concat_axis=0, tiled=True)  20.4 us
    ppermute x14, starting transfers between devices, step_on(): return lax.ppermute(value, 'expert', onward)  16.7 us
    ppermute x3, waiting for transfers between devices, other_replica(): return lax.ppermute(value, 'dp', [(0, 1), (1, 0)])  12.3 us
    unnamed x89, local copies, waits for them, and re-layouts  12.1 us
  transfers between devices with their start and end apart: 38, of which 17 were waited for; matrix products, arithmetic and copies ran while one was open for 10% of the time, Pallas kernels for 18%

profile of v3, /device:TPU:0, one launch (start us, length us, event | category | flops | bytes accessed | tf_op | source)
XLA Modules:
  0.0 269.2 jit_solution(12834539303271391722)
XLA Ops:
  7.6 11.5 %collective-permute-done.refs_2_ = bf16[128,2176]{1,0:T(8,128)(2,1)S(1)} collective-permute-done((bf16[128,2176]{1,0:T(8,128)(2,1)S(1)}, bf16[128,2176]{1,0:T(8,128)(2,1)S(1)}, u32[]{:S(2)}, u32[]{:S(2)}) %collective-permute-start) | collective-permute-done | bytes 557088 | tf_op jit(solution)/shard_map/ppermute | solution.py:293
  21.5 5.0 %all-to-all-start = ((bf16[16,160,128]{2,1,0:T(8,128)(2,1)}), bf16[16,160,128]{2,1,0:T(8,128)(2,1)S(1)}, u32[]{:S(2)}, u32[]{:S(2)}) async-start(bf16[16,160,128]{2,1,0:T(8,128)(2,1)} %pad_maximum_fusion), calls=%async_computation | async-start | bytes 1310720 | tf_op jit(solution)/shard_map/all_to_all | solution.py:270
  26.5 16.5 %all-to-all-done = bf16[16,160,128]{2,1,0:T(8,128)(2,1)S(1)} async-done(((bf16[16,160,128]{2,1,0:T(8,128)(2,1)}), bf16[16,160,128]{2,1,0:T(8,128)(2,1)S(1)}, u32[]{:S(2)}, u32[]{:S(2)}) %all-to-all-start) | async-done | bytes 655392 | tf_op jit(solution)/shard_map/all_to_all | solution.py:270
  46.7 4.8 %all-to-all-start.1 = ((bf16[16,144,128]{2,1,0:T(8,128)(2,1)}), bf16[16,144,128]{2,1,0:T(8,128)(2,1)S(1)}, u32[]{:S(2)}, u32[]{:S(2)}) async-start(bf16[16,144,128]{2,1,0:T(8,128)(2,1)} %broadcast_select_fusion.2), calls=%async_computation.1 | async-start | bytes 1179648 | tf_op jit(solution)/shard_map/all_to_all | solution.py:270
  55.4 12.0 %all-to-all-done.1 = bf16[16,144,128]{2,1,0:T(8,128)(2,1)S(1)} async-done(((bf16[16,144,128]{2,1,0:T(8,128)(2,1)}), bf16[16,144,128]{2,1,0:T(8,128)(2,1)S(1)}, u32[]{:S(2)}, u32[]{:S(2)}) %all-to-all-start.1) | async-done | bytes 589856 | tf_op jit(solution)/shard_map/all_to_all | solution.py:270
  69.9 3.6 %collective-permute-done.2.refs_4_ = bf16[128,2048]{1,0:T(8,128)(2,1)} collective-permute-done((bf16[128,2048]{1,0:T(8,128)(2,1)}, bf16[128,2048]{1,0:T(8,128)(2,1)}, u32[]{:S(2)}, u32[]{:S(2)}) %collective-permute-start.2) | collective-permute-done | bytes 524320 | tf_op jit(solution)/shard_map/ppermute | solution.py:296
  73.6 5.1 %collective-permute-start.10 = (bf16[128,2048]{1,0:T(8,128)(2,1)}, bf16[128,2048]{1,0:T(8,128)(2,1)}, u32[]{:S(2)}, u32[]{:S(2)}) collective-permute-start(bf16[128,2048]{1,0:T(8,128)(2,1)} %collective-permute-done.2.refs_4_), channel_id=1, source_target_pairs={{2,0},{3,1},{6,2},{7,3},{10,6},{11,7},{14,10},{15,11},{12,14},{13,... | collective-permute-start | bytes 1572872 | tf_op jit(solution)/shard_map/ppermute | solution.py:296
  79.4 8.0 %collective-permute-done.3.refs_5_ = bf16[128,2048]{1,0:T(8,128)(2,1)} collective-permute-done((bf16[128,2048]{1,0:T(8,128)(2,1)}, bf16[128,2048]{1,0:T(8,128)(2,1)}, u32[]{:S(2)}, u32[]{:S(2)}) %collective-permute-start.3) | collective-permute-done | bytes 524320 | tf_op jit(solution)/shard_map/ppermute | solution.py:293
  87.3 4.2 %collective-permute-start.8 = (bf16[128,2176]{1,0:T(8,128)(2,1)}, bf16[128,2176]{1,0:T(8,128)(2,1)}, u32[]{:S(2)}, u32[]{:S(2)}) collective-permute-start(bf16[128,2176]{1,0:T(8,128)(2,1)} %collective-permute-done.7.refs_1_), channel_id=1, source_target_pairs={{0,2},{1,3},{2,6},{3,7},{6,10},{7,11},{10,14},{11,15},{14,12},{15,... | collective-permute-start | bytes 1671176 | tf_op jit(solution)/shard_map/ppermute | solution.py:293
  92.7 3.8 %collective-permute-done.10.refs_4_ = bf16[128,2048]{1,0:T(8,128)(2,1)} collective-permute-done((bf16[128,2048]{1,0:T(8,128)(2,1)}, bf16[128,2048]{1,0:T(8,128)(2,1)}, u32[]{:S(2)}, u32[]{:S(2)}) %collective-permute-start.10) | collective-permute-done | bytes 524320 | tf_op jit(solution)/shard_map/ppermute | solution.py:296
  96.5 4.8 %collective-permute-start.11 = (bf16[128,2048]{1,0:T(8,128)(2,1)}, bf16[128,2048]{1,0:T(8,128)(2,1)}, u32[]{:S(2)}, u32[]{:S(2)}) collective-permute-start(bf16[128,2048]{1,0:T(8,128)(2,1)} %collective-permute-done.10.refs_4_), channel_id=1, source_target_pairs={{2,0},{3,1},{6,2},{7,3},{10,6},{11,7},{14,10},{15,11},{12,14},{13,... | collective-permute-start | bytes 1572872 | tf_op jit(solution)/shard_map/ppermute | solution.py:296
  107.2 8.8 %collective-permute-done.8.refs_3_ = bf16[128,2176]{1,0:T(8,128)(2,1)} collective-permute-done((bf16[128,2176]{1,0:T(8,128)(2,1)}, bf16[128,2176]{1,0:T(8,128)(2,1)}, u32[]{:S(2)}, u32[]{:S(2)}) %collective-permute-start.8) | collective-permute-done | bytes 557088 | tf_op jit(solution)/shard_map/ppermute | solution.py:293
  120.2 4.6 %all-to-all-start.2 = ((bf16[16,144,128]{2,1,0:T(8,128)(2,1)}), bf16[16,144,128]{2,1,0:T(8,128)(2,1)}, u32[]{:S(2)}, u32[]{:S(2)}) async-start(bf16[16,144,128]{2,1,0:T(8,128)(2,1)} %bitcast.57), calls=%async_computation.2 | async-start | bytes 1179648 | tf_op jit(solution)/shard_map/all_to_all | solution.py:270
  130.4 11.9 %shard_map.111 = (bf16[128,1024]{1,0:T(8,128)(2,1)S(1)}, bf16[128,1024]{1,0:T(8,128)(2,1)S(1)}, bf16[128,1024]{1,0:T(8,128)(2,1)S(1)}, bf16[128,1152]{1,0:T(8,12...) custom-call(s32[144]{0:T(256)S(1)} %reshape.298.lay_ref, ...), custom_call_target="tpu_custom_call" | custom-call | flops 5435817984 | bytes 12091392 | tf_op jit(solution)/shard_map/pallas_call | solution.py:224
  146.6 16.3 %shard_map.112 = (bf16[128,1024]{1,0:T(8,128)(2,1)S(1)}, bf16[128,1024]{1,0:T(8,128)(2,1)S(1)}, bf16[128,1024]{1,0:T(8,128)(2,1)S(1)}, bf16[128,1024]{1,0:T(8,12...) custom-call(s32[144]{0:T(256)S(1)} %reshape.298.lay_ref, ...), custom_call_target="tpu_custom_call" | custom-call | flops 7247757312 | bytes 13762560 | tf_op jit(solution)/shard_map/pallas_call | solution.py:224
  165.6 19.9 %shard_map.113 = (bf16[128,1024]{1,0:T(8,128)(2,1)}, bf16[128,1152]{1,0:T(8,128)(2,1)S(1)}, bf16[36,128,128]{2,1,0:T(8,128)(2,1)S(1)}, bf16[36,128,128]{2,1,0:T(8,128)(2,1)S(1)}) custom-call(s32[144]{0:T(256)S(1)} %reshape.298.lay_ref, s32[2]{0:T(128)S(1)} %get-tuple-element.70.expert_ref, s32[2]{0:T(128)S(1)} %pad_add_fusion.place_ref, ...), custom_call_target="tpu_custom_call" | custom-call | flops 1811939328 | bytes 8749056 | tf_op jit(solution)/shard_map/pallas_call | solution.py:224
  192.2 6.1 %all-to-all-start.3 = ((bf16[16,144,128]{2,1,0:T(8,128)(2,1)}), bf16[16,144,128]{2,1,0:T(8,128)(2,1)}, u32[]{:S(2)}, u32[]{:S(2)}) async-start(bf16[16,144,128]{2,1,0:T(8,128)(2,1)} %broadcast_select_fusion.1), calls=%async_computation.3 | async-start | bytes 1179648 | tf_op jit(solution)/shard_map/all_to_all | solution.py:270
  205.0 12.6 %collective-permute-done.24 = bf16[128,1152]{1,0:T(8,128)(2,1)S(1)} collective-permute-done((bf16[128,1152]{1,0:T(8,128)(2,1)}, bf16[128,1152]{1,0:T(8,128)(2,1)S(1)}, u32[]{:S(2)}, u32[]{:S(2)}) %collective-permute-start.24) | collective-permute-done | bytes 294944 | tf_op jit(solution)/shard_map/ppermute | solution.py:293
  217.9 4.7 %collective-permute-start.28 = (bf16[128,1152]{1,0:T(8,128)(2,1)S(1)}, bf16[128,1152]{1,0:T(8,128)(2,1)S(1)}, u32[]{:S(2)}, u32[]{:S(2)}) collective-permute-start(bf16[128,1152]{1,0:T(8,128)(2,1)S(1)} %add_convert_fusion.4), channel_id=1, source_target_pairs={{2,0},{3,1},{6,2},{7,3},{10,6},{11,7},{14,10},{15,11},{12,14},{13,... | collective-permute-start | bytes 884744 | tf_op jit(solution)/shard_map/ppermute | solution.py:296
  224.0 4.9 %collective-permute-start.23 = (bf16[128,1024]{1,0:T(8,128)(2,1)}, bf16[128,1024]{1,0:T(8,128)(2,1)}, u32[]{:S(2)}, u32[]{:S(2)}) collective-permute-start(bf16[128,1024]{1,0:T(8,128)(2,1)} %add_convert_fusion.8), channel_id=1, source_target_pairs={{2,0},{3,1},{6,2},{7,3},{10,6},{11,7},{14,10},{15,11},{12,14},{13,... | collective-permute-start | bytes 786440 | tf_op jit(solution)/shard_map/ppermute | solution.py:296
  230.3 4.2 %collective-permute-start.29 = (bf16[128,1152]{1,0:T(8,128)(2,1)S(1)}, bf16[128,1152]{1,0:T(8,128)(2,1)S(1)}, u32[]{:S(2)}, u32[]{:S(2)}) collective-permute-start(bf16[128,1152]{1,0:T(8,128)(2,1)S(1)} %add_convert_fusion.3), channel_id=1, source_target_pairs={{2,0},{3,1},{6,2},{7,3},{10,6},{11,7},{14,10},{15,11},{12,14},{13,... | collective-permute-start | bytes 884744 | tf_op jit(solution)/shard_map/ppermute | solution.py:296
  241.1 3.5 %collective-permute-start.30 = (bf16[128,1152]{1,0:T(8,128)(2,1)}, bf16[128,1152]{1,0:T(8,128)(2,1)}, u32[]{:S(2)}, u32[]{:S(2)}) collective-permute-start(bf16[128,1152]{1,0:T(8,128)(2,1)} %add_convert_fusion.2), channel_id=1, source_target_pairs={{2,0},{3,1},{6,2},{7,3},{10,6},{11,7},{14,10},{15,11},{12,14},{13,... | collective-permute-start | bytes 884744 | tf_op jit(solution)/shard_map/ppermute | solution.py:296
  247.9 3.6 %collective-permute-done.32 = bf16[3,12,64,128]{3,2,1,0:T(8,128)(2,1)} collective-permute-done((bf16[3,12,64,128]{3,2,1,0:T(8,128)(2,1)}, bf16[3,12,64,128]{3,2,1,0:T(8,128)(2,1)}, u32[]{:S(2)}, u32[]{:S(2)}) %collective-permute-start.32) | collective-permute-done | bytes 589856 | tf_op jit(solution)/shard_map/ppermute | solution.py:302
  258.6 8.7 %collective-permute-done.33 = bf16[3,12,64,128]{3,2,1,0:T(8,128)(2,1)S(1)} collective-permute-done((bf16[3,12,64,128]{3,2,1,0:T(8,128)(2,1)S(1)}, bf16[3,12,64,128]{3,2,1,0:T(8,128)(2,1)S(1)}, u32[]{:S(2)}, u32[]{:S(2)}) %collective-permute-start.33) | collective-permute-done | bytes 589856 | tf_op jit(solution)/shard_map/ppermute | solution.py:302
  (200 shorter events, 78.7 us)
Async XLA Ops:
  21.5 21.6 %all-to-all-start = ((bf16[16,160,128]{2,1,0:T(8,128)(2,1)}), bf16[16,160,128]{2,1,0:T(8,128)(2,1)S(1)}, u32[]{:S(2)}, u32[]{:S(2)}) async-start(bf16[16,160,128]{2,1,0:T(8,128)(2,1)} %pad_maximum_fusion), calls=%async_computation | async-start | bytes 1310720 | tf_op jit(solution)/shard_map/all_to_all | solution.py:270
  46.7 20.7 %all-to-all-start.1 = ((bf16[16,144,128]{2,1,0:T(8,128)(2,1)}), bf16[16,144,128]{2,1,0:T(8,128)(2,1)S(1)}, u32[]{:S(2)}, u32[]{:S(2)}) async-start(bf16[16,144,128]{2,1,0:T(8,128)(2,1)} %broadcast_select_fusion.2), calls=%async_computation.1 | async-start | bytes 1179648 | tf_op jit(solution)/shard_map/all_to_all | solution.py:270
  51.5 22.1 %collective-permute-start.2 = (bf16[128,2048]{1,0:T(8,128)(2,1)}, bf16[128,2048]{1,0:T(8,128)(2,1)}, u32[]{:S(2)}, u32[]{:S(2)}) collective-permute-start(bf16[128,2048]{1,0:T(8,128)(2,1)} %refs_3_), channel_id=1, source_target_pairs={{2,0},{3,1},{6,2},{7,3},{10,6},{11,7},{14,10},{15,11},{12,14},{13,... | collective-permute-start | bytes 1572872 | tf_op jit(solution)/shard_map/ppermute | solution.py:296
  53.4 34.0 %collective-permute-start.7 = (bf16[128,2176]{1,0:T(8,128)(2,1)S(1)}, bf16[128,2176]{1,0:T(8,128)(2,1)}, u32[]{:S(2)}, u32[]{:S(2)}) collective-permute-start(bf16[128,2176]{1,0:T(8,128)(2,1)S(1)} %collective-permute-done.refs_2_), channel_id=1, source_target_pairs={{0,2},{1,3},{2,6},{3,7},{6,10},{7,11},{10,14},{11,15},{14,12},{15,... | collective-permute-start | bytes 1671176 | tf_op jit(solution)/shard_map/ppermute | solution.py:293
  53.5 33.8 %collective-permute-start.3 = (bf16[128,2048]{1,0:T(8,128)(2,1)}, bf16[128,2048]{1,0:T(8,128)(2,1)}, u32[]{:S(2)}, u32[]{:S(2)}) collective-permute-start(bf16[128,2048]{1,0:T(8,128)(2,1)} %refs_3_), channel_id=1, source_target_pairs={{0,2},{1,3},{2,6},{3,7},{6,10},{7,11},{10,14},{11,15},{14,12},{15,... | collective-permute-start | bytes 1572872 | tf_op jit(solution)/shard_map/ppermute | solution.py:293
  67.4 24.3 %collective-permute-start.4 = (bf16[3,12,64,128]{3,2,1,0:T(8,128)(2,1)S(1)}, bf16[3,12,64,128]{3,2,1,0:T(8,128)(2,1)S(1)}, u32[]{:S(2)}, u32[]{:S(2)}) collective-permute-start(bf16[3,12,64,128]{3,2,1,0:T(8,128)(2,1)S(1)} %bitcast.36), channel_id=1, source_target_pairs={{0,16},{16,0},{1,17},{17,1},{2,18},{18,2},{3,19},{19,3},{4,20},{20... | collective-permute-start | bytes 1769480 | tf_op jit(solution)/shard_map/ppermute | solution.py:302
  68.9 22.7 %collective-permute-start.13 = (bf16[128,2176]{1,0:T(8,128)(2,1)S(1)}, bf16[128,2176]{1,0:T(8,128)(2,1)}, u32[]{:S(2)}, u32[]{:S(2)}) collective-permute-start(bf16[128,2176]{1,0:T(8,128)(2,1)S(1)} %collective-permute-done.1.refs_1_), channel_id=1, source_target_pairs={{2,0},{3,1},{6,2},{7,3},{10,6},{11,7},{14,10},{15,11},{12,14},{13,... | collective-permute-start | bytes 1671176 | tf_op jit(solution)/shard_map/ppermute | solution.py:296
  73.6 23.0 %collective-permute-start.10 = (bf16[128,2048]{1,0:T(8,128)(2,1)}, bf16[128,2048]{1,0:T(8,128)(2,1)}, u32[]{:S(2)}, u32[]{:S(2)}) collective-permute-start(bf16[128,2048]{1,0:T(8,128)(2,1)} %collective-permute-done.2.refs_4_), channel_id=1, source_target_pairs={{2,0},{3,1},{6,2},{7,3},{10,6},{11,7},{14,10},{15,11},{12,14},{13,... | collective-permute-start | bytes 1572872 | tf_op jit(solution)/shard_map/ppermute | solution.py:296
  87.3 28.6 %collective-permute-start.8 = (bf16[128,2176]{1,0:T(8,128)(2,1)}, bf16[128,2176]{1,0:T(8,128)(2,1)}, u32[]{:S(2)}, u32[]{:S(2)}) collective-permute-start(bf16[128,2176]{1,0:T(8,128)(2,1)} %collective-permute-done.7.refs_1_), channel_id=1, source_target_pairs={{0,2},{1,3},{2,6},{3,7},{6,10},{7,11},{10,14},{11,15},{14,12},{15,... | collective-permute-start | bytes 1671176 | tf_op jit(solution)/shard_map/ppermute | solution.py:293
  91.6 35.2 %collective-permute-start.5 = (bf16[3,12,64,128]{3,2,1,0:T(8,128)(2,1)S(1)}, bf16[3,12,64,128]{3,2,1,0:T(8,128)(2,1)S(1)}, u32[]{:S(2)}, u32[]{:S(2)}) collective-permute-start(bf16[3,12,64,128]{3,2,1,0:T(8,128)(2,1)S(1)} %bitcast.37), channel_id=1, source_target_pairs={{0,1},{1,0},{2,3},{3,2},{4,5},{5,4},{6,7},{7,6},{8,9},{9,8},{10,11... | collective-permute-start | bytes 1769480 | tf_op jit(solution)/shard_map/ppermute | solution.py:305
  91.7 35.3 %collective-permute-start.6 = (bf16[3,12,64,128]{3,2,1,0:T(8,128)(2,1)S(1)}, bf16[3,12,64,128]{3,2,1,0:T(8,128)(2,1)S(1)}, u32[]{:S(2)}, u32[]{:S(2)}) collective-permute-start(bf16[3,12,64,128]{3,2,1,0:T(8,128)(2,1)S(1)} %collective-permute-done.4), channel_id=1, source_target_pairs={{0,1},{1,0},{2,3},{3,2},{4,5},{5,4},{6,7},{7,6},{8,9},{9,8},{10,11... | collective-permute-start | bytes 1769480 | tf_op jit(solution)/shard_map/ppermute | solution.py:305
  96.5 28.3 %collective-permute-start.11 = (bf16[128,2048]{1,0:T(8,128)(2,1)}, bf16[128,2048]{1,0:T(8,128)(2,1)}, u32[]{:S(2)}, u32[]{:S(2)}) collective-permute-start(bf16[128,2048]{1,0:T(8,128)(2,1)} %collective-permute-done.10.refs_4_), channel_id=1, source_target_pairs={{2,0},{3,1},{6,2},{7,3},{10,6},{11,7},{14,10},{15,11},{12,14},{13,... | collective-permute-start | bytes 1572872 | tf_op jit(solution)/shard_map/ppermute | solution.py:296
  105.1 41.5 %collective-permute-start.14 = (bf16[128,2176]{1,0:T(8,128)(2,1)}, bf16[128,2176]{1,0:T(8,128)(2,1)}, u32[]{:S(2)}, u32[]{:S(2)}) collective-permute-start(bf16[128,2176]{1,0:T(8,128)(2,1)} %collective-permute-done.13.refs_0_), channel_id=1, source_target_pairs={{2,0},{3,1},{6,2},{7,3},{10,6},{11,7},{14,10},{15,11},{12,14},{13,... | collective-permute-start | bytes 1671176 | tf_op jit(solution)/shard_map/ppermute | solution.py:296
  116.0 30.6 %collective-permute-start.16 = (bf16[128,2048]{1,0:T(8,128)(2,1)}, bf16[128,2048]{1,0:T(8,128)(2,1)}, u32[]{:S(2)}, u32[]{:S(2)}) collective-permute-start(bf16[128,2048]{1,0:T(8,128)(2,1)} %collective-permute-done.15.refs_5_), channel_id=1, source_target_pairs={{0,2},{1,3},{2,6},{3,7},{6,10},{7,11},{10,14},{11,15},{14,12},{15,... | collective-permute-start | bytes 1572872 | tf_op jit(solution)/shard_map/ppermute | solution.py:293
  120.2 69.0 %all-to-all-start.2 = ((bf16[16,144,128]{2,1,0:T(8,128)(2,1)}), bf16[16,144,128]{2,1,0:T(8,128)(2,1)}, u32[]{:S(2)}, u32[]{:S(2)}) async-start(bf16[16,144,128]{2,1,0:T(8,128)(2,1)} %bitcast.57), calls=%async_computation.2 | async-start | bytes 1179648 | tf_op jit(solution)/shard_map/all_to_all | solution.py:270
  124.9 38.1 %collective-permute-start.9 = (bf16[128,2176]{1,0:T(8,128)(2,1)}, bf16[128,2176]{1,0:T(8,128)(2,1)S(1)}, u32[]{:S(2)}, u32[]{:S(2)}) collective-permute-start(bf16[128,2176]{1,0:T(8,128)(2,1)} %collective-permute-done.8.refs_3_), channel_id=1, source_target_pairs={{0,2},{1,3},{2,6},{3,7},{6,10},{7,11},{10,14},{11,15},{14,12},{15,... | collective-permute-start | bytes 1671176 | tf_op jit(solution)/shard_map/ppermute | solution.py:293
  126.8 36.2 %collective-permute-start.12 = (bf16[128,2048]{1,0:T(8,128)(2,1)}, bf16[128,2048]{1,0:T(8,128)(2,1)S(1)}, u32[]{:S(2)}, u32[]{:S(2)}) collective-permute-start(bf16[128,2048]{1,0:T(8,128)(2,1)} %collective-permute-done.11.refs_6_), channel_id=1, source_target_pairs={{2,0},{3,1},{6,2},{7,3},{10,6},{11,7},{14,10},{15,11},{12,14},{13,... | collective-permute-start | bytes 1572872 | tf_op jit(solution)/shard_map/ppermute | solution.py:296
  192.2 52.4 %all-to-all-start.3 = ((bf16[16,144,128]{2,1,0:T(8,128)(2,1)}), bf16[16,144,128]{2,1,0:T(8,128)(2,1)}, u32[]{:S(2)}, u32[]{:S(2)}) async-start(bf16[16,144,128]{2,1,0:T(8,128)(2,1)} %broadcast_select_fusion.1), calls=%async_computation.3 | async-start | bytes 1179648 | tf_op jit(solution)/shard_map/all_to_all | solution.py:270
  198.3 37.6 %collective-permute-start.31 = (bf16[3,12,128,128]{3,2,1,0:T(8,128)(2,1)}, bf16[3,12,128,128]{3,2,1,0:T(8,128)(2,1)S(1)}, u32[]{:S(2)}, u32[]{:S(2)}) collective-permute-start(bf16[3,12,128,128]{3,2,1,0:T(8,128)(2,1)} %bitcast.53), channel_id=1, source_target_pairs={{0,1},{1,0},{2,3},{3,2},{4,5},{5,4},{6,7},{7,6},{8,9},{9,8},{10,11... | collective-permute-start | bytes 3538952 | tf_op jit(solution)/shard_map/ppermute | solution.py:305
  198.6 19.0 %collective-permute-start.24 = (bf16[128,1152]{1,0:T(8,128)(2,1)}, bf16[128,1152]{1,0:T(8,128)(2,1)S(1)}, u32[]{:S(2)}, u32[]{:S(2)}) collective-permute-start(bf16[128,1152]{1,0:T(8,128)(2,1)} %copy-done.35), channel_id=1, source_target_pairs={{0,2},{1,3},{2,6},{3,7},{6,10},{7,11},{10,14},{11,15},{14,12},{15,... | collective-permute-start | bytes 884744 | tf_op jit(solution)/shard_map/ppermute | solution.py:293
  201.8 21.2 %collective-permute-start.18 = (bf16[128,1024]{1,0:T(8,128)(2,1)S(1)}, bf16[128,1024]{1,0:T(8,128)(2,1)S(1)}, u32[]{:S(2)}, u32[]{:S(2)}) collective-permute-start(bf16[128,1024]{1,0:T(8,128)(2,1)S(1)} %add_convert_fusion.12), channel_id=1, source_target_pairs={{0,2},{1,3},{2,6},{3,7},{6,10},{7,11},{10,14},{11,15},{14,12},{15,... | collective-permute-start | bytes 786440 | tf_op jit(solution)/shard_map/ppermute | solution.py:293
  204.6 18.6 %collective-permute-start.22 = (bf16[128,1024]{1,0:T(8,128)(2,1)S(1)}, bf16[128,1024]{1,0:T(8,128)(2,1)S(1)}, u32[]{:S(2)}, u32[]{:S(2)}) collective-permute-start(bf16[128,1024]{1,0:T(8,128)(2,1)S(1)} %add_convert_fusion.9), channel_id=1, source_target_pairs={{2,0},{3,1},{6,2},{7,3},{10,6},{11,7},{14,10},{15,11},{12,14},{13,... | collective-permute-start | bytes 786440 | tf_op jit(solution)/shard_map/ppermute | solution.py:296
  224.0 21.9 %collective-permute-start.23 = (bf16[128,1024]{1,0:T(8,128)(2,1)}, bf16[128,1024]{1,0:T(8,128)(2,1)}, u32[]{:S(2)}, u32[]{:S(2)}) collective-permute-start(bf16[128,1024]{1,0:T(8,128)(2,1)} %add_convert_fusion.8), channel_id=1, source_target_pairs={{2,0},{3,1},{6,2},{7,3},{10,6},{11,7},{14,10},{15,11},{12,14},{13,... | collective-permute-start | bytes 786440 | tf_op jit(solution)/shard_map/ppermute | solution.py:296
  230.2 25.5 %collective-permute-start.26 = (bf16[128,1152]{1,0:T(8,128)(2,1)S(1)}, bf16[128,1152]{1,0:T(8,128)(2,1)}, u32[]{:S(2)}, u32[]{:S(2)}) collective-permute-start(bf16[128,1152]{1,0:T(8,128)(2,1)S(1)} %add_convert_fusion.5), channel_id=1, source_target_pairs={{0,2},{1,3},{2,6},{3,7},{6,10},{7,11},{10,14},{11,15},{14,12},{15,... | collective-permute-start | bytes 884744 | tf_op jit(solution)/shard_map/ppermute | solution.py:293
  (58 other events, 680.3 us)

commit v4 on v3

--- a/solution.py
+++ b/solution.py
@@ -28,7 +28,6 @@
     half,
     pieces,
     resumed,
-    final,
     lay_ref,
     expert_ref,
     place_ref,
@@ -41,11 +40,8 @@
         so_far_ref, refs = refs[0], refs[1:]
     low_refs, refs = refs[:shards], refs[shards:]
     high_refs, refs = refs[:shards], refs[shards:]
-    if final:
-        own_ref, other_ref, refs = refs[0], refs[1], refs[2:]
-    else:
-        dw_ref, refs = refs[0], refs[1:]
     (
+        dw_ref,
         w_ref,
         xs,
         gs,
@@ -135,17 +131,7 @@
         def keep(b, grad):
             if resumed:
                 grad = grad + so_far_ref[first + b]
-            if not final:
-                dw_ref[first + b] = grad
-                return
-
-            @pl.when(q == 0)
-            def _():
-                own_ref[b] = grad.astype(jnp.bfloat16)
-
-            @pl.when(q == 1)
-            def _():
-                other_ref[b] = grad.astype(jnp.bfloat16)
+            dw_ref[first + b] = grad.astype(dw_ref.dtype)
 
         def place(m, b):
             at = 2 * (first + m * count + b)
@@ -217,19 +203,17 @@
     bf16, f32 = jnp.bfloat16, jnp.float32
     smem = pl.BlockSpec(memory_space=pltpu.SMEM)
     vmem = pl.BlockSpec(memory_space=pltpu.VMEM)
-    grads = jax.ShapeDtypeStruct((block_count, LANES, LANES), f32)
-    one_grads = jax.ShapeDtypeStruct((block_count // 2, LANES, LANES), bf16)
-    grad_out = [one_grads, one_grads] if final else [grads]
+    grads = jax.ShapeDtypeStruct((block_count, LANES, LANES), bf16 if final else f32)
     operands = [*x_list, *g_list, *weights] + ([so_far] if resumed else [])
     outs = pl.pallas_call(
         functools.partial(
-            expert_kernel, shards, slots, half, len(weights), resumed, final
+            expert_kernel, shards, slots, half, len(weights), resumed
         ),
         in_specs=[smem] * 3 + [vmem] * len(operands),
-        out_specs=[vmem] * (2 * shards + len(grad_out)),
+        out_specs=[vmem] * (2 * shards + 1),
         out_shape=[jax.ShapeDtypeStruct((tok, half), bf16)] * shards
         + [jax.ShapeDtypeStruct((tok, table_width - half), bf16)] * shards
-        + grad_out,
+        + [grads],
         scratch_shapes=[
             pltpu.VMEM((block_count, LANES, LANES), bf16),
             pltpu.VMEM((2, feat, rows, LANES), bf16),
@@ -253,7 +237,7 @@
             transcendentals=0,
         ),
     )(layouts, experts, places, *operands)
-    return outs[:shards], outs[shards : 2 * shards], outs[2 * shards :]
+    return outs[:shards], outs[shards : 2 * shards], outs[2 * shards]
 
 
 def chip_ring(chips):
@@ -336,62 +320,22 @@
     slots_here = jnp.stack([me, me ^ 1])
     experts = jnp.take(partner, slots_here).astype(jnp.int32)
 
-    x_at = {0: jnp.concatenate([tokens, table], axis=1)}
-    most = chips // 2
-    x_at[-1], x_at[1] = step_on(x_at[0]), step_back(x_at[0])
-    rows_now = own_rows(blocks[0])
-    x_at[-1], x_at[1], rows_ready, g_ready = lax.optimization_barrier(
-        (x_at[-1], x_at[1], rows_now, out_grad)
-    )
-
     note_rows = 16
     layout_flat = layout.reshape(-1)
     layout_note = jnp.zeros((note_rows * LANES,), bf16).at[: layout_flat.shape[0]].set(
         layout_flat.astype(bf16)
     )
-    pieces = rows_ready.reshape(expert_count, -1, LANES)
+    rows_now = own_rows(blocks[0])
+    pieces = rows_now.reshape(expert_count, -1, LANES)
     piece_rows = pieces.shape[1]
-    pieces = jnp.concatenate(
-        [
-            pieces,
-            jnp.broadcast_to(
-                layout_note.reshape(1, note_rows, LANES), (expert_count, note_rows, LANES)
-            ),
-        ],
-        axis=1,
+    note = jnp.broadcast_to(
+        layout_note.reshape(1, note_rows, LANES), (expert_count, note_rows, LANES)
     )
-    spread = swap_all(pieces)
-    layouts = spread[:, piece_rows:].reshape(expert_count, -1)[:, : layout_flat.shape[0]]
-    layouts = jnp.take(layouts, experts, axis=0).reshape(-1).astype(jnp.int32)
-    moved_rows = swap_all(jnp.take(spread[:, :piece_rows], partner, axis=0)).reshape(
-        rows_now.shape
-    )
-    moved_rows, moments_ready = lax.optimization_barrier((moved_rows, moments))
-    moment_pieces = moments_ready[0].astype(bf16).reshape(expert_count, -1, LANES)
-    moved_moments = swap_all(jnp.take(swap_all(moment_pieces), partner, axis=0)).reshape(
-        rows_now.shape
-    )
-
-    g_at = {0: g_ready}
-    for s in range(1, most + 1):
-        if s > 1:
-            x_at[-s] = step_on(x_at[1 - s])
-            if s < most:
-                x_at[s] = step_back(x_at[s - 1])
-        g_at[s] = step_back(g_at[s - 1])
-        if s < most:
-            g_at[-s] = step_on(g_at[1 - s])
-    x_at[most] = x_at[-most]
-
-    if replica_count == 2:
-        halves = [moved_rows, other_replica(moved_rows)]
-        places = jnp.stack([replica * row_share, (1 - replica) * row_share]).astype(jnp.int32)
-    else:
-        halves = [join_rows(moved_rows)]
-        places = jnp.zeros((1,), jnp.int32)
-    weights = halves + [other_core(value) for value in halves]
-    weights = [value.reshape(-1, value.shape[2], LANES) for value in weights]
-
+    state = {"pieces": jnp.concatenate([pieces, note], axis=1)}
+    moment_pieces = moments[0].astype(bf16).reshape(expert_count, -1, LANES)
+    x_at = {0: jnp.concatenate([tokens, table], axis=1)}
+    g_at = {0: out_grad}
+    most = chips // 2
     near = [0]
     for s in range(1, most):
         near += [s, -s]
@@ -400,50 +344,97 @@
         groups = [near[:3], near[3:-1], near[-1:]]
     else:
         groups = [near[i : i + 8] for i in range(0, chips, 8)]
-    parts, sums = {}, [None]
-    for group in groups:
+    parts = {}
+
+    def run_group(group, so_far):
         lows, highs, sums = run_experts(
             [x_at[d] for d in group],
             [g_at[d] for d in group],
-            weights,
+            state["weights"],
             places,
-            layouts,
+            state["layouts"],
             experts,
             slots,
-            sums[0],
+            so_far,
             group is groups[-1],
         )
         for d, low, high in zip(group, lows, highs):
             parts[d] = (low, high)
-    own_grad, other_grad = (value.reshape(blocks[0].shape) for value in sums)
-    from_sister = other_core(other_grad)
-
-    def carry_home(part, direction, move, include):
-        held = parts[most][part] if include else parts[direction * (most - 1)][part]
-        if include:
-            held = move(held)
-            held = add(held, parts[direction * (most - 1)][part])
-        for s in range(most - 2, 0, -1):
-            held = add(move(held), parts[direction * s][part])
-        return move(held)
-
-    homes = []
-    for part in range(2):
-        up_way = carry_home(part, 1, step_on, part == 0)
-        down_way = carry_home(part, -1, step_back, part == 1)
-        homes.append(
-            (
-                parts[0][part].astype(f32) + up_way.astype(f32) + down_way.astype(f32)
-            ).astype(bf16)
+        return sums
+
+    if replica_count == 2:
+        places = jnp.stack([replica * row_share, (1 - replica) * row_share]).astype(jnp.int32)
+    else:
+        places = jnp.zeros((1,), jnp.int32)
+    for s in range(1, most + 1):
+        x_at[-s] = step_on(x_at[1 - s])
+        g_at[s] = step_back(g_at[s - 1])
+        if s < most:
+            x_at[s] = step_back(x_at[s - 1])
+            g_at[-s] = step_on(g_at[1 - s])
+        if s == 1:
+            state["spread"] = swap_all(state.pop("pieces"))
+        elif s == 2:
+            spread = state.pop("spread")
+            layouts = spread[:, piece_rows:].reshape(expert_count, -1)[:, : layout_flat.shape[0]]
+            state["layouts"] = jnp.take(layouts, experts, axis=0).reshape(-1).astype(jnp.int32)
+            state["rows"] = swap_all(jnp.take(spread[:, :piece_rows], partner, axis=0)).reshape(
+                rows_now.shape
+            )
+        elif s == 3:
+            halves = [state["rows"]]
+            if replica_count == 2:
+                halves.append(other_replica(state["rows"]))
+            else:
+                halves = [join_rows(state["rows"])]
+            weights = halves + [other_core(value) for value in halves]
+            state["weights"] = [value.reshape(-1, value.shape[2], LANES) for value in weights]
+            state["moments"] = swap_all(moment_pieces)
+        elif s == 4:
+            state["sums"] = run_group(groups[0], None)
+        x_at, g_at, state, parts = lax.optimization_barrier((x_at, g_at, state, parts))
+    x_at[most] = x_at[-most]
+    sums = state["sums"]
+    moved_moments = swap_all(jnp.take(state["moments"], partner, axis=0)).reshape(rows_now.shape)
+    for group in groups[1:-1]:
+        sums = run_group(group, sums)
+    sums, moved_moments = lax.optimization_barrier((sums, moved_moments))
+    sums = run_group(groups[-1], sums)
+    half_count = sums.shape[0] // 2
+    own_grad = sums[:half_count].reshape(blocks[0].shape)
+    from_sister = other_core(sums[half_count:].reshape(blocks[0].shape))
+    moved_rows = state["rows"]
+
+    def own_share(distance, part):
+        return parts[distance][part]
+
+    upward = [step_on(own_share(most, 0)), None]
+    downward = [None, step_back(own_share(most, 1))]
+    for s in range(most - 1, 0, -1):
+        for part in range(2):
+            share = own_share(s, part)
+            upward[part] = step_on(share if upward[part] is None else add(upward[part], share))
+            share = own_share(-s, part)
+            downward[part] = step_back(
+                share if downward[part] is None else add(downward[part], share)
+            )
+        if s == most - 1:
+            upward[0], from_sister = lax.optimization_barrier((upward[0], from_sister))
+            shard_grad = sum_rows(own_grad, from_sister)
+        elif s == most - 2:
+            upward[0], shard_grad = lax.optimization_barrier((upward[0], shard_grad))
+            new_moment = momentum_decay * moved_moments.astype(f32) + shard_grad
+            new_shard = (moved_rows.astype(f32) - step_rate * new_moment).astype(bf16)
+    homes = [
+        (parts[0][part].astype(f32) + upward[part].astype(f32) + downward[part].astype(f32)).astype(
+            bf16
         )
+        for part in range(2)
+    ]
     half = homes[0].shape[1]
     token_grad = jnp.concatenate([homes[0], homes[1][:, : width - half]], axis=1)
     scores = homes[1][:, width - half :]
     route_grad = jnp.sum(jnp.where(named, scores[:, None, :].astype(f32), 0.0), axis=2).astype(bf16)
-
-    shard_grad = sum_rows(own_grad, from_sister)
-    new_moment = momentum_decay * moved_moments.astype(f32) + shard_grad
-    new_shard = (moved_rows.astype(f32) - step_rate * new_moment).astype(bf16)
     return (token_grad, route_grad, join_rows(new_shard)[None], new_moment[None])
 
 

time: 273 us -> 288 us (1.055)
  waiting for transfers between devices: 96.1 us -> 135 us
  Pallas kernels: 48.2 us -> 34.8 us
  local copies, waits for them, and re-layouts: 20.9 us -> 31.2 us
  starting transfers between devices: 76.3 us -> 66.5 us
  other arithmetic: 26.5 us -> 17.9 us
    ppermute x14, waiting for transfers between devices: 44.7 us -> 75 us  [step_on(): return lax.ppermute(value, 'expert', onward)]
    ppermute x14, waiting for transfers between devices: 10.6 us -> 40.8 us  [step_back(): return lax.ppermute(value, 'expert', backward)]
    all_to_all x4, waiting for transfers between devices: 28.5 us -> 0.01 us  [swap_all(): lax.all_to_all(pieces, 'expert', split_axis=0, concat_axis=0, tiled=True)]
    pallas_call x3, Pallas kernels: 48.2 us -> 34.8 us  [run_experts(): pl.pallas_call(functools.partial(expert_kernel, shards, slots, half, len(...]
    ppermute x14, starting transfers between devices: 33.6 us -> 24.1 us  [step_back(): return lax.ppermute(value, 'expert', backward)]
    unnamed x89 -> x101, local copies, waits for them, and re-layouts: 12.1 us -> 21.6 us
    ppermute x3, waiting for transfers between devices: 12.3 us -> 19.7 us  [other_replica(): return lax.ppermute(value, 'dp', [(0, 1), (1, 0)])]
    all_to_all x4, starting transfers between devices: 20.4 us -> 26.5 us  [swap_all(): lax.all_to_all(pieces, 'expert', split_axis=0, concat_axis=0, tiled=True)]
  transfers between devices with their start and end apart: 38 -> 38, of which waited for: 17 -> 16; matrix products, arithmetic and copies ran while one was open for 10% -> 5% of each run, Pallas kernels for 18% -> 12%
where the time goes in v4:
time: 288 us; the launch traced here: 287 us
  waiting for transfers between devices  135 us (47%)
  starting transfers between devices  66.5 us (23%)
  Pallas kernels  34.8 us (12%)
  local copies, waits for them, and re-layouts  31.2 us (11%)
  other arithmetic  17.9 us (6%)
    ppermute x14, waiting for transfers between devices, step_on(): return lax.ppermute(value, 'expert', onward)  75 us
    ppermute x14, waiting for transfers between devices, step_back(): return lax.ppermute(value, 'expert', backward)  40.8 us
    pallas_call x3, Pallas kernels, run_experts(): pl.pallas_call(functools.partial(expert_kernel, shards, slots, half, len(...  34.8 us
    all_to_all x4, starting transfers between devices, swap_all(): lax.all_to_all(pieces, 'expert', split_axis=0, concat_axis=0, tiled=True)  26.5 us
    ppermute x14, starting transfers between devices, step_back(): return lax.ppermute(value, 'expert', backward)  24.1 us
    unnamed x101, local copies, waits for them, and re-layouts  21.6 us
    ppermute x3, waiting for transfers between devices, other_replica(): return lax.ppermute(value, 'dp', [(0, 1), (1, 0)])  19.7 us
    ppermute x14, starting transfers between devices, step_on(): return lax.ppermute(value, 'expert', onward)  13.2 us
  transfers between devices with their start and end apart: 38, of which 16 were waited for; matrix products, arithmetic and copies ran while one was open for 5% of the time, Pallas kernels for 12%

profile of v4, /device:TPU:0, one launch (start us, length us, event | category | flops | bytes accessed | tf_op | source)
XLA Modules:
  0.0 287.0 jit_solution(12489941597697528367)
XLA Ops:
  2.9 7.5 %all-to-all-start = ((bf16[16,160,128]{2,1,0:T(8,128)(2,1)}), bf16[16,160,128]{2,1,0:T(8,128)(2,1)S(1)}, u32[]{:S(2)}, u32[]{:S(2)}) async-start(bf16[16,160,128]{2,1,0:T(8,128)(2,1)} %pad_maximum_fusion), calls=%async_computation | async-start | bytes 1310720 | tf_op jit(solution)/shard_map/all_to_all | solution.py:254
  15.8 20.1 %collective-permute-done.2.refs_5_ = bf16[128,2048]{1,0:T(8,128)(2,1)} collective-permute-done((bf16[128,2048]{1,0:T(8,128)(2,1)S(1)}, bf16[128,2048]{1,0:T(8,128)(2,1)}, u32[]{:S(2)}, u32[]{:S(2)}) %collective-permute-start.2) | collective-permute-done | bytes 524320 | tf_op jit(solution)/shard_map/ppermute | solution.py:277
  35.9 9.3 %collective-permute-done.1.refs_1_ = bf16[128,2176]{1,0:T(8,128)(2,1)S(1)} collective-permute-done((bf16[128,2176]{1,0:T(8,128)(2,1)S(1)}, bf16[128,2176]{1,0:T(8,128)(2,1)S(1)}, u32[]{:S(2)}, u32[]{:S(2)}) %collective-permute-start.1) | collective-permute-done | bytes 557088 | tf_op jit(solution)/shard_map/ppermute | solution.py:280
  50.9 7.5 %all-to-all-start.1 = ((bf16[16,144,128]{2,1,0:T(8,128)(2,1)}), bf16[16,144,128]{2,1,0:T(8,128)(2,1)S(1)}, u32[]{:S(2)}, u32[]{:S(2)}) async-start(bf16[16,144,128]{2,1,0:T(8,128)(2,1)} %broadcast_select_fusion.2), calls=%async_computation.1 | async-start | bytes 1179648 | tf_op jit(solution)/shard_map/all_to_all | solution.py:254
  64.1 18.7 %collective-permute-done.6.refs_5_ = bf16[128,2048]{1,0:T(8,128)(2,1)} collective-permute-done((bf16[128,2048]{1,0:T(8,128)(2,1)}, bf16[128,2048]{1,0:T(8,128)(2,1)}, u32[]{:S(2)}, u32[]{:S(2)}) %collective-permute-start.6) | collective-permute-done | bytes 524320 | tf_op jit(solution)/shard_map/ppermute | solution.py:277
  82.8 11.4 %collective-permute-done.4.refs_1_ = bf16[128,2176]{1,0:T(8,128)(2,1)S(1)} collective-permute-done((bf16[128,2176]{1,0:T(8,128)(2,1)S(1)}, bf16[128,2176]{1,0:T(8,128)(2,1)S(1)}, u32[]{:S(2)}, u32[]{:S(2)}) %collective-permute-start.4) | collective-permute-done | bytes 557088 | tf_op jit(solution)/shard_map/ppermute | solution.py:277
  98.0 7.1 %all-to-all-start.2 = ((bf16[16,144,128]{2,1,0:T(8,128)(2,1)}), bf16[16,144,128]{2,1,0:T(8,128)(2,1)}, u32[]{:S(2)}, u32[]{:S(2)}) async-start(bf16[16,144,128]{2,1,0:T(8,128)(2,1)} %bitcast.54), calls=%async_computation.2 | async-start | bytes 1179648 | tf_op jit(solution)/shard_map/all_to_all | solution.py:254
  110.6 3.2 %collective-permute-start.9 = (bf16[128,2176]{1,0:T(8,128)(2,1)}, bf16[128,2176]{1,0:T(8,128)(2,1)}, u32[]{:S(2)}, u32[]{:S(2)}) collective-permute-start(bf16[128,2176]{1,0:T(8,128)(2,1)} %collective-permute-done.5.refs_0_), channel_id=1, source_target_pairs={{2,0},{3,1},{6,2},{7,3},{10,6},{11,7},{14,10},{15,11},{12,14},{13,... | collective-permute-start | bytes 1671176 | tf_op jit(solution)/shard_map/ppermute | solution.py:280
  113.8 15.5 %collective-permute-done.10.refs_7_ = bf16[128,2048]{1,0:T(8,128)(2,1)S(1)} collective-permute-done((bf16[128,2048]{1,0:T(8,128)(2,1)}, bf16[128,2048]{1,0:T(8,128)(2,1)S(1)}, u32[]{:S(2)}, u32[]{:S(2)}) %collective-permute-start.10) | collective-permute-done | bytes 524320 | tf_op jit(solution)/shard_map/ppermute | solution.py:277
  130.1 4.7 %collective-permute-start.11 = (bf16[128,2048]{1,0:T(8,128)(2,1)}, bf16[128,2048]{1,0:T(8,128)(2,1)}, u32[]{:S(2)}, u32[]{:S(2)}) collective-permute-start(bf16[128,2048]{1,0:T(8,128)(2,1)} %collective-permute-done.7.refs_4_), channel_id=1, source_target_pairs={{2,0},{3,1},{6,2},{7,3},{10,6},{11,7},{14,10},{15,11},{12,14},{13,... | collective-permute-start | bytes 1572872 | tf_op jit(solution)/shard_map/ppermute | solution.py:280
  134.8 10.8 %collective-permute-done.11.refs_6_ = bf16[128,2048]{1,0:T(8,128)(2,1)} collective-permute-done((bf16[128,2048]{1,0:T(8,128)(2,1)}, bf16[128,2048]{1,0:T(8,128)(2,1)}, u32[]{:S(2)}, u32[]{:S(2)}) %collective-permute-start.11) | collective-permute-done | bytes 524320 | tf_op jit(solution)/shard_map/ppermute | solution.py:280
  145.6 2.5 collective-permute-start.16
  152.4 11.6 %shard_map.111 = (bf16[128,1024]{1,0:T(8,128)(2,1)S(1)}, bf16[128,1024]{1,0:T(8,128)(2,1)S(1)}, bf16[128,1024]{1,0:T(8,128)(2,1)S(1)}, bf16[128,1152]{1,0:T(8,12...) custom-call(s32[144]{0:T(256)S(1)} %reshape.299.lay_ref, ...), custom_call_target="tpu_custom_call" | custom-call | flops 5435817984 | bytes 12091392 | tf_op jit(solution)/shard_map/pallas_call | solution.py:208
  170.0 2.6 gather_fusion.3
  174.6 4.5 %all-to-all-start.3 = ((bf16[16,144,128]{2,1,0:T(8,128)(2,1)}), bf16[16,144,128]{2,1,0:T(8,128)(2,1)}, u32[]{:S(2)}, u32[]{:S(2)}) async-start(bf16[16,144,128]{2,1,0:T(8,128)(2,1)} %broadcast_select_fusion.1), calls=%async_computation.3 | async-start | bytes 1179648 | tf_op jit(solution)/shard_map/all_to_all | solution.py:254
  181.2 15.8 %shard_map.112 = (bf16[128,1024]{1,0:T(8,128)(2,1)S(1)}, bf16[128,1024]{1,0:T(8,128)(2,1)S(1)}, bf16[128,1024]{1,0:T(8,128)(2,1)S(1)}, bf16[128,1024]{1,0:T(8,12...) custom-call(s32[144]{0:T(256)S(1)} %reshape.299.lay_ref, ...), custom_call_target="tpu_custom_call" | custom-call | flops 7247757312 | bytes 13762560 | tf_op jit(solution)/shard_map/pallas_call | solution.py:208
  205.9 4.9 %collective-permute-done.23 = bf16[128,1024]{1,0:T(8,128)(2,1)} collective-permute-done((bf16[128,1024]{1,0:T(8,128)(2,1)}, bf16[128,1024]{1,0:T(8,128)(2,1)}, u32[]{:S(2)}, u32[]{:S(2)}) %collective-permute-start.23) | collective-permute-done | bytes 262176 | tf_op jit(solution)/shard_map/ppermute | solution.py:280
  216.4 7.3 %shard_map.113 = (bf16[128,1024]{1,0:T(8,128)(2,1)S(1)}, bf16[128,1152]{1,0:T(8,128)(2,1)S(1)}, bf16[72,128,128]{2,1,0:T(8,128)(2,1)S(1)}) custom-call(s32[144]{0:T(256)S(1)} %reshape.299.lay_ref, s32[2]{0:T(128)S(1)} %get-tuple-element.196.expert_ref, s32[2]{0:T(128)S(1)} %pad_add_fusion.place_ref, bf16[128,2176]{1,0:T(8,128)(2,1)S(1)} %copy-done.2, ...), custom_call_target="tpu_custom_call" | custom-call | flops 1811939328 | bytes 8749056 | tf_op jit(solution)/shard_map/pallas_call | solution.py:208
  230.0 3.7 %collective-permute-done.29 = bf16[128,1152]{1,0:T(8,128)(2,1)S(1)} collective-permute-done((bf16[128,1152]{1,0:T(8,128)(2,1)S(1)}, bf16[128,1152]{1,0:T(8,128)(2,1)S(1)}, u32[]{:S(2)}, u32[]{:S(2)}) %collective-permute-start.29) | collective-permute-done | bytes 294944 | tf_op jit(solution)/shard_map/ppermute | solution.py:280
  235.6 7.9 %collective-permute-done.30 = bf16[128,1152]{1,0:T(8,128)(2,1)S(1)} collective-permute-done((bf16[128,1152]{1,0:T(8,128)(2,1)S(1)}, bf16[128,1152]{1,0:T(8,128)(2,1)S(1)}, u32[]{:S(2)}, u32[]{:S(2)}) %collective-permute-start.30) | collective-permute-done | bytes 294944 | tf_op jit(solution)/shard_map/ppermute | solution.py:280
  246.6 4.1 %collective-permute-done.31 = bf16[128,1152]{1,0:T(8,128)(2,1)S(1)} collective-permute-done((bf16[128,1152]{1,0:T(8,128)(2,1)S(1)}, bf16[128,1152]{1,0:T(8,128)(2,1)S(1)}, u32[]{:S(2)}, u32[]{:S(2)}) %collective-permute-start.31) | collective-permute-done | bytes 294944 | tf_op jit(solution)/shard_map/ppermute | solution.py:280
  252.4 5.6 %collective-permute-done.18 = bf16[128,1024]{1,0:T(8,128)(2,1)S(1)} collective-permute-done((bf16[128,1024]{1,0:T(8,128)(2,1)S(1)}, bf16[128,1024]{1,0:T(8,128)(2,1)S(1)}, u32[]{:S(2)}, u32[]{:S(2)}) %collective-permute-start.18) | collective-permute-done | bytes 262176 | tf_op jit(solution)/shard_map/ppermute | solution.py:277
  259.5 10.8 %collective-permute-done.21 = bf16[3,12,64,128]{3,2,1,0:T(8,128)(2,1)S(1)} collective-permute-done((bf16[3,12,64,128]{3,2,1,0:T(8,128)(2,1)S(1)}, bf16[3,12,64,128]{3,2,1,0:T(8,128)(2,1)S(1)}, u32[]{:S(2)}, u32[]{:S(2)}) %collective-permute-start.21) | collective-permute-done | bytes 589856 | tf_op jit(solution)/shard_map/ppermute | solution.py:286
  278.1 6.7 %collective-permute-done.33 = bf16[3,12,64,128]{3,2,1,0:T(8,128)(2,1)S(1)} collective-permute-done((bf16[3,12,64,128]{3,2,1,0:T(8,128)(2,1)S(1)}, bf16[3,12,64,128]{3,2,1,0:T(8,128)(2,1)S(1)}, u32[]{:S(2)}, u32[]{:S(2)}) %collective-permute-start.33) | collective-permute-done | bytes 589856 | tf_op jit(solution)/shard_map/ppermute | solution.py:286
  (215 shorter events, 82.0 us)
Async XLA Ops:
  2.9 44.3 %all-to-all-start = ((bf16[16,160,128]{2,1,0:T(8,128)(2,1)}), bf16[16,160,128]{2,1,0:T(8,128)(2,1)S(1)}, u32[]{:S(2)}, u32[]{:S(2)}) async-start(bf16[16,160,128]{2,1,0:T(8,128)(2,1)} %pad_maximum_fusion), calls=%async_computation | async-start | bytes 1310720 | tf_op jit(solution)/shard_map/all_to_all | solution.py:254
  10.4 25.5 %collective-permute-start.2 = (bf16[128,2048]{1,0:T(8,128)(2,1)S(1)}, bf16[128,2048]{1,0:T(8,128)(2,1)}, u32[]{:S(2)}, u32[]{:S(2)}) collective-permute-start(bf16[128,2048]{1,0:T(8,128)(2,1)S(1)} %copy-done.36), channel_id=1, source_target_pairs={{0,2},{1,3},{2,6},{3,7},{6,10},{7,11},{10,14},{11,15},{14,12},{15,... | collective-permute-start | bytes 1572872 | tf_op jit(solution)/shard_map/ppermute | solution.py:277
  12.4 23.5 %collective-permute-start.3 = (bf16[128,2048]{1,0:T(8,128)(2,1)S(1)}, bf16[128,2048]{1,0:T(8,128)(2,1)}, u32[]{:S(2)}, u32[]{:S(2)}) collective-permute-start(bf16[128,2048]{1,0:T(8,128)(2,1)S(1)} %copy-done.36), channel_id=1, source_target_pairs={{2,0},{3,1},{6,2},{7,3},{10,6},{11,7},{14,10},{15,11},{12,14},{13,... | collective-permute-start | bytes 1572872 | tf_op jit(solution)/shard_map/ppermute | solution.py:280
  12.8 32.4 %collective-permute-start.1 = (bf16[128,2176]{1,0:T(8,128)(2,1)S(1)}, bf16[128,2176]{1,0:T(8,128)(2,1)S(1)}, u32[]{:S(2)}, u32[]{:S(2)}) collective-permute-start(bf16[128,2176]{1,0:T(8,128)(2,1)S(1)} %pad_maximum_fusion.1.refs_0_), channel_id=1, source_target_pairs={{2,0},{3,1},{6,2},{7,3},{10,6},{11,7},{14,10},{15,11},{12,14},{13,... | collective-permute-start | bytes 1671176 | tf_op jit(solution)/shard_map/ppermute | solution.py:280
  14.8 32.4 %collective-permute-start = (bf16[128,2176]{1,0:T(8,128)(2,1)S(1)}, bf16[128,2176]{1,0:T(8,128)(2,1)S(1)}, u32[]{:S(2)}, u32[]{:S(2)}) collective-permute-start(bf16[128,2176]{1,0:T(8,128)(2,1)S(1)} %pad_maximum_fusion.1.refs_0_), channel_id=1, source_target_pairs={{0,2},{1,3},{2,6},{3,7},{6,10},{7,11},{10,14},{11,15},{14,12},{15,... | collective-permute-start | bytes 1671176 | tf_op jit(solution)/shard_map/ppermute | solution.py:277
  50.9 43.3 %all-to-all-start.1 = ((bf16[16,144,128]{2,1,0:T(8,128)(2,1)}), bf16[16,144,128]{2,1,0:T(8,128)(2,1)S(1)}, u32[]{:S(2)}, u32[]{:S(2)}) async-start(bf16[16,144,128]{2,1,0:T(8,128)(2,1)} %broadcast_select_fusion.2), calls=%async_computation.1 | async-start | bytes 1179648 | tf_op jit(solution)/shard_map/all_to_all | solution.py:254
  59.2 23.6 %collective-permute-start.6 = (bf16[128,2048]{1,0:T(8,128)(2,1)}, bf16[128,2048]{1,0:T(8,128)(2,1)}, u32[]{:S(2)}, u32[]{:S(2)}) collective-permute-start(bf16[128,2048]{1,0:T(8,128)(2,1)} %collective-permute-done.2.refs_5_), channel_id=1, source_target_pairs={{0,2},{1,3},{2,6},{3,7},{6,10},{7,11},{10,14},{11,15},{14,12},{15,... | collective-permute-start | bytes 1572872 | tf_op jit(solution)/shard_map/ppermute | solution.py:277
  61.1 21.7 %collective-permute-start.7 = (bf16[128,2048]{1,0:T(8,128)(2,1)}, bf16[128,2048]{1,0:T(8,128)(2,1)}, u32[]{:S(2)}, u32[]{:S(2)}) collective-permute-start(bf16[128,2048]{1,0:T(8,128)(2,1)} %collective-permute-done.3.refs_4_), channel_id=1, source_target_pairs={{2,0},{3,1},{6,2},{7,3},{10,6},{11,7},{14,10},{15,11},{12,14},{13,... | collective-permute-start | bytes 1572872 | tf_op jit(solution)/shard_map/ppermute | solution.py:280
  61.2 32.9 %collective-permute-start.4 = (bf16[128,2176]{1,0:T(8,128)(2,1)S(1)}, bf16[128,2176]{1,0:T(8,128)(2,1)S(1)}, u32[]{:S(2)}, u32[]{:S(2)}) collective-permute-start(bf16[128,2176]{1,0:T(8,128)(2,1)S(1)} %collective-permute-done.refs_2_), channel_id=1, source_target_pairs={{0,2},{1,3},{2,6},{3,7},{6,10},{7,11},{10,14},{11,15},{14,12},{15,... | collective-permute-start | bytes 1671176 | tf_op jit(solution)/shard_map/ppermute | solution.py:277
  63.2 31.0 %collective-permute-start.5 = (bf16[128,2176]{1,0:T(8,128)(2,1)S(1)}, bf16[128,2176]{1,0:T(8,128)(2,1)}, u32[]{:S(2)}, u32[]{:S(2)}) collective-permute-start(bf16[128,2176]{1,0:T(8,128)(2,1)S(1)} %collective-permute-done.1.refs_1_), channel_id=1, source_target_pairs={{2,0},{3,1},{6,2},{7,3},{10,6},{11,7},{14,10},{15,11},{12,14},{13,... | collective-permute-start | bytes 1671176 | tf_op jit(solution)/shard_map/ppermute | solution.py:280
  98.0 36.8 %all-to-all-start.2 = ((bf16[16,144,128]{2,1,0:T(8,128)(2,1)}), bf16[16,144,128]{2,1,0:T(8,128)(2,1)}, u32[]{:S(2)}, u32[]{:S(2)}) async-start(bf16[16,144,128]{2,1,0:T(8,128)(2,1)} %bitcast.54), calls=%async_computation.2 | async-start | bytes 1179648 | tf_op jit(solution)/shard_map/all_to_all | solution.py:254
  105.0 24.3 %collective-permute-start.10 = (bf16[128,2048]{1,0:T(8,128)(2,1)}, bf16[128,2048]{1,0:T(8,128)(2,1)S(1)}, u32[]{:S(2)}, u32[]{:S(2)}) collective-permute-start(bf16[128,2048]{1,0:T(8,128)(2,1)} %collective-permute-done.6.refs_5_), channel_id=1, source_target_pairs={{0,2},{1,3},{2,6},{3,7},{6,10},{7,11},{10,14},{11,15},{14,12},{15,... | collective-permute-start | bytes 1572872 | tf_op jit(solution)/shard_map/ppermute | solution.py:277
  106.9 38.7 %collective-permute-start.13 = (bf16[3,12,64,128]{3,2,1,0:T(8,128)(2,1)S(1)}, bf16[3,12,64,128]{3,2,1,0:T(8,128)(2,1)S(1)}, u32[]{:S(2)}, u32[]{:S(2)}) collective-permute-start(bf16[3,12,64,128]{3,2,1,0:T(8,128)(2,1)S(1)} %bitcast.35), channel_id=1, source_target_pairs={{0,1},{1,0},{2,3},{3,2},{4,5},{5,4},{6,7},{7,6},{8,9},{9,8},{10,11... | collective-permute-start | bytes 1769480 | tf_op jit(solution)/shard_map/ppermute | solution.py:289
  109.1 36.5 %collective-permute-start.14 = (bf16[3,12,64,128]{3,2,1,0:T(8,128)(2,1)S(1)}, bf16[3,12,64,128]{3,2,1,0:T(8,128)(2,1)S(1)}, u32[]{:S(2)}, u32[]{:S(2)}) collective-permute-start(bf16[3,12,64,128]{3,2,1,0:T(8,128)(2,1)S(1)} %collective-permute-done.12), channel_id=1, source_target_pairs={{0,1},{1,0},{2,3},{3,2},{4,5},{5,4},{6,7},{7,6},{8,9},{9,8},{10,11... | collective-permute-start | bytes 1769480 | tf_op jit(solution)/shard_map/ppermute | solution.py:289
  109.1 36.5 %collective-permute-start.8 = (bf16[128,2176]{1,0:T(8,128)(2,1)}, bf16[128,2176]{1,0:T(8,128)(2,1)}, u32[]{:S(2)}, u32[]{:S(2)}) collective-permute-start(bf16[128,2176]{1,0:T(8,128)(2,1)} %copy-done.34), channel_id=1, source_target_pairs={{0,2},{1,3},{2,6},{3,7},{6,10},{7,11},{10,14},{11,15},{14,12},{15,... | collective-permute-start | bytes 1671176 | tf_op jit(solution)/shard_map/ppermute | solution.py:277
  110.6 35.0 %collective-permute-start.9 = (bf16[128,2176]{1,0:T(8,128)(2,1)}, bf16[128,2176]{1,0:T(8,128)(2,1)}, u32[]{:S(2)}, u32[]{:S(2)}) collective-permute-start(bf16[128,2176]{1,0:T(8,128)(2,1)} %collective-permute-done.5.refs_0_), channel_id=1, source_target_pairs={{2,0},{3,1},{6,2},{7,3},{10,6},{11,7},{14,10},{15,11},{12,14},{13,... | collective-permute-start | bytes 1671176 | tf_op jit(solution)/shard_map/ppermute | solution.py:280
  145.6 22.7 %collective-permute-start.16 = (bf16[128,2048]{1,0:T(8,128)(2,1)}, bf16[128,2048]{1,0:T(8,128)(2,1)S(1)}, u32[]{:S(2)}, u32[]{:S(2)}) collective-permute-start(bf16[128,2048]{1,0:T(8,128)(2,1)} %collective-permute-done.11.refs_6_), channel_id=1, source_target_pairs={{2,0},{3,1},{6,2},{7,3},{10,6},{11,7},{14,10},{15,11},{12,14},{13,... | collective-permute-start | bytes 1572872 | tf_op jit(solution)/shard_map/ppermute | solution.py:280
  148.2 21.0 %collective-permute-start.15 = (bf16[128,2176]{1,0:T(8,128)(2,1)}, bf16[128,2176]{1,0:T(8,128)(2,1)S(1)}, u32[]{:S(2)}, u32[]{:S(2)}) collective-permute-start(bf16[128,2176]{1,0:T(8,128)(2,1)} %collective-permute-done.8.refs_3_), channel_id=1, source_target_pairs={{0,2},{1,3},{2,6},{3,7},{6,10},{7,11},{10,14},{11,15},{14,12},{15,... | collective-permute-start | bytes 1671176 | tf_op jit(solution)/shard_map/ppermute | solution.py:277
  174.6 39.7 %all-to-all-start.3 = ((bf16[16,144,128]{2,1,0:T(8,128)(2,1)}), bf16[16,144,128]{2,1,0:T(8,128)(2,1)}, u32[]{:S(2)}, u32[]{:S(2)}) async-start(bf16[16,144,128]{2,1,0:T(8,128)(2,1)} %broadcast_select_fusion.1), calls=%async_computation.3 | async-start | bytes 1179648 | tf_op jit(solution)/shard_map/all_to_all | solution.py:254
  205.8 19.4 %collective-permute-start.26 = (bf16[128,1152]{1,0:T(8,128)(2,1)}, bf16[128,1152]{1,0:T(8,128)(2,1)}, u32[]{:S(2)}, u32[]{:S(2)}) collective-permute-start(bf16[128,1152]{1,0:T(8,128)(2,1)} %copy-done.40), channel_id=1, source_target_pairs={{0,2},{1,3},{2,6},{3,7},{6,10},{7,11},{10,14},{11,15},{14,12},{15,... | collective-permute-start | bytes 884744 | tf_op jit(solution)/shard_map/ppermute | solution.py:277
  226.3 19.0 %collective-permute-start.27 = (bf16[128,1152]{1,0:T(8,128)(2,1)S(1)}, bf16[128,1152]{1,0:T(8,128)(2,1)S(1)}, u32[]{:S(2)}, u32[]{:S(2)}) collective-permute-start(bf16[128,1152]{1,0:T(8,128)(2,1)S(1)} %add_convert_fusion.6), channel_id=1, source_target_pairs={{0,2},{1,3},{2,6},{3,7},{6,10},{7,11},{10,14},{11,15},{14,12},{15,... | collective-permute-start | bytes 884744 | tf_op jit(solution)/shard_map/ppermute | solution.py:277
  227.9 47.6 %collective-permute-start.25 = (bf16[128,1024]{1,0:T(8,128)(2,1)S(1)}, bf16[128,1024]{1,0:T(8,128)(2,1)S(1)}, u32[]{:S(2)}, u32[]{:S(2)}) collective-permute-start(bf16[128,1024]{1,0:T(8,128)(2,1)S(1)} %add_convert_fusion.8), channel_id=1, source_target_pairs={{2,0},{3,1},{6,2},{7,3},{10,6},{11,7},{14,10},{15,11},{12,14},{13,... | collective-permute-start | bytes 786440 | tf_op jit(solution)/shard_map/ppermute | solution.py:280
  229.4 16.4 %collective-permute-start.17 = (bf16[128,1024]{1,0:T(8,128)(2,1)S(1)}, bf16[128,1024]{1,0:T(8,128)(2,1)S(1)}, u32[]{:S(2)}, u32[]{:S(2)}) collective-permute-start(bf16[128,1024]{1,0:T(8,128)(2,1)S(1)} %get-tuple-element.173), channel_id=1, source_target_pairs={{0,2},{1,3},{2,6},{3,7},{6,10},{7,11},{10,14},{11,15},{14,12},{15,... | collective-permute-start | bytes 786440 | tf_op jit(solution)/shard_map/ppermute | solution.py:277
  235.6 22.5 %collective-permute-start.19 = (bf16[3,12,128,128]{3,2,1,0:T(8,128)(2,1)S(1)}, bf16[3,12,128,128]{3,2,1,0:T(8,128)(2,1)S(1)}, u32[]{:S(2)}, u32[]{:S(2)}) collective-permute-start(bf16[3,12,128,128]{3,2,1,0:T(8,128)(2,1)S(1)} %bitcast.56), channel_id=1, source_target_pairs={{0,1},{1,0},{2,3},{3,2},{4,5},{5,4},{6,7},{7,6},{8,9},{9,8},{10,11... | collective-permute-start | bytes 3538952 | tf_op jit(solution)/shard_map/ppermute | solution.py:289
  (66 other events, 463.7 us)

commit v5 on v4

--- a/solution.py
+++ b/solution.py
@@ -28,6 +28,7 @@
     half,
     pieces,
     resumed,
+    added,
     lay_ref,
     expert_ref,
     place_ref,
@@ -38,6 +39,9 @@
     piece_refs, refs = refs[:pieces], refs[pieces:]
     if resumed:
         so_far_ref, refs = refs[0], refs[1:]
+    if added:
+        low_so_far, refs = refs[:shards], refs[shards:]
+        high_so_far, refs = refs[:shards], refs[shards:]
     low_refs, refs = refs[:shards], refs[shards:]
     high_refs, refs = refs[:shards], refs[shards:]
     (
@@ -186,11 +190,17 @@
     lax.fori_loop(0, 2, one_expert, 0)
     for s in range(shards):
         total = dot(spread[s, 0], wide[s, 0], NN) + dot(spread[s, 1], wide[s, 1], NN)
-        low_refs[s][...] = total[:, :half].astype(jnp.bfloat16)
-        high_refs[s][...] = total[:, half:].astype(jnp.bfloat16)
-
-
-def run_experts(x_list, g_list, weights, places, layouts, experts, slots, so_far, final):
+        low, high = total[:, :half], total[:, half:]
+        if added:
+            low = low + low_so_far[s][...].astype(jnp.float32)
+            high = high + high_so_far[s][...].astype(jnp.float32)
+        low_refs[s][...] = low.astype(jnp.bfloat16)
+        high_refs[s][...] = high.astype(jnp.bfloat16)
+
+
+def run_experts(
+    x_list, g_list, weights, places, layouts, experts, slots, so_far, parts_so_far, final
+):
     shards = len(x_list)
     tok, table_width = x_list[0].shape
     width = g_list[0].shape[1]
@@ -204,10 +214,12 @@
     smem = pl.BlockSpec(memory_space=pltpu.SMEM)
     vmem = pl.BlockSpec(memory_space=pltpu.VMEM)
     grads = jax.ShapeDtypeStruct((block_count, LANES, LANES), bf16 if final else f32)
+    added = len(parts_so_far) > 0
     operands = [*x_list, *g_list, *weights] + ([so_far] if resumed else [])
+    operands += [low for low, _ in parts_so_far] + [high for _, high in parts_so_far]
     outs = pl.pallas_call(
         functools.partial(
-            expert_kernel, shards, slots, half, len(weights), resumed
+            expert_kernel, shards, slots, half, len(weights), resumed, added
         ),
         in_specs=[smem] * 3 + [vmem] * len(operands),
         out_specs=[vmem] * (2 * shards + 1),
@@ -230,7 +242,7 @@
             pltpu.VMEM((shards, 2, tok, slots), bf16),
             pltpu.VMEM((rows, LANES), f32),
         ],
-        compiler_params=pltpu.CompilerParams(vmem_limit_bytes=44 * 1024 * 1024),
+        compiler_params=pltpu.CompilerParams(vmem_limit_bytes=40 * 1024 * 1024),
         cost_estimate=pl.CostEstimate(
             flops=2 * 2 * 108 * rows * LANES * LANES * 4,
             bytes_accessed=shards * tok * table_width * 6 + block_count * LANES * LANES * 6,
@@ -241,13 +253,8 @@
 
 
 def chip_ring(chips):
-    tall, broad = 4, chips // 4
-    walk = []
-    for row in range(tall):
-        columns = list(range(0 if row == 0 else 1, broad))
-        walk += [(row, c) for c in (columns if row % 2 == 0 else columns[::-1])]
-    walk += [(row, 0) for row in range(tall - 1, 0, -1)]
-    return [row * broad + c for row, c in walk]
+    broad = chips // 2
+    return list(range(broad)) + list(range(chips - 1, broad - 1, -1))
 
 
 def swap_all(pieces):
@@ -264,12 +271,18 @@
     slots = -(-capacity // 16) * 16
     table_lanes = -(-expert_count // LANES) * LANES
     bf16, f32 = jnp.bfloat16, jnp.float32
-    chips = expert_count // 2
+    chips = expert_count // 4
     ring = chip_ring(chips)
-    steps = list(zip(ring, ring[1:] + ring[:1]))
+    steps = [
+        (a + side * chips, b + side * chips)
+        for a, b in zip(ring, ring[1:] + ring[:1])
+        for side in range(2)
+    ]
     onward = [(2 * a + core, 2 * b + core) for a, b in steps for core in range(2)]
     backward = [(b, a) for a, b in onward]
     sister = [(i, i ^ 1) for i in range(expert_count)]
+    far = expert_count // 2
+    mirror = [(i, i ^ far) for i in range(expert_count)]
     row_share = block_size // replica_count
     replica = lax.axis_index("dp")
 
@@ -317,8 +330,6 @@
         bf16
     )
     me = lax.axis_index("expert")
-    slots_here = jnp.stack([me, me ^ 1])
-    experts = jnp.take(partner, slots_here).astype(jnp.int32)
 
     note_rows = 16
     layout_flat = layout.reshape(-1)
@@ -331,79 +342,85 @@
     note = jnp.broadcast_to(
         layout_note.reshape(1, note_rows, LANES), (expert_count, note_rows, LANES)
     )
-    state = {"pieces": jnp.concatenate([pieces, note], axis=1)}
-    moment_pieces = moments[0].astype(bf16).reshape(expert_count, -1, LANES)
+    spread = swap_all(jnp.concatenate([pieces, note], axis=1))
+    all_layouts = spread[:, piece_rows:].reshape(expert_count, -1)[:, : layout_flat.shape[0]]
+    all_slots = jnp.arange(expert_count, dtype=jnp.int32)
+
+    def collect(spread_state, slot_order):
+        moved = jnp.take(spread_state, jnp.take(partner, slot_order), axis=0)
+        return swap_all(moved).reshape(rows_now.shape)
+
+    rows_far = collect(spread[:, :piece_rows], all_slots ^ far)
+    rows_far, spread = lax.optimization_barrier((rows_far, spread))
+    rows_near = collect(spread[:, :piece_rows], all_slots)
+
     x_at = {0: jnp.concatenate([tokens, table], axis=1)}
     g_at = {0: out_grad}
     most = chips // 2
-    near = [0]
-    for s in range(1, most):
-        near += [s, -s]
-    near += [most]
-    if chips <= 8:
-        groups = [near[:3], near[3:-1], near[-1:]]
-    else:
-        groups = [near[i : i + 8] for i in range(0, chips, 8)]
-    parts = {}
-
-    def run_group(group, so_far):
-        lows, highs, sums = run_experts(
-            [x_at[d] for d in group],
-            [g_at[d] for d in group],
-            state["weights"],
-            places,
-            state["layouts"],
-            experts,
-            slots,
-            so_far,
-            group is groups[-1],
-        )
-        for d, low, high in zip(group, lows, highs):
-            parts[d] = (low, high)
-        return sums
-
-    if replica_count == 2:
-        places = jnp.stack([replica * row_share, (1 - replica) * row_share]).astype(jnp.int32)
-    else:
-        places = jnp.zeros((1,), jnp.int32)
     for s in range(1, most + 1):
         x_at[-s] = step_on(x_at[1 - s])
         g_at[s] = step_back(g_at[s - 1])
         if s < most:
             x_at[s] = step_back(x_at[s - 1])
             g_at[-s] = step_on(g_at[1 - s])
-        if s == 1:
-            state["spread"] = swap_all(state.pop("pieces"))
-        elif s == 2:
-            spread = state.pop("spread")
-            layouts = spread[:, piece_rows:].reshape(expert_count, -1)[:, : layout_flat.shape[0]]
-            state["layouts"] = jnp.take(layouts, experts, axis=0).reshape(-1).astype(jnp.int32)
-            state["rows"] = swap_all(jnp.take(spread[:, :piece_rows], partner, axis=0)).reshape(
-                rows_now.shape
-            )
-        elif s == 3:
-            halves = [state["rows"]]
-            if replica_count == 2:
-                halves.append(other_replica(state["rows"]))
-            else:
-                halves = [join_rows(state["rows"])]
-            weights = halves + [other_core(value) for value in halves]
-            state["weights"] = [value.reshape(-1, value.shape[2], LANES) for value in weights]
-            state["moments"] = swap_all(moment_pieces)
-        elif s == 4:
-            state["sums"] = run_group(groups[0], None)
-        x_at, g_at, state, parts = lax.optimization_barrier((x_at, g_at, state, parts))
     x_at[most] = x_at[-most]
-    sums = state["sums"]
-    moved_moments = swap_all(jnp.take(state["moments"], partner, axis=0)).reshape(rows_now.shape)
-    for group in groups[1:-1]:
-        sums = run_group(group, sums)
-    sums, moved_moments = lax.optimization_barrier((sums, moved_moments))
-    sums = run_group(groups[-1], sums)
-    half_count = sums.shape[0] // 2
-    own_grad = sums[:half_count].reshape(blocks[0].shape)
-    from_sister = other_core(sums[half_count:].reshape(blocks[0].shape))
-    moved_rows = state["rows"]
+    shards = [0]
+    for s in range(1, most):
+        shards += [s, -s]
+    shards += [most]
+    groups = [shards[i : i + 8] for i in range(0, len(shards), 8)]
+
+    if replica_count == 2:
+        places = jnp.stack([replica * row_share, (1 - replica) * row_share]).astype(jnp.int32)
+    else:
+        places = jnp.zeros((1,), jnp.int32)
+
+    def both_cores(rows):
+        halves = [rows, other_replica(rows)] if replica_count == 2 else [join_rows(rows)]
+        weights = halves + [other_core(value) for value in halves]
+        return [value.reshape(-1, value.shape[2], LANES) for value in weights]
+
+    def run_pair(slot, weights, earlier):
+        experts = jnp.take(partner, jnp.stack([slot, slot ^ 1])).astype(jnp.int32)
+        layouts = jnp.take(all_layouts, experts, axis=0).reshape(-1).astype(jnp.int32)
+        parts, sums = {}, None
+        for group in groups:
+            lows, highs, sums = run_experts(
+                [x_at[d] for d in group],
+                [g_at[d] for d in group],
+                weights,
+                places,
+                layouts,
+                experts,
+                slots,
+                sums,
+                [earlier[d] for d in group] if earlier else [],
+                group is groups[-1],
+            )
+            for d, low, high in zip(group, lows, highs):
+                parts[d] = (low, high)
+        half_count = sums.shape[0] // 2
+        from_sister = other_core(sums[half_count:].reshape(blocks[0].shape))
+        return parts, sums[:half_count].reshape(blocks[0].shape), from_sister
+
+    moment_pieces = moments[0].astype(bf16).reshape(expert_count, -1, LANES)
+    weights_far = both_cores(rows_far)
+    weights_near = both_cores(rows_near)
+    weights_far, moment_pieces, rows_near = lax.optimization_barrier(
+        (weights_far, moment_pieces, rows_near)
+    )
+    moment_spread = swap_all(moment_pieces)
+    parts, far_grad, far_sister = run_pair(me ^ far, weights_far, None)
+    parts, far_grad, far_sister, weights_near, moment_spread = lax.optimization_barrier(
+        (parts, far_grad, far_sister, weights_near, moment_spread)
+    )
+    moved_moments = collect(moment_spread, all_slots)
+    far_sum = sum_rows(far_grad, far_sister).astype(bf16)
+    from_mirror = lax.ppermute(far_sum, "expert", mirror)
+    parts, near_grad, near_sister = run_pair(me, weights_near, parts)
+    shard_grad = sum_rows(near_grad, near_sister) + from_mirror.astype(f32)
+    new_moment = momentum_decay * moved_moments.astype(f32) + shard_grad
+    new_shard = (rows_near.astype(f32) - step_rate * new_moment).astype(bf16)
 
     def own_share(distance, part):
         return parts[distance][part]
@@ -418,13 +435,6 @@
             downward[part] = step_back(
                 share if downward[part] is None else add(downward[part], share)
             )
-        if s == most - 1:
-            upward[0], from_sister = lax.optimization_barrier((upward[0], from_sister))
-            shard_grad = sum_rows(own_grad, from_sister)
-        elif s == most - 2:
-            upward[0], shard_grad = lax.optimization_barrier((upward[0], shard_grad))
-            new_moment = momentum_decay * moved_moments.astype(f32) + shard_grad
-            new_shard = (moved_rows.astype(f32) - step_rate * new_moment).astype(bf16)
     homes = [
         (parts[0][part].astype(f32) + upward[part].astype(f32) + downward[part].astype(f32)).astype(
             bf16

time: 288 us -> 235 us (0.82)
  waiting for transfers between devices: 135 us -> 106 us
  starting transfers between devices: 66.5 us -> 49.5 us
  local copies, waits for them, and re-layouts: 31.2 us -> 22.6 us
  other arithmetic: 17.9 us -> 26.3 us
  Pallas kernels: 34.8 us -> 27.5 us
    ppermute x14 -> x6, waiting for transfers between devices: 75 us -> 1.21 us  [step_on(): return lax.ppermute(value, 'expert', onward)]
    all_to_all x4 -> x5, waiting for transfers between devices: 0.01 us -> 38.6 us  [swap_all(): lax.all_to_all(pieces, 'expert', split_axis=0, concat_axis=0, tiled=True)]
    ppermute x0 -> x1, waiting for transfers between devices: none -> 18.2 us  [body(): from_mirror = lax.ppermute(far_sum, 'expert', mirror)]
    ppermute x14 -> x6, starting transfers between devices: 24.1 us -> 8.08 us  [step_back(): return lax.ppermute(value, 'expert', backward)]
    ppermute x14 -> x6, waiting for transfers between devices: 40.8 us -> 27.9 us  [step_back(): return lax.ppermute(value, 'expert', backward)]
    unnamed x101 -> x63, local copies, waits for them, and re-layouts: 21.6 us -> 10 us
    pallas_call x3 -> x2, Pallas kernels: 34.8 us -> 27.5 us  [run_experts(): pl.pallas_call(functools.partial(expert_kernel, shards, slots, half, len(...]
    convert_element_type x1 -> x4, other arithmetic: 0.08 us -> 6 us  [the longest x1 3.3 us: body(): new_shard = (rows_near.astype(f32) - step_rate * new_moment).astype(bf16)]
  transfers between devices with their start and end apart: 38 -> 29, of which waited for: 16 -> 14; matrix products, arithmetic and copies ran while one was open for 5% -> 14% of each run, Pallas kernels for 12% -> 6%
where the time goes in v5:
time: 235 us; the launch traced here: 233 us
  waiting for transfers between devices  106 us (45%)
  starting transfers between devices  49.5 us (21%)
  Pallas kernels  27.5 us (12%)
  other arithmetic  26.3 us (11%)
  local copies, waits for them, and re-layouts  22.6 us (10%)
    all_to_all x5, waiting for transfers between devices, swap_all(): lax.all_to_all(pieces, 'expert', split_axis=0, concat_axis=0, tiled=True)  38.6 us
    ppermute x6, waiting for transfers between devices, step_back(): return lax.ppermute(value, 'expert', backward)  27.9 us
    pallas_call x2, Pallas kernels, run_experts(): pl.pallas_call(functools.partial(expert_kernel, shards, slots, half, len(...  27.5 us
    all_to_all x5, starting transfers between devices, swap_all(): lax.all_to_all(pieces, 'expert', split_axis=0, concat_axis=0, tiled=True)  25.5 us
    ppermute x5, waiting for transfers between devices, other_replica(): return lax.ppermute(value, 'dp', [(0, 1), (1, 0)])  19.3 us
    ppermute x1, waiting for transfers between devices, body(): from_mirror = lax.ppermute(far_sum, 'expert', mirror)  18.2 us
    unnamed x63, local copies, waits for them, and re-layouts  10 us
    ppermute x6, starting transfers between devices, step_on(): return lax.ppermute(value, 'expert', onward)  9.09 us
  transfers between devices with their start and end apart: 29, of which 14 were waited for; matrix products, arithmetic and copies ran while one was open for 14% of the time, Pallas kernels for 6%

profile of v5, /device:TPU:0, one launch (start us, length us, event | category | flops | bytes accessed | tf_op | source)
XLA Modules:
  0.0 233.3 jit_solution(15519920610834624072)
XLA Ops:
  2.9 7.5 %all-to-all-start = ((bf16[16,160,128]{2,1,0:T(8,128)(2,1)}), bf16[16,160,128]{2,1,0:T(8,128)(2,1)S(1)}, u32[]{:S(2)}, u32[]{:S(2)}) async-start(bf16[16,160,128]{2,1,0:T(8,128)(2,1)} %pad_maximum_fusion), calls=%async_computation | async-start | bytes 1310720 | tf_op jit(solution)/shard_map/all_to_all | solution.py:261
  13.5 13.9 %all-to-all-done = bf16[16,160,128]{2,1,0:T(8,128)(2,1)S(1)} async-done(((bf16[16,160,128]{2,1,0:T(8,128)(2,1)}), bf16[16,160,128]{2,1,0:T(8,128)(2,1)S(1)}, u32[]{:S(2)}, u32[]{:S(2)}) %all-to-all-start) | async-done | bytes 655392 | tf_op jit(solution)/shard_map/all_to_all | solution.py:261
  29.2 4.6 %all-to-all-start.1 = ((bf16[16,144,128]{2,1,0:T(8,128)(2,1)}), bf16[16,144,128]{2,1,0:T(8,128)(2,1)S(1)}, u32[]{:S(2)}, u32[]{:S(2)}) async-start(bf16[16,144,128]{2,1,0:T(8,128)(2,1)} %broadcast_select_fusion.3), calls=%async_computation.1 | async-start | bytes 1179648 | tf_op jit(solution)/shard_map/all_to_all | solution.py:261
  37.9 11.4 %all-to-all-done.1 = bf16[16,144,128]{2,1,0:T(8,128)(2,1)S(1)} async-done(((bf16[16,144,128]{2,1,0:T(8,128)(2,1)}), bf16[16,144,128]{2,1,0:T(8,128)(2,1)S(1)}, u32[]{:S(2)}, u32[]{:S(2)}) %all-to-all-start.1) | async-done | bytes 589856 | tf_op jit(solution)/shard_map/all_to_all | solution.py:261
  52.4 4.7 %all-to-all-start.2 = ((bf16[16,144,128]{2,1,0:T(8,128)(2,1)}), bf16[16,144,128]{2,1,0:T(8,128)(2,1)S(1)}, u32[]{:S(2)}, u32[]{:S(2)}) async-start(bf16[16,144,128]{2,1,0:T(8,128)(2,1)} %broadcast_select_fusion.2), calls=%async_computation.2 | async-start | bytes 1179648 | tf_op jit(solution)/shard_map/all_to_all | solution.py:261
  57.3 7.8 %collective-permute-done.6 = bf16[3,12,64,128]{3,2,1,0:T(8,128)(2,1)} collective-permute-done((bf16[3,12,64,128]{3,2,1,0:T(8,128)(2,1)S(1)}, bf16[3,12,64,128]{3,2,1,0:T(8,128)(2,1)}, u32[]{:S(2)}, u32[]{:S(2)}) %collective-permute-start.6) | collective-permute-done | bytes 589856 | tf_op jit(solution)/shard_map/ppermute | solution.py:299
  65.2 2.2 convert_element_type.139
  73.4 10.8 %collective-permute-done.refs_1_ = bf16[128,2176]{1,0:T(8,128)(2,1)} collective-permute-done((bf16[128,2176]{1,0:T(8,128)(2,1)S(1)}, bf16[128,2176]{1,0:T(8,128)(2,1)}, u32[]{:S(2)}, u32[]{:S(2)}) %collective-permute-start) | collective-permute-done | bytes 557088 | tf_op jit(solution)/shard_map/ppermute | solution.py:293
  84.3 11.0 %collective-permute-done.5.refs_7_ = bf16[128,2048]{1,0:T(8,128)(2,1)} collective-permute-done((bf16[128,2048]{1,0:T(8,128)(2,1)}, bf16[128,2048]{1,0:T(8,128)(2,1)}, u32[]{:S(2)}, u32[]{:S(2)}) %collective-permute-start.5) | collective-permute-done | bytes 524320 | tf_op jit(solution)/shard_map/ppermute | solution.py:293
  95.2 13.9 %shard_map.111 = (bf16[128,1024]{1,0:T(8,128)(2,1)S(1)}, bf16[128,1024]{1,0:T(8,128)(2,1)S(1)}, bf16[128,1024]{1,0:T(8,128)(2,1)S(1)}, bf16[128,1024]{1,0:T(8,12...) custom-call(s32[144]{0:T(256)S(1)} %reshape.163.lay_ref, ...), custom_call_target="tpu_custom_call" | custom-call | flops 7247757312 | bytes 13762560 | tf_op jit(solution)/shard_map/pallas_call | solution.py:220
  111.3 4.5 %all-to-all-start.3 = ((bf16[16,144,128]{2,1,0:T(8,128)(2,1)}), bf16[16,144,128]{2,1,0:T(8,128)(2,1)}, u32[]{:S(2)}, u32[]{:S(2)}) async-start(bf16[16,144,128]{2,1,0:T(8,128)(2,1)} %bitcast.13), calls=%async_computation.3 | async-start | bytes 1179648 | tf_op jit(solution)/shard_map/all_to_all | solution.py:261
  119.0 12.1 %all-to-all-done.3 = bf16[16,144,128]{2,1,0:T(8,128)(2,1)} async-done(((bf16[16,144,128]{2,1,0:T(8,128)(2,1)}), bf16[16,144,128]{2,1,0:T(8,128)(2,1)}, u32[]{:S(2)}, u32[]{:S(2)}) %all-to-all-start.3) | async-done | bytes 589856 | tf_op jit(solution)/shard_map/all_to_all | solution.py:261
  139.8 13.7 %shard_map.112 = (bf16[128,1024]{1,0:T(8,128)(2,1)S(1)}, bf16[128,1024]{1,0:T(8,128)(2,1)S(1)}, bf16[128,1024]{1,0:T(8,128)(2,1)S(1)}, bf16[128,1024]{1,0:T(8,12...) custom-call(s32[144]{0:T(256)S(1)} %reshape.162.lay_ref, ...), custom_call_target="tpu_custom_call" | custom-call | flops 7247757312 | bytes 13762560 | tf_op jit(solution)/shard_map/pallas_call | solution.py:220
  156.7 2.3 add_convert_fusion.1
  162.5 2.5 %gather_fusion.8 = bf16[16,144,128]{2,1,0:T(8,128)(2,1)} fusion(bf16[16,144,128]{2,1,0:T(8,128)(2,1)} %all-to-all-done.3, s32[1024]{0:T(1024)S(1)} %pad_clamp_fusion), kind=kCustom, calls=%fused_computation.8.clone | custom fusion | bytes 1179712 | tf_op jit(solution)/shard_map/jit(_take)/gather | solution.py:350
  165.0 2.0 broadcast_select_fusion.1
  167.0 4.3 %all-to-all-start.4 = ((bf16[16,144,128]{2,1,0:T(8,128)(2,1)}), bf16[16,144,128]{2,1,0:T(8,128)(2,1)}, u32[]{:S(2)}, u32[]{:S(2)}) async-start(bf16[16,144,128]{2,1,0:T(8,128)(2,1)} %broadcast_select_fusion.1), calls=%async_computation.4 | async-start | bytes 1179648 | tf_op jit(solution)/shard_map/all_to_all | solution.py:261
  176.2 2.6 %add_convert_fusion = bf16[3,12,64,128]{3,2,1,0:T(8,128)(2,1)} fusion(bf16[3,12,64,128]{3,2,1,0:T(8,128)(2,1)} %collective-permute-done.21, bf16[3,12,128,128]{3,2,1,0:T(8,128)(2,1)} %collective-permute-done.9, s32[]{:T(128)S(6)} %select_n.58, bf16[3,12,128,128]{3,2,1,0:T(8,128)(2,1)} %bitcast.44), kind=kLoop, calls=%fused_computation.11 | loop fusion | flops 1769472 | bytes 2359300 | tf_op jit(solution)/shard_map/convert_element_type | solution.py:418
  180.2 2.1 add_convert_fusion.2
  182.3 6.1 %collective-permute-done.17 = bf16[128,1152]{1,0:T(8,128)(2,1)S(1)} collective-permute-done((bf16[128,1152]{1,0:T(8,128)(2,1)}, bf16[128,1152]{1,0:T(8,128)(2,1)S(1)}, u32[]{:S(2)}, u32[]{:S(2)}) %collective-permute-start.17) | collective-permute-done | bytes 294944 | tf_op jit(solution)/shard_map/ppermute | solution.py:293
  189.2 2.4 %collective-permute-start.18 = (bf16[128,1152]{1,0:T(8,128)(2,1)S(1)}, bf16[128,1152]{1,0:T(8,128)(2,1)S(1)}, u32[]{:S(2)}, u32[]{:S(2)}) collective-permute-start(bf16[128,1152]{1,0:T(8,128)(2,1)S(1)} %add_convert_fusion.4), channel_id=1, source_target_pairs={{2,0},{3,1},{10,8},{11,9},{6,2},{7,3},{14,10},{15,11},{4,6},{5,7},... | collective-permute-start | bytes 884744 | tf_op jit(solution)/shard_map/ppermute | solution.py:293
  195.1 18.2 %collective-permute-done.22 = bf16[3,12,64,128]{3,2,1,0:T(8,128)(2,1)} collective-permute-done((bf16[3,12,64,128]{3,2,1,0:T(8,128)(2,1)}, bf16[3,12,64,128]{3,2,1,0:T(8,128)(2,1)}, u32[]{:S(2)}, u32[]{:S(2)}) %collective-permute-start.22) | collective-permute-done | bytes 589856 | tf_op jit(solution)/shard_map/ppermute | solution.py:419
  213.3 3.3 %subtract_convert_fusion = (bf16[3,12,64,128]{3,2,1,0:T(8,128)(2,1)S(1)}, f32[3,12,64,128]{3,2,1,0:T(8,128)}) fusion(bf16[3,12,64,128]{3,2,1,0:T(8,128)(2,1)S(1)} %bitcast.35, f32[3,12,64,128]{3,2,1,0:T(8,128)S(1)} %bitcast.45, bf16[3,12,64,128]{3,2,1,0:T(8,128)(2,1)} %collective-permute-done.22, bf16[3,12,64,128]{3,2,1,0:T(8,128)(2,1)} %collective-permute-done.20, ...), kind=kLoop, calls=%fused_computation.9 | loop fusion | flops 3538944 | bytes 5898244 | tf_op jit(solution)/shard_map/convert_element_type | solution.py:423
  220.2 11.2 %collective-permute-done.23 = bf16[3,12,64,128]{3,2,1,0:T(8,128)(2,1)S(1)} collective-permute-done((bf16[3,12,64,128]{3,2,1,0:T(8,128)(2,1)S(1)}, bf16[3,12,64,128]{3,2,1,0:T(8,128)(2,1)S(1)}, u32[]{:S(2)}, u32[]{:S(2)}) %collective-permute-start.23) | collective-permute-done | bytes 589856 | tf_op jit(solution)/shard_map/ppermute | solution.py:299
  (171 shorter events, 57.3 us)
Async XLA Ops:
  2.9 24.5 %all-to-all-start = ((bf16[16,160,128]{2,1,0:T(8,128)(2,1)}), bf16[16,160,128]{2,1,0:T(8,128)(2,1)S(1)}, u32[]{:S(2)}, u32[]{:S(2)}) async-start(bf16[16,160,128]{2,1,0:T(8,128)(2,1)} %pad_maximum_fusion), calls=%async_computation | async-start | bytes 1310720 | tf_op jit(solution)/shard_map/all_to_all | solution.py:261
  10.4 63.0 %collective-permute-start.4 = (bf16[128,2048]{1,0:T(8,128)(2,1)}, bf16[128,2048]{1,0:T(8,128)(2,1)}, u32[]{:S(2)}, u32[]{:S(2)}) collective-permute-start(bf16[128,2048]{1,0:T(8,128)(2,1)} %refs_4_.3), channel_id=1, source_target_pairs={{0,2},{1,3},{8,10},{9,11},{2,6},{3,7},{10,14},{11,15},{6,4},{7,5},... | collective-permute-start | bytes 1572872 | tf_op jit(solution)/shard_map/ppermute | solution.py:290
  12.3 55.1 %collective-permute-start.3 = (bf16[128,2048]{1,0:T(8,128)(2,1)}, bf16[128,2048]{1,0:T(8,128)(2,1)}, u32[]{:S(2)}, u32[]{:S(2)}) collective-permute-start(bf16[128,2048]{1,0:T(8,128)(2,1)} %refs_4_.3), channel_id=1, source_target_pairs={{2,0},{3,1},{10,8},{11,9},{6,2},{7,3},{14,10},{15,11},{4,6},{5,7},... | collective-permute-start | bytes 1572872 | tf_op jit(solution)/shard_map/ppermute | solution.py:293
  29.2 20.1 %all-to-all-start.1 = ((bf16[16,144,128]{2,1,0:T(8,128)(2,1)}), bf16[16,144,128]{2,1,0:T(8,128)(2,1)S(1)}, u32[]{:S(2)}, u32[]{:S(2)}) async-start(bf16[16,144,128]{2,1,0:T(8,128)(2,1)} %broadcast_select_fusion.3), calls=%async_computation.1 | async-start | bytes 1179648 | tf_op jit(solution)/shard_map/all_to_all | solution.py:261
  33.8 35.3 %collective-permute-start.1 = (bf16[128,2176]{1,0:T(8,128)(2,1)S(1)}, bf16[128,2176]{1,0:T(8,128)(2,1)}, u32[]{:S(2)}, u32[]{:S(2)}) collective-permute-start(bf16[128,2176]{1,0:T(8,128)(2,1)S(1)} %pad_maximum_fusion.1.refs_0_), channel_id=1, source_target_pairs={{0,2},{1,3},{8,10},{9,11},{2,6},{3,7},{10,14},{11,15},{6,4},{7,5},... | collective-permute-start | bytes 1671176 | tf_op jit(solution)/shard_map/ppermute | solution.py:290
  49.3 21.0 %collective-permute-start.7 = (bf16[3,12,64,128]{3,2,1,0:T(8,128)(2,1)S(1)}, bf16[3,12,64,128]{3,2,1,0:T(8,128)(2,1)}, u32[]{:S(2)}, u32[]{:S(2)}) collective-permute-start(bf16[3,12,64,128]{3,2,1,0:T(8,128)(2,1)S(1)} %bitcast.36), channel_id=1, source_target_pairs={{0,1},{1,0},{2,3},{3,2},{4,5},{5,4},{6,7},{7,6},{8,9},{9,8},{10,11... | collective-permute-start | bytes 1769480 | tf_op jit(solution)/shard_map/ppermute | solution.py:302
  49.3 15.8 %collective-permute-start.6 = (bf16[3,12,64,128]{3,2,1,0:T(8,128)(2,1)S(1)}, bf16[3,12,64,128]{3,2,1,0:T(8,128)(2,1)}, u32[]{:S(2)}, u32[]{:S(2)}) collective-permute-start(bf16[3,12,64,128]{3,2,1,0:T(8,128)(2,1)S(1)} %bitcast.37), channel_id=1, source_target_pairs={{0,16},{16,0},{1,17},{17,1},{2,18},{18,2},{3,19},{19,3},{4,20},{20... | collective-permute-start | bytes 1769480 | tf_op jit(solution)/shard_map/ppermute | solution.py:299
  52.4 20.6 %all-to-all-start.2 = ((bf16[16,144,128]{2,1,0:T(8,128)(2,1)}), bf16[16,144,128]{2,1,0:T(8,128)(2,1)S(1)}, u32[]{:S(2)}, u32[]{:S(2)}) async-start(bf16[16,144,128]{2,1,0:T(8,128)(2,1)} %broadcast_select_fusion.2), calls=%async_computation.2 | async-start | bytes 1179648 | tf_op jit(solution)/shard_map/all_to_all | solution.py:261
  67.4 16.9 %collective-permute-start = (bf16[128,2176]{1,0:T(8,128)(2,1)S(1)}, bf16[128,2176]{1,0:T(8,128)(2,1)}, u32[]{:S(2)}, u32[]{:S(2)}) collective-permute-start(bf16[128,2176]{1,0:T(8,128)(2,1)S(1)} %pad_maximum_fusion.1.refs_0_), channel_id=1, source_target_pairs={{2,0},{3,1},{10,8},{11,9},{6,2},{7,3},{14,10},{15,11},{4,6},{5,7},... | collective-permute-start | bytes 1671176 | tf_op jit(solution)/shard_map/ppermute | solution.py:293
  69.1 26.2 %collective-permute-start.5 = (bf16[128,2048]{1,0:T(8,128)(2,1)}, bf16[128,2048]{1,0:T(8,128)(2,1)}, u32[]{:S(2)}, u32[]{:S(2)}) collective-permute-start(bf16[128,2048]{1,0:T(8,128)(2,1)} %collective-permute-done.3.refs_5_), channel_id=1, source_target_pairs={{2,0},{3,1},{10,8},{11,9},{6,2},{7,3},{14,10},{15,11},{4,6},{5,7},... | collective-permute-start | bytes 1572872 | tf_op jit(solution)/shard_map/ppermute | solution.py:293
  70.3 24.9 %collective-permute-start.2 = (bf16[128,2176]{1,0:T(8,128)(2,1)}, bf16[128,2176]{1,0:T(8,128)(2,1)}, u32[]{:S(2)}, u32[]{:S(2)}) collective-permute-start(bf16[128,2176]{1,0:T(8,128)(2,1)} %collective-permute-done.1.refs_2_), channel_id=1, source_target_pairs={{0,2},{1,3},{8,10},{9,11},{2,6},{3,7},{10,14},{11,15},{6,4},{7,5},... | collective-permute-start | bytes 1671176 | tf_op jit(solution)/shard_map/ppermute | solution.py:290
  73.1 43.1 %collective-permute-start.10 = (bf16[3,12,64,128]{3,2,1,0:T(8,128)(2,1)S(1)}, bf16[3,12,64,128]{3,2,1,0:T(8,128)(2,1)}, u32[]{:S(2)}, u32[]{:S(2)}) collective-permute-start(bf16[3,12,64,128]{3,2,1,0:T(8,128)(2,1)S(1)} %bitcast.32), channel_id=1, source_target_pairs={{0,16},{16,0},{1,17},{17,1},{2,18},{18,2},{3,19},{19,3},{4,20},{20... | collective-permute-start | bytes 1769480 | tf_op jit(solution)/shard_map/ppermute | solution.py:299
  111.2 19.9 %collective-permute-start.9 = (bf16[3,12,128,128]{3,2,1,0:T(8,128)(2,1)}, bf16[3,12,128,128]{3,2,1,0:T(8,128)(2,1)}, u32[]{:S(2)}, u32[]{:S(2)}) collective-permute-start(bf16[3,12,128,128]{3,2,1,0:T(8,128)(2,1)} %bitcast.16), channel_id=1, source_target_pairs={{0,1},{1,0},{2,3},{3,2},{4,5},{5,4},{6,7},{7,6},{8,9},{9,8},{10,11... | collective-permute-start | bytes 3538952 | tf_op jit(solution)/shard_map/ppermute | solution.py:302
  111.3 19.8 %all-to-all-start.3 = ((bf16[16,144,128]{2,1,0:T(8,128)(2,1)}), bf16[16,144,128]{2,1,0:T(8,128)(2,1)}, u32[]{:S(2)}, u32[]{:S(2)}) async-start(bf16[16,144,128]{2,1,0:T(8,128)(2,1)} %bitcast.13), calls=%async_computation.3 | async-start | bytes 1179648 | tf_op jit(solution)/shard_map/all_to_all | solution.py:261
  155.3 23.4 %collective-permute-start.19 = (bf16[3,12,128,128]{3,2,1,0:T(8,128)(2,1)}, bf16[3,12,128,128]{3,2,1,0:T(8,128)(2,1)}, u32[]{:S(2)}, u32[]{:S(2)}) collective-permute-start(bf16[3,12,128,128]{3,2,1,0:T(8,128)(2,1)} %bitcast.23), channel_id=1, source_target_pairs={{0,1},{1,0},{2,3},{3,2},{4,5},{5,4},{6,7},{7,6},{8,9},{9,8},{10,11... | collective-permute-start | bytes 3538952 | tf_op jit(solution)/shard_map/ppermute | solution.py:302
  155.4 15.8 %collective-permute-start.13 = (bf16[128,1024]{1,0:T(8,128)(2,1)}, bf16[128,1024]{1,0:T(8,128)(2,1)}, u32[]{:S(2)}, u32[]{:S(2)}) collective-permute-start(bf16[128,1024]{1,0:T(8,128)(2,1)} %copy-done.8), channel_id=1, source_target_pairs={{0,2},{1,3},{8,10},{9,11},{2,6},{3,7},{10,14},{11,15},{6,4},{7,5},... | collective-permute-start | bytes 786440 | tf_op jit(solution)/shard_map/ppermute | solution.py:290
  160.4 28.8 %collective-permute-start.15 = (bf16[128,1024]{1,0:T(8,128)(2,1)S(1)}, bf16[128,1024]{1,0:T(8,128)(2,1)}, u32[]{:S(2)}, u32[]{:S(2)}) collective-permute-start(bf16[128,1024]{1,0:T(8,128)(2,1)S(1)} %copy-done.7), channel_id=1, source_target_pairs={{2,0},{3,1},{10,8},{11,9},{6,2},{7,3},{14,10},{15,11},{4,6},{5,7},... | collective-permute-start | bytes 786440 | tf_op jit(solution)/shard_map/ppermute | solution.py:293
  161.2 56.2 %collective-permute-start.16 = (bf16[128,1152]{1,0:T(8,128)(2,1)S(1)}, bf16[128,1152]{1,0:T(8,128)(2,1)}, u32[]{:S(2)}, u32[]{:S(2)}) collective-permute-start(bf16[128,1152]{1,0:T(8,128)(2,1)S(1)} %copy-done.4), channel_id=1, source_target_pairs={{0,2},{1,3},{8,10},{9,11},{2,6},{3,7},{10,14},{11,15},{6,4},{7,5},... | collective-permute-start | bytes 884744 | tf_op jit(solution)/shard_map/ppermute | solution.py:290
  167.0 27.0 %all-to-all-start.4 = ((bf16[16,144,128]{2,1,0:T(8,128)(2,1)}), bf16[16,144,128]{2,1,0:T(8,128)(2,1)}, u32[]{:S(2)}, u32[]{:S(2)}) async-start(bf16[16,144,128]{2,1,0:T(8,128)(2,1)} %broadcast_select_fusion.1), calls=%async_computation.4 | async-start | bytes 1179648 | tf_op jit(solution)/shard_map/all_to_all | solution.py:261
  171.3 17.1 %collective-permute-start.17 = (bf16[128,1152]{1,0:T(8,128)(2,1)}, bf16[128,1152]{1,0:T(8,128)(2,1)S(1)}, u32[]{:S(2)}, u32[]{:S(2)}) collective-permute-start(bf16[128,1152]{1,0:T(8,128)(2,1)} %copy-done.5), channel_id=1, source_target_pairs={{2,0},{3,1},{10,8},{11,9},{6,2},{7,3},{14,10},{15,11},{4,6},{5,7},... | collective-permute-start | bytes 884744 | tf_op jit(solution)/shard_map/ppermute | solution.py:293
  174.4 18.5 %collective-permute-start.14 = (bf16[128,1024]{1,0:T(8,128)(2,1)S(1)}, bf16[128,1024]{1,0:T(8,128)(2,1)S(1)}, u32[]{:S(2)}, u32[]{:S(2)}) collective-permute-start(bf16[128,1024]{1,0:T(8,128)(2,1)S(1)} %add_convert_fusion.6), channel_id=1, source_target_pairs={{0,2},{1,3},{8,10},{9,11},{2,6},{3,7},{10,14},{11,15},{6,4},{7,5},... | collective-permute-start | bytes 786440 | tf_op jit(solution)/shard_map/ppermute | solution.py:290
  178.7 34.5 %collective-permute-start.22 = (bf16[3,12,64,128]{3,2,1,0:T(8,128)(2,1)}, bf16[3,12,64,128]{3,2,1,0:T(8,128)(2,1)}, u32[]{:S(2)}, u32[]{:S(2)}) collective-permute-start(bf16[3,12,64,128]{3,2,1,0:T(8,128)(2,1)} %add_convert_fusion), channel_id=1, source_target_pairs={{0,8},{1,9},{2,10},{3,11},{4,12},{5,13},{6,14},{7,15},{8,0},{9,1},... | collective-permute-start | bytes 1769480 | tf_op jit(solution)/shard_map/ppermute | solution.py:419
  188.4 24.9 %collective-permute-start.20 = (bf16[3,12,64,128]{3,2,1,0:T(8,128)(2,1)}, bf16[3,12,64,128]{3,2,1,0:T(8,128)(2,1)}, u32[]{:S(2)}, u32[]{:S(2)}) collective-permute-start(bf16[3,12,64,128]{3,2,1,0:T(8,128)(2,1)} %add_convert_fusion.2), channel_id=1, source_target_pairs={{0,16},{16,0},{1,17},{17,1},{2,18},{18,2},{3,19},{19,3},{4,20},{20... | collective-permute-start | bytes 1769480 | tf_op jit(solution)/shard_map/ppermute | solution.py:299
  189.2 28.1 %collective-permute-start.18 = (bf16[128,1152]{1,0:T(8,128)(2,1)S(1)}, bf16[128,1152]{1,0:T(8,128)(2,1)S(1)}, u32[]{:S(2)}, u32[]{:S(2)}) collective-permute-start(bf16[128,1152]{1,0:T(8,128)(2,1)S(1)} %add_convert_fusion.4), channel_id=1, source_target_pairs={{2,0},{3,1},{10,8},{11,9},{6,2},{7,3},{14,10},{15,11},{4,6},{5,7},... | collective-permute-start | bytes 884744 | tf_op jit(solution)/shard_map/ppermute | solution.py:293
  (38 other events, 160.2 us)

commit v6 on v5

--- a/solution.py
+++ b/solution.py
@@ -343,16 +343,12 @@
         layout_note.reshape(1, note_rows, LANES), (expert_count, note_rows, LANES)
     )
     spread = swap_all(jnp.concatenate([pieces, note], axis=1))
-    all_layouts = spread[:, piece_rows:].reshape(expert_count, -1)[:, : layout_flat.shape[0]]
     all_slots = jnp.arange(expert_count, dtype=jnp.int32)
 
     def collect(spread_state, slot_order):
-        moved = jnp.take(spread_state, jnp.take(partner, slot_order), axis=0)
+        order = partner.at[slot_order].get(mode="promise_in_bounds")
+        moved = spread_state.at[order].get(mode="promise_in_bounds")
         return swap_all(moved).reshape(rows_now.shape)
-
-    rows_far = collect(spread[:, :piece_rows], all_slots ^ far)
-    rows_far, spread = lax.optimization_barrier((rows_far, spread))
-    rows_near = collect(spread[:, :piece_rows], all_slots)
 
     x_at = {0: jnp.concatenate([tokens, table], axis=1)}
     g_at = {0: out_grad}
@@ -363,7 +359,13 @@
         if s < most:
             x_at[s] = step_back(x_at[s - 1])
             g_at[-s] = step_on(g_at[1 - s])
+        if s == 1:
+            x_at, g_at, spread = lax.optimization_barrier((x_at, g_at, spread))
+            rows_far = collect(spread[:, :piece_rows], all_slots ^ far)
     x_at[most] = x_at[-most]
+    x_at, g_at, rows_far, spread = lax.optimization_barrier((x_at, g_at, rows_far, spread))
+    rows_near = collect(spread[:, :piece_rows], all_slots)
+    all_layouts = spread[:, piece_rows:].reshape(expert_count, -1)[:, : layout_flat.shape[0]]
     shards = [0]
     for s in range(1, most):
         shards += [s, -s]
@@ -381,8 +383,10 @@
         return [value.reshape(-1, value.shape[2], LANES) for value in weights]
 
     def run_pair(slot, weights, earlier):
-        experts = jnp.take(partner, jnp.stack([slot, slot ^ 1])).astype(jnp.int32)
-        layouts = jnp.take(all_layouts, experts, axis=0).reshape(-1).astype(jnp.int32)
+        pair = jnp.stack([slot, slot ^ 1])
+        experts = partner.at[pair].get(mode="promise_in_bounds").astype(jnp.int32)
+        layouts = all_layouts.at[experts].get(mode="promise_in_bounds")
+        layouts = layouts.reshape(-1).astype(jnp.int32)
         parts, sums = {}, None
         for group in groups:
             lows, highs, sums = run_experts(
@@ -411,22 +415,19 @@
     )
     moment_spread = swap_all(moment_pieces)
     parts, far_grad, far_sister = run_pair(me ^ far, weights_far, None)
-    parts, far_grad, far_sister, weights_near, moment_spread = lax.optimization_barrier(
-        (parts, far_grad, far_sister, weights_near, moment_spread)
-    )
+    far_sum = sum_rows(far_grad, far_sister).astype(bf16)
+    far_sum, weights_near, moment_spread = lax.optimization_barrier(
+        (far_sum, weights_near, moment_spread)
+    )
+    from_mirror = lax.ppermute(far_sum, "expert", mirror)
     moved_moments = collect(moment_spread, all_slots)
-    far_sum = sum_rows(far_grad, far_sister).astype(bf16)
-    from_mirror = lax.ppermute(far_sum, "expert", mirror)
     parts, near_grad, near_sister = run_pair(me, weights_near, parts)
-    shard_grad = sum_rows(near_grad, near_sister) + from_mirror.astype(f32)
-    new_moment = momentum_decay * moved_moments.astype(f32) + shard_grad
-    new_shard = (rows_near.astype(f32) - step_rate * new_moment).astype(bf16)
-
     def own_share(distance, part):
         return parts[distance][part]
 
     upward = [step_on(own_share(most, 0)), None]
     downward = [None, step_back(own_share(most, 1))]
+    upward[0], from_mirror = lax.optimization_barrier((upward[0], from_mirror))
     for s in range(most - 1, 0, -1):
         for part in range(2):
             share = own_share(s, part)
@@ -435,6 +436,10 @@
             downward[part] = step_back(
                 share if downward[part] is None else add(downward[part], share)
             )
+    shard_grad = sum_rows(near_grad, near_sister) + from_mirror.astype(f32)
+    new_moment = momentum_decay * moved_moments.astype(f32) + shard_grad
+    new_shard = (rows_near.astype(f32) - step_rate * new_moment).astype(bf16)
+
     homes = [
         (parts[0][part].astype(f32) + upward[part].astype(f32) + downward[part].astype(f32)).astype(
             bf16

time: 235 us -> 258 us (1.098)
  local copies, waits for them, and re-layouts: 22.6 us -> 43.9 us
  waiting for transfers between devices: 106 us -> 114 us
  other arithmetic: 26.3 us -> 21.5 us
    all_to_all x5, waiting for transfers between devices: 38.6 us -> 7.12 us  [swap_all(): lax.all_to_all(pieces, 'expert', split_axis=0, concat_axis=0, tiled=True)]
    ppermute x5, waiting for transfers between devices: 19.3 us -> 41.2 us  [other_replica(): return lax.ppermute(value, 'dp', [(0, 1), (1, 0)])]
    unnamed x63 -> x95, local copies, waits for them, and re-layouts: 10 us -> 23.2 us
    ppermute x6, waiting for transfers between devices: 27.9 us -> 39.2 us  [step_back(): return lax.ppermute(value, 'expert', backward)]
    ppermute x6, waiting for transfers between devices: 1.21 us -> 6.17 us  [step_on(): return lax.ppermute(value, 'expert', onward)]
    ppermute x6, starting transfers between devices: 8.08 us -> 3.91 us  [step_back(): return lax.ppermute(value, 'expert', backward)]
    select_n x7 -> x5, other arithmetic: 4.04 us -> 0.1 us  [the longest x1 0.08 us: run_pair(): experts = partner.at[pair].get(mode='promise_in_bounds').astype(jnp.int32)]
    gather x9, local copies, waits for them, and re-layouts: 7.54 us -> 11.2 us  [the longest x3 7.5 us: collect(): moved = spread_state.at[order].get(mode='promise_in_bounds')]
  transfers between devices with their start and end apart: 29 -> 29, of which waited for: 14 -> 14; matrix products, arithmetic and copies ran while one was open for 14% -> 13% of each run, Pallas kernels for 6% -> 0%
where the time goes in v6:
time: 258 us; the launch traced here: 256 us
  waiting for transfers between devices  114 us (44%)
  starting transfers between devices  49.3 us (19%)
  local copies, waits for them, and re-layouts  43.9 us (17%)
  Pallas kernels  26.2 us (10%)
  other arithmetic  21.5 us (8%)
    ppermute x5, waiting for transfers between devices, other_replica(): return lax.ppermute(value, 'dp', [(0, 1), (1, 0)])  41.2 us
    ppermute x6, waiting for transfers between devices, step_back(): return lax.ppermute(value, 'expert', backward)  39.2 us
    all_to_all x5, starting transfers between devices, swap_all(): lax.all_to_all(pieces, 'expert', split_axis=0, concat_axis=0, tiled=True)  27.1 us
    pallas_call x2, Pallas kernels, run_experts(): pl.pallas_call(functools.partial(expert_kernel, shards, slots, half, len(...  26.2 us
    unnamed x95, local copies, waits for them, and re-layouts  23.2 us
    ppermute x1, waiting for transfers between devices, body(): from_mirror = lax.ppermute(far_sum, 'expert', mirror)  20.3 us
    ppermute x6, starting transfers between devices, step_on(): return lax.ppermute(value, 'expert', onward)  11.9 us
    gather x3, local copies, waits for them, and re-layouts, collect(): moved = spread_state.at[order].get(mode='promise_in_bounds')  7.5 us
  transfers between devices with their start and end apart: 29, of which 14 were waited for; matrix products, arithmetic and copies ran while one was open for 13% of the time, Pallas kernels for 0%

profile of v6, /device:TPU:0, one launch (start us, length us, event | category | flops | bytes accessed | tf_op | source)
XLA Modules:
  0.0 256.0 jit_solution(3965744865495529921)
XLA Ops:
  0.6 3.0 %collective-permute-start.2 = (bf16[128,2048]{1,0:T(8,128)(2,1)}, bf16[128,2048]{1,0:T(8,128)(2,1)S(1)}, u32[]{:S(2)}, u32[]{:S(2)}) collective-permute-start(bf16[128,2048]{1,0:T(8,128)(2,1)} %refs_4_.1), channel_id=1, source_target_pairs={{0,2},{1,3},{8,10},{9,11},{2,6},{3,7},{10,14},{11,15},{6,4},{7,5},... | collective-permute-start | bytes 1572872 | tf_op jit(solution)/shard_map/ppermute | solution.py:290
  5.7 6.5 %all-to-all-start = ((bf16[16,160,128]{2,1,0:T(8,128)(2,1)}), bf16[16,160,128]{2,1,0:T(8,128)(2,1)}, u32[]{:S(2)}, u32[]{:S(2)}) async-start(bf16[16,160,128]{2,1,0:T(8,128)(2,1)} %pad_maximum_fusion), calls=%async_computation | async-start | bytes 1310720 | tf_op jit(solution)/shard_map/all_to_all | solution.py:261
  20.1 17.6 %collective-permute-done.1.refs_1_ = bf16[128,2176]{1,0:T(8,128)(2,1)S(1)} collective-permute-done((bf16[128,2176]{1,0:T(8,128)(2,1)S(1)}, bf16[128,2176]{1,0:T(8,128)(2,1)S(1)}, u32[]{:S(2)}, u32[]{:S(2)}) %collective-permute-start.1) | collective-permute-done | bytes 557088 | tf_op jit(solution)/shard_map/ppermute | solution.py:293
  40.5 2.5 gather_fusion.1
  43.0 6.6 %all-to-all-start.1 = ((bf16[16,144,128]{2,1,0:T(8,128)(2,1)}), bf16[16,144,128]{2,1,0:T(8,128)(2,1)S(1)}, u32[]{:S(2)}, u32[]{:S(2)}) async-start(bf16[16,144,128]{2,1,0:T(8,128)(2,1)} %gather_fusion.1), calls=%async_computation.1 | async-start | bytes 1179648 | tf_op jit(solution)/shard_map/all_to_all | solution.py:261
  51.7 19.8 %collective-permute-done.5.refs_7_ = bf16[128,2048]{1,0:T(8,128)(2,1)S(1)} collective-permute-done((bf16[128,2048]{1,0:T(8,128)(2,1)}, bf16[128,2048]{1,0:T(8,128)(2,1)S(1)}, u32[]{:S(2)}, u32[]{:S(2)}) %collective-permute-start.5) | collective-permute-done | bytes 524320 | tf_op jit(solution)/shard_map/ppermute | solution.py:293
  77.6 2.5 gather_fusion.7
  80.1 5.0 %all-to-all-start.2 = ((bf16[16,144,128]{2,1,0:T(8,128)(2,1)}), bf16[16,144,128]{2,1,0:T(8,128)(2,1)S(1)}, u32[]{:S(2)}, u32[]{:S(2)}) async-start(bf16[16,144,128]{2,1,0:T(8,128)(2,1)} %gather_fusion.7), calls=%async_computation.2 | async-start | bytes 1179648 | tf_op jit(solution)/shard_map/all_to_all | solution.py:261
  85.5 3.5 %collective-permute-done.6 = bf16[3,12,64,128]{3,2,1,0:T(8,128)(2,1)S(1)} collective-permute-done((bf16[3,12,64,128]{3,2,1,0:T(8,128)(2,1)S(1)}, bf16[3,12,64,128]{3,2,1,0:T(8,128)(2,1)S(1)}, u32[]{:S(2)}, u32[]{:S(2)}) %collective-permute-start.6) | collective-permute-done | bytes 589856 | tf_op jit(solution)/shard_map/ppermute | solution.py:299
  93.5 7.1 %all-to-all-done.2 = bf16[16,144,128]{2,1,0:T(8,128)(2,1)S(1)} async-done(((bf16[16,144,128]{2,1,0:T(8,128)(2,1)}), bf16[16,144,128]{2,1,0:T(8,128)(2,1)S(1)}, u32[]{:S(2)}, u32[]{:S(2)}) %all-to-all-start.2) | async-done | bytes 589856 | tf_op jit(solution)/shard_map/all_to_all | solution.py:261
  106.9 12.7 %shard_map.111 = (bf16[128,1024]{1,0:T(8,128)(2,1)S(1)}, bf16[128,1024]{1,0:T(8,128)(2,1)S(1)}, bf16[128,1024]{1,0:T(8,128)(2,1)S(1)}, bf16[128,1024]{1,0:T(8,12...) custom-call(s32[144]{0:T(256)S(1)} %reshape.381.lay_ref, ...), custom_call_target="tpu_custom_call" | custom-call | flops 7247757312 | bytes 13762560 | tf_op jit(solution)/shard_map/pallas_call | solution.py:220
  122.3 4.7 %all-to-all-start.3 = ((bf16[16,144,128]{2,1,0:T(8,128)(2,1)}), bf16[16,144,128]{2,1,0:T(8,128)(2,1)}, u32[]{:S(2)}, u32[]{:S(2)}) async-start(bf16[16,144,128]{2,1,0:T(8,128)(2,1)} %bitcast.22), calls=%async_computation.3 | async-start | bytes 1179648 | tf_op jit(solution)/shard_map/all_to_all | solution.py:261
  127.1 2.3 add_convert_fusion.2
  131.6 6.3 %collective-permute-done.11 = bf16[3,12,64,128]{3,2,1,0:T(8,128)(2,1)S(1)} collective-permute-done((bf16[3,12,64,128]{3,2,1,0:T(8,128)(2,1)S(1)}, bf16[3,12,64,128]{3,2,1,0:T(8,128)(2,1)S(1)}, u32[]{:S(2)}, u32[]{:S(2)}) %collective-permute-start.11) | collective-permute-done | bytes 589856 | tf_op jit(solution)/shard_map/ppermute | solution.py:299
  138.6 11.7 %collective-permute-done.10 = bf16[3,12,64,128]{3,2,1,0:T(8,128)(2,1)} collective-permute-done((bf16[3,12,64,128]{3,2,1,0:T(8,128)(2,1)}, bf16[3,12,64,128]{3,2,1,0:T(8,128)(2,1)}, u32[]{:S(2)}, u32[]{:S(2)}) %collective-permute-start.10) | collective-permute-done | bytes 589856 | tf_op jit(solution)/shard_map/ppermute | solution.py:299
  150.3 2.5 add_convert_fusion.1
  167.8 13.4 %shard_map.112 = (bf16[128,1024]{1,0:T(8,128)(2,1)S(1)}, bf16[128,1024]{1,0:T(8,128)(2,1)S(1)}, bf16[128,1024]{1,0:T(8,128)(2,1)S(1)}, bf16[128,1024]{1,0:T(8,12...) custom-call(s32[144]{0:T(256)S(1)} %reshape.380.lay_ref, ...), custom_call_target="tpu_custom_call" | custom-call | flops 7247757312 | bytes 13762560 | tf_op jit(solution)/shard_map/pallas_call | solution.py:220
  188.0 2.5 gather_fusion.8
  190.5 4.2 %all-to-all-start.4 = ((bf16[16,144,128]{2,1,0:T(8,128)(2,1)}), bf16[16,144,128]{2,1,0:T(8,128)(2,1)}, u32[]{:S(2)}, u32[]{:S(2)}) async-start(bf16[16,144,128]{2,1,0:T(8,128)(2,1)} %gather_fusion.8), calls=%async_computation.4 | async-start | bytes 1179648 | tf_op jit(solution)/shard_map/all_to_all | solution.py:261
  194.8 4.8 %collective-permute-start.18 = (bf16[128,1152]{1,0:T(8,128)(2,1)S(1)}, bf16[128,1152]{1,0:T(8,128)(2,1)S(1)}, u32[]{:S(2)}, u32[]{:S(2)}) collective-permute-start(bf16[128,1152]{1,0:T(8,128)(2,1)S(1)} %copy-done.21), channel_id=1, source_target_pairs={{0,2},{1,3},{8,10},{9,11},{2,6},{3,7},{10,14},{11,15},{6,4},{7,5},... | collective-permute-start | bytes 884744 | tf_op jit(solution)/shard_map/ppermute | solution.py:290
  200.7 20.3 %collective-permute-done.15 = bf16[3,12,64,128]{3,2,1,0:T(8,128)(2,1)} collective-permute-done((bf16[3,12,64,128]{3,2,1,0:T(8,128)(2,1)}, bf16[3,12,64,128]{3,2,1,0:T(8,128)(2,1)}, u32[]{:S(2)}, u32[]{:S(2)}) %collective-permute-start.15) | collective-permute-done | bytes 589856 | tf_op jit(solution)/shard_map/ppermute | solution.py:422
  227.9 10.2 %collective-permute-done.22 = bf16[3,12,64,128]{3,2,1,0:T(8,128)(2,1)} collective-permute-done((bf16[3,12,64,128]{3,2,1,0:T(8,128)(2,1)}, bf16[3,12,64,128]{3,2,1,0:T(8,128)(2,1)}, u32[]{:S(2)}, u32[]{:S(2)}) %collective-permute-start.22) | collective-permute-done | bytes 589856 | tf_op jit(solution)/shard_map/ppermute | solution.py:299
  238.1 3.1 %subtract_convert_fusion = (bf16[3,12,64,128]{3,2,1,0:T(8,128)(2,1)S(1)}, f32[3,12,64,128]{3,2,1,0:T(8,128)}) fusion(bf16[3,12,64,128]{3,2,1,0:T(8,128)(2,1)S(1)} %bitcast.57, f32[3,12,64,128]{3,2,1,0:T(8,128)S(1)} %bitcast.67, bf16[3,12,64,128]{3,2,1,0:T(8,128)(2,1)} %collective-permute-done.15, bf16[3,12,64,128]{3,2,1,0:T(8,128)(2,1)} %collective-permute-done.22, ...), kind=kLoop, calls=%fused_computation.9 | loop fusion | flops 3538944 | bytes 5898244 | tf_op jit(solution)/shard_map/convert_element_type | solution.py:441
  244.7 9.6 %collective-permute-done.23 = bf16[3,12,64,128]{3,2,1,0:T(8,128)(2,1)S(1)} collective-permute-done((bf16[3,12,64,128]{3,2,1,0:T(8,128)(2,1)S(1)}, bf16[3,12,64,128]{3,2,1,0:T(8,128)(2,1)S(1)}, u32[]{:S(2)}, u32[]{:S(2)}) %collective-permute-start.23) | collective-permute-done | bytes 589856 | tf_op jit(solution)/shard_map/ppermute | solution.py:299
  (196 shorter events, 72.3 us)
Async XLA Ops:
  0.6 17.7 %collective-permute-start.2 = (bf16[128,2048]{1,0:T(8,128)(2,1)}, bf16[128,2048]{1,0:T(8,128)(2,1)S(1)}, u32[]{:S(2)}, u32[]{:S(2)}) collective-permute-start(bf16[128,2048]{1,0:T(8,128)(2,1)} %refs_4_.1), channel_id=1, source_target_pairs={{0,2},{1,3},{8,10},{9,11},{2,6},{3,7},{10,14},{11,15},{6,4},{7,5},... | collective-permute-start | bytes 1572872 | tf_op jit(solution)/shard_map/ppermute | solution.py:290
  3.6 16.5 %collective-permute-start.3 = (bf16[128,2048]{1,0:T(8,128)(2,1)}, bf16[128,2048]{1,0:T(8,128)(2,1)}, u32[]{:S(2)}, u32[]{:S(2)}) collective-permute-start(bf16[128,2048]{1,0:T(8,128)(2,1)} %refs_4_.1), channel_id=1, source_target_pairs={{2,0},{3,1},{10,8},{11,9},{6,2},{7,3},{14,10},{15,11},{4,6},{5,7},... | collective-permute-start | bytes 1572872 | tf_op jit(solution)/shard_map/ppermute | solution.py:293
  5.7 32.6 %all-to-all-start = ((bf16[16,160,128]{2,1,0:T(8,128)(2,1)}), bf16[16,160,128]{2,1,0:T(8,128)(2,1)}, u32[]{:S(2)}, u32[]{:S(2)}) async-start(bf16[16,160,128]{2,1,0:T(8,128)(2,1)} %pad_maximum_fusion), calls=%async_computation | async-start | bytes 1310720 | tf_op jit(solution)/shard_map/all_to_all | solution.py:261
  12.6 25.1 %collective-permute-start.1 = (bf16[128,2176]{1,0:T(8,128)(2,1)S(1)}, bf16[128,2176]{1,0:T(8,128)(2,1)S(1)}, u32[]{:S(2)}, u32[]{:S(2)}) collective-permute-start(bf16[128,2176]{1,0:T(8,128)(2,1)S(1)} %pad_maximum_fusion.1.refs_0_), channel_id=1, source_target_pairs={{2,0},{3,1},{10,8},{11,9},{6,2},{7,3},{14,10},{15,11},{4,6},{5,7},... | collective-permute-start | bytes 1671176 | tf_op jit(solution)/shard_map/ppermute | solution.py:293
  14.5 23.8 %collective-permute-start = (bf16[128,2176]{1,0:T(8,128)(2,1)S(1)}, bf16[128,2176]{1,0:T(8,128)(2,1)S(1)}, u32[]{:S(2)}, u32[]{:S(2)}) collective-permute-start(bf16[128,2176]{1,0:T(8,128)(2,1)S(1)} %pad_maximum_fusion.1.refs_0_), channel_id=1, source_target_pairs={{0,2},{1,3},{8,10},{9,11},{2,6},{3,7},{10,14},{11,15},{6,4},{7,5},... | collective-permute-start | bytes 1671176 | tf_op jit(solution)/shard_map/ppermute | solution.py:290
  43.0 31.2 %all-to-all-start.1 = ((bf16[16,144,128]{2,1,0:T(8,128)(2,1)}), bf16[16,144,128]{2,1,0:T(8,128)(2,1)S(1)}, u32[]{:S(2)}, u32[]{:S(2)}) async-start(bf16[16,144,128]{2,1,0:T(8,128)(2,1)} %gather_fusion.1), calls=%async_computation.1 | async-start | bytes 1179648 | tf_op jit(solution)/shard_map/all_to_all | solution.py:261
  49.6 24.5 %collective-permute-start.4 = (bf16[128,2176]{1,0:T(8,128)(2,1)S(1)}, bf16[128,2176]{1,0:T(8,128)(2,1)S(1)}, u32[]{:S(2)}, u32[]{:S(2)}) collective-permute-start(bf16[128,2176]{1,0:T(8,128)(2,1)S(1)} %collective-permute-done.refs_2_), channel_id=1, source_target_pairs={{0,2},{1,3},{8,10},{9,11},{2,6},{3,7},{10,14},{11,15},{6,4},{7,5},... | collective-permute-start | bytes 1671176 | tf_op jit(solution)/shard_map/ppermute | solution.py:290
  51.6 19.9 %collective-permute-start.5 = (bf16[128,2048]{1,0:T(8,128)(2,1)}, bf16[128,2048]{1,0:T(8,128)(2,1)S(1)}, u32[]{:S(2)}, u32[]{:S(2)}) collective-permute-start(bf16[128,2048]{1,0:T(8,128)(2,1)} %collective-permute-done.3.refs_5_), channel_id=1, source_target_pairs={{2,0},{3,1},{10,8},{11,9},{6,2},{7,3},{14,10},{15,11},{4,6},{5,7},... | collective-permute-start | bytes 1572872 | tf_op jit(solution)/shard_map/ppermute | solution.py:293
  74.1 14.9 %collective-permute-start.6 = (bf16[3,12,64,128]{3,2,1,0:T(8,128)(2,1)S(1)}, bf16[3,12,64,128]{3,2,1,0:T(8,128)(2,1)S(1)}, u32[]{:S(2)}, u32[]{:S(2)}) collective-permute-start(bf16[3,12,64,128]{3,2,1,0:T(8,128)(2,1)S(1)} %bitcast.58), channel_id=1, source_target_pairs={{0,16},{16,0},{1,17},{17,1},{2,18},{18,2},{3,19},{19,3},{4,20},{20... | collective-permute-start | bytes 1769480 | tf_op jit(solution)/shard_map/ppermute | solution.py:299
  80.1 20.6 %all-to-all-start.2 = ((bf16[16,144,128]{2,1,0:T(8,128)(2,1)}), bf16[16,144,128]{2,1,0:T(8,128)(2,1)S(1)}, u32[]{:S(2)}, u32[]{:S(2)}) async-start(bf16[16,144,128]{2,1,0:T(8,128)(2,1)} %gather_fusion.7), calls=%async_computation.2 | async-start | bytes 1179648 | tf_op jit(solution)/shard_map/all_to_all | solution.py:261
  121.8 16.1 %collective-permute-start.11 = (bf16[3,12,64,128]{3,2,1,0:T(8,128)(2,1)S(1)}, bf16[3,12,64,128]{3,2,1,0:T(8,128)(2,1)S(1)}, u32[]{:S(2)}, u32[]{:S(2)}) collective-permute-start(bf16[3,12,64,128]{3,2,1,0:T(8,128)(2,1)S(1)} %bitcast.54), channel_id=1, source_target_pairs={{0,16},{16,0},{1,17},{17,1},{2,18},{18,2},{3,19},{19,3},{4,20},{20... | collective-permute-start | bytes 1769480 | tf_op jit(solution)/shard_map/ppermute | solution.py:299
  122.3 30.5 %all-to-all-start.3 = ((bf16[16,144,128]{2,1,0:T(8,128)(2,1)}), bf16[16,144,128]{2,1,0:T(8,128)(2,1)}, u32[]{:S(2)}, u32[]{:S(2)}) async-start(bf16[16,144,128]{2,1,0:T(8,128)(2,1)} %bitcast.22), calls=%async_computation.3 | async-start | bytes 1179648 | tf_op jit(solution)/shard_map/all_to_all | solution.py:261
  129.4 20.9 %collective-permute-start.10 = (bf16[3,12,64,128]{3,2,1,0:T(8,128)(2,1)}, bf16[3,12,64,128]{3,2,1,0:T(8,128)(2,1)}, u32[]{:S(2)}, u32[]{:S(2)}) collective-permute-start(bf16[3,12,64,128]{3,2,1,0:T(8,128)(2,1)} %add_convert_fusion.2), channel_id=1, source_target_pairs={{0,16},{16,0},{1,17},{17,1},{2,18},{18,2},{3,19},{19,3},{4,20},{20... | collective-permute-start | bytes 1769480 | tf_op jit(solution)/shard_map/ppermute | solution.py:299
  131.5 21.3 %collective-permute-start.12 = (bf16[3,12,64,128]{3,2,1,0:T(8,128)(2,1)S(1)}, bf16[3,12,64,128]{3,2,1,0:T(8,128)(2,1)}, u32[]{:S(2)}, u32[]{:S(2)}) collective-permute-start(bf16[3,12,64,128]{3,2,1,0:T(8,128)(2,1)S(1)} %bitcast.55), channel_id=1, source_target_pairs={{0,1},{1,0},{2,3},{3,2},{4,5},{5,4},{6,7},{7,6},{8,9},{9,8},{10,11... | collective-permute-start | bytes 1769480 | tf_op jit(solution)/shard_map/ppermute | solution.py:302
  137.9 14.9 %collective-permute-start.13 = (bf16[3,12,64,128]{3,2,1,0:T(8,128)(2,1)S(1)}, bf16[3,12,64,128]{3,2,1,0:T(8,128)(2,1)}, u32[]{:S(2)}, u32[]{:S(2)}) collective-permute-start(bf16[3,12,64,128]{3,2,1,0:T(8,128)(2,1)S(1)} %collective-permute-done.11), channel_id=1, source_target_pairs={{0,1},{1,0},{2,3},{3,2},{4,5},{5,4},{6,7},{7,6},{8,9},{9,8},{10,11... | collective-permute-start | bytes 1769480 | tf_op jit(solution)/shard_map/ppermute | solution.py:302
  183.0 38.8 %collective-permute-start.21 = (bf16[3,12,128,128]{3,2,1,0:T(8,128)(2,1)}, bf16[3,12,128,128]{3,2,1,0:T(8,128)(2,1)}, u32[]{:S(2)}, u32[]{:S(2)}) collective-permute-start(bf16[3,12,128,128]{3,2,1,0:T(8,128)(2,1)} %bitcast.34), channel_id=1, source_target_pairs={{0,1},{1,0},{2,3},{3,2},{4,5},{5,4},{6,7},{7,6},{8,9},{9,8},{10,11... | collective-permute-start | bytes 3538952 | tf_op jit(solution)/shard_map/ppermute | solution.py:302
  184.6 36.3 %collective-permute-start.15 = (bf16[3,12,64,128]{3,2,1,0:T(8,128)(2,1)}, bf16[3,12,64,128]{3,2,1,0:T(8,128)(2,1)}, u32[]{:S(2)}, u32[]{:S(2)}) collective-permute-start(bf16[3,12,64,128]{3,2,1,0:T(8,128)(2,1)} %add_convert_fusion.1), channel_id=1, source_target_pairs={{0,8},{1,9},{2,10},{3,11},{4,12},{5,13},{6,14},{7,15},{8,0},{9,1},... | collective-permute-start | bytes 1769480 | tf_op jit(solution)/shard_map/ppermute | solution.py:422
  185.9 14.7 %collective-permute-start.14 = (bf16[128,1024]{1,0:T(8,128)(2,1)}, bf16[128,1024]{1,0:T(8,128)(2,1)S(1)}, u32[]{:S(2)}, u32[]{:S(2)}) collective-permute-start(bf16[128,1024]{1,0:T(8,128)(2,1)} %copy-done.23), channel_id=1, source_target_pairs={{0,2},{1,3},{8,10},{9,11},{2,6},{3,7},{10,14},{11,15},{6,4},{7,5},... | collective-permute-start | bytes 786440 | tf_op jit(solution)/shard_map/ppermute | solution.py:290
  187.9 54.8 %collective-permute-start.17 = (bf16[128,1024]{1,0:T(8,128)(2,1)}, bf16[128,1024]{1,0:T(8,128)(2,1)}, u32[]{:S(2)}, u32[]{:S(2)}) collective-permute-start(bf16[128,1024]{1,0:T(8,128)(2,1)} %copy-done.22), channel_id=1, source_target_pairs={{2,0},{3,1},{10,8},{11,9},{6,2},{7,3},{14,10},{15,11},{4,6},{5,7},... | collective-permute-start | bytes 786440 | tf_op jit(solution)/shard_map/ppermute | solution.py:293
  190.5 36.3 %all-to-all-start.4 = ((bf16[16,144,128]{2,1,0:T(8,128)(2,1)}), bf16[16,144,128]{2,1,0:T(8,128)(2,1)}, u32[]{:S(2)}, u32[]{:S(2)}) async-start(bf16[16,144,128]{2,1,0:T(8,128)(2,1)} %gather_fusion.8), calls=%async_computation.4 | async-start | bytes 1179648 | tf_op jit(solution)/shard_map/all_to_all | solution.py:261
  194.8 31.1 %collective-permute-start.18 = (bf16[128,1152]{1,0:T(8,128)(2,1)S(1)}, bf16[128,1152]{1,0:T(8,128)(2,1)S(1)}, u32[]{:S(2)}, u32[]{:S(2)}) collective-permute-start(bf16[128,1152]{1,0:T(8,128)(2,1)S(1)} %copy-done.21), channel_id=1, source_target_pairs={{0,2},{1,3},{8,10},{9,11},{2,6},{3,7},{10,14},{11,15},{6,4},{7,5},... | collective-permute-start | bytes 884744 | tf_op jit(solution)/shard_map/ppermute | solution.py:290
  200.6 25.3 %collective-permute-start.20 = (bf16[128,1152]{1,0:T(8,128)(2,1)S(1)}, bf16[128,1152]{1,0:T(8,128)(2,1)S(1)}, u32[]{:S(2)}, u32[]{:S(2)}) collective-permute-start(bf16[128,1152]{1,0:T(8,128)(2,1)S(1)} %add_convert_fusion.4), channel_id=1, source_target_pairs={{2,0},{3,1},{10,8},{11,9},{6,2},{7,3},{14,10},{15,11},{4,6},{5,7},... | collective-permute-start | bytes 884744 | tf_op jit(solution)/shard_map/ppermute | solution.py:293
  221.7 20.9 %collective-permute-start.16 = (bf16[128,1024]{1,0:T(8,128)(2,1)}, bf16[128,1024]{1,0:T(8,128)(2,1)}, u32[]{:S(2)}, u32[]{:S(2)}) collective-permute-start(bf16[128,1024]{1,0:T(8,128)(2,1)} %add_convert_fusion.6), channel_id=1, source_target_pairs={{0,2},{1,3},{8,10},{9,11},{2,6},{3,7},{10,14},{11,15},{6,4},{7,5},... | collective-permute-start | bytes 786440 | tf_op jit(solution)/shard_map/ppermute | solution.py:290
  223.9 14.2 %collective-permute-start.22 = (bf16[3,12,64,128]{3,2,1,0:T(8,128)(2,1)}, bf16[3,12,64,128]{3,2,1,0:T(8,128)(2,1)}, u32[]{:S(2)}, u32[]{:S(2)}) collective-permute-start(bf16[3,12,64,128]{3,2,1,0:T(8,128)(2,1)} %add_convert_fusion), channel_id=1, source_target_pairs={{0,16},{16,0},{1,17},{17,1},{2,18},{18,2},{3,19},{19,3},{4,20},{20... | collective-permute-start | bytes 1769480 | tf_op jit(solution)/shard_map/ppermute | solution.py:299
  (53 other events, 239.4 us)

commit v7 on v6

--- a/solution.py
+++ b/solution.py
@@ -242,9 +242,9 @@
             pltpu.VMEM((shards, 2, tok, slots), bf16),
             pltpu.VMEM((rows, LANES), f32),
         ],
-        compiler_params=pltpu.CompilerParams(vmem_limit_bytes=40 * 1024 * 1024),
+        compiler_params=pltpu.CompilerParams(vmem_limit_bytes=30 * 1024 * 1024),
         cost_estimate=pl.CostEstimate(
-            flops=2 * 2 * 108 * rows * LANES * LANES * 4,
+            flops=2 * 2 * 108 * rows * LANES * LANES * 8,
             bytes_accessed=shards * tok * table_width * 6 + block_count * LANES * LANES * 6,
             transcendentals=0,
         ),
@@ -347,9 +347,10 @@
 
     def collect(spread_state, slot_order):
         order = partner.at[slot_order].get(mode="promise_in_bounds")
-        moved = spread_state.at[order].get(mode="promise_in_bounds")
+        moved = spread_state.at[order, :piece_rows].get(mode="promise_in_bounds")
         return swap_all(moved).reshape(rows_now.shape)
 
+    rows_far = collect(spread, all_slots ^ far)
     x_at = {0: jnp.concatenate([tokens, table], axis=1)}
     g_at = {0: out_grad}
     most = chips // 2
@@ -360,11 +361,9 @@
             x_at[s] = step_back(x_at[s - 1])
             g_at[-s] = step_on(g_at[1 - s])
         if s == 1:
-            x_at, g_at, spread = lax.optimization_barrier((x_at, g_at, spread))
-            rows_far = collect(spread[:, :piece_rows], all_slots ^ far)
+            x_at, g_at, rows_far, spread = lax.optimization_barrier((x_at, g_at, rows_far, spread))
     x_at[most] = x_at[-most]
-    x_at, g_at, rows_far, spread = lax.optimization_barrier((x_at, g_at, rows_far, spread))
-    rows_near = collect(spread[:, :piece_rows], all_slots)
+    rows_near = collect(spread, all_slots)
     all_layouts = spread[:, piece_rows:].reshape(expert_count, -1)[:, : layout_flat.shape[0]]
     shards = [0]
     for s in range(1, most):
@@ -379,10 +378,13 @@
 
     def both_cores(rows):
         halves = [rows, other_replica(rows)] if replica_count == 2 else [join_rows(rows)]
+        return halves
+
+    def to_weights(halves):
         weights = halves + [other_core(value) for value in halves]
         return [value.reshape(-1, value.shape[2], LANES) for value in weights]
 
-    def run_pair(slot, weights, earlier):
+    def run_pair(slot, weights, earlier, beside):
         pair = jnp.stack([slot, slot ^ 1])
         experts = partner.at[pair].get(mode="promise_in_bounds").astype(jnp.int32)
         layouts = all_layouts.at[experts].get(mode="promise_in_bounds")
@@ -403,31 +405,33 @@
             )
             for d, low, high in zip(group, lows, highs):
                 parts[d] = (low, high)
+        sums, beside = lax.optimization_barrier((sums, beside))
         half_count = sums.shape[0] // 2
         from_sister = other_core(sums[half_count:].reshape(blocks[0].shape))
-        return parts, sums[:half_count].reshape(blocks[0].shape), from_sister
+        return parts, sums[:half_count].reshape(blocks[0].shape), from_sister, beside
 
     moment_pieces = moments[0].astype(bf16).reshape(expert_count, -1, LANES)
-    weights_far = both_cores(rows_far)
-    weights_near = both_cores(rows_near)
+    halves_far = both_cores(rows_far)
+    halves_far, x_at, g_at = lax.optimization_barrier((halves_far, x_at, g_at))
+    weights_far = to_weights(halves_far)
     weights_far, moment_pieces, rows_near = lax.optimization_barrier(
         (weights_far, moment_pieces, rows_near)
     )
-    moment_spread = swap_all(moment_pieces)
-    parts, far_grad, far_sister = run_pair(me ^ far, weights_far, None)
+    weights_near = to_weights(both_cores(rows_near))
+    parts, far_grad, far_sister, moment_spread = run_pair(
+        me ^ far, weights_far, None, swap_all(moment_pieces)
+    )
     far_sum = sum_rows(far_grad, far_sister).astype(bf16)
-    far_sum, weights_near, moment_spread = lax.optimization_barrier(
-        (far_sum, weights_near, moment_spread)
-    )
+    far_sum, weights_near = lax.optimization_barrier((far_sum, weights_near))
     from_mirror = lax.ppermute(far_sum, "expert", mirror)
-    moved_moments = collect(moment_spread, all_slots)
-    parts, near_grad, near_sister = run_pair(me, weights_near, parts)
+    parts, near_grad, near_sister, moved_moments = run_pair(
+        me, weights_near, parts, collect(moment_spread, all_slots)
+    )
     def own_share(distance, part):
         return parts[distance][part]
 
     upward = [step_on(own_share(most, 0)), None]
     downward = [None, step_back(own_share(most, 1))]
-    upward[0], from_mirror = lax.optimization_barrier((upward[0], from_mirror))
     for s in range(most - 1, 0, -1):
         for part in range(2):
             share = own_share(s, part)

time: 258 us -> 264 us (1.023)
  local copies, waits for them, and re-layouts: 43.9 us -> 65 us
  waiting for transfers between devices: 114 us -> 98.2 us
    ppermute x6, waiting for transfers between devices: 39.2 us -> 0.82 us  [step_back(): return lax.ppermute(value, 'expert', backward)]
    ppermute x6, waiting for transfers between devices: 6.17 us -> 42.9 us  [step_on(): return lax.ppermute(value, 'expert', onward)]
    ppermute x5, waiting for transfers between devices: 41.2 us -> 19.4 us  [other_replica(): return lax.ppermute(value, 'dp', [(0, 1), (1, 0)])]
    unnamed x95 -> x141, local copies, waits for them, and re-layouts: 23.2 us -> 40.4 us
    all_to_all x5, waiting for transfers between devices: 7.12 us -> 21.5 us  [swap_all(): lax.all_to_all(pieces, 'expert', split_axis=0, concat_axis=0, tiled=True)]
    ppermute x1, waiting for transfers between devices: 20.3 us -> 11.3 us  [body(): from_mirror = lax.ppermute(far_sum, 'expert', mirror)]
    slice x4 -> x2, local copies, waits for them, and re-layouts: 7.47 us -> 3.12 us  [run_pair(): sums[:half_count].reshape(blocks[0].shape)]
    ppermute x6, starting transfers between devices: 11.9 us -> 7.63 us  [step_on(): return lax.ppermute(value, 'expert', onward)]
  transfers between devices with their start and end apart: 29 -> 29, of which waited for: 14 -> 10; matrix products, arithmetic and copies ran while one was open for 13% -> 15% of each run, Pallas kernels for 0% -> 10%
where the time goes in v7:
time: 264 us; the launch traced here: 262 us
  waiting for transfers between devices  98.2 us (37%)
  local copies, waits for them, and re-layouts  65 us (25%)
  starting transfers between devices  47.8 us (18%)
  Pallas kernels  25.8 us (10%)
  other arithmetic  23.9 us (9%)
    ppermute x6, waiting for transfers between devices, step_on(): return lax.ppermute(value, 'expert', onward)  42.9 us
    unnamed x141, local copies, waits for them, and re-layouts  40.4 us
    all_to_all x5, starting transfers between devices, swap_all(): lax.all_to_all(pieces, 'expert', split_axis=0, concat_axis=0, tiled=True)  27.3 us
    pallas_call x2, Pallas kernels, run_experts(): pl.pallas_call(functools.partial(expert_kernel, shards, slots, half, len(...  25.8 us
    all_to_all x5, waiting for transfers between devices, swap_all(): lax.all_to_all(pieces, 'expert', split_axis=0, concat_axis=0, tiled=True)  21.5 us
    ppermute x5, waiting for transfers between devices, other_replica(): return lax.ppermute(value, 'dp', [(0, 1), (1, 0)])  19.4 us
    gather x5, local copies, waits for them, and re-layouts, collect(): moved = spread_state.at[order, :piece_rows].get(mode='promise_in_bounds')  11.4 us
    ppermute x1, waiting for transfers between devices, body(): from_mirror = lax.ppermute(far_sum, 'expert', mirror)  11.3 us
  transfers between devices with their start and end apart: 29, of which 10 were waited for; matrix products, arithmetic and copies ran while one was open for 15% of the time, Pallas kernels for 10%

profile of v7, /device:TPU:0, one launch (start us, length us, event | category | flops | bytes accessed | tf_op | source)
XLA Modules:
  0.0 261.9 jit_solution(7969761838850535944)
XLA Ops:
  2.9 7.4 %all-to-all-start = ((bf16[16,160,128]{2,1,0:T(8,128)(2,1)}), bf16[16,160,128]{2,1,0:T(8,128)(2,1)S(1)}, u32[]{:S(2)}, u32[]{:S(2)}) async-start(bf16[16,160,128]{2,1,0:T(8,128)(2,1)} %pad_maximum_fusion), calls=%async_computation | async-start | bytes 1310720 | tf_op jit(solution)/shard_map/all_to_all | solution.py:261
  12.2 14.7 %all-to-all-done = bf16[16,160,128]{2,1,0:T(8,128)(2,1)S(1)} async-done(((bf16[16,160,128]{2,1,0:T(8,128)(2,1)}), bf16[16,160,128]{2,1,0:T(8,128)(2,1)S(1)}, u32[]{:S(2)}, u32[]{:S(2)}) %all-to-all-start) | async-done | bytes 655392 | tf_op jit(solution)/shard_map/all_to_all | solution.py:261
  27.1 2.3 gather_fusion.1
  30.4 4.9 %all-to-all-start.1 = ((bf16[16,144,128]{2,1,0:T(8,128)(2,1)}), bf16[16,144,128]{2,1,0:T(8,128)(2,1)S(1)}, u32[]{:S(2)}, u32[]{:S(2)}) async-start(bf16[16,144,128]{2,1,0:T(8,128)(2,1)} %copy.31), calls=%async_computation.1 | async-start | bytes 1179648 | tf_op jit(solution)/shard_map/all_to_all | solution.py:261
  40.6 30.5 %collective-permute-done.2.refs_6_ = bf16[128,2048]{1,0:T(8,128)(2,1)S(1)} collective-permute-done((bf16[128,2048]{1,0:T(8,128)(2,1)S(1)}, bf16[128,2048]{1,0:T(8,128)(2,1)S(1)}, u32[]{:S(2)}, u32[]{:S(2)}) %collective-permute-start.2) | collective-permute-done | bytes 524320 | tf_op jit(solution)/shard_map/ppermute | solution.py:290
  78.6 3.6 %gather_fusion.7 = bf16[16,144,128]{2,0,1:T(8,128)(2,1)} fusion(bf16[16,160,128]{2,0,1:T(8,128)(2,1)} %copy.32, s32[16]{0:T(128)S(1)} %get-tuple-element.125), kind=kCustom, calls=%fused_computation.7 | custom fusion | bytes 1179776 | tf_op jit(solution)/shard_map/gather | solution.py:350
  84.2 4.7 %all-to-all-start.2 = ((bf16[16,144,128]{2,1,0:T(8,128)(2,1)}), bf16[16,144,128]{2,1,0:T(8,128)(2,1)}, u32[]{:S(2)}, u32[]{:S(2)}) async-start(bf16[16,144,128]{2,1,0:T(8,128)(2,1)} %copy.33), calls=%async_computation.2 | async-start | bytes 1179648 | tf_op jit(solution)/shard_map/all_to_all | solution.py:261
  91.6 2.2 convert_element_type.138
  97.7 6.8 %all-to-all-done.2 = bf16[16,144,128]{2,1,0:T(8,128)(2,1)} async-done(((bf16[16,144,128]{2,1,0:T(8,128)(2,1)}), bf16[16,144,128]{2,1,0:T(8,128)(2,1)}, u32[]{:S(2)}, u32[]{:S(2)}) %all-to-all-start.2) | async-done | bytes 589856 | tf_op jit(solution)/shard_map/all_to_all | solution.py:261
  105.5 4.5 %all-to-all-start.3 = ((bf16[16,144,128]{2,1,0:T(8,128)(2,1)}), bf16[16,144,128]{2,1,0:T(8,128)(2,1)}, u32[]{:S(2)}, u32[]{:S(2)}) async-start(bf16[16,144,128]{2,1,0:T(8,128)(2,1)} %bitcast.77), calls=%async_computation.3 | async-start | bytes 1179648 | tf_op jit(solution)/shard_map/all_to_all | solution.py:261
  120.6 12.5 %shard_map.111 = (bf16[128,1024]{1,0:T(8,128)(2,1)S(1)}, bf16[128,1024]{1,0:T(8,128)(2,1)S(1)}, bf16[128,1024]{1,0:T(8,128)(2,1)S(1)}, bf16[128,1024]{1,0:T(8,12...) custom-call(s32[144]{0:T(256)S(1)} %reshape.385.lay_ref, ...), custom_call_target="tpu_custom_call" | custom-call | flops 14495514624 | bytes 13762560 | tf_op jit(solution)/shard_map/pallas_call | solution.py:220
  141.3 2.2 collective-permute-done.9
  143.5 2.5 add_convert_fusion.2
  148.6 8.6 %collective-permute-done.11 = bf16[3,12,64,128]{3,2,1,0:T(8,128)(2,1)S(1)} collective-permute-done((bf16[3,12,64,128]{3,2,1,0:T(8,128)(2,1)}, bf16[3,12,64,128]{3,2,1,0:T(8,128)(2,1)S(1)}, u32[]{:S(2)}, u32[]{:S(2)}) %collective-permute-start.11) | collective-permute-done | bytes 589856 | tf_op jit(solution)/shard_map/ppermute | solution.py:299
  160.9 2.5 gather_fusion.8
  163.4 5.9 %all-to-all-start.4 = ((bf16[16,144,128]{2,1,0:T(8,128)(2,1)}), bf16[16,144,128]{2,1,0:T(8,128)(2,1)}, u32[]{:S(2)}, u32[]{:S(2)}) async-start(bf16[16,144,128]{2,1,0:T(8,128)(2,1)} %gather_fusion.8), calls=%async_computation.4 | async-start | bytes 1179648 | tf_op jit(solution)/shard_map/all_to_all | solution.py:261
  169.3 2.5 add_convert_fusion.1
  186.4 13.3 %shard_map.112 = (bf16[128,1024]{1,0:T(8,128)(2,1)S(1)}, bf16[128,1024]{1,0:T(8,128)(2,1)S(1)}, bf16[128,1024]{1,0:T(8,128)(2,1)S(1)}, bf16[128,1024]{1,0:T(8,12...) custom-call(s32[144]{0:T(256)S(1)} %reshape.384.lay_ref, ...), custom_call_target="tpu_custom_call" | custom-call | flops 14495514624 | bytes 13762560 | tf_op jit(solution)/shard_map/pallas_call | solution.py:220
  210.8 5.1 %collective-permute-done.14 = bf16[128,1024]{1,0:T(8,128)(2,1)S(1)} collective-permute-done((bf16[128,1024]{1,0:T(8,128)(2,1)}, bf16[128,1024]{1,0:T(8,128)(2,1)S(1)}, u32[]{:S(2)}, u32[]{:S(2)}) %collective-permute-start.14) | collective-permute-done | bytes 262176 | tf_op jit(solution)/shard_map/ppermute | solution.py:290
  215.9 2.6 collective-permute-start.22
  225.2 7.3 %collective-permute-done.15 = bf16[128,1024]{1,0:T(8,128)(2,1)S(1)} collective-permute-done((bf16[128,1024]{1,0:T(8,128)(2,1)S(1)}, bf16[128,1024]{1,0:T(8,128)(2,1)S(1)}, u32[]{:S(2)}, u32[]{:S(2)}) %collective-permute-start.15) | collective-permute-done | bytes 262176 | tf_op jit(solution)/shard_map/ppermute | solution.py:290
  232.6 11.3 %collective-permute-done.22 = bf16[3,12,64,128]{3,2,1,0:T(8,128)(2,1)S(1)} collective-permute-done((bf16[3,12,64,128]{3,2,1,0:T(8,128)(2,1)}, bf16[3,12,64,128]{3,2,1,0:T(8,128)(2,1)S(1)}, u32[]{:S(2)}, u32[]{:S(2)}) %collective-permute-start.22) | collective-permute-done | bytes 589856 | tf_op jit(solution)/shard_map/ppermute | solution.py:426
  243.9 3.0 %fusion.9 = (f32[1,3,12,64,128]{4,3,2,1,0:T(8,128)}, bf16[3,12,64,128]{3,2,1,0:T(8,128)(2,1)S(1)}) fusion(bf16[3,12,64,128]{3,2,1,0:T(8,128)(2,1)S(1)} %collective-permute-done.22, bf16[3,12,64,128]{3,2,1,0:T(8,128)(2,1)S(1)} %collective-permute-done.21, bf16[3,12,128,128]{3,2,1,0:T(8,128)(2,1)S(1)} %collective-permute-done.20, s32[]{:T(128)S(6)} %select_n.106, ...), kind=kLoop, calls=%fused_computation.55 | loop fusion | flops 4128768 | bytes 5308420 | tf_op jit(solution)/shard_map/broadcast_in_dim | solution.py:457
  249.3 10.8 %collective-permute-done.23 = bf16[3,12,64,128]{3,2,1,0:T(8,128)(2,1)S(1)} collective-permute-done((bf16[3,12,64,128]{3,2,1,0:T(8,128)(2,1)S(1)}, bf16[3,12,64,128]{3,2,1,0:T(8,128)(2,1)S(1)}, u32[]{:S(2)}, u32[]{:S(2)}) %collective-permute-start.23) | collective-permute-done | bytes 589856 | tf_op jit(solution)/shard_map/ppermute | solution.py:299
  (242 shorter events, 89.1 us)
Async XLA Ops:
  2.9 24.0 %all-to-all-start = ((bf16[16,160,128]{2,1,0:T(8,128)(2,1)}), bf16[16,160,128]{2,1,0:T(8,128)(2,1)S(1)}, u32[]{:S(2)}, u32[]{:S(2)}) async-start(bf16[16,160,128]{2,1,0:T(8,128)(2,1)} %pad_maximum_fusion), calls=%async_computation | async-start | bytes 1310720 | tf_op jit(solution)/shard_map/all_to_all | solution.py:261
  30.4 42.3 %all-to-all-start.1 = ((bf16[16,144,128]{2,1,0:T(8,128)(2,1)}), bf16[16,144,128]{2,1,0:T(8,128)(2,1)S(1)}, u32[]{:S(2)}, u32[]{:S(2)}) async-start(bf16[16,144,128]{2,1,0:T(8,128)(2,1)} %copy.31), calls=%async_computation.1 | async-start | bytes 1179648 | tf_op jit(solution)/shard_map/all_to_all | solution.py:261
  35.7 36.2 %collective-permute-start.1 = (bf16[128,2176]{1,0:T(8,128)(2,1)S(1)}, bf16[128,2176]{1,0:T(8,128)(2,1)S(1)}, u32[]{:S(2)}, u32[]{:S(2)}) collective-permute-start(bf16[128,2176]{1,0:T(8,128)(2,1)S(1)} %pad_maximum_fusion.1.refs_0_), channel_id=1, source_target_pairs={{2,0},{3,1},{10,8},{11,9},{6,2},{7,3},{14,10},{15,11},{4,6},{5,7},... | collective-permute-start | bytes 1671176 | tf_op jit(solution)/shard_map/ppermute | solution.py:293
  37.7 35.1 %collective-permute-start = (bf16[128,2176]{1,0:T(8,128)(2,1)S(1)}, bf16[128,2176]{1,0:T(8,128)(2,1)S(1)}, u32[]{:S(2)}, u32[]{:S(2)}) collective-permute-start(bf16[128,2176]{1,0:T(8,128)(2,1)S(1)} %pad_maximum_fusion.1.refs_0_), channel_id=1, source_target_pairs={{0,2},{1,3},{8,10},{9,11},{2,6},{3,7},{10,14},{11,15},{6,4},{7,5},... | collective-permute-start | bytes 1671176 | tf_op jit(solution)/shard_map/ppermute | solution.py:290
  38.6 32.5 %collective-permute-start.2 = (bf16[128,2048]{1,0:T(8,128)(2,1)S(1)}, bf16[128,2048]{1,0:T(8,128)(2,1)S(1)}, u32[]{:S(2)}, u32[]{:S(2)}) collective-permute-start(bf16[128,2048]{1,0:T(8,128)(2,1)S(1)} %copy-done.34), channel_id=1, source_target_pairs={{0,2},{1,3},{8,10},{9,11},{2,6},{3,7},{10,14},{11,15},{6,4},{7,5},... | collective-permute-start | bytes 1572872 | tf_op jit(solution)/shard_map/ppermute | solution.py:290
  40.5 31.4 %collective-permute-start.3 = (bf16[128,2048]{1,0:T(8,128)(2,1)S(1)}, bf16[128,2048]{1,0:T(8,128)(2,1)}, u32[]{:S(2)}, u32[]{:S(2)}) collective-permute-start(bf16[128,2048]{1,0:T(8,128)(2,1)S(1)} %copy-done.34), channel_id=1, source_target_pairs={{2,0},{3,1},{10,8},{11,9},{6,2},{7,3},{14,10},{15,11},{4,6},{5,7},... | collective-permute-start | bytes 1572872 | tf_op jit(solution)/shard_map/ppermute | solution.py:293
  72.8 17.0 %collective-permute-start.4 = (bf16[3,12,64,128]{3,2,1,0:T(8,128)(2,1)S(1)}, bf16[3,12,64,128]{3,2,1,0:T(8,128)(2,1)S(1)}, u32[]{:S(2)}, u32[]{:S(2)}) collective-permute-start(bf16[3,12,64,128]{3,2,1,0:T(8,128)(2,1)S(1)} %bitcast.61), channel_id=1, source_target_pairs={{0,16},{16,0},{1,17},{17,1},{2,18},{18,2},{3,19},{19,3},{4,20},{20... | collective-permute-start | bytes 1769480 | tf_op jit(solution)/shard_map/ppermute | solution.py:299
  74.4 14.5 %collective-permute-start.5 = (bf16[128,2176]{1,0:T(8,128)(2,1)S(1)}, bf16[128,2176]{1,0:T(8,128)(2,1)S(1)}, u32[]{:S(2)}, u32[]{:S(2)}) collective-permute-start(bf16[128,2176]{1,0:T(8,128)(2,1)S(1)} %collective-permute-done.refs_2_), channel_id=1, source_target_pairs={{0,2},{1,3},{8,10},{9,11},{2,6},{3,7},{10,14},{11,15},{6,4},{7,5},... | collective-permute-start | bytes 1671176 | tf_op jit(solution)/shard_map/ppermute | solution.py:290
  75.1 13.8 %collective-permute-start.6 = (bf16[128,2048]{1,0:T(8,128)(2,1)}, bf16[128,2048]{1,0:T(8,128)(2,1)}, u32[]{:S(2)}, u32[]{:S(2)}) collective-permute-start(bf16[128,2048]{1,0:T(8,128)(2,1)} %collective-permute-done.3.refs_5_), channel_id=1, source_target_pairs={{2,0},{3,1},{10,8},{11,9},{6,2},{7,3},{14,10},{15,11},{4,6},{5,7},... | collective-permute-start | bytes 1572872 | tf_op jit(solution)/shard_map/ppermute | solution.py:293
  84.2 20.3 %all-to-all-start.2 = ((bf16[16,144,128]{2,1,0:T(8,128)(2,1)}), bf16[16,144,128]{2,1,0:T(8,128)(2,1)}, u32[]{:S(2)}, u32[]{:S(2)}) async-start(bf16[16,144,128]{2,1,0:T(8,128)(2,1)} %copy.33), calls=%async_computation.2 | async-start | bytes 1179648 | tf_op jit(solution)/shard_map/all_to_all | solution.py:261
  89.7 14.8 %collective-permute-start.7 = (bf16[3,12,64,128]{3,2,1,0:T(8,128)(2,1)S(1)}, bf16[3,12,64,128]{3,2,1,0:T(8,128)(2,1)S(1)}, u32[]{:S(2)}, u32[]{:S(2)}) collective-permute-start(bf16[3,12,64,128]{3,2,1,0:T(8,128)(2,1)S(1)} %bitcast.62), channel_id=1, source_target_pairs={{0,1},{1,0},{2,3},{3,2},{4,5},{5,4},{6,7},{7,6},{8,9},{9,8},{10,11... | collective-permute-start | bytes 1769480 | tf_op jit(solution)/shard_map/ppermute | solution.py:302
  90.2 14.3 %collective-permute-start.8 = (bf16[3,12,64,128]{3,2,1,0:T(8,128)(2,1)S(1)}, bf16[3,12,64,128]{3,2,1,0:T(8,128)(2,1)S(1)}, u32[]{:S(2)}, u32[]{:S(2)}) collective-permute-start(bf16[3,12,64,128]{3,2,1,0:T(8,128)(2,1)S(1)} %collective-permute-done.4), channel_id=1, source_target_pairs={{0,1},{1,0},{2,3},{3,2},{4,5},{5,4},{6,7},{7,6},{8,9},{9,8},{10,11... | collective-permute-start | bytes 1769480 | tf_op jit(solution)/shard_map/ppermute | solution.py:302
  105.5 33.4 %all-to-all-start.3 = ((bf16[16,144,128]{2,1,0:T(8,128)(2,1)}), bf16[16,144,128]{2,1,0:T(8,128)(2,1)}, u32[]{:S(2)}, u32[]{:S(2)}) async-start(bf16[16,144,128]{2,1,0:T(8,128)(2,1)} %bitcast.77), calls=%async_computation.3 | async-start | bytes 1179648 | tf_op jit(solution)/shard_map/all_to_all | solution.py:261
  140.8 16.4 %collective-permute-start.11 = (bf16[3,12,64,128]{3,2,1,0:T(8,128)(2,1)}, bf16[3,12,64,128]{3,2,1,0:T(8,128)(2,1)S(1)}, u32[]{:S(2)}, u32[]{:S(2)}) collective-permute-start(bf16[3,12,64,128]{3,2,1,0:T(8,128)(2,1)} %bitcast.25), channel_id=1, source_target_pairs={{0,16},{16,0},{1,17},{17,1},{2,18},{18,2},{3,19},{19,3},{4,20},{20... | collective-permute-start | bytes 1769480 | tf_op jit(solution)/shard_map/ppermute | solution.py:299
  146.0 23.3 %collective-permute-start.10 = (bf16[3,12,64,128]{3,2,1,0:T(8,128)(2,1)}, bf16[3,12,64,128]{3,2,1,0:T(8,128)(2,1)S(1)}, u32[]{:S(2)}, u32[]{:S(2)}) collective-permute-start(bf16[3,12,64,128]{3,2,1,0:T(8,128)(2,1)} %add_convert_fusion.2), channel_id=1, source_target_pairs={{0,16},{16,0},{1,17},{17,1},{2,18},{18,2},{3,19},{19,3},{4,20},{20... | collective-permute-start | bytes 1769480 | tf_op jit(solution)/shard_map/ppermute | solution.py:299
  148.5 23.3 %collective-permute-start.12 = (bf16[3,12,64,128]{3,2,1,0:T(8,128)(2,1)}, bf16[3,12,64,128]{3,2,1,0:T(8,128)(2,1)S(1)}, u32[]{:S(2)}, u32[]{:S(2)}) collective-permute-start(bf16[3,12,64,128]{3,2,1,0:T(8,128)(2,1)} %bitcast.25), channel_id=1, source_target_pairs={{0,1},{1,0},{2,3},{3,2},{4,5},{5,4},{6,7},{7,6},{8,9},{9,8},{10,11... | collective-permute-start | bytes 1769480 | tf_op jit(solution)/shard_map/ppermute | solution.py:302
  157.2 15.5 %collective-permute-start.13 = (bf16[3,12,64,128]{3,2,1,0:T(8,128)(2,1)S(1)}, bf16[3,12,64,128]{3,2,1,0:T(8,128)(2,1)S(1)}, u32[]{:S(2)}, u32[]{:S(2)}) collective-permute-start(bf16[3,12,64,128]{3,2,1,0:T(8,128)(2,1)S(1)} %collective-permute-done.11), channel_id=1, source_target_pairs={{0,1},{1,0},{2,3},{3,2},{4,5},{5,4},{6,7},{7,6},{8,9},{9,8},{10,11... | collective-permute-start | bytes 1769480 | tf_op jit(solution)/shard_map/ppermute | solution.py:302
  163.4 41.3 %all-to-all-start.4 = ((bf16[16,144,128]{2,1,0:T(8,128)(2,1)}), bf16[16,144,128]{2,1,0:T(8,128)(2,1)}, u32[]{:S(2)}, u32[]{:S(2)}) async-start(bf16[16,144,128]{2,1,0:T(8,128)(2,1)} %gather_fusion.8), calls=%async_computation.4 | async-start | bytes 1179648 | tf_op jit(solution)/shard_map/all_to_all | solution.py:261
  206.2 13.3 %collective-permute-start.20 = (bf16[3,12,128,128]{3,2,1,0:T(8,128)(2,1)}, bf16[3,12,128,128]{3,2,1,0:T(8,128)(2,1)S(1)}, u32[]{:S(2)}, u32[]{:S(2)}) collective-permute-start(bf16[3,12,128,128]{3,2,1,0:T(8,128)(2,1)} %bitcast.35), channel_id=1, source_target_pairs={{0,1},{1,0},{2,3},{3,2},{4,5},{5,4},{6,7},{7,6},{8,9},{9,8},{10,11... | collective-permute-start | bytes 3538952 | tf_op jit(solution)/shard_map/ppermute | solution.py:302
  208.4 15.4 %collective-permute-start.16 = (bf16[128,1024]{1,0:T(8,128)(2,1)}, bf16[128,1024]{1,0:T(8,128)(2,1)S(1)}, u32[]{:S(2)}, u32[]{:S(2)}) collective-permute-start(bf16[128,1024]{1,0:T(8,128)(2,1)} %copy-done.42), channel_id=1, source_target_pairs={{2,0},{3,1},{10,8},{11,9},{6,2},{7,3},{14,10},{15,11},{4,6},{5,7},... | collective-permute-start | bytes 786440 | tf_op jit(solution)/shard_map/ppermute | solution.py:293
  208.8 38.6 %collective-permute-start.17 = (bf16[128,1152]{1,0:T(8,128)(2,1)}, bf16[128,1152]{1,0:T(8,128)(2,1)S(1)}, u32[]{:S(2)}, u32[]{:S(2)}) collective-permute-start(bf16[128,1152]{1,0:T(8,128)(2,1)} %copy-done.40), channel_id=1, source_target_pairs={{0,2},{1,3},{8,10},{9,11},{2,6},{3,7},{10,14},{11,15},{6,4},{7,5},... | collective-permute-start | bytes 884744 | tf_op jit(solution)/shard_map/ppermute | solution.py:290
  215.9 27.9 %collective-permute-start.22 = (bf16[3,12,64,128]{3,2,1,0:T(8,128)(2,1)}, bf16[3,12,64,128]{3,2,1,0:T(8,128)(2,1)S(1)}, u32[]{:S(2)}, u32[]{:S(2)}) collective-permute-start(bf16[3,12,64,128]{3,2,1,0:T(8,128)(2,1)} %add_convert_fusion.1), channel_id=1, source_target_pairs={{0,8},{1,9},{2,10},{3,11},{4,12},{5,13},{6,14},{7,15},{8,0},{9,1},... | collective-permute-start | bytes 1769480 | tf_op jit(solution)/shard_map/ppermute | solution.py:426
  223.2 20.6 %collective-permute-start.21 = (bf16[3,12,64,128]{3,2,1,0:T(8,128)(2,1)S(1)}, bf16[3,12,64,128]{3,2,1,0:T(8,128)(2,1)S(1)}, u32[]{:S(2)}, u32[]{:S(2)}) collective-permute-start(bf16[3,12,64,128]{3,2,1,0:T(8,128)(2,1)S(1)} %add_convert_fusion), channel_id=1, source_target_pairs={{0,16},{16,0},{1,17},{17,1},{2,18},{18,2},{3,19},{19,3},{4,20},{20... | collective-permute-start | bytes 1769480 | tf_op jit(solution)/shard_map/ppermute | solution.py:299
  223.9 23.6 %collective-permute-start.19 = (bf16[128,1152]{1,0:T(8,128)(2,1)S(1)}, bf16[128,1152]{1,0:T(8,128)(2,1)S(1)}, u32[]{:S(2)}, u32[]{:S(2)}) collective-permute-start(bf16[128,1152]{1,0:T(8,128)(2,1)S(1)} %add_convert_fusion.4), channel_id=1, source_target_pairs={{2,0},{3,1},{10,8},{11,9},{6,2},{7,3},{14,10},{15,11},{4,6},{5,7},... | collective-permute-start | bytes 884744 | tf_op jit(solution)/shard_map/ppermute | solution.py:293
  (76 other events, 269.3 us)

commit v8 on v7

--- a/solution.py
+++ b/solution.py
@@ -212,8 +212,14 @@
     resumed = so_far is not None
     bf16, f32 = jnp.bfloat16, jnp.float32
     smem = pl.BlockSpec(memory_space=pltpu.SMEM)
-    vmem = pl.BlockSpec(memory_space=pltpu.VMEM)
     grads = jax.ShapeDtypeStruct((block_count, LANES, LANES), bf16 if final else f32)
+    out_shape = [jax.ShapeDtypeStruct((tok, half), bf16)] * shards
+    out_shape += [jax.ShapeDtypeStruct((tok, table_width - half), bf16)] * shards
+    out_shape += [grads]
+
+    def whole(value):
+        return pl.BlockSpec(value.shape, lambda i: (0,) * len(value.shape))
+
     added = len(parts_so_far) > 0
     operands = [*x_list, *g_list, *weights] + ([so_far] if resumed else [])
     operands += [low for low, _ in parts_so_far] + [high for _, high in parts_so_far]
@@ -221,11 +227,10 @@
         functools.partial(
             expert_kernel, shards, slots, half, len(weights), resumed, added
         ),
-        in_specs=[smem] * 3 + [vmem] * len(operands),
-        out_specs=[vmem] * (2 * shards + 1),
-        out_shape=[jax.ShapeDtypeStruct((tok, half), bf16)] * shards
-        + [jax.ShapeDtypeStruct((tok, table_width - half), bf16)] * shards
-        + [grads],
+        grid=(1,),
+        in_specs=[smem] * 3 + [whole(value) for value in operands],
+        out_specs=[whole(value) for value in out_shape],
+        out_shape=out_shape,
         scratch_shapes=[
             pltpu.VMEM((block_count, LANES, LANES), bf16),
             pltpu.VMEM((2, feat, rows, LANES), bf16),
@@ -242,7 +247,7 @@
             pltpu.VMEM((shards, 2, tok, slots), bf16),
             pltpu.VMEM((rows, LANES), f32),
         ],
-        compiler_params=pltpu.CompilerParams(vmem_limit_bytes=30 * 1024 * 1024),
+        compiler_params=pltpu.CompilerParams(vmem_limit_bytes=58 * 1024 * 1024),
         cost_estimate=pl.CostEstimate(
             flops=2 * 2 * 108 * rows * LANES * LANES * 8,
             bytes_accessed=shards * tok * table_width * 6 + block_count * LANES * LANES * 6,
@@ -345,12 +350,10 @@
     spread = swap_all(jnp.concatenate([pieces, note], axis=1))
     all_slots = jnp.arange(expert_count, dtype=jnp.int32)
 
-    def collect(spread_state, slot_order):
+    def ordered(spread_state, slot_order):
         order = partner.at[slot_order].get(mode="promise_in_bounds")
-        moved = spread_state.at[order, :piece_rows].get(mode="promise_in_bounds")
-        return swap_all(moved).reshape(rows_now.shape)
-
-    rows_far = collect(spread, all_slots ^ far)
+        return spread_state.at[order].get(mode="promise_in_bounds")
+
     x_at = {0: jnp.concatenate([tokens, table], axis=1)}
     g_at = {0: out_grad}
     most = chips // 2
@@ -361,9 +364,14 @@
             x_at[s] = step_back(x_at[s - 1])
             g_at[-s] = step_on(g_at[1 - s])
         if s == 1:
-            x_at, g_at, rows_far, spread = lax.optimization_barrier((x_at, g_at, rows_far, spread))
+            x_at, g_at, spread = lax.optimization_barrier((x_at, g_at, spread))
+            state_pieces = spread[:, :piece_rows]
+            far_pieces = ordered(state_pieces, all_slots ^ far)
+            near_pieces = ordered(state_pieces, all_slots)
+            rows_far, near_pieces = lax.optimization_barrier((swap_all(far_pieces), near_pieces))
+            rows_far = rows_far.reshape(rows_now.shape)
     x_at[most] = x_at[-most]
-    rows_near = collect(spread, all_slots)
+    rows_near = swap_all(near_pieces).reshape(rows_now.shape)
     all_layouts = spread[:, piece_rows:].reshape(expert_count, -1)[:, : layout_flat.shape[0]]
     shards = [0]
     for s in range(1, most):
@@ -422,11 +430,12 @@
         me ^ far, weights_far, None, swap_all(moment_pieces)
     )
     far_sum = sum_rows(far_grad, far_sister).astype(bf16)
-    far_sum, weights_near = lax.optimization_barrier((far_sum, weights_near))
+    moved_moments = swap_all(ordered(moment_spread, all_slots)).reshape(rows_now.shape)
+    far_sum, weights_near, moved_moments = lax.optimization_barrier(
+        (far_sum, weights_near, moved_moments)
+    )
     from_mirror = lax.ppermute(far_sum, "expert", mirror)
-    parts, near_grad, near_sister, moved_moments = run_pair(
-        me, weights_near, parts, collect(moment_spread, all_slots)
-    )
+    parts, near_grad, near_sister, _ = run_pair(me, weights_near, parts, ())
     def own_share(distance, part):
         return parts[distance][part]
 

time: 264 us -> 220 us (0.83)
  local copies, waits for them, and re-layouts: 65 us -> 16.9 us
  Pallas kernels: 25.8 us -> 32.3 us
  other arithmetic: 23.9 us -> 19.6 us
  waiting for transfers between devices: 98.2 us -> 101 us
    unnamed x141 -> x35, local copies, waits for them, and re-layouts: 40.4 us -> 0.1 us
    ppermute x6, waiting for transfers between devices: 0.82 us -> 30.9 us  [step_back(): return lax.ppermute(value, 'expert', backward)]
    ppermute x6, waiting for transfers between devices: 42.9 us -> 19.8 us  [step_on(): return lax.ppermute(value, 'expert', onward)]
    all_to_all x5, waiting for transfers between devices: 21.5 us -> 14.1 us  [swap_all(): lax.all_to_all(pieces, 'expert', split_axis=0, concat_axis=0, tiled=True)]
    gather x7 -> x5, local copies, waits for them, and re-layouts: 12.7 us -> 5.64 us  [the longest x3 4.32 us: ordered(): return spread_state.at[order].get(mode='promise_in_bounds')]
    pallas_call x2, Pallas kernels: 25.8 us -> 32.3 us  [run_experts(): pl.pallas_call(functools.partial(expert_kernel, shards, slots, half, len(...]
    ppermute x5, waiting for transfers between devices: 19.4 us -> 24.4 us  [other_replica(): return lax.ppermute(value, 'dp', [(0, 1), (1, 0)])]
    slice x2, local copies, waits for them, and re-layouts: 3.12 us -> 5.78 us  [run_pair(): sums[:half_count].reshape(blocks[0].shape)]
  transfers between devices with their start and end apart: 29 -> 29, of which waited for: 10 -> 14; matrix products, arithmetic and copies ran while one was open for 15% -> 12% of each run, Pallas kernels for 10% -> 7%
where the time goes in v8:
time: 220 us; the launch traced here: 219 us
  waiting for transfers between devices  101 us (46%)
  starting transfers between devices  48.6 us (22%)
  Pallas kernels  32.3 us (15%)
  other arithmetic  19.6 us (9%)
  local copies, waits for them, and re-layouts  16.9 us (8%)
    pallas_call x2, Pallas kernels, run_experts(): pl.pallas_call(functools.partial(expert_kernel, shards, slots, half, len(...  32.3 us
    ppermute x6, waiting for transfers between devices, step_back(): return lax.ppermute(value, 'expert', backward)  30.9 us
    all_to_all x5, starting transfers between devices, swap_all(): lax.all_to_all(pieces, 'expert', split_axis=0, concat_axis=0, tiled=True)  26.6 us
    ppermute x5, waiting for transfers between devices, other_replica(): return lax.ppermute(value, 'dp', [(0, 1), (1, 0)])  24.4 us
    ppermute x6, waiting for transfers between devices, step_on(): return lax.ppermute(value, 'expert', onward)  19.8 us
    all_to_all x5, waiting for transfers between devices, swap_all(): lax.all_to_all(pieces, 'expert', split_axis=0, concat_axis=0, tiled=True)  14.1 us
    ppermute x1, waiting for transfers between devices, body(): from_mirror = lax.ppermute(far_sum, 'expert', mirror)  11.7 us
    ppermute x6, starting transfers between devices, step_on(): return lax.ppermute(value, 'expert', onward)  8.84 us
  transfers between devices with their start and end apart: 29, of which 14 were waited for; matrix products, arithmetic and copies ran while one was open for 12% of the time, Pallas kernels for 7%

profile of v8, /device:TPU:0, one launch (start us, length us, event | category | flops | bytes accessed | tf_op | source)
XLA Modules:
  0.0 219.3 jit_solution(1835980084746946367)
XLA Ops:
  0.6 3.0 %collective-permute-start.2 = (bf16[128,2048]{1,0:T(8,128)(2,1)}, bf16[128,2048]{1,0:T(8,128)(2,1)S(1)}, u32[]{:S(2)}, u32[]{:S(2)}) collective-permute-start(bf16[128,2048]{1,0:T(8,128)(2,1)} %refs_4_.1), channel_id=1, source_target_pairs={{0,2},{1,3},{8,10},{9,11},{2,6},{3,7},{10,14},{11,15},{6,4},{7,5},... | collective-permute-start | bytes 1572872 | tf_op jit(solution)/shard_map/ppermute | solution.py:295
  5.7 6.4 %all-to-all-start = ((bf16[16,160,128]{2,1,0:T(8,128)(2,1)}), bf16[16,160,128]{2,1,0:T(8,128)(2,1)S(1)}, u32[]{:S(2)}, u32[]{:S(2)}) async-start(bf16[16,160,128]{2,1,0:T(8,128)(2,1)} %pad_maximum_fusion), calls=%async_computation | async-start | bytes 1310720 | tf_op jit(solution)/shard_map/all_to_all | solution.py:266
  16.0 2.3 %collective-permute-done.2.refs_6_ = bf16[128,2048]{1,0:T(8,128)(2,1)S(1)} collective-permute-done((bf16[128,2048]{1,0:T(8,128)(2,1)}, bf16[128,2048]{1,0:T(8,128)(2,1)S(1)}, u32[]{:S(2)}, u32[]{:S(2)}) %collective-permute-start.2) | collective-permute-done | bytes 524320 | tf_op jit(solution)/shard_map/ppermute | solution.py:295
  20.1 17.6 %collective-permute-done.1.refs_1_ = bf16[128,2176]{1,0:T(8,128)(2,1)S(1)} collective-permute-done((bf16[128,2176]{1,0:T(8,128)(2,1)S(1)}, bf16[128,2176]{1,0:T(8,128)(2,1)S(1)}, u32[]{:S(2)}, u32[]{:S(2)}) %collective-permute-start.1) | collective-permute-done | bytes 557088 | tf_op jit(solution)/shard_map/ppermute | solution.py:298
  39.9 6.3 %all-to-all-start.1 = ((bf16[16,144,128]{2,1,0:T(8,128)(2,1)}), bf16[16,144,128]{2,1,0:T(8,128)(2,1)S(1)}, u32[]{:S(2)}, u32[]{:S(2)}) async-start(bf16[16,144,128]{2,1,0:T(8,128)(2,1)} %gather_fusion.3), calls=%async_computation.1 | async-start | bytes 1179648 | tf_op jit(solution)/shard_map/all_to_all | solution.py:266
  47.7 14.1 %all-to-all-done.1 = bf16[16,144,128]{2,1,0:T(8,128)(2,1)S(1)} async-done(((bf16[16,144,128]{2,1,0:T(8,128)(2,1)}), bf16[16,144,128]{2,1,0:T(8,128)(2,1)S(1)}, u32[]{:S(2)}, u32[]{:S(2)}) %all-to-all-start.1) | async-done | bytes 589856 | tf_op jit(solution)/shard_map/all_to_all | solution.py:266
  65.3 4.4 %all-to-all-start.2 = ((bf16[16,144,128]{2,1,0:T(8,128)(2,1)}), bf16[16,144,128]{2,1,0:T(8,128)(2,1)S(1)}, u32[]{:S(2)}, u32[]{:S(2)}) async-start(bf16[16,144,128]{2,1,0:T(8,128)(2,1)} %gather_fusion.5), calls=%async_computation.2 | async-start | bytes 1179648 | tf_op jit(solution)/shard_map/all_to_all | solution.py:266
  69.8 10.7 %collective-permute-done.6.refs_7_ = bf16[128,2048]{1,0:T(8,128)(2,1)S(1)} collective-permute-done((bf16[128,2048]{1,0:T(8,128)(2,1)}, bf16[128,2048]{1,0:T(8,128)(2,1)S(1)}, u32[]{:S(2)}, u32[]{:S(2)}) %collective-permute-start.6) | collective-permute-done | bytes 524320 | tf_op jit(solution)/shard_map/ppermute | solution.py:298
  80.5 4.1 %collective-permute-done.5.refs_3_ = bf16[128,2176]{1,0:T(8,128)(2,1)} collective-permute-done((bf16[128,2176]{1,0:T(8,128)(2,1)}, bf16[128,2176]{1,0:T(8,128)(2,1)}, u32[]{:S(2)}, u32[]{:S(2)}) %collective-permute-start.5) | collective-permute-done | bytes 557088 | tf_op jit(solution)/shard_map/ppermute | solution.py:295
  90.5 3.6 %all-to-all-start.3 = ((bf16[16,144,128]{2,1,0:T(8,128)(2,1)}), bf16[16,144,128]{2,1,0:T(8,128)(2,1)S(1)}, u32[]{:S(2)}, u32[]{:S(2)}) async-start(bf16[16,144,128]{2,1,0:T(8,128)(2,1)} %bitcast.24), calls=%async_computation.3 | async-start | bytes 1179648 | tf_op jit(solution)/shard_map/all_to_all | solution.py:266
  94.1 15.8 %shard_map.111 = (bf16[128,1024]{1,0:T(8,128)(2,1)}, bf16[128,1024]{1,0:T(8,128)(2,1)}, bf16[128,1024]{1,0:T(8,128)(2,1)}, bf16[128,1024]{1,0:T(8,128)(2,1)}, bf...) custom-call(s32[144]{0:T(256)} %reshape.385.lay_ref, ...), custom_call_target="tpu_custom_call" | custom-call | flops 14495514624 | bytes 13762560 | tf_op jit(solution)/shard_map/pallas_call | solution.py:226
  110.0 2.9 %fusion.9 = (bf16[36,128,128]{2,1,0:T(8,128)(2,1)S(1)}, bf16[36,128,128]{2,1,0:T(8,128)(2,1)}) fusion(bf16[72,128,128]{2,1,0:T(8,128)(2,1)} %get-tuple-element.92), kind=kLoop, calls=%fused_computation.55 | loop fusion | bytes 4718592 | tf_op jit(solution)/shard_map/slice | solution.py:419
  115.1 5.8 %all-to-all-start.4 = ((bf16[16,144,128]{2,1,0:T(8,128)(2,1)}), bf16[16,144,128]{2,1,0:T(8,128)(2,1)S(1)}, u32[]{:S(2)}, u32[]{:S(2)}) async-start(bf16[16,144,128]{2,1,0:T(8,128)(2,1)} %gather_fusion.8), calls=%async_computation.4 | async-start | bytes 1179648 | tf_op jit(solution)/shard_map/all_to_all | solution.py:266
  126.5 2.9 %collective-permute-done.11 = bf16[3,12,64,128]{3,2,1,0:T(8,128)(2,1)} collective-permute-done((bf16[3,12,64,128]{3,2,1,0:T(8,128)(2,1)S(1)}, bf16[3,12,64,128]{3,2,1,0:T(8,128)(2,1)}, u32[]{:S(2)}, u32[]{:S(2)}) %collective-permute-start.11) | collective-permute-done | bytes 589856 | tf_op jit(solution)/shard_map/ppermute | solution.py:304
  131.3 10.0 %collective-permute-done.10 = bf16[3,12,64,128]{3,2,1,0:T(8,128)(2,1)} collective-permute-done((bf16[3,12,64,128]{3,2,1,0:T(8,128)(2,1)}, bf16[3,12,64,128]{3,2,1,0:T(8,128)(2,1)}, u32[]{:S(2)}, u32[]{:S(2)}) %collective-permute-start.10) | collective-permute-done | bytes 589856 | tf_op jit(solution)/shard_map/ppermute | solution.py:304
  141.3 2.3 %add_convert_fusion.1 = bf16[3,12,64,128]{3,2,1,0:T(8,128)(2,1)} fusion(bf16[3,12,64,128]{3,2,1,0:T(8,128)(2,1)} %collective-permute-done.10, bf16[3,12,128,128]{3,2,1,0:T(8,128)(2,1)} %collective-permute-done.9, s32[]{:T(128)S(6)} %select_n.106, bf16[3,12,128,128]{3,2,1,0:T(8,128)(2,1)S(1)} %bitcast.56), kind=kLoop, calls=%fused_computation.12 | loop fusion | flops 1769472 | bytes 2359300 | tf_op jit(solution)/shard_map/convert_element_type | solution.py:432
  143.7 16.5 %shard_map.112 = (bf16[128,1024]{1,0:T(8,128)(2,1)}, bf16[128,1024]{1,0:T(8,128)(2,1)}, bf16[128,1024]{1,0:T(8,128)(2,1)}, bf16[128,1024]{1,0:T(8,128)(2,1)}, bf...) custom-call(s32[144]{0:T(256)} %reshape.384.lay_ref, ...), custom_call_target="tpu_custom_call" | custom-call | flops 14495514624 | bytes 13762560 | tf_op jit(solution)/shard_map/pallas_call | solution.py:226
  160.1 2.9 %fusion.8 = (bf16[36,128,128]{2,1,0:T(8,128)(2,1)S(1)}, bf16[36,128,128]{2,1,0:T(8,128)(2,1)}) fusion(bf16[72,128,128]{2,1,0:T(8,128)(2,1)} %get-tuple-element.116), kind=kLoop, calls=%fused_computation.54 | loop fusion | bytes 4718592 | tf_op jit(solution)/shard_map/slice | solution.py:419
  167.3 5.2 %collective-permute-done.14 = bf16[128,1024]{1,0:T(8,128)(2,1)} collective-permute-done((bf16[128,1024]{1,0:T(8,128)(2,1)}, bf16[128,1024]{1,0:T(8,128)(2,1)}, u32[]{:S(2)}, u32[]{:S(2)}) %collective-permute-start.14) | collective-permute-done | bytes 262176 | tf_op jit(solution)/shard_map/ppermute | solution.py:295
  172.5 2.7 %collective-permute-start.22 = (bf16[3,12,64,128]{3,2,1,0:T(8,128)(2,1)S(1)}, bf16[3,12,64,128]{3,2,1,0:T(8,128)(2,1)S(1)}, u32[]{:S(2)}, u32[]{:S(2)}) collective-permute-start(bf16[3,12,64,128]{3,2,1,0:T(8,128)(2,1)S(1)} %copy-done.4), channel_id=1, source_target_pairs={{0,8},{1,9},{2,10},{3,11},{4,12},{5,13},{6,14},{7,15},{8,0},{9,1},... | collective-permute-start | bytes 1769480 | tf_op jit(solution)/shard_map/ppermute | solution.py:437
  181.6 7.5 %collective-permute-done.15 = bf16[128,1024]{1,0:T(8,128)(2,1)S(1)} collective-permute-done((bf16[128,1024]{1,0:T(8,128)(2,1)S(1)}, bf16[128,1024]{1,0:T(8,128)(2,1)S(1)}, u32[]{:S(2)}, u32[]{:S(2)}) %collective-permute-start.15) | collective-permute-done | bytes 262176 | tf_op jit(solution)/shard_map/ppermute | solution.py:295
  189.2 11.7 %collective-permute-done.22 = bf16[3,12,64,128]{3,2,1,0:T(8,128)(2,1)S(1)} collective-permute-done((bf16[3,12,64,128]{3,2,1,0:T(8,128)(2,1)S(1)}, bf16[3,12,64,128]{3,2,1,0:T(8,128)(2,1)S(1)}, u32[]{:S(2)}, u32[]{:S(2)}) %collective-permute-start.22) | collective-permute-done | bytes 589856 | tf_op jit(solution)/shard_map/ppermute | solution.py:437
  200.8 2.8 %fusion.7 = (f32[1,3,12,64,128]{4,3,2,1,0:T(8,128)}, bf16[3,12,64,128]{3,2,1,0:T(8,128)(2,1)S(1)}) fusion(bf16[3,12,64,128]{3,2,1,0:T(8,128)(2,1)S(1)} %collective-permute-done.22, bf16[3,12,64,128]{3,2,1,0:T(8,128)(2,1)S(1)} %collective-permute-done.21, bf16[3,12,128,128]{3,2,1,0:T(8,128)(2,1)} %collective-permute-done.20, s32[]{:T(128)S(6)} %select_n.106, ...), kind=kLoop, calls=%fused_computation.53 | loop fusion | flops 4128768 | bytes 5308420 | tf_op jit(solution)/shard_map/broadcast_in_dim | solution.py:466
  206.0 11.5 %collective-permute-done.23 = bf16[3,12,64,128]{3,2,1,0:T(8,128)(2,1)S(1)} collective-permute-done((bf16[3,12,64,128]{3,2,1,0:T(8,128)(2,1)S(1)}, bf16[3,12,64,128]{3,2,1,0:T(8,128)(2,1)S(1)}, u32[]{:S(2)}, u32[]{:S(2)}) %collective-permute-start.23) | collective-permute-done | bytes 589856 | tf_op jit(solution)/shard_map/ppermute | solution.py:304
  (133 shorter events, 45.2 us)
Async XLA Ops:
  0.6 17.7 %collective-permute-start.2 = (bf16[128,2048]{1,0:T(8,128)(2,1)}, bf16[128,2048]{1,0:T(8,128)(2,1)S(1)}, u32[]{:S(2)}, u32[]{:S(2)}) collective-permute-start(bf16[128,2048]{1,0:T(8,128)(2,1)} %refs_4_.1), channel_id=1, source_target_pairs={{0,2},{1,3},{8,10},{9,11},{2,6},{3,7},{10,14},{11,15},{6,4},{7,5},... | collective-permute-start | bytes 1572872 | tf_op jit(solution)/shard_map/ppermute | solution.py:295
  3.6 16.5 %collective-permute-start.3 = (bf16[128,2048]{1,0:T(8,128)(2,1)}, bf16[128,2048]{1,0:T(8,128)(2,1)}, u32[]{:S(2)}, u32[]{:S(2)}) collective-permute-start(bf16[128,2048]{1,0:T(8,128)(2,1)} %refs_4_.1), channel_id=1, source_target_pairs={{2,0},{3,1},{10,8},{11,9},{6,2},{7,3},{14,10},{15,11},{4,6},{5,7},... | collective-permute-start | bytes 1572872 | tf_op jit(solution)/shard_map/ppermute | solution.py:298
  5.7 32.7 %all-to-all-start = ((bf16[16,160,128]{2,1,0:T(8,128)(2,1)}), bf16[16,160,128]{2,1,0:T(8,128)(2,1)S(1)}, u32[]{:S(2)}, u32[]{:S(2)}) async-start(bf16[16,160,128]{2,1,0:T(8,128)(2,1)} %pad_maximum_fusion), calls=%async_computation | async-start | bytes 1310720 | tf_op jit(solution)/shard_map/all_to_all | solution.py:266
  12.5 25.2 %collective-permute-start.1 = (bf16[128,2176]{1,0:T(8,128)(2,1)S(1)}, bf16[128,2176]{1,0:T(8,128)(2,1)S(1)}, u32[]{:S(2)}, u32[]{:S(2)}) collective-permute-start(bf16[128,2176]{1,0:T(8,128)(2,1)S(1)} %pad_maximum_fusion.1.refs_0_), channel_id=1, source_target_pairs={{2,0},{3,1},{10,8},{11,9},{6,2},{7,3},{14,10},{15,11},{4,6},{5,7},... | collective-permute-start | bytes 1671176 | tf_op jit(solution)/shard_map/ppermute | solution.py:298
  14.5 23.9 %collective-permute-start = (bf16[128,2176]{1,0:T(8,128)(2,1)S(1)}, bf16[128,2176]{1,0:T(8,128)(2,1)}, u32[]{:S(2)}, u32[]{:S(2)}) collective-permute-start(bf16[128,2176]{1,0:T(8,128)(2,1)S(1)} %pad_maximum_fusion.1.refs_0_), channel_id=1, source_target_pairs={{0,2},{1,3},{8,10},{9,11},{2,6},{3,7},{10,14},{11,15},{6,4},{7,5},... | collective-permute-start | bytes 1671176 | tf_op jit(solution)/shard_map/ppermute | solution.py:295
  39.9 21.9 %all-to-all-start.1 = ((bf16[16,144,128]{2,1,0:T(8,128)(2,1)}), bf16[16,144,128]{2,1,0:T(8,128)(2,1)S(1)}, u32[]{:S(2)}, u32[]{:S(2)}) async-start(bf16[16,144,128]{2,1,0:T(8,128)(2,1)} %gather_fusion.3), calls=%async_computation.1 | async-start | bytes 1179648 | tf_op jit(solution)/shard_map/all_to_all | solution.py:266
  61.8 22.9 %collective-permute-start.4 = (bf16[3,12,64,128]{3,2,1,0:T(8,128)(2,1)S(1)}, bf16[3,12,64,128]{3,2,1,0:T(8,128)(2,1)}, u32[]{:S(2)}, u32[]{:S(2)}) collective-permute-start(bf16[3,12,64,128]{3,2,1,0:T(8,128)(2,1)S(1)} %bitcast.67), channel_id=1, source_target_pairs={{0,16},{16,0},{1,17},{17,1},{2,18},{18,2},{3,19},{19,3},{4,20},{20... | collective-permute-start | bytes 1769480 | tf_op jit(solution)/shard_map/ppermute | solution.py:304
  63.3 21.3 %collective-permute-start.5 = (bf16[128,2176]{1,0:T(8,128)(2,1)}, bf16[128,2176]{1,0:T(8,128)(2,1)}, u32[]{:S(2)}, u32[]{:S(2)}) collective-permute-start(bf16[128,2176]{1,0:T(8,128)(2,1)} %collective-permute-done.refs_2_), channel_id=1, source_target_pairs={{0,2},{1,3},{8,10},{9,11},{2,6},{3,7},{10,14},{11,15},{6,4},{7,5},... | collective-permute-start | bytes 1671176 | tf_op jit(solution)/shard_map/ppermute | solution.py:295
  63.9 16.6 %collective-permute-start.6 = (bf16[128,2048]{1,0:T(8,128)(2,1)}, bf16[128,2048]{1,0:T(8,128)(2,1)S(1)}, u32[]{:S(2)}, u32[]{:S(2)}) collective-permute-start(bf16[128,2048]{1,0:T(8,128)(2,1)} %collective-permute-done.3.refs_5_), channel_id=1, source_target_pairs={{2,0},{3,1},{10,8},{11,9},{6,2},{7,3},{14,10},{15,11},{4,6},{5,7},... | collective-permute-start | bytes 1572872 | tf_op jit(solution)/shard_map/ppermute | solution.py:298
  65.3 25.1 %all-to-all-start.2 = ((bf16[16,144,128]{2,1,0:T(8,128)(2,1)}), bf16[16,144,128]{2,1,0:T(8,128)(2,1)S(1)}, u32[]{:S(2)}, u32[]{:S(2)}) async-start(bf16[16,144,128]{2,1,0:T(8,128)(2,1)} %gather_fusion.5), calls=%async_computation.2 | async-start | bytes 1179648 | tf_op jit(solution)/shard_map/all_to_all | solution.py:266
  90.5 19.4 %all-to-all-start.3 = ((bf16[16,144,128]{2,1,0:T(8,128)(2,1)}), bf16[16,144,128]{2,1,0:T(8,128)(2,1)S(1)}, u32[]{:S(2)}, u32[]{:S(2)}) async-start(bf16[16,144,128]{2,1,0:T(8,128)(2,1)} %bitcast.24), calls=%async_computation.3 | async-start | bytes 1179648 | tf_op jit(solution)/shard_map/all_to_all | solution.py:266
  113.1 16.3 %collective-permute-start.11 = (bf16[3,12,64,128]{3,2,1,0:T(8,128)(2,1)S(1)}, bf16[3,12,64,128]{3,2,1,0:T(8,128)(2,1)}, u32[]{:S(2)}, u32[]{:S(2)}) collective-permute-start(bf16[3,12,64,128]{3,2,1,0:T(8,128)(2,1)S(1)} %bitcast.62), channel_id=1, source_target_pairs={{0,16},{16,0},{1,17},{17,1},{2,18},{18,2},{3,19},{19,3},{4,20},{20... | collective-permute-start | bytes 1769480 | tf_op jit(solution)/shard_map/ppermute | solution.py:304
  115.1 28.6 %all-to-all-start.4 = ((bf16[16,144,128]{2,1,0:T(8,128)(2,1)}), bf16[16,144,128]{2,1,0:T(8,128)(2,1)S(1)}, u32[]{:S(2)}, u32[]{:S(2)}) async-start(bf16[16,144,128]{2,1,0:T(8,128)(2,1)} %gather_fusion.8), calls=%async_computation.4 | async-start | bytes 1179648 | tf_op jit(solution)/shard_map/all_to_all | solution.py:266
  123.0 18.3 %collective-permute-start.10 = (bf16[3,12,64,128]{3,2,1,0:T(8,128)(2,1)}, bf16[3,12,64,128]{3,2,1,0:T(8,128)(2,1)}, u32[]{:S(2)}, u32[]{:S(2)}) collective-permute-start(bf16[3,12,64,128]{3,2,1,0:T(8,128)(2,1)} %add_convert_fusion.2), channel_id=1, source_target_pairs={{0,16},{16,0},{1,17},{17,1},{2,18},{18,2},{3,19},{19,3},{4,20},{20... | collective-permute-start | bytes 1769480 | tf_op jit(solution)/shard_map/ppermute | solution.py:304
  126.4 17.3 %collective-permute-start.12 = (bf16[3,12,64,128]{3,2,1,0:T(8,128)(2,1)S(1)}, bf16[3,12,64,128]{3,2,1,0:T(8,128)(2,1)}, u32[]{:S(2)}, u32[]{:S(2)}) collective-permute-start(bf16[3,12,64,128]{3,2,1,0:T(8,128)(2,1)S(1)} %bitcast.63), channel_id=1, source_target_pairs={{0,1},{1,0},{2,3},{3,2},{4,5},{5,4},{6,7},{7,6},{8,9},{9,8},{10,11... | collective-permute-start | bytes 1769480 | tf_op jit(solution)/shard_map/ppermute | solution.py:307
  129.4 14.3 %collective-permute-start.13 = (bf16[3,12,64,128]{3,2,1,0:T(8,128)(2,1)}, bf16[3,12,64,128]{3,2,1,0:T(8,128)(2,1)}, u32[]{:S(2)}, u32[]{:S(2)}) collective-permute-start(bf16[3,12,64,128]{3,2,1,0:T(8,128)(2,1)} %collective-permute-done.11), channel_id=1, source_target_pairs={{0,1},{1,0},{2,3},{3,2},{4,5},{5,4},{6,7},{7,6},{8,9},{9,8},{10,11... | collective-permute-start | bytes 1769480 | tf_op jit(solution)/shard_map/ppermute | solution.py:307
  163.1 13.3 %collective-permute-start.20 = (bf16[3,12,128,128]{3,2,1,0:T(8,128)(2,1)}, bf16[3,12,128,128]{3,2,1,0:T(8,128)(2,1)}, u32[]{:S(2)}, u32[]{:S(2)}) collective-permute-start(bf16[3,12,128,128]{3,2,1,0:T(8,128)(2,1)} %bitcast.34), channel_id=1, source_target_pairs={{0,1},{1,0},{2,3},{3,2},{4,5},{5,4},{6,7},{7,6},{8,9},{9,8},{10,11... | collective-permute-start | bytes 3538952 | tf_op jit(solution)/shard_map/ppermute | solution.py:307
  165.0 15.6 %collective-permute-start.16 = (bf16[128,1024]{1,0:T(8,128)(2,1)}, bf16[128,1024]{1,0:T(8,128)(2,1)S(1)}, u32[]{:S(2)}, u32[]{:S(2)}) collective-permute-start(bf16[128,1024]{1,0:T(8,128)(2,1)} %get-tuple-element.110), channel_id=1, source_target_pairs={{2,0},{3,1},{10,8},{11,9},{6,2},{7,3},{14,10},{15,11},{4,6},{5,7},... | collective-permute-start | bytes 786440 | tf_op jit(solution)/shard_map/ppermute | solution.py:298
  165.3 38.9 %collective-permute-start.17 = (bf16[128,1152]{1,0:T(8,128)(2,1)}, bf16[128,1152]{1,0:T(8,128)(2,1)S(1)}, u32[]{:S(2)}, u32[]{:S(2)}) collective-permute-start(bf16[128,1152]{1,0:T(8,128)(2,1)} %get-tuple-element.112), channel_id=1, source_target_pairs={{0,2},{1,3},{8,10},{9,11},{2,6},{3,7},{10,14},{11,15},{6,4},{7,5},... | collective-permute-start | bytes 884744 | tf_op jit(solution)/shard_map/ppermute | solution.py:295
  167.1 12.9 %collective-permute-start.18 = (bf16[128,1152]{1,0:T(8,128)(2,1)}, bf16[128,1152]{1,0:T(8,128)(2,1)S(1)}, u32[]{:S(2)}, u32[]{:S(2)}) collective-permute-start(bf16[128,1152]{1,0:T(8,128)(2,1)} %get-tuple-element.113), channel_id=1, source_target_pairs={{2,0},{3,1},{10,8},{11,9},{6,2},{7,3},{14,10},{15,11},{4,6},{5,7},... | collective-permute-start | bytes 884744 | tf_op jit(solution)/shard_map/ppermute | solution.py:298
  172.5 28.4 %collective-permute-start.22 = (bf16[3,12,64,128]{3,2,1,0:T(8,128)(2,1)S(1)}, bf16[3,12,64,128]{3,2,1,0:T(8,128)(2,1)S(1)}, u32[]{:S(2)}, u32[]{:S(2)}) collective-permute-start(bf16[3,12,64,128]{3,2,1,0:T(8,128)(2,1)S(1)} %copy-done.4), channel_id=1, source_target_pairs={{0,8},{1,9},{2,10},{3,11},{4,12},{5,13},{6,14},{7,15},{8,0},{9,1},... | collective-permute-start | bytes 1769480 | tf_op jit(solution)/shard_map/ppermute | solution.py:437
  180.0 20.8 %collective-permute-start.21 = (bf16[3,12,64,128]{3,2,1,0:T(8,128)(2,1)S(1)}, bf16[3,12,64,128]{3,2,1,0:T(8,128)(2,1)S(1)}, u32[]{:S(2)}, u32[]{:S(2)}) collective-permute-start(bf16[3,12,64,128]{3,2,1,0:T(8,128)(2,1)S(1)} %add_convert_fusion), channel_id=1, source_target_pairs={{0,16},{16,0},{1,17},{17,1},{2,18},{18,2},{3,19},{19,3},{4,20},{20... | collective-permute-start | bytes 1769480 | tf_op jit(solution)/shard_map/ppermute | solution.py:304
  180.6 23.5 %collective-permute-start.19 = (bf16[128,1152]{1,0:T(8,128)(2,1)S(1)}, bf16[128,1152]{1,0:T(8,128)(2,1)S(1)}, u32[]{:S(2)}, u32[]{:S(2)}) collective-permute-start(bf16[128,1152]{1,0:T(8,128)(2,1)S(1)} %add_convert_fusion.4), channel_id=1, source_target_pairs={{2,0},{3,1},{10,8},{11,9},{6,2},{7,3},{14,10},{15,11},{4,6},{5,7},... | collective-permute-start | bytes 884744 | tf_op jit(solution)/shard_map/ppermute | solution.py:298
  203.7 13.9 %collective-permute-start.23 = (bf16[3,12,64,128]{3,2,1,0:T(8,128)(2,1)S(1)}, bf16[3,12,64,128]{3,2,1,0:T(8,128)(2,1)S(1)}, u32[]{:S(2)}, u32[]{:S(2)}) collective-permute-start(bf16[3,12,64,128]{3,2,1,0:T(8,128)(2,1)S(1)} %get-tuple-element.119), channel_id=1, source_target_pairs={{0,16},{16,0},{1,17},{17,1},{2,18},{18,2},{3,19},{19,3},{4,20},{20... | collective-permute-start | bytes 1769480 | tf_op jit(solution)/shard_map/ppermute | solution.py:304
  (22 other events, 263.8 us)

commit v9 on v8

--- a/solution.py
+++ b/solution.py
@@ -38,14 +38,14 @@
     g_refs, refs = refs[:shards], refs[shards:]
     piece_refs, refs = refs[:pieces], refs[pieces:]
     if resumed:
-        so_far_ref, refs = refs[0], refs[1:]
+        so_far_refs, refs = refs[:2], refs[2:]
     if added:
         low_so_far, refs = refs[:shards], refs[shards:]
         high_so_far, refs = refs[:shards], refs[shards:]
     low_refs, refs = refs[:shards], refs[shards:]
     high_refs, refs = refs[:shards], refs[shards:]
+    grad_refs, refs = refs[:2], refs[2:]
     (
-        dw_ref,
         w_ref,
         xs,
         gs,
@@ -125,7 +125,7 @@
                 gs[q, c, there, :] = g_rows[own, cut]
                 ss[q, c, there, :] = s_rows[own, cut]
 
-    def one_expert(q, carry):
+    def one_expert(q):
         gate[...] = jnp.zeros_like(gate)
         up[...] = jnp.zeros_like(up)
         hgrad[...] = jnp.zeros_like(hgrad)
@@ -134,8 +134,8 @@
 
         def keep(b, grad):
             if resumed:
-                grad = grad + so_far_ref[first + b]
-            dw_ref[first + b] = grad.astype(dw_ref.dtype)
+                grad = grad + so_far_refs[q][b]
+            grad_refs[q][b] = grad.astype(grad_refs[q].dtype)
 
         def place(m, b):
             at = 2 * (first + m * count + b)
@@ -185,9 +185,9 @@
             wide[s, q, :, width:] = jnp.where(own_lane, score.astype(jnp.float32), 0.0).astype(
                 jnp.bfloat16
             )
-        return carry
-
-    lax.fori_loop(0, 2, one_expert, 0)
+
+    for q in range(2):
+        one_expert(q)
     for s in range(shards):
         total = dot(spread[s, 0], wide[s, 0], NN) + dot(spread[s, 1], wide[s, 1], NN)
         low, high = total[:, :half], total[:, half:]
@@ -212,16 +212,16 @@
     resumed = so_far is not None
     bf16, f32 = jnp.bfloat16, jnp.float32
     smem = pl.BlockSpec(memory_space=pltpu.SMEM)
-    grads = jax.ShapeDtypeStruct((block_count, LANES, LANES), bf16 if final else f32)
+    grads = jax.ShapeDtypeStruct((block_count // 2, LANES, LANES), bf16 if final else f32)
     out_shape = [jax.ShapeDtypeStruct((tok, half), bf16)] * shards
     out_shape += [jax.ShapeDtypeStruct((tok, table_width - half), bf16)] * shards
-    out_shape += [grads]
+    out_shape += [grads, grads]
 
     def whole(value):
         return pl.BlockSpec(value.shape, lambda i: (0,) * len(value.shape))
 
     added = len(parts_so_far) > 0
-    operands = [*x_list, *g_list, *weights] + ([so_far] if resumed else [])
+    operands = [*x_list, *g_list, *weights] + (list(so_far) if resumed else [])
     operands += [low for low, _ in parts_so_far] + [high for _, high in parts_so_far]
     outs = pl.pallas_call(
         functools.partial(
@@ -254,7 +254,7 @@
             transcendentals=0,
         ),
     )(layouts, experts, places, *operands)
-    return outs[:shards], outs[shards : 2 * shards], outs[2 * shards]
+    return outs[:shards], outs[shards : 2 * shards], outs[2 * shards :]
 
 
 def chip_ring(chips):
@@ -315,7 +315,8 @@
 
     def sum_rows(one, two):
         if replica_count != 2:
-            return lax.psum_scatter(add(one, two), "dp", scatter_dimension=2, tiled=True).astype(f32)
+            whole = lax.psum_scatter(add(one, two), "dp", scatter_dimension=2, tiled=True)
+            return whole.astype(f32), None
 
         def half_of(index):
             return sum(
@@ -323,8 +324,10 @@
                 for value in (one, two)
             )
 
-        theirs = other_replica(half_of(1 - replica).astype(bf16))
-        return half_of(replica) + theirs.astype(f32)
+        return half_of(replica), other_replica(half_of(1 - replica).astype(bf16))
+
+    def rows_total(mine, theirs):
+        return mine if theirs is None else mine + theirs.astype(f32)
 
     def add(left, right):
         return (left.astype(f32) + right.astype(f32)).astype(bf16)
@@ -414,9 +417,8 @@
             for d, low, high in zip(group, lows, highs):
                 parts[d] = (low, high)
         sums, beside = lax.optimization_barrier((sums, beside))
-        half_count = sums.shape[0] // 2
-        from_sister = other_core(sums[half_count:].reshape(blocks[0].shape))
-        return parts, sums[:half_count].reshape(blocks[0].shape), from_sister, beside
+        own_grad, other_grad = (value.reshape(blocks[0].shape) for value in sums)
+        return parts, own_grad, other_core(other_grad), beside
 
     moment_pieces = moments[0].astype(bf16).reshape(expert_count, -1, LANES)
     halves_far = both_cores(rows_far)
@@ -425,22 +427,27 @@
     weights_far, moment_pieces, rows_near = lax.optimization_barrier(
         (weights_far, moment_pieces, rows_near)
     )
-    weights_near = to_weights(both_cores(rows_near))
-    parts, far_grad, far_sister, moment_spread = run_pair(
-        me ^ far, weights_far, None, swap_all(moment_pieces)
-    )
-    far_sum = sum_rows(far_grad, far_sister).astype(bf16)
+    parts, far_grad, far_sister, (moment_spread, halves_near) = run_pair(
+        me ^ far, weights_far, None, (swap_all(moment_pieces), both_cores(rows_near))
+    )
+    weights_near = to_weights(halves_near)
     moved_moments = swap_all(ordered(moment_spread, all_slots)).reshape(rows_now.shape)
-    far_sum, weights_near, moved_moments = lax.optimization_barrier(
-        (far_sum, weights_near, moved_moments)
-    )
+    far_mine, far_theirs = sum_rows(far_grad, far_sister)
+    parts, near_grad, near_sister, (far_theirs, moved_moments) = run_pair(
+        me, weights_near, parts, (far_theirs, moved_moments)
+    )
+    far_sum = rows_total(far_mine, far_theirs).astype(bf16)
     from_mirror = lax.ppermute(far_sum, "expert", mirror)
-    parts, near_grad, near_sister, _ = run_pair(me, weights_near, parts, ())
+    near_mine, near_theirs = sum_rows(near_grad, near_sister)
+
     def own_share(distance, part):
         return parts[distance][part]
 
     upward = [step_on(own_share(most, 0)), None]
     downward = [None, step_back(own_share(most, 1))]
+    upward, downward, from_mirror, near_theirs = lax.optimization_barrier(
+        (upward, downward, from_mirror, near_theirs)
+    )
     for s in range(most - 1, 0, -1):
         for part in range(2):
             share = own_share(s, part)
@@ -449,7 +456,7 @@
             downward[part] = step_back(
                 share if downward[part] is None else add(downward[part], share)
             )
-    shard_grad = sum_rows(near_grad, near_sister) + from_mirror.astype(f32)
+    shard_grad = rows_total(near_mine, near_theirs) + from_mirror.astype(f32)
     new_moment = momentum_decay * moved_moments.astype(f32) + shard_grad
     new_shard = (rows_near.astype(f32) - step_rate * new_moment).astype(bf16)
 

time: 220 us -> 196 us (0.89)
  waiting for transfers between devices: 101 us -> 75.5 us
  starting transfers between devices: 48.6 us -> 57.6 us
  local copies, waits for them, and re-layouts: 16.9 us -> 10.8 us
    ppermute x5, waiting for transfers between devices: 24.4 us -> 7.67 us  [other_replica(): return lax.ppermute(value, 'dp', [(0, 1), (1, 0)])]
    ppermute x6, starting transfers between devices: 8.84 us -> 15.3 us  [step_on(): return lax.ppermute(value, 'expert', onward)]
    slice x2 -> x0, local copies, waits for them, and re-layouts: 5.78 us -> none  [run_pair(): sums[:half_count].reshape(blocks[0].shape)]
    ppermute x6, waiting for transfers between devices: 19.8 us -> 14.3 us  [step_on(): return lax.ppermute(value, 'expert', onward)]
    ppermute x1, waiting for transfers between devices: 11.7 us -> 6.33 us  [body(): from_mirror = lax.ppermute(far_sum, 'expert', mirror)]
  transfers between devices with their start and end apart: 29 -> 29, of which waited for: 14 -> 12; matrix products, arithmetic and copies ran while one was open for 12% -> 13% of each run, Pallas kernels for 7% -> 16%
where the time goes in v9:
time: 196 us; the launch traced here: 195 us
  waiting for transfers between devices  75.5 us (39%)
  starting transfers between devices  57.6 us (29%)
  Pallas kernels  31.3 us (16%)
  other arithmetic  19 us (10%)
  local copies, waits for them, and re-layouts  10.8 us (6%)
    ppermute x6, waiting for transfers between devices, step_back(): return lax.ppermute(value, 'expert', backward)  33 us
    pallas_call x2, Pallas kernels, run_experts(): pl.pallas_call(functools.partial(expert_kernel, shards, slots, half, len(...  31.3 us
    all_to_all x5, starting transfers between devices, swap_all(): lax.all_to_all(pieces, 'expert', split_axis=0, concat_axis=0, tiled=True)  26.8 us
    ppermute x6, starting transfers between devices, step_on(): return lax.ppermute(value, 'expert', onward)  15.3 us
    ppermute x6, waiting for transfers between devices, step_on(): return lax.ppermute(value, 'expert', onward)  14.3 us
    all_to_all x5, waiting for transfers between devices, swap_all(): lax.all_to_all(pieces, 'expert', split_axis=0, concat_axis=0, tiled=True)  14.1 us
    ppermute x5, waiting for transfers between devices, other_replica(): return lax.ppermute(value, 'dp', [(0, 1), (1, 0)])  7.67 us
    ppermute x6, starting transfers between devices, step_back(): return lax.ppermute(value, 'expert', backward)  6.83 us
  transfers between devices with their start and end apart: 29, of which 12 were waited for; matrix products, arithmetic and copies ran while one was open for 13% of the time, Pallas kernels for 16%

profile of v9, /device:TPU:0, one launch (start us, length us, event | category | flops | bytes accessed | tf_op | source)
XLA Modules:
  0.0 195.2 jit_solution(1149559515751780016)
XLA Ops:
  0.6 3.0 %collective-permute-start.2 = (bf16[128,2048]{1,0:T(8,128)(2,1)}, bf16[128,2048]{1,0:T(8,128)(2,1)}, u32[]{:S(2)}, u32[]{:S(2)}) collective-permute-start(bf16[128,2048]{1,0:T(8,128)(2,1)} %refs_4_.1), channel_id=1, source_target_pairs={{0,2},{1,3},{8,10},{9,11},{2,6},{3,7},{10,14},{11,15},{6,4},{7,5},... | collective-permute-start | bytes 1572872 | tf_op jit(solution)/shard_map/ppermute | solution.py:295
  5.7 6.4 %all-to-all-start = ((bf16[16,160,128]{2,1,0:T(8,128)(2,1)}), bf16[16,160,128]{2,1,0:T(8,128)(2,1)S(1)}, u32[]{:S(2)}, u32[]{:S(2)}) async-start(bf16[16,160,128]{2,1,0:T(8,128)(2,1)} %pad_maximum_fusion), calls=%async_computation | async-start | bytes 1310720 | tf_op jit(solution)/shard_map/all_to_all | solution.py:266
  12.5 2.0 %collective-permute-start.1 = (bf16[128,2176]{1,0:T(8,128)(2,1)S(1)}, bf16[128,2176]{1,0:T(8,128)(2,1)S(1)}, u32[]{:S(2)}, u32[]{:S(2)}) collective-permute-start(bf16[128,2176]{1,0:T(8,128)(2,1)S(1)} %pad_maximum_fusion.1.refs_0_), channel_id=1, source_target_pairs={{2,0},{3,1},{10,8},{11,9},{6,2},{7,3},{14,10},{15,11},{4,6},{5,7},... | collective-permute-start | bytes 1671176 | tf_op jit(solution)/shard_map/ppermute | solution.py:298
  16.0 2.4 %collective-permute-done.2.refs_6_ = bf16[128,2048]{1,0:T(8,128)(2,1)} collective-permute-done((bf16[128,2048]{1,0:T(8,128)(2,1)}, bf16[128,2048]{1,0:T(8,128)(2,1)}, u32[]{:S(2)}, u32[]{:S(2)}) %collective-permute-start.2) | collective-permute-done | bytes 524320 | tf_op jit(solution)/shard_map/ppermute | solution.py:295
  20.1 17.6 %collective-permute-done.1.refs_1_ = bf16[128,2176]{1,0:T(8,128)(2,1)S(1)} collective-permute-done((bf16[128,2176]{1,0:T(8,128)(2,1)S(1)}, bf16[128,2176]{1,0:T(8,128)(2,1)S(1)}, u32[]{:S(2)}, u32[]{:S(2)}) %collective-permute-start.1) | collective-permute-done | bytes 557088 | tf_op jit(solution)/shard_map/ppermute | solution.py:298
  39.9 6.3 %all-to-all-start.1 = ((bf16[16,144,128]{2,1,0:T(8,128)(2,1)}), bf16[16,144,128]{2,1,0:T(8,128)(2,1)S(1)}, u32[]{:S(2)}, u32[]{:S(2)}) async-start(bf16[16,144,128]{2,1,0:T(8,128)(2,1)} %gather_fusion.3), calls=%async_computation.1 | async-start | bytes 1179648 | tf_op jit(solution)/shard_map/all_to_all | solution.py:266
  47.7 14.1 %all-to-all-done.1 = bf16[16,144,128]{2,1,0:T(8,128)(2,1)S(1)} async-done(((bf16[16,144,128]{2,1,0:T(8,128)(2,1)}), bf16[16,144,128]{2,1,0:T(8,128)(2,1)S(1)}, u32[]{:S(2)}, u32[]{:S(2)}) %all-to-all-start.1) | async-done | bytes 589856 | tf_op jit(solution)/shard_map/all_to_all | solution.py:266
  65.3 4.4 %all-to-all-start.2 = ((bf16[16,144,128]{2,1,0:T(8,128)(2,1)}), bf16[16,144,128]{2,1,0:T(8,128)(2,1)S(1)}, u32[]{:S(2)}, u32[]{:S(2)}) async-start(bf16[16,144,128]{2,1,0:T(8,128)(2,1)} %gather_fusion.5), calls=%async_computation.2 | async-start | bytes 1179648 | tf_op jit(solution)/shard_map/all_to_all | solution.py:266
  69.8 10.7 %collective-permute-done.6.refs_7_ = bf16[128,2048]{1,0:T(8,128)(2,1)S(1)} collective-permute-done((bf16[128,2048]{1,0:T(8,128)(2,1)}, bf16[128,2048]{1,0:T(8,128)(2,1)S(1)}, u32[]{:S(2)}, u32[]{:S(2)}) %collective-permute-start.6) | collective-permute-done | bytes 524320 | tf_op jit(solution)/shard_map/ppermute | solution.py:298
  80.5 4.1 %collective-permute-done.5.refs_3_ = bf16[128,2176]{1,0:T(8,128)(2,1)} collective-permute-done((bf16[128,2176]{1,0:T(8,128)(2,1)}, bf16[128,2176]{1,0:T(8,128)(2,1)}, u32[]{:S(2)}, u32[]{:S(2)}) %collective-permute-start.5) | collective-permute-done | bytes 557088 | tf_op jit(solution)/shard_map/ppermute | solution.py:295
  85.9 2.2 %convert_element_type.138 = bf16[1,3,12,64,128]{4,3,2,1,0:T(8,128)(2,1)} convert(f32[1,3,12,64,128]{4,3,2,1,0:T(8,128)} %param.16) | non-fusion elementwise | flops 294912 | bytes 1769472 | tf_op jit(solution)/shard_map/convert_element_type | solution.py:423
  90.0 3.8 %all-to-all-start.3 = ((bf16[16,144,128]{2,1,0:T(8,128)(2,1)}), bf16[16,144,128]{2,1,0:T(8,128)(2,1)S(1)}, u32[]{:S(2)}, u32[]{:S(2)}) async-start(bf16[16,144,128]{2,1,0:T(8,128)(2,1)} %bitcast.24), calls=%async_computation.3 | async-start | bytes 1179648 | tf_op jit(solution)/shard_map/all_to_all | solution.py:266
  94.3 15.5 %shard_map.111 = (bf16[128,1024]{1,0:T(8,128)(2,1)}, bf16[128,1024]{1,0:T(8,128)(2,1)}, bf16[128,1024]{1,0:T(8,128)(2,1)}, bf16[128,1024]{1,0:T(8,128)(2,1)}, bf...) custom-call(s32[144]{0:T(256)} %reshape.385.lay_ref, ...), custom_call_target="tpu_custom_call" | custom-call | flops 14495514624 | bytes 13762560 | tf_op jit(solution)/shard_map/pallas_call | solution.py:226
  113.9 5.8 %all-to-all-start.4 = ((bf16[16,144,128]{2,1,0:T(8,128)(2,1)}), bf16[16,144,128]{2,1,0:T(8,128)(2,1)S(1)}, u32[]{:S(2)}, u32[]{:S(2)}) async-start(bf16[16,144,128]{2,1,0:T(8,128)(2,1)} %gather_fusion.8), calls=%async_computation.4 | async-start | bytes 1179648 | tf_op jit(solution)/shard_map/all_to_all | solution.py:266
  119.7 2.1 %add_convert_fusion.2 = bf16[3,12,64,128]{3,2,1,0:T(8,128)(2,1)} fusion(bf16[3,12,128,128]{3,2,1,0:T(8,128)(2,1)} %collective-permute-done.14, s32[]{:T(128)S(6)} %select_n.114, bf16[3,12,128,128]{3,2,1,0:T(8,128)(2,1)S(1)} %bitcast.63), kind=kLoop, calls=%fused_computation.13 | loop fusion | flops 1179648 | bytes 1769476 | tf_op jit(solution)/shard_map/convert_element_type | solution.py:327
  123.4 15.8 %shard_map.112 = (bf16[128,1024]{1,0:T(8,128)(2,1)}, bf16[128,1024]{1,0:T(8,128)(2,1)}, bf16[128,1024]{1,0:T(8,128)(2,1)}, bf16[128,1024]{1,0:T(8,128)(2,1)}, bf...) custom-call(s32[144]{0:T(256)} %reshape.384.lay_ref, ...), custom_call_target="tpu_custom_call" | custom-call | flops 14495514624 | bytes 13762560 | tf_op jit(solution)/shard_map/pallas_call | solution.py:226
  139.4 2.5 %add_convert_fusion.1 = bf16[3,12,64,128]{3,2,1,0:T(8,128)(2,1)} fusion(bf16[3,12,64,128]{3,2,1,0:T(8,128)(2,1)} %collective-permute-done.15, bf16[3,12,128,128]{3,2,1,0:T(8,128)(2,1)} %collective-permute-done.14, s32[]{:T(128)S(6)} %select_n.106, bf16[3,12,128,128]{3,2,1,0:T(8,128)(2,1)S(1)} %bitcast.64), kind=kLoop, calls=%fused_computation.12 | loop fusion | flops 1769472 | bytes 2359300 | tf_op jit(solution)/shard_map/convert_element_type | solution.py:439
  141.8 2.7 %collective-permute-start.16 = (bf16[3,12,64,128]{3,2,1,0:T(8,128)(2,1)}, bf16[3,12,64,128]{3,2,1,0:T(8,128)(2,1)}, u32[]{:S(2)}, u32[]{:S(2)}) collective-permute-start(bf16[3,12,64,128]{3,2,1,0:T(8,128)(2,1)} %add_convert_fusion.1), channel_id=1, source_target_pairs={{0,8},{1,9},{2,10},{3,11},{4,12},{5,13},{6,14},{7,15},{8,0},{9,1},... | collective-permute-start | bytes 1769480 | tf_op jit(solution)/shard_map/ppermute | solution.py:440
  149.9 5.9 %collective-permute-done.12 = bf16[128,1024]{1,0:T(8,128)(2,1)} collective-permute-done((bf16[128,1024]{1,0:T(8,128)(2,1)}, bf16[128,1024]{1,0:T(8,128)(2,1)}, u32[]{:S(2)}, u32[]{:S(2)}) %collective-permute-start.12) | collective-permute-done | bytes 262176 | tf_op jit(solution)/shard_map/ppermute | solution.py:295
  155.8 9.3 %collective-permute-start.21 = (bf16[128,1152]{1,0:T(8,128)(2,1)}, bf16[128,1152]{1,0:T(8,128)(2,1)S(1)}, u32[]{:S(2)}, u32[]{:S(2)}) collective-permute-start(bf16[128,1152]{1,0:T(8,128)(2,1)} %get-tuple-element.126), channel_id=1, source_target_pairs={{0,2},{1,3},{8,10},{9,11},{2,6},{3,7},{10,14},{11,15},{6,4},{7,5},... | collective-permute-start | bytes 884744 | tf_op jit(solution)/shard_map/ppermute | solution.py:295
  165.1 6.3 %collective-permute-done.16 = bf16[3,12,64,128]{3,2,1,0:T(8,128)(2,1)} collective-permute-done((bf16[3,12,64,128]{3,2,1,0:T(8,128)(2,1)}, bf16[3,12,64,128]{3,2,1,0:T(8,128)(2,1)}, u32[]{:S(2)}, u32[]{:S(2)}) %collective-permute-start.16) | collective-permute-done | bytes 589856 | tf_op jit(solution)/shard_map/ppermute | solution.py:440
  175.8 3.2 %fusion.7 = (f32[1,3,12,64,128]{4,3,2,1,0:T(8,128)}, bf16[3,12,64,128]{3,2,1,0:T(8,128)(2,1)S(1)}) fusion(bf16[3,12,64,128]{3,2,1,0:T(8,128)(2,1)} %collective-permute-done.16, bf16[3,12,64,128]{3,2,1,0:T(8,128)(2,1)} %collective-permute-done.18, bf16[3,12,128,128]{3,2,1,0:T(8,128)(2,1)} %copy-done.7, s32[]{:T(128)S(6)} %select_n.106, ...), kind=kLoop, calls=%fused_computation.53 | loop fusion | flops 4128768 | bytes 5308420 | tf_op jit(solution)/shard_map/broadcast_in_dim | solution.py:473
  180.8 3.0 %collective-permute-done.22 = bf16[128,1152]{1,0:T(8,128)(2,1)S(1)} collective-permute-done((bf16[128,1152]{1,0:T(8,128)(2,1)S(1)}, bf16[128,1152]{1,0:T(8,128)(2,1)S(1)}, u32[]{:S(2)}, u32[]{:S(2)}) %collective-permute-start.22) | collective-permute-done | bytes 294944 | tf_op jit(solution)/shard_map/ppermute | solution.py:298
  185.7 7.7 %collective-permute-done.23 = bf16[3,12,64,128]{3,2,1,0:T(8,128)(2,1)S(1)} collective-permute-done((bf16[3,12,64,128]{3,2,1,0:T(8,128)(2,1)S(1)}, bf16[3,12,64,128]{3,2,1,0:T(8,128)(2,1)S(1)}, u32[]{:S(2)}, u32[]{:S(2)}) %collective-permute-start.23) | collective-permute-done | bytes 589856 | tf_op jit(solution)/shard_map/ppermute | solution.py:304
  (135 shorter events, 37.4 us)
Async XLA Ops:
  0.6 17.8 %collective-permute-start.2 = (bf16[128,2048]{1,0:T(8,128)(2,1)}, bf16[128,2048]{1,0:T(8,128)(2,1)}, u32[]{:S(2)}, u32[]{:S(2)}) collective-permute-start(bf16[128,2048]{1,0:T(8,128)(2,1)} %refs_4_.1), channel_id=1, source_target_pairs={{0,2},{1,3},{8,10},{9,11},{2,6},{3,7},{10,14},{11,15},{6,4},{7,5},... | collective-permute-start | bytes 1572872 | tf_op jit(solution)/shard_map/ppermute | solution.py:295
  3.6 16.5 %collective-permute-start.3 = (bf16[128,2048]{1,0:T(8,128)(2,1)}, bf16[128,2048]{1,0:T(8,128)(2,1)}, u32[]{:S(2)}, u32[]{:S(2)}) collective-permute-start(bf16[128,2048]{1,0:T(8,128)(2,1)} %refs_4_.1), channel_id=1, source_target_pairs={{2,0},{3,1},{10,8},{11,9},{6,2},{7,3},{14,10},{15,11},{4,6},{5,7},... | collective-permute-start | bytes 1572872 | tf_op jit(solution)/shard_map/ppermute | solution.py:298
  5.7 32.7 %all-to-all-start = ((bf16[16,160,128]{2,1,0:T(8,128)(2,1)}), bf16[16,160,128]{2,1,0:T(8,128)(2,1)S(1)}, u32[]{:S(2)}, u32[]{:S(2)}) async-start(bf16[16,160,128]{2,1,0:T(8,128)(2,1)} %pad_maximum_fusion), calls=%async_computation | async-start | bytes 1310720 | tf_op jit(solution)/shard_map/all_to_all | solution.py:266
  12.5 25.2 %collective-permute-start.1 = (bf16[128,2176]{1,0:T(8,128)(2,1)S(1)}, bf16[128,2176]{1,0:T(8,128)(2,1)S(1)}, u32[]{:S(2)}, u32[]{:S(2)}) collective-permute-start(bf16[128,2176]{1,0:T(8,128)(2,1)S(1)} %pad_maximum_fusion.1.refs_0_), channel_id=1, source_target_pairs={{2,0},{3,1},{10,8},{11,9},{6,2},{7,3},{14,10},{15,11},{4,6},{5,7},... | collective-permute-start | bytes 1671176 | tf_op jit(solution)/shard_map/ppermute | solution.py:298
  14.5 23.9 %collective-permute-start = (bf16[128,2176]{1,0:T(8,128)(2,1)S(1)}, bf16[128,2176]{1,0:T(8,128)(2,1)}, u32[]{:S(2)}, u32[]{:S(2)}) collective-permute-start(bf16[128,2176]{1,0:T(8,128)(2,1)S(1)} %pad_maximum_fusion.1.refs_0_), channel_id=1, source_target_pairs={{0,2},{1,3},{8,10},{9,11},{2,6},{3,7},{10,14},{11,15},{6,4},{7,5},... | collective-permute-start | bytes 1671176 | tf_op jit(solution)/shard_map/ppermute | solution.py:295
  39.9 21.9 %all-to-all-start.1 = ((bf16[16,144,128]{2,1,0:T(8,128)(2,1)}), bf16[16,144,128]{2,1,0:T(8,128)(2,1)S(1)}, u32[]{:S(2)}, u32[]{:S(2)}) async-start(bf16[16,144,128]{2,1,0:T(8,128)(2,1)} %gather_fusion.3), calls=%async_computation.1 | async-start | bytes 1179648 | tf_op jit(solution)/shard_map/all_to_all | solution.py:266
  61.8 22.9 %collective-permute-start.4 = (bf16[3,12,64,128]{3,2,1,0:T(8,128)(2,1)S(1)}, bf16[3,12,64,128]{3,2,1,0:T(8,128)(2,1)}, u32[]{:S(2)}, u32[]{:S(2)}) collective-permute-start(bf16[3,12,64,128]{3,2,1,0:T(8,128)(2,1)S(1)} %bitcast.67), channel_id=1, source_target_pairs={{0,16},{16,0},{1,17},{17,1},{2,18},{18,2},{3,19},{19,3},{4,20},{20... | collective-permute-start | bytes 1769480 | tf_op jit(solution)/shard_map/ppermute | solution.py:304
  63.3 21.3 %collective-permute-start.5 = (bf16[128,2176]{1,0:T(8,128)(2,1)}, bf16[128,2176]{1,0:T(8,128)(2,1)}, u32[]{:S(2)}, u32[]{:S(2)}) collective-permute-start(bf16[128,2176]{1,0:T(8,128)(2,1)} %collective-permute-done.refs_2_), channel_id=1, source_target_pairs={{0,2},{1,3},{8,10},{9,11},{2,6},{3,7},{10,14},{11,15},{6,4},{7,5},... | collective-permute-start | bytes 1671176 | tf_op jit(solution)/shard_map/ppermute | solution.py:295
  63.9 16.6 %collective-permute-start.6 = (bf16[128,2048]{1,0:T(8,128)(2,1)}, bf16[128,2048]{1,0:T(8,128)(2,1)S(1)}, u32[]{:S(2)}, u32[]{:S(2)}) collective-permute-start(bf16[128,2048]{1,0:T(8,128)(2,1)} %collective-permute-done.3.refs_5_), channel_id=1, source_target_pairs={{2,0},{3,1},{10,8},{11,9},{6,2},{7,3},{14,10},{15,11},{4,6},{5,7},... | collective-permute-start | bytes 1572872 | tf_op jit(solution)/shard_map/ppermute | solution.py:298
  65.3 24.6 %all-to-all-start.2 = ((bf16[16,144,128]{2,1,0:T(8,128)(2,1)}), bf16[16,144,128]{2,1,0:T(8,128)(2,1)S(1)}, u32[]{:S(2)}, u32[]{:S(2)}) async-start(bf16[16,144,128]{2,1,0:T(8,128)(2,1)} %gather_fusion.5), calls=%async_computation.2 | async-start | bytes 1179648 | tf_op jit(solution)/shard_map/all_to_all | solution.py:266
  90.0 19.9 %all-to-all-start.3 = ((bf16[16,144,128]{2,1,0:T(8,128)(2,1)}), bf16[16,144,128]{2,1,0:T(8,128)(2,1)S(1)}, u32[]{:S(2)}, u32[]{:S(2)}) async-start(bf16[16,144,128]{2,1,0:T(8,128)(2,1)} %bitcast.24), calls=%async_computation.3 | async-start | bytes 1179648 | tf_op jit(solution)/shard_map/all_to_all | solution.py:266
  93.7 16.1 %collective-permute-start.9 = (bf16[3,12,64,128]{3,2,1,0:T(8,128)(2,1)S(1)}, bf16[3,12,64,128]{3,2,1,0:T(8,128)(2,1)}, u32[]{:S(2)}, u32[]{:S(2)}) collective-permute-start(bf16[3,12,64,128]{3,2,1,0:T(8,128)(2,1)S(1)} %bitcast.58), channel_id=1, source_target_pairs={{0,16},{16,0},{1,17},{17,1},{2,18},{18,2},{3,19},{19,3},{4,20},{20... | collective-permute-start | bytes 1769480 | tf_op jit(solution)/shard_map/ppermute | solution.py:304
  109.9 9.9 %collective-permute-start.14 = (bf16[3,12,128,128]{3,2,1,0:T(8,128)(2,1)}, bf16[3,12,128,128]{3,2,1,0:T(8,128)(2,1)}, u32[]{:S(2)}, u32[]{:S(2)}) collective-permute-start(bf16[3,12,128,128]{3,2,1,0:T(8,128)(2,1)} %bitcast.72), channel_id=1, source_target_pairs={{0,1},{1,0},{2,3},{3,2},{4,5},{5,4},{6,7},{7,6},{8,9},{9,8},{10,11... | collective-permute-start | bytes 3538952 | tf_op jit(solution)/shard_map/ppermute | solution.py:307
  110.0 13.4 %collective-permute-start.10 = (bf16[3,12,64,128]{3,2,1,0:T(8,128)(2,1)S(1)}, bf16[3,12,64,128]{3,2,1,0:T(8,128)(2,1)}, u32[]{:S(2)}, u32[]{:S(2)}) collective-permute-start(bf16[3,12,64,128]{3,2,1,0:T(8,128)(2,1)S(1)} %bitcast.59), channel_id=1, source_target_pairs={{0,1},{1,0},{2,3},{3,2},{4,5},{5,4},{6,7},{7,6},{8,9},{9,8},{10,11... | collective-permute-start | bytes 1769480 | tf_op jit(solution)/shard_map/ppermute | solution.py:307
  110.4 12.9 %collective-permute-start.11 = (bf16[3,12,64,128]{3,2,1,0:T(8,128)(2,1)}, bf16[3,12,64,128]{3,2,1,0:T(8,128)(2,1)}, u32[]{:S(2)}, u32[]{:S(2)}) collective-permute-start(bf16[3,12,64,128]{3,2,1,0:T(8,128)(2,1)} %collective-permute-done.9), channel_id=1, source_target_pairs={{0,1},{1,0},{2,3},{3,2},{4,5},{5,4},{6,7},{7,6},{8,9},{9,8},{10,11... | collective-permute-start | bytes 1769480 | tf_op jit(solution)/shard_map/ppermute | solution.py:307
  113.9 25.3 %all-to-all-start.4 = ((bf16[16,144,128]{2,1,0:T(8,128)(2,1)}), bf16[16,144,128]{2,1,0:T(8,128)(2,1)S(1)}, u32[]{:S(2)}, u32[]{:S(2)}) async-start(bf16[16,144,128]{2,1,0:T(8,128)(2,1)} %gather_fusion.8), calls=%async_computation.4 | async-start | bytes 1179648 | tf_op jit(solution)/shard_map/all_to_all | solution.py:266
  121.8 17.3 %collective-permute-start.15 = (bf16[3,12,64,128]{3,2,1,0:T(8,128)(2,1)}, bf16[3,12,64,128]{3,2,1,0:T(8,128)(2,1)}, u32[]{:S(2)}, u32[]{:S(2)}) collective-permute-start(bf16[3,12,64,128]{3,2,1,0:T(8,128)(2,1)} %add_convert_fusion.2), channel_id=1, source_target_pairs={{0,16},{16,0},{1,17},{17,1},{2,18},{18,2},{3,19},{19,3},{4,20},{20... | collective-permute-start | bytes 1769480 | tf_op jit(solution)/shard_map/ppermute | solution.py:304
  141.8 29.6 %collective-permute-start.16 = (bf16[3,12,64,128]{3,2,1,0:T(8,128)(2,1)}, bf16[3,12,64,128]{3,2,1,0:T(8,128)(2,1)}, u32[]{:S(2)}, u32[]{:S(2)}) collective-permute-start(bf16[3,12,64,128]{3,2,1,0:T(8,128)(2,1)} %add_convert_fusion.1), channel_id=1, source_target_pairs={{0,8},{1,9},{2,10},{3,11},{4,12},{5,13},{6,14},{7,15},{8,0},{9,1},... | collective-permute-start | bytes 1769480 | tf_op jit(solution)/shard_map/ppermute | solution.py:440
  145.8 25.7 %collective-permute-start.18 = (bf16[3,12,64,128]{3,2,1,0:T(8,128)(2,1)}, bf16[3,12,64,128]{3,2,1,0:T(8,128)(2,1)}, u32[]{:S(2)}, u32[]{:S(2)}) collective-permute-start(bf16[3,12,64,128]{3,2,1,0:T(8,128)(2,1)} %add_convert_fusion), channel_id=1, source_target_pairs={{0,16},{16,0},{1,17},{17,1},{2,18},{18,2},{3,19},{19,3},{4,20},{20... | collective-permute-start | bytes 1769480 | tf_op jit(solution)/shard_map/ppermute | solution.py:304
  146.3 18.9 %collective-permute-start.13 = (bf16[128,1152]{1,0:T(8,128)(2,1)}, bf16[128,1152]{1,0:T(8,128)(2,1)}, u32[]{:S(2)}, u32[]{:S(2)}) collective-permute-start(bf16[128,1152]{1,0:T(8,128)(2,1)} %get-tuple-element.113), channel_id=1, source_target_pairs={{2,0},{3,1},{10,8},{11,9},{6,2},{7,3},{14,10},{15,11},{4,6},{5,7},... | collective-permute-start | bytes 884744 | tf_op jit(solution)/shard_map/ppermute | solution.py:298
  148.5 31.1 %collective-permute-start.20 = (bf16[128,1024]{1,0:T(8,128)(2,1)}, bf16[128,1024]{1,0:T(8,128)(2,1)S(1)}, u32[]{:S(2)}, u32[]{:S(2)}) collective-permute-start(bf16[128,1024]{1,0:T(8,128)(2,1)} %get-tuple-element.124), channel_id=1, source_target_pairs={{2,0},{3,1},{10,8},{11,9},{6,2},{7,3},{14,10},{15,11},{4,6},{5,7},... | collective-permute-start | bytes 786440 | tf_op jit(solution)/shard_map/ppermute | solution.py:298
  155.8 24.9 %collective-permute-start.21 = (bf16[128,1152]{1,0:T(8,128)(2,1)}, bf16[128,1152]{1,0:T(8,128)(2,1)S(1)}, u32[]{:S(2)}, u32[]{:S(2)}) collective-permute-start(bf16[128,1152]{1,0:T(8,128)(2,1)} %get-tuple-element.126), channel_id=1, source_target_pairs={{0,2},{1,3},{8,10},{9,11},{2,6},{3,7},{10,14},{11,15},{6,4},{7,5},... | collective-permute-start | bytes 884744 | tf_op jit(solution)/shard_map/ppermute | solution.py:295
  175.5 8.3 %collective-permute-start.22 = (bf16[128,1152]{1,0:T(8,128)(2,1)S(1)}, bf16[128,1152]{1,0:T(8,128)(2,1)S(1)}, u32[]{:S(2)}, u32[]{:S(2)}) collective-permute-start(bf16[128,1152]{1,0:T(8,128)(2,1)S(1)} %add_convert_fusion.4), channel_id=1, source_target_pairs={{2,0},{3,1},{10,8},{11,9},{6,2},{7,3},{14,10},{15,11},{4,6},{5,7},... | collective-permute-start | bytes 884744 | tf_op jit(solution)/shard_map/ppermute | solution.py:298
  179.0 14.3 %collective-permute-start.23 = (bf16[3,12,64,128]{3,2,1,0:T(8,128)(2,1)S(1)}, bf16[3,12,64,128]{3,2,1,0:T(8,128)(2,1)S(1)}, u32[]{:S(2)}, u32[]{:S(2)}) collective-permute-start(bf16[3,12,64,128]{3,2,1,0:T(8,128)(2,1)S(1)} %get-tuple-element.133), channel_id=1, source_target_pairs={{0,16},{16,0},{1,17},{17,1},{2,18},{18,2},{3,19},{19,3},{4,20},{20... | collective-permute-start | bytes 1769480 | tf_op jit(solution)/shard_map/ppermute | solution.py:304
  (24 other events, 238.5 us)

commit v10 on v9

--- a/solution.py
+++ b/solution.py
@@ -360,6 +360,7 @@
     x_at = {0: jnp.concatenate([tokens, table], axis=1)}
     g_at = {0: out_grad}
     most = chips // 2
+    moment_pieces = moments[0].astype(bf16).reshape(expert_count, -1, LANES)
     for s in range(1, most + 1):
         x_at[-s] = step_on(x_at[1 - s])
         g_at[s] = step_back(g_at[s - 1])
@@ -367,7 +368,9 @@
             x_at[s] = step_back(x_at[s - 1])
             g_at[-s] = step_on(g_at[1 - s])
         if s == 1:
-            x_at, g_at, spread = lax.optimization_barrier((x_at, g_at, spread))
+            x_at, g_at, spread, moment_pieces = lax.optimization_barrier(
+                (x_at, g_at, spread, moment_pieces)
+            )
             state_pieces = spread[:, :piece_rows]
             far_pieces = ordered(state_pieces, all_slots ^ far)
             near_pieces = ordered(state_pieces, all_slots)
@@ -395,11 +398,14 @@
         weights = halves + [other_core(value) for value in halves]
         return [value.reshape(-1, value.shape[2], LANES) for value in weights]
 
-    def run_pair(slot, weights, earlier, beside):
+    def pair_of(slot):
         pair = jnp.stack([slot, slot ^ 1])
         experts = partner.at[pair].get(mode="promise_in_bounds").astype(jnp.int32)
         layouts = all_layouts.at[experts].get(mode="promise_in_bounds")
-        layouts = layouts.reshape(-1).astype(jnp.int32)
+        return experts, layouts.reshape(-1).astype(jnp.int32)
+
+    def run_pair(pair, weights, earlier, beside):
+        experts, layouts = pair
         parts, sums = {}, None
         for group in groups:
             lows, highs, sums = run_experts(
@@ -420,21 +426,23 @@
         own_grad, other_grad = (value.reshape(blocks[0].shape) for value in sums)
         return parts, own_grad, other_core(other_grad), beside
 
-    moment_pieces = moments[0].astype(bf16).reshape(expert_count, -1, LANES)
     halves_far = both_cores(rows_far)
-    halves_far, x_at, g_at = lax.optimization_barrier((halves_far, x_at, g_at))
+    far_pair, near_pair = pair_of(me ^ far), pair_of(me)
+    halves_far, x_at, g_at, far_pair, near_pair, places = lax.optimization_barrier(
+        (halves_far, x_at, g_at, far_pair, near_pair, places)
+    )
     weights_far = to_weights(halves_far)
     weights_far, moment_pieces, rows_near = lax.optimization_barrier(
         (weights_far, moment_pieces, rows_near)
     )
     parts, far_grad, far_sister, (moment_spread, halves_near) = run_pair(
-        me ^ far, weights_far, None, (swap_all(moment_pieces), both_cores(rows_near))
+        far_pair, weights_far, None, (swap_all(moment_pieces), both_cores(rows_near))
     )
     weights_near = to_weights(halves_near)
     moved_moments = swap_all(ordered(moment_spread, all_slots)).reshape(rows_now.shape)
     far_mine, far_theirs = sum_rows(far_grad, far_sister)
     parts, near_grad, near_sister, (far_theirs, moved_moments) = run_pair(
-        me, weights_near, parts, (far_theirs, moved_moments)
+        near_pair, weights_near, parts, (far_theirs, moved_moments)
     )
     far_sum = rows_total(far_mine, far_theirs).astype(bf16)
     from_mirror = lax.ppermute(far_sum, "expert", mirror)
@@ -445,9 +453,11 @@
 
     upward = [step_on(own_share(most, 0)), None]
     downward = [None, step_back(own_share(most, 1))]
-    upward, downward, from_mirror, near_theirs = lax.optimization_barrier(
-        (upward, downward, from_mirror, near_theirs)
-    )
+    shard_grad = rows_total(near_mine, near_theirs) + from_mirror.astype(f32)
+    new_moment = momentum_decay * moved_moments.astype(f32) + shard_grad
+    new_shard = (rows_near.astype(f32) - step_rate * new_moment).astype(bf16)
+
+    upward, downward, new_shard = lax.optimization_barrier((upward, downward, new_shard))
     for s in range(most - 1, 0, -1):
         for part in range(2):
             share = own_share(s, part)
@@ -456,10 +466,6 @@
             downward[part] = step_back(
                 share if downward[part] is None else add(downward[part], share)
             )
-    shard_grad = rows_total(near_mine, near_theirs) + from_mirror.astype(f32)
-    new_moment = momentum_decay * moved_moments.astype(f32) + shard_grad
-    new_shard = (rows_near.astype(f32) - step_rate * new_moment).astype(bf16)
-
     homes = [
         (parts[0][part].astype(f32) + upward[part].astype(f32) + downward[part].astype(f32)).astype(
             bf16

time: 196 us -> 192 us (0.980)
  starting transfers between devices: 57.6 us -> 50.4 us
  waiting for transfers between devices: 75.5 us -> 82.5 us
  other arithmetic: 19 us -> 14.5 us
    ppermute x1, waiting for transfers between devices: 6.33 us -> 22.2 us  [body(): from_mirror = lax.ppermute(far_sum, 'expert', mirror)]
    ppermute x6, starting transfers between devices: 15.3 us -> 7.5 us  [step_on(): return lax.ppermute(value, 'expert', onward)]
    ppermute x6, waiting for transfers between devices: 33 us -> 25.7 us  [step_back(): return lax.ppermute(value, 'expert', backward)]
    ppermute x5, waiting for transfers between devices: 7.67 us -> 2.56 us  [other_replica(): return lax.ppermute(value, 'dp', [(0, 1), (1, 0)])]
    convert_element_type x2, other arithmetic: 2.22 us -> 0.14 us  [add(): return (left.astype(f32) + right.astype(f32)).astype(bf16)]
  transfers between devices with their start and end apart: 29 -> 29, of which waited for: 12 -> 13; matrix products, arithmetic and copies ran while one was open for 13% -> 11% of each run, Pallas kernels for 16% -> 16%
where the time goes in v10:
time: 192 us; the launch traced here: 191 us
  waiting for transfers between devices  82.5 us (43%)
  starting transfers between devices  50.4 us (26%)
  Pallas kernels  31.4 us (16%)
  other arithmetic  14.5 us (8%)
  local copies, waits for them, and re-layouts  11.1 us (6%)
    pallas_call x2, Pallas kernels, run_experts(): pl.pallas_call(functools.partial(expert_kernel, shards, slots, half, len(...  31.4 us
    all_to_all x5, starting transfers between devices, swap_all(): lax.all_to_all(pieces, 'expert', split_axis=0, concat_axis=0, tiled=True)  26.9 us
    ppermute x6, waiting for transfers between devices, step_back(): return lax.ppermute(value, 'expert', backward)  25.7 us
    ppermute x1, waiting for transfers between devices, body(): from_mirror = lax.ppermute(far_sum, 'expert', mirror)  22.2 us
    ppermute x6, waiting for transfers between devices, step_on(): return lax.ppermute(value, 'expert', onward)  16 us
    all_to_all x5, waiting for transfers between devices, swap_all(): lax.all_to_all(pieces, 'expert', split_axis=0, concat_axis=0, tiled=True)  15 us
    ppermute x6, starting transfers between devices, step_on(): return lax.ppermute(value, 'expert', onward)  7.5 us
    ppermute x6, starting transfers between devices, step_back(): return lax.ppermute(value, 'expert', backward)  7.21 us
  transfers between devices with their start and end apart: 29, of which 13 were waited for; matrix products, arithmetic and copies ran while one was open for 11% of the time, Pallas kernels for 16%

profile of v10, /device:TPU:0, one launch (start us, length us, event | category | flops | bytes accessed | tf_op | source)
XLA Modules:
  0.0 190.9 jit_solution(821686485444453728)
XLA Ops:
  0.6 3.0 %collective-permute-start.2 = (bf16[128,2048]{1,0:T(8,128)(2,1)}, bf16[128,2048]{1,0:T(8,128)(2,1)}, u32[]{:S(2)}, u32[]{:S(2)}) collective-permute-start(bf16[128,2048]{1,0:T(8,128)(2,1)} %refs_4_.1), channel_id=1, source_target_pairs={{0,2},{1,3},{8,10},{9,11},{2,6},{3,7},{10,14},{11,15},{6,4},{7,5},... | collective-permute-start | bytes 1572872 | tf_op jit(solution)/shard_map/ppermute | solution.py:295
  5.7 6.4 %all-to-all-start = ((bf16[16,160,128]{2,1,0:T(8,128)(2,1)}), bf16[16,160,128]{2,1,0:T(8,128)(2,1)S(1)}, u32[]{:S(2)}, u32[]{:S(2)}) async-start(bf16[16,160,128]{2,1,0:T(8,128)(2,1)} %pad_maximum_fusion), calls=%async_computation | async-start | bytes 1310720 | tf_op jit(solution)/shard_map/all_to_all | solution.py:266
  13.4 1.9 %collective-permute-start.1 = (bf16[128,2176]{1,0:T(8,128)(2,1)}, bf16[128,2176]{1,0:T(8,128)(2,1)}, u32[]{:S(2)}, u32[]{:S(2)}) collective-permute-start(bf16[128,2176]{1,0:T(8,128)(2,1)} %pad_maximum_fusion.1.refs_0_), channel_id=1, source_target_pairs={{2,0},{3,1},{10,8},{11,9},{6,2},{7,3},{14,10},{15,11},{4,6},{5,7},... | collective-permute-start | bytes 1671176 | tf_op jit(solution)/shard_map/ppermute | solution.py:298
  18.4 1.7 collective-permute-done.3.refs_5_
  20.1 17.7 %collective-permute-done.1.refs_1_ = bf16[128,2176]{1,0:T(8,128)(2,1)} collective-permute-done((bf16[128,2176]{1,0:T(8,128)(2,1)}, bf16[128,2176]{1,0:T(8,128)(2,1)}, u32[]{:S(2)}, u32[]{:S(2)}) %collective-permute-start.1) | collective-permute-done | bytes 557088 | tf_op jit(solution)/shard_map/ppermute | solution.py:298
  39.9 6.4 %all-to-all-start.1 = ((bf16[16,144,128]{2,1,0:T(8,128)(2,1)}), bf16[16,144,128]{2,1,0:T(8,128)(2,1)S(1)}, u32[]{:S(2)}, u32[]{:S(2)}) async-start(bf16[16,144,128]{2,1,0:T(8,128)(2,1)} %gather_fusion.1), calls=%async_computation.1 | async-start | bytes 1179648 | tf_op jit(solution)/shard_map/all_to_all | solution.py:266
  48.5 13.4 %all-to-all-done.1 = bf16[16,144,128]{2,1,0:T(8,128)(2,1)S(1)} async-done(((bf16[16,144,128]{2,1,0:T(8,128)(2,1)}), bf16[16,144,128]{2,1,0:T(8,128)(2,1)S(1)}, u32[]{:S(2)}, u32[]{:S(2)}) %all-to-all-start.1) | async-done | bytes 589856 | tf_op jit(solution)/shard_map/all_to_all | solution.py:266
  61.9 1.5 collective-permute-start.4
  66.1 4.4 %all-to-all-start.2 = ((bf16[16,144,128]{2,1,0:T(8,128)(2,1)}), bf16[16,144,128]{2,1,0:T(8,128)(2,1)S(1)}, u32[]{:S(2)}, u32[]{:S(2)}) async-start(bf16[16,144,128]{2,1,0:T(8,128)(2,1)} %gather_fusion.3), calls=%async_computation.2 | async-start | bytes 1179648 | tf_op jit(solution)/shard_map/all_to_all | solution.py:266
  73.7 6.3 %collective-permute-done.6.refs_7_ = bf16[128,2048]{1,0:T(8,128)(2,1)} collective-permute-done((bf16[128,2048]{1,0:T(8,128)(2,1)}, bf16[128,2048]{1,0:T(8,128)(2,1)}, u32[]{:S(2)}, u32[]{:S(2)}) %collective-permute-start.6) | collective-permute-done | bytes 524320 | tf_op jit(solution)/shard_map/ppermute | solution.py:298
  80.0 6.8 %collective-permute-done.5.refs_3_ = bf16[128,2176]{1,0:T(8,128)(2,1)} collective-permute-done((bf16[128,2176]{1,0:T(8,128)(2,1)}, bf16[128,2176]{1,0:T(8,128)(2,1)}, u32[]{:S(2)}, u32[]{:S(2)}) %collective-permute-start.5) | collective-permute-done | bytes 557088 | tf_op jit(solution)/shard_map/ppermute | solution.py:295
  87.2 1.6 all-to-all-done.2
  90.4 3.8 %all-to-all-start.3 = ((bf16[16,144,128]{2,1,0:T(8,128)(2,1)}), bf16[16,144,128]{2,1,0:T(8,128)(2,1)S(1)}, u32[]{:S(2)}, u32[]{:S(2)}) async-start(bf16[16,144,128]{2,1,0:T(8,128)(2,1)} %bitcast.2), calls=%async_computation.3 | async-start | bytes 1179648 | tf_op jit(solution)/shard_map/all_to_all | solution.py:266
  94.7 15.5 %shard_map.111 = (bf16[128,1024]{1,0:T(8,128)(2,1)}, bf16[128,1024]{1,0:T(8,128)(2,1)}, bf16[128,1024]{1,0:T(8,128)(2,1)}, bf16[128,1024]{1,0:T(8,128)(2,1)}, bf...) custom-call(s32[144]{0:T(256)} %reshape.384.lay_ref, ...), custom_call_target="tpu_custom_call" | custom-call | flops 14495514624 | bytes 13762560 | tf_op jit(solution)/shard_map/pallas_call | solution.py:226
  112.4 5.9 %all-to-all-start.4 = ((bf16[16,144,128]{2,1,0:T(8,128)(2,1)}), bf16[16,144,128]{2,1,0:T(8,128)(2,1)S(1)}, u32[]{:S(2)}, u32[]{:S(2)}) async-start(bf16[16,144,128]{2,1,0:T(8,128)(2,1)} %gather_fusion.8), calls=%async_computation.4 | async-start | bytes 1179648 | tf_op jit(solution)/shard_map/all_to_all | solution.py:266
  118.2 2.3 %add_convert_fusion.2 = bf16[3,12,64,128]{3,2,1,0:T(8,128)(2,1)} fusion(bf16[3,12,128,128]{3,2,1,0:T(8,128)(2,1)} %collective-permute-done.14, s32[]{:T(128)S(6)} %select_n.114, bf16[3,12,128,128]{3,2,1,0:T(8,128)(2,1)} %bitcast.63), kind=kLoop, calls=%fused_computation.13 | loop fusion | flops 1179648 | bytes 1769476 | tf_op jit(solution)/shard_map/convert_element_type | solution.py:327
  122.1 15.9 %shard_map.112 = (bf16[128,1024]{1,0:T(8,128)(2,1)}, bf16[128,1024]{1,0:T(8,128)(2,1)}, bf16[128,1024]{1,0:T(8,128)(2,1)}, bf16[128,1024]{1,0:T(8,128)(2,1)}, bf...) custom-call(s32[144]{0:T(256)} %reshape.385.lay_ref, ...), custom_call_target="tpu_custom_call" | custom-call | flops 14495514624 | bytes 13762560 | tf_op jit(solution)/shard_map/pallas_call | solution.py:226
  139.7 2.7 %collective-permute-start.18 = (bf16[3,12,64,128]{3,2,1,0:T(8,128)(2,1)S(1)}, bf16[3,12,64,128]{3,2,1,0:T(8,128)(2,1)S(1)}, u32[]{:S(2)}, u32[]{:S(2)}) collective-permute-start(bf16[3,12,64,128]{3,2,1,0:T(8,128)(2,1)S(1)} %add_convert_fusion), channel_id=1, source_target_pairs={{0,8},{1,9},{2,10},{3,11},{4,12},{5,13},{6,14},{7,15},{8,0},{9,1},... | collective-permute-start | bytes 1769480 | tf_op jit(solution)/shard_map/ppermute | solution.py:448
  146.7 22.2 %collective-permute-done.18 = bf16[3,12,64,128]{3,2,1,0:T(8,128)(2,1)S(1)} collective-permute-done((bf16[3,12,64,128]{3,2,1,0:T(8,128)(2,1)S(1)}, bf16[3,12,64,128]{3,2,1,0:T(8,128)(2,1)S(1)}, u32[]{:S(2)}, u32[]{:S(2)}) %collective-permute-start.18) | collective-permute-done | bytes 589856 | tf_op jit(solution)/shard_map/ppermute | solution.py:448
  169.0 1.9 collective-permute-start.21
  170.9 1.7 fusion.7
  173.2 1.7 collective-permute-start.22
  175.6 7.8 %collective-permute-done.19 = bf16[128,1024]{1,0:T(8,128)(2,1)} collective-permute-done((bf16[128,1024]{1,0:T(8,128)(2,1)S(1)}, bf16[128,1024]{1,0:T(8,128)(2,1)}, u32[]{:S(2)}, u32[]{:S(2)}) %collective-permute-start.19) | collective-permute-done | bytes 262176 | tf_op jit(solution)/shard_map/ppermute | solution.py:295
  186.5 2.6 %collective-permute-done.23 = bf16[3,12,64,128]{3,2,1,0:T(8,128)(2,1)S(1)} collective-permute-done((bf16[3,12,64,128]{3,2,1,0:T(8,128)(2,1)S(1)}, bf16[3,12,64,128]{3,2,1,0:T(8,128)(2,1)S(1)}, u32[]{:S(2)}, u32[]{:S(2)}) %collective-permute-start.23) | collective-permute-done | bytes 589856 | tf_op jit(solution)/shard_map/ppermute | solution.py:304
  (137 shorter events, 34.7 us)
Async XLA Ops:
  0.6 17.8 %collective-permute-start.2 = (bf16[128,2048]{1,0:T(8,128)(2,1)}, bf16[128,2048]{1,0:T(8,128)(2,1)}, u32[]{:S(2)}, u32[]{:S(2)}) collective-permute-start(bf16[128,2048]{1,0:T(8,128)(2,1)} %refs_4_.1), channel_id=1, source_target_pairs={{0,2},{1,3},{8,10},{9,11},{2,6},{3,7},{10,14},{11,15},{6,4},{7,5},... | collective-permute-start | bytes 1572872 | tf_op jit(solution)/shard_map/ppermute | solution.py:295
  3.6 16.5 %collective-permute-start.3 = (bf16[128,2048]{1,0:T(8,128)(2,1)}, bf16[128,2048]{1,0:T(8,128)(2,1)}, u32[]{:S(2)}, u32[]{:S(2)}) collective-permute-start(bf16[128,2048]{1,0:T(8,128)(2,1)} %refs_4_.1), channel_id=1, source_target_pairs={{2,0},{3,1},{10,8},{11,9},{6,2},{7,3},{14,10},{15,11},{4,6},{5,7},... | collective-permute-start | bytes 1572872 | tf_op jit(solution)/shard_map/ppermute | solution.py:298
  5.7 32.7 %all-to-all-start = ((bf16[16,160,128]{2,1,0:T(8,128)(2,1)}), bf16[16,160,128]{2,1,0:T(8,128)(2,1)S(1)}, u32[]{:S(2)}, u32[]{:S(2)}) async-start(bf16[16,160,128]{2,1,0:T(8,128)(2,1)} %pad_maximum_fusion), calls=%async_computation | async-start | bytes 1310720 | tf_op jit(solution)/shard_map/all_to_all | solution.py:266
  13.4 24.4 %collective-permute-start.1 = (bf16[128,2176]{1,0:T(8,128)(2,1)}, bf16[128,2176]{1,0:T(8,128)(2,1)}, u32[]{:S(2)}, u32[]{:S(2)}) collective-permute-start(bf16[128,2176]{1,0:T(8,128)(2,1)} %pad_maximum_fusion.1.refs_0_), channel_id=1, source_target_pairs={{2,0},{3,1},{10,8},{11,9},{6,2},{7,3},{14,10},{15,11},{4,6},{5,7},... | collective-permute-start | bytes 1671176 | tf_op jit(solution)/shard_map/ppermute | solution.py:298
  15.3 23.1 %collective-permute-start = (bf16[128,2176]{1,0:T(8,128)(2,1)}, bf16[128,2176]{1,0:T(8,128)(2,1)}, u32[]{:S(2)}, u32[]{:S(2)}) collective-permute-start(bf16[128,2176]{1,0:T(8,128)(2,1)} %pad_maximum_fusion.1.refs_0_), channel_id=1, source_target_pairs={{0,2},{1,3},{8,10},{9,11},{2,6},{3,7},{10,14},{11,15},{6,4},{7,5},... | collective-permute-start | bytes 1671176 | tf_op jit(solution)/shard_map/ppermute | solution.py:295
  39.9 22.0 %all-to-all-start.1 = ((bf16[16,144,128]{2,1,0:T(8,128)(2,1)}), bf16[16,144,128]{2,1,0:T(8,128)(2,1)S(1)}, u32[]{:S(2)}, u32[]{:S(2)}) async-start(bf16[16,144,128]{2,1,0:T(8,128)(2,1)} %gather_fusion.1), calls=%async_computation.1 | async-start | bytes 1179648 | tf_op jit(solution)/shard_map/all_to_all | solution.py:266
  61.9 24.9 %collective-permute-start.4 = (bf16[3,12,64,128]{3,2,1,0:T(8,128)(2,1)S(1)}, bf16[3,12,64,128]{3,2,1,0:T(8,128)(2,1)}, u32[]{:S(2)}, u32[]{:S(2)}) collective-permute-start(bf16[3,12,64,128]{3,2,1,0:T(8,128)(2,1)S(1)} %bitcast.67), channel_id=1, source_target_pairs={{0,16},{16,0},{1,17},{17,1},{2,18},{18,2},{3,19},{19,3},{4,20},{20... | collective-permute-start | bytes 1769480 | tf_op jit(solution)/shard_map/ppermute | solution.py:304
  64.0 15.9 %collective-permute-start.6 = (bf16[128,2048]{1,0:T(8,128)(2,1)}, bf16[128,2048]{1,0:T(8,128)(2,1)}, u32[]{:S(2)}, u32[]{:S(2)}) collective-permute-start(bf16[128,2048]{1,0:T(8,128)(2,1)} %collective-permute-done.3.refs_5_), channel_id=1, source_target_pairs={{2,0},{3,1},{10,8},{11,9},{6,2},{7,3},{14,10},{15,11},{4,6},{5,7},... | collective-permute-start | bytes 1572872 | tf_op jit(solution)/shard_map/ppermute | solution.py:298
  65.4 21.3 %collective-permute-start.5 = (bf16[128,2176]{1,0:T(8,128)(2,1)}, bf16[128,2176]{1,0:T(8,128)(2,1)}, u32[]{:S(2)}, u32[]{:S(2)}) collective-permute-start(bf16[128,2176]{1,0:T(8,128)(2,1)} %collective-permute-done.refs_2_), channel_id=1, source_target_pairs={{0,2},{1,3},{8,10},{9,11},{2,6},{3,7},{10,14},{11,15},{6,4},{7,5},... | collective-permute-start | bytes 1671176 | tf_op jit(solution)/shard_map/ppermute | solution.py:295
  66.1 22.8 %all-to-all-start.2 = ((bf16[16,144,128]{2,1,0:T(8,128)(2,1)}), bf16[16,144,128]{2,1,0:T(8,128)(2,1)S(1)}, u32[]{:S(2)}, u32[]{:S(2)}) async-start(bf16[16,144,128]{2,1,0:T(8,128)(2,1)} %gather_fusion.3), calls=%async_computation.2 | async-start | bytes 1179648 | tf_op jit(solution)/shard_map/all_to_all | solution.py:266
  90.4 19.9 %all-to-all-start.3 = ((bf16[16,144,128]{2,1,0:T(8,128)(2,1)}), bf16[16,144,128]{2,1,0:T(8,128)(2,1)S(1)}, u32[]{:S(2)}, u32[]{:S(2)}) async-start(bf16[16,144,128]{2,1,0:T(8,128)(2,1)} %bitcast.2), calls=%async_computation.3 | async-start | bytes 1179648 | tf_op jit(solution)/shard_map/all_to_all | solution.py:266
  94.1 16.1 %collective-permute-start.9 = (bf16[3,12,64,128]{3,2,1,0:T(8,128)(2,1)S(1)}, bf16[3,12,64,128]{3,2,1,0:T(8,128)(2,1)}, u32[]{:S(2)}, u32[]{:S(2)}) collective-permute-start(bf16[3,12,64,128]{3,2,1,0:T(8,128)(2,1)S(1)} %bitcast.58), channel_id=1, source_target_pairs={{0,16},{16,0},{1,17},{17,1},{2,18},{18,2},{3,19},{19,3},{4,20},{20... | collective-permute-start | bytes 1769480 | tf_op jit(solution)/shard_map/ppermute | solution.py:304
  110.3 11.7 %collective-permute-start.10 = (bf16[3,12,64,128]{3,2,1,0:T(8,128)(2,1)S(1)}, bf16[3,12,64,128]{3,2,1,0:T(8,128)(2,1)}, u32[]{:S(2)}, u32[]{:S(2)}) collective-permute-start(bf16[3,12,64,128]{3,2,1,0:T(8,128)(2,1)S(1)} %bitcast.59), channel_id=1, source_target_pairs={{0,1},{1,0},{2,3},{3,2},{4,5},{5,4},{6,7},{7,6},{8,9},{9,8},{10,11... | collective-permute-start | bytes 1769480 | tf_op jit(solution)/shard_map/ppermute | solution.py:307
  110.8 11.2 %collective-permute-start.11 = (bf16[3,12,64,128]{3,2,1,0:T(8,128)(2,1)}, bf16[3,12,64,128]{3,2,1,0:T(8,128)(2,1)}, u32[]{:S(2)}, u32[]{:S(2)}) collective-permute-start(bf16[3,12,64,128]{3,2,1,0:T(8,128)(2,1)} %collective-permute-done.9), channel_id=1, source_target_pairs={{0,1},{1,0},{2,3},{3,2},{4,5},{5,4},{6,7},{7,6},{8,9},{9,8},{10,11... | collective-permute-start | bytes 1769480 | tf_op jit(solution)/shard_map/ppermute | solution.py:307
  112.4 25.6 %all-to-all-start.4 = ((bf16[16,144,128]{2,1,0:T(8,128)(2,1)}), bf16[16,144,128]{2,1,0:T(8,128)(2,1)S(1)}, u32[]{:S(2)}, u32[]{:S(2)}) async-start(bf16[16,144,128]{2,1,0:T(8,128)(2,1)} %gather_fusion.8), calls=%async_computation.4 | async-start | bytes 1179648 | tf_op jit(solution)/shard_map/all_to_all | solution.py:266
  120.6 17.4 %collective-permute-start.15 = (bf16[3,12,64,128]{3,2,1,0:T(8,128)(2,1)}, bf16[3,12,64,128]{3,2,1,0:T(8,128)(2,1)S(1)}, u32[]{:S(2)}, u32[]{:S(2)}) collective-permute-start(bf16[3,12,64,128]{3,2,1,0:T(8,128)(2,1)} %add_convert_fusion.2), channel_id=1, source_target_pairs={{0,16},{16,0},{1,17},{17,1},{2,18},{18,2},{3,19},{19,3},{4,20},{20... | collective-permute-start | bytes 1769480 | tf_op jit(solution)/shard_map/ppermute | solution.py:304
  139.7 29.2 %collective-permute-start.18 = (bf16[3,12,64,128]{3,2,1,0:T(8,128)(2,1)S(1)}, bf16[3,12,64,128]{3,2,1,0:T(8,128)(2,1)S(1)}, u32[]{:S(2)}, u32[]{:S(2)}) collective-permute-start(bf16[3,12,64,128]{3,2,1,0:T(8,128)(2,1)S(1)} %add_convert_fusion), channel_id=1, source_target_pairs={{0,8},{1,9},{2,10},{3,11},{4,12},{5,13},{6,14},{7,15},{8,0},{9,1},... | collective-permute-start | bytes 1769480 | tf_op jit(solution)/shard_map/ppermute | solution.py:448
  142.7 28.2 %collective-permute-start.17 = (bf16[3,12,64,128]{3,2,1,0:T(8,128)(2,1)S(1)}, bf16[3,12,64,128]{3,2,1,0:T(8,128)(2,1)S(1)}, u32[]{:S(2)}, u32[]{:S(2)}) collective-permute-start(bf16[3,12,64,128]{3,2,1,0:T(8,128)(2,1)S(1)} %add_convert_fusion.1), channel_id=1, source_target_pairs={{0,16},{16,0},{1,17},{17,1},{2,18},{18,2},{3,19},{19,3},{4,20},{20... | collective-permute-start | bytes 1769480 | tf_op jit(solution)/shard_map/ppermute | solution.py:304
  143.2 29.4 %collective-permute-start.12 = (bf16[128,1024]{1,0:T(8,128)(2,1)S(1)}, bf16[128,1024]{1,0:T(8,128)(2,1)S(1)}, u32[]{:S(2)}, u32[]{:S(2)}) collective-permute-start(bf16[128,1024]{1,0:T(8,128)(2,1)S(1)} %copy-done.19), channel_id=1, source_target_pairs={{0,2},{1,3},{8,10},{9,11},{2,6},{3,7},{10,14},{11,15},{6,4},{7,5},... | collective-permute-start | bytes 786440 | tf_op jit(solution)/shard_map/ppermute | solution.py:295
  144.7 30.9 %collective-permute-start.20 = (bf16[128,1024]{1,0:T(8,128)(2,1)}, bf16[128,1024]{1,0:T(8,128)(2,1)}, u32[]{:S(2)}, u32[]{:S(2)}) collective-permute-start(bf16[128,1024]{1,0:T(8,128)(2,1)} %get-tuple-element.136), channel_id=1, source_target_pairs={{2,0},{3,1},{10,8},{11,9},{6,2},{7,3},{14,10},{15,11},{4,6},{5,7},... | collective-permute-start | bytes 786440 | tf_op jit(solution)/shard_map/ppermute | solution.py:298
  145.3 27.4 %collective-permute-start.13 = (bf16[128,1152]{1,0:T(8,128)(2,1)S(1)}, bf16[128,1152]{1,0:T(8,128)(2,1)S(1)}, u32[]{:S(2)}, u32[]{:S(2)}) collective-permute-start(bf16[128,1152]{1,0:T(8,128)(2,1)S(1)} %copy-done.18), channel_id=1, source_target_pairs={{2,0},{3,1},{10,8},{11,9},{6,2},{7,3},{14,10},{15,11},{4,6},{5,7},... | collective-permute-start | bytes 884744 | tf_op jit(solution)/shard_map/ppermute | solution.py:298
  169.0 15.6 %collective-permute-start.21 = (bf16[128,1152]{1,0:T(8,128)(2,1)}, bf16[128,1152]{1,0:T(8,128)(2,1)S(1)}, u32[]{:S(2)}, u32[]{:S(2)}) collective-permute-start(bf16[128,1152]{1,0:T(8,128)(2,1)} %get-tuple-element.138), channel_id=1, source_target_pairs={{0,2},{1,3},{8,10},{9,11},{2,6},{3,7},{10,14},{11,15},{6,4},{7,5},... | collective-permute-start | bytes 884744 | tf_op jit(solution)/shard_map/ppermute | solution.py:295
  173.2 11.4 %collective-permute-start.22 = (bf16[128,1152]{1,0:T(8,128)(2,1)S(1)}, bf16[128,1152]{1,0:T(8,128)(2,1)S(1)}, u32[]{:S(2)}, u32[]{:S(2)}) collective-permute-start(bf16[128,1152]{1,0:T(8,128)(2,1)S(1)} %add_convert_fusion.4), channel_id=1, source_target_pairs={{2,0},{3,1},{10,8},{11,9},{6,2},{7,3},{14,10},{15,11},{4,6},{5,7},... | collective-permute-start | bytes 884744 | tf_op jit(solution)/shard_map/ppermute | solution.py:298
  175.1 14.0 %collective-permute-start.23 = (bf16[3,12,64,128]{3,2,1,0:T(8,128)(2,1)S(1)}, bf16[3,12,64,128]{3,2,1,0:T(8,128)(2,1)S(1)}, u32[]{:S(2)}, u32[]{:S(2)}) collective-permute-start(bf16[3,12,64,128]{3,2,1,0:T(8,128)(2,1)S(1)} %get-tuple-element.141), channel_id=1, source_target_pairs={{0,16},{16,0},{1,17},{17,1},{2,18},{18,2},{3,19},{19,3},{4,20},{20... | collective-permute-start | bytes 1769480 | tf_op jit(solution)/shard_map/ppermute | solution.py:304
  (25 other events, 257.4 us)

commit v11 on v10

--- a/solution.py
+++ b/solution.py
@@ -363,18 +363,22 @@
     moment_pieces = moments[0].astype(bf16).reshape(expert_count, -1, LANES)
     for s in range(1, most + 1):
         x_at[-s] = step_on(x_at[1 - s])
-        g_at[s] = step_back(g_at[s - 1])
         if s < most:
             x_at[s] = step_back(x_at[s - 1])
-            g_at[-s] = step_on(g_at[1 - s])
         if s == 1:
             x_at, g_at, spread, moment_pieces = lax.optimization_barrier(
                 (x_at, g_at, spread, moment_pieces)
             )
+        g_at[s] = step_back(g_at[s - 1])
+        if s < most:
+            g_at[-s] = step_on(g_at[1 - s])
+        if s == 1:
             state_pieces = spread[:, :piece_rows]
             far_pieces = ordered(state_pieces, all_slots ^ far)
             near_pieces = ordered(state_pieces, all_slots)
-            rows_far, near_pieces = lax.optimization_barrier((swap_all(far_pieces), near_pieces))
+            rows_far, near_pieces, g_at = lax.optimization_barrier(
+                (swap_all(far_pieces), near_pieces, g_at)
+            )
             rows_far = rows_far.reshape(rows_now.shape)
     x_at[most] = x_at[-most]
     rows_near = swap_all(near_pieces).reshape(rows_now.shape)

time: 192 us -> 204 us (1.062)
  waiting for transfers between devices: 82.5 us -> 92.1 us
  starting transfers between devices: 50.4 us -> 52.9 us
    ppermute x6, waiting for transfers between devices: 25.7 us -> 41.8 us  [step_back(): return lax.ppermute(value, 'expert', backward)]
    all_to_all x5, waiting for transfers between devices: 15 us -> 0.01 us  [swap_all(): lax.all_to_all(pieces, 'expert', split_axis=0, concat_axis=0, tiled=True)]
    ppermute x6, waiting for transfers between devices: 16 us -> 22.7 us  [step_on(): return lax.ppermute(value, 'expert', onward)]
    ppermute x6, starting transfers between devices: 7.21 us -> 9.51 us  [step_back(): return lax.ppermute(value, 'expert', backward)]
    all_to_all x5, starting transfers between devices: 26.9 us -> 29 us  [swap_all(): lax.all_to_all(pieces, 'expert', split_axis=0, concat_axis=0, tiled=True)]
  transfers between devices with their start and end apart: 29 -> 29, of which waited for: 13 -> 11; matrix products, arithmetic and copies ran while one was open for 11% -> 10% of each run, Pallas kernels for 16% -> 15%
where the time goes in v11:
time: 204 us; the launch traced here: 203 us
  waiting for transfers between devices  92.1 us (45%)
  starting transfers between devices  52.9 us (26%)
  Pallas kernels  31.4 us (15%)
  other arithmetic  14.6 us (7%)
  local copies, waits for them, and re-layouts  11.3 us (6%)
    ppermute x6, waiting for transfers between devices, step_back(): return lax.ppermute(value, 'expert', backward)  41.8 us
    pallas_call x2, Pallas kernels, run_experts(): pl.pallas_call(functools.partial(expert_kernel, shards, slots, half, len(...  31.4 us
    all_to_all x5, starting transfers between devices, swap_all(): lax.all_to_all(pieces, 'expert', split_axis=0, concat_axis=0, tiled=True)  29 us
    ppermute x6, waiting for transfers between devices, step_on(): return lax.ppermute(value, 'expert', onward)  22.7 us
    ppermute x1, waiting for transfers between devices, body(): from_mirror = lax.ppermute(far_sum, 'expert', mirror)  22.3 us
    ppermute x6, starting transfers between devices, step_back(): return lax.ppermute(value, 'expert', backward)  9.51 us
    ppermute x6, starting transfers between devices, step_on(): return lax.ppermute(value, 'expert', onward)  5.54 us
    ppermute x5, starting transfers between devices, other_replica(): return lax.ppermute(value, 'dp', [(0, 1), (1, 0)])  4.68 us
  transfers between devices with their start and end apart: 29, of which 11 were waited for; matrix products, arithmetic and copies ran while one was open for 10% of the time, Pallas kernels for 15%

profile of v11, /device:TPU:0, one launch (start us, length us, event | category | flops | bytes accessed | tf_op | source)
XLA Modules:
  0.0 203.3 jit_solution(3252129174610358490)
XLA Ops:
  2.9 7.5 %all-to-all-start = ((bf16[16,160,128]{2,1,0:T(8,128)(2,1)}), bf16[16,160,128]{2,1,0:T(8,128)(2,1)S(1)}, u32[]{:S(2)}, u32[]{:S(2)}) async-start(bf16[16,160,128]{2,1,0:T(8,128)(2,1)} %pad_maximum_fusion), calls=%async_computation | async-start | bytes 1310720 | tf_op jit(solution)/shard_map/all_to_all | solution.py:266
  11.6 1.9 collective-permute-start.1
  15.9 18.1 %collective-permute-done.1.refs_1_ = bf16[128,2176]{1,0:T(8,128)(2,1)} collective-permute-done((bf16[128,2176]{1,0:T(8,128)(2,1)}, bf16[128,2176]{1,0:T(8,128)(2,1)}, u32[]{:S(2)}, u32[]{:S(2)}) %collective-permute-start.1) | collective-permute-done | bytes 557088 | tf_op jit(solution)/shard_map/ppermute | solution.py:298
  34.1 2.0 %collective-permute-done.refs_2_ = bf16[128,2176]{1,0:T(8,128)(2,1)} collective-permute-done((bf16[128,2176]{1,0:T(8,128)(2,1)}, bf16[128,2176]{1,0:T(8,128)(2,1)}, u32[]{:S(2)}, u32[]{:S(2)}) %collective-permute-start) | collective-permute-done | bytes 557088 | tf_op jit(solution)/shard_map/ppermute | solution.py:295
  37.6 4.8 %all-to-all-start.1 = ((bf16[16,144,128]{2,1,0:T(8,128)(2,1)}), bf16[16,144,128]{2,1,0:T(8,128)(2,1)S(1)}, u32[]{:S(2)}, u32[]{:S(2)}) async-start(bf16[16,144,128]{2,1,0:T(8,128)(2,1)} %gather_fusion.1), calls=%async_computation.1 | async-start | bytes 1179648 | tf_op jit(solution)/shard_map/all_to_all | solution.py:266
  42.4 1.9 collective-permute-start.3
  46.7 17.6 %collective-permute-done.3.refs_5_ = bf16[128,2048]{1,0:T(8,128)(2,1)} collective-permute-done((bf16[128,2048]{1,0:T(8,128)(2,1)}, bf16[128,2048]{1,0:T(8,128)(2,1)}, u32[]{:S(2)}, u32[]{:S(2)}) %collective-permute-start.3) | collective-permute-done | bytes 524320 | tf_op jit(solution)/shard_map/ppermute | solution.py:298
  64.3 2.0 %collective-permute-done.2.refs_6_ = bf16[128,2048]{1,0:T(8,128)(2,1)} collective-permute-done((bf16[128,2048]{1,0:T(8,128)(2,1)}, bf16[128,2048]{1,0:T(8,128)(2,1)}, u32[]{:S(2)}, u32[]{:S(2)}) %collective-permute-start.2) | collective-permute-done | bytes 524320 | tf_op jit(solution)/shard_map/ppermute | solution.py:295
  70.1 3.9 %all-to-all-start.2 = ((bf16[16,144,128]{2,1,0:T(8,128)(2,1)}), bf16[16,144,128]{2,1,0:T(8,128)(2,1)S(1)}, u32[]{:S(2)}, u32[]{:S(2)}) async-start(bf16[16,144,128]{2,1,0:T(8,128)(2,1)} %gather_fusion.3), calls=%async_computation.2 | async-start | bytes 1179648 | tf_op jit(solution)/shard_map/all_to_all | solution.py:266
  73.9 1.9 collective-permute-start.6
  79.0 10.8 %collective-permute-done.5.refs_3_ = bf16[128,2176]{1,0:T(8,128)(2,1)} collective-permute-done((bf16[128,2176]{1,0:T(8,128)(2,1)}, bf16[128,2176]{1,0:T(8,128)(2,1)}, u32[]{:S(2)}, u32[]{:S(2)}) %collective-permute-start.5) | collective-permute-done | bytes 557088 | tf_op jit(solution)/shard_map/ppermute | solution.py:295
  89.8 6.0 %collective-permute-done.6.refs_7_ = bf16[128,2048]{1,0:T(8,128)(2,1)} collective-permute-done((bf16[128,2048]{1,0:T(8,128)(2,1)}, bf16[128,2048]{1,0:T(8,128)(2,1)}, u32[]{:S(2)}, u32[]{:S(2)}) %collective-permute-start.6) | collective-permute-done | bytes 524320 | tf_op jit(solution)/shard_map/ppermute | solution.py:298
  96.4 2.3 %collective-permute-done.7 = bf16[3,12,64,128]{3,2,1,0:T(8,128)(2,1)S(1)} collective-permute-done((bf16[3,12,64,128]{3,2,1,0:T(8,128)(2,1)S(1)}, bf16[3,12,64,128]{3,2,1,0:T(8,128)(2,1)S(1)}, u32[]{:S(2)}, u32[]{:S(2)}) %collective-permute-start.7) | collective-permute-done | bytes 589856 | tf_op jit(solution)/shard_map/ppermute | solution.py:307
  99.5 6.8 %all-to-all-start.3 = ((bf16[16,144,128]{2,1,0:T(8,128)(2,1)}), bf16[16,144,128]{2,1,0:T(8,128)(2,1)S(1)}, u32[]{:S(2)}, u32[]{:S(2)}) async-start(bf16[16,144,128]{2,1,0:T(8,128)(2,1)} %bitcast.2), calls=%async_computation.3 | async-start | bytes 1179648 | tf_op jit(solution)/shard_map/all_to_all | solution.py:266
  106.9 15.5 %shard_map.111 = (bf16[128,1024]{1,0:T(8,128)(2,1)}, bf16[128,1024]{1,0:T(8,128)(2,1)}, bf16[128,1024]{1,0:T(8,128)(2,1)}, bf16[128,1024]{1,0:T(8,128)(2,1)}, bf...) custom-call(s32[144]{0:T(256)} %reshape.384.lay_ref, ...), custom_call_target="tpu_custom_call" | custom-call | flops 14495514624 | bytes 13762560 | tf_op jit(solution)/shard_map/pallas_call | solution.py:226
  124.6 6.0 %all-to-all-start.4 = ((bf16[16,144,128]{2,1,0:T(8,128)(2,1)}), bf16[16,144,128]{2,1,0:T(8,128)(2,1)S(1)}, u32[]{:S(2)}, u32[]{:S(2)}) async-start(bf16[16,144,128]{2,1,0:T(8,128)(2,1)} %gather_fusion.8), calls=%async_computation.4 | async-start | bytes 1179648 | tf_op jit(solution)/shard_map/all_to_all | solution.py:266
  130.6 2.3 %add_convert_fusion.2 = bf16[3,12,64,128]{3,2,1,0:T(8,128)(2,1)} fusion(bf16[3,12,128,128]{3,2,1,0:T(8,128)(2,1)} %collective-permute-done.14, s32[]{:T(128)S(6)} %select_n.114, bf16[3,12,128,128]{3,2,1,0:T(8,128)(2,1)} %bitcast.63), kind=kLoop, calls=%fused_computation.13 | loop fusion | flops 1179648 | bytes 1769476 | tf_op jit(solution)/shard_map/convert_element_type | solution.py:327
  134.5 15.9 %shard_map.112 = (bf16[128,1024]{1,0:T(8,128)(2,1)}, bf16[128,1024]{1,0:T(8,128)(2,1)}, bf16[128,1024]{1,0:T(8,128)(2,1)}, bf16[128,1024]{1,0:T(8,128)(2,1)}, bf...) custom-call(s32[144]{0:T(256)} %reshape.385.lay_ref, ...), custom_call_target="tpu_custom_call" | custom-call | flops 14495514624 | bytes 13762560 | tf_op jit(solution)/shard_map/pallas_call | solution.py:226
  152.1 2.7 %collective-permute-start.18 = (bf16[3,12,64,128]{3,2,1,0:T(8,128)(2,1)S(1)}, bf16[3,12,64,128]{3,2,1,0:T(8,128)(2,1)S(1)}, u32[]{:S(2)}, u32[]{:S(2)}) collective-permute-start(bf16[3,12,64,128]{3,2,1,0:T(8,128)(2,1)S(1)} %add_convert_fusion), channel_id=1, source_target_pairs={{0,8},{1,9},{2,10},{3,11},{4,12},{5,13},{6,14},{7,15},{8,0},{9,1},... | collective-permute-start | bytes 1769480 | tf_op jit(solution)/shard_map/ppermute | solution.py:452
  159.1 22.3 %collective-permute-done.18 = bf16[3,12,64,128]{3,2,1,0:T(8,128)(2,1)S(1)} collective-permute-done((bf16[3,12,64,128]{3,2,1,0:T(8,128)(2,1)S(1)}, bf16[3,12,64,128]{3,2,1,0:T(8,128)(2,1)S(1)}, u32[]{:S(2)}, u32[]{:S(2)}) %collective-permute-start.18) | collective-permute-done | bytes 589856 | tf_op jit(solution)/shard_map/ppermute | solution.py:452
  181.4 1.9 collective-permute-start.21
  183.3 1.7 fusion.7
  188.0 7.9 %collective-permute-done.19 = bf16[128,1024]{1,0:T(8,128)(2,1)} collective-permute-done((bf16[128,1024]{1,0:T(8,128)(2,1)S(1)}, bf16[128,1024]{1,0:T(8,128)(2,1)}, u32[]{:S(2)}, u32[]{:S(2)}) %collective-permute-start.19) | collective-permute-done | bytes 262176 | tf_op jit(solution)/shard_map/ppermute | solution.py:295
  199.0 2.5 %collective-permute-done.23 = bf16[3,12,64,128]{3,2,1,0:T(8,128)(2,1)S(1)} collective-permute-done((bf16[3,12,64,128]{3,2,1,0:T(8,128)(2,1)S(1)}, bf16[3,12,64,128]{3,2,1,0:T(8,128)(2,1)S(1)}, u32[]{:S(2)}, u32[]{:S(2)}) %collective-permute-start.23) | collective-permute-done | bytes 589856 | tf_op jit(solution)/shard_map/ppermute | solution.py:304
  (137 shorter events, 35.8 us)
Async XLA Ops:
  2.9 33.2 %all-to-all-start = ((bf16[16,160,128]{2,1,0:T(8,128)(2,1)}), bf16[16,160,128]{2,1,0:T(8,128)(2,1)S(1)}, u32[]{:S(2)}, u32[]{:S(2)}) async-start(bf16[16,160,128]{2,1,0:T(8,128)(2,1)} %pad_maximum_fusion), calls=%async_computation | async-start | bytes 1310720 | tf_op jit(solution)/shard_map/all_to_all | solution.py:266
  11.6 22.5 %collective-permute-start.1 = (bf16[128,2176]{1,0:T(8,128)(2,1)}, bf16[128,2176]{1,0:T(8,128)(2,1)}, u32[]{:S(2)}, u32[]{:S(2)}) collective-permute-start(bf16[128,2176]{1,0:T(8,128)(2,1)} %pad_maximum_fusion.1.refs_0_), channel_id=1, source_target_pairs={{2,0},{3,1},{10,8},{11,9},{6,2},{7,3},{14,10},{15,11},{4,6},{5,7},... | collective-permute-start | bytes 1671176 | tf_op jit(solution)/shard_map/ppermute | solution.py:298
  13.5 22.6 %collective-permute-start = (bf16[128,2176]{1,0:T(8,128)(2,1)}, bf16[128,2176]{1,0:T(8,128)(2,1)}, u32[]{:S(2)}, u32[]{:S(2)}) collective-permute-start(bf16[128,2176]{1,0:T(8,128)(2,1)} %pad_maximum_fusion.1.refs_0_), channel_id=1, source_target_pairs={{0,2},{1,3},{8,10},{9,11},{2,6},{3,7},{10,14},{11,15},{6,4},{7,5},... | collective-permute-start | bytes 1671176 | tf_op jit(solution)/shard_map/ppermute | solution.py:295
  37.6 28.7 %all-to-all-start.1 = ((bf16[16,144,128]{2,1,0:T(8,128)(2,1)}), bf16[16,144,128]{2,1,0:T(8,128)(2,1)S(1)}, u32[]{:S(2)}, u32[]{:S(2)}) async-start(bf16[16,144,128]{2,1,0:T(8,128)(2,1)} %gather_fusion.1), calls=%async_computation.1 | async-start | bytes 1179648 | tf_op jit(solution)/shard_map/all_to_all | solution.py:266
  42.4 21.9 %collective-permute-start.3 = (bf16[128,2048]{1,0:T(8,128)(2,1)}, bf16[128,2048]{1,0:T(8,128)(2,1)}, u32[]{:S(2)}, u32[]{:S(2)}) collective-permute-start(bf16[128,2048]{1,0:T(8,128)(2,1)} %refs_4_.1), channel_id=1, source_target_pairs={{2,0},{3,1},{10,8},{11,9},{6,2},{7,3},{14,10},{15,11},{4,6},{5,7},... | collective-permute-start | bytes 1572872 | tf_op jit(solution)/shard_map/ppermute | solution.py:298
  44.3 22.0 %collective-permute-start.2 = (bf16[128,2048]{1,0:T(8,128)(2,1)}, bf16[128,2048]{1,0:T(8,128)(2,1)}, u32[]{:S(2)}, u32[]{:S(2)}) collective-permute-start(bf16[128,2048]{1,0:T(8,128)(2,1)} %refs_4_.1), channel_id=1, source_target_pairs={{0,2},{1,3},{8,10},{9,11},{2,6},{3,7},{10,14},{11,15},{6,4},{7,5},... | collective-permute-start | bytes 1572872 | tf_op jit(solution)/shard_map/ppermute | solution.py:295
  66.3 29.5 %collective-permute-start.4 = (bf16[3,12,64,128]{3,2,1,0:T(8,128)(2,1)S(1)}, bf16[3,12,64,128]{3,2,1,0:T(8,128)(2,1)}, u32[]{:S(2)}, u32[]{:S(2)}) collective-permute-start(bf16[3,12,64,128]{3,2,1,0:T(8,128)(2,1)S(1)} %bitcast.67), channel_id=1, source_target_pairs={{0,16},{16,0},{1,17},{17,1},{2,18},{18,2},{3,19},{19,3},{4,20},{20... | collective-permute-start | bytes 1769480 | tf_op jit(solution)/shard_map/ppermute | solution.py:304
  68.5 21.3 %collective-permute-start.5 = (bf16[128,2176]{1,0:T(8,128)(2,1)}, bf16[128,2176]{1,0:T(8,128)(2,1)}, u32[]{:S(2)}, u32[]{:S(2)}) collective-permute-start(bf16[128,2176]{1,0:T(8,128)(2,1)} %collective-permute-done.refs_2_), channel_id=1, source_target_pairs={{0,2},{1,3},{8,10},{9,11},{2,6},{3,7},{10,14},{11,15},{6,4},{7,5},... | collective-permute-start | bytes 1671176 | tf_op jit(solution)/shard_map/ppermute | solution.py:295
  70.1 26.3 %all-to-all-start.2 = ((bf16[16,144,128]{2,1,0:T(8,128)(2,1)}), bf16[16,144,128]{2,1,0:T(8,128)(2,1)S(1)}, u32[]{:S(2)}, u32[]{:S(2)}) async-start(bf16[16,144,128]{2,1,0:T(8,128)(2,1)} %gather_fusion.3), calls=%async_computation.2 | async-start | bytes 1179648 | tf_op jit(solution)/shard_map/all_to_all | solution.py:266
  73.9 21.9 %collective-permute-start.6 = (bf16[128,2048]{1,0:T(8,128)(2,1)}, bf16[128,2048]{1,0:T(8,128)(2,1)}, u32[]{:S(2)}, u32[]{:S(2)}) collective-permute-start(bf16[128,2048]{1,0:T(8,128)(2,1)} %collective-permute-done.3.refs_5_), channel_id=1, source_target_pairs={{2,0},{3,1},{10,8},{11,9},{6,2},{7,3},{14,10},{15,11},{4,6},{5,7},... | collective-permute-start | bytes 1572872 | tf_op jit(solution)/shard_map/ppermute | solution.py:298
  99.5 22.9 %all-to-all-start.3 = ((bf16[16,144,128]{2,1,0:T(8,128)(2,1)}), bf16[16,144,128]{2,1,0:T(8,128)(2,1)S(1)}, u32[]{:S(2)}, u32[]{:S(2)}) async-start(bf16[16,144,128]{2,1,0:T(8,128)(2,1)} %bitcast.2), calls=%async_computation.3 | async-start | bytes 1179648 | tf_op jit(solution)/shard_map/all_to_all | solution.py:266
  106.3 16.1 %collective-permute-start.9 = (bf16[3,12,64,128]{3,2,1,0:T(8,128)(2,1)S(1)}, bf16[3,12,64,128]{3,2,1,0:T(8,128)(2,1)}, u32[]{:S(2)}, u32[]{:S(2)}) collective-permute-start(bf16[3,12,64,128]{3,2,1,0:T(8,128)(2,1)S(1)} %bitcast.58), channel_id=1, source_target_pairs={{0,16},{16,0},{1,17},{17,1},{2,18},{18,2},{3,19},{19,3},{4,20},{20... | collective-permute-start | bytes 1769480 | tf_op jit(solution)/shard_map/ppermute | solution.py:304
  122.7 11.8 %collective-permute-start.10 = (bf16[3,12,64,128]{3,2,1,0:T(8,128)(2,1)S(1)}, bf16[3,12,64,128]{3,2,1,0:T(8,128)(2,1)}, u32[]{:S(2)}, u32[]{:S(2)}) collective-permute-start(bf16[3,12,64,128]{3,2,1,0:T(8,128)(2,1)S(1)} %bitcast.59), channel_id=1, source_target_pairs={{0,1},{1,0},{2,3},{3,2},{4,5},{5,4},{6,7},{7,6},{8,9},{9,8},{10,11... | collective-permute-start | bytes 1769480 | tf_op jit(solution)/shard_map/ppermute | solution.py:307
  123.0 11.5 %collective-permute-start.11 = (bf16[3,12,64,128]{3,2,1,0:T(8,128)(2,1)}, bf16[3,12,64,128]{3,2,1,0:T(8,128)(2,1)}, u32[]{:S(2)}, u32[]{:S(2)}) collective-permute-start(bf16[3,12,64,128]{3,2,1,0:T(8,128)(2,1)} %collective-permute-done.9), channel_id=1, source_target_pairs={{0,1},{1,0},{2,3},{3,2},{4,5},{5,4},{6,7},{7,6},{8,9},{9,8},{10,11... | collective-permute-start | bytes 1769480 | tf_op jit(solution)/shard_map/ppermute | solution.py:307
  124.6 25.8 %all-to-all-start.4 = ((bf16[16,144,128]{2,1,0:T(8,128)(2,1)}), bf16[16,144,128]{2,1,0:T(8,128)(2,1)S(1)}, u32[]{:S(2)}, u32[]{:S(2)}) async-start(bf16[16,144,128]{2,1,0:T(8,128)(2,1)} %gather_fusion.8), calls=%async_computation.4 | async-start | bytes 1179648 | tf_op jit(solution)/shard_map/all_to_all | solution.py:266
  132.9 17.4 %collective-permute-start.15 = (bf16[3,12,64,128]{3,2,1,0:T(8,128)(2,1)}, bf16[3,12,64,128]{3,2,1,0:T(8,128)(2,1)S(1)}, u32[]{:S(2)}, u32[]{:S(2)}) collective-permute-start(bf16[3,12,64,128]{3,2,1,0:T(8,128)(2,1)} %add_convert_fusion.2), channel_id=1, source_target_pairs={{0,16},{16,0},{1,17},{17,1},{2,18},{18,2},{3,19},{19,3},{4,20},{20... | collective-permute-start | bytes 1769480 | tf_op jit(solution)/shard_map/ppermute | solution.py:304
  152.1 29.3 %collective-permute-start.18 = (bf16[3,12,64,128]{3,2,1,0:T(8,128)(2,1)S(1)}, bf16[3,12,64,128]{3,2,1,0:T(8,128)(2,1)S(1)}, u32[]{:S(2)}, u32[]{:S(2)}) collective-permute-start(bf16[3,12,64,128]{3,2,1,0:T(8,128)(2,1)S(1)} %add_convert_fusion), channel_id=1, source_target_pairs={{0,8},{1,9},{2,10},{3,11},{4,12},{5,13},{6,14},{7,15},{8,0},{9,1},... | collective-permute-start | bytes 1769480 | tf_op jit(solution)/shard_map/ppermute | solution.py:452
  155.1 28.2 %collective-permute-start.17 = (bf16[3,12,64,128]{3,2,1,0:T(8,128)(2,1)S(1)}, bf16[3,12,64,128]{3,2,1,0:T(8,128)(2,1)S(1)}, u32[]{:S(2)}, u32[]{:S(2)}) collective-permute-start(bf16[3,12,64,128]{3,2,1,0:T(8,128)(2,1)S(1)} %add_convert_fusion.1), channel_id=1, source_target_pairs={{0,16},{16,0},{1,17},{17,1},{2,18},{18,2},{3,19},{19,3},{4,20},{20... | collective-permute-start | bytes 1769480 | tf_op jit(solution)/shard_map/ppermute | solution.py:304
  155.6 29.4 %collective-permute-start.12 = (bf16[128,1024]{1,0:T(8,128)(2,1)S(1)}, bf16[128,1024]{1,0:T(8,128)(2,1)S(1)}, u32[]{:S(2)}, u32[]{:S(2)}) collective-permute-start(bf16[128,1024]{1,0:T(8,128)(2,1)S(1)} %copy-done.19), channel_id=1, source_target_pairs={{0,2},{1,3},{8,10},{9,11},{2,6},{3,7},{10,14},{11,15},{6,4},{7,5},... | collective-permute-start | bytes 786440 | tf_op jit(solution)/shard_map/ppermute | solution.py:295
  157.1 30.9 %collective-permute-start.20 = (bf16[128,1024]{1,0:T(8,128)(2,1)}, bf16[128,1024]{1,0:T(8,128)(2,1)}, u32[]{:S(2)}, u32[]{:S(2)}) collective-permute-start(bf16[128,1024]{1,0:T(8,128)(2,1)} %get-tuple-element.138), channel_id=1, source_target_pairs={{2,0},{3,1},{10,8},{11,9},{6,2},{7,3},{14,10},{15,11},{4,6},{5,7},... | collective-permute-start | bytes 786440 | tf_op jit(solution)/shard_map/ppermute | solution.py:298
  157.7 27.4 %collective-permute-start.13 = (bf16[128,1152]{1,0:T(8,128)(2,1)S(1)}, bf16[128,1152]{1,0:T(8,128)(2,1)S(1)}, u32[]{:S(2)}, u32[]{:S(2)}) collective-permute-start(bf16[128,1152]{1,0:T(8,128)(2,1)S(1)} %copy-done.18), channel_id=1, source_target_pairs={{2,0},{3,1},{10,8},{11,9},{6,2},{7,3},{14,10},{15,11},{4,6},{5,7},... | collective-permute-start | bytes 884744 | tf_op jit(solution)/shard_map/ppermute | solution.py:298
  181.4 15.6 %collective-permute-start.21 = (bf16[128,1152]{1,0:T(8,128)(2,1)}, bf16[128,1152]{1,0:T(8,128)(2,1)S(1)}, u32[]{:S(2)}, u32[]{:S(2)}) collective-permute-start(bf16[128,1152]{1,0:T(8,128)(2,1)} %get-tuple-element.140), channel_id=1, source_target_pairs={{0,2},{1,3},{8,10},{9,11},{2,6},{3,7},{10,14},{11,15},{6,4},{7,5},... | collective-permute-start | bytes 884744 | tf_op jit(solution)/shard_map/ppermute | solution.py:295
  185.6 11.4 %collective-permute-start.22 = (bf16[128,1152]{1,0:T(8,128)(2,1)S(1)}, bf16[128,1152]{1,0:T(8,128)(2,1)S(1)}, u32[]{:S(2)}, u32[]{:S(2)}) collective-permute-start(bf16[128,1152]{1,0:T(8,128)(2,1)S(1)} %add_convert_fusion.4), channel_id=1, source_target_pairs={{2,0},{3,1},{10,8},{11,9},{6,2},{7,3},{14,10},{15,11},{4,6},{5,7},... | collective-permute-start | bytes 884744 | tf_op jit(solution)/shard_map/ppermute | solution.py:298
  187.5 14.0 %collective-permute-start.23 = (bf16[3,12,64,128]{3,2,1,0:T(8,128)(2,1)S(1)}, bf16[3,12,64,128]{3,2,1,0:T(8,128)(2,1)S(1)}, u32[]{:S(2)}, u32[]{:S(2)}) collective-permute-start(bf16[3,12,64,128]{3,2,1,0:T(8,128)(2,1)S(1)} %get-tuple-element.143), channel_id=1, source_target_pairs={{0,16},{16,0},{1,17},{17,1},{2,18},{18,2},{3,19},{19,3},{4,20},{20... | collective-permute-start | bytes 1769480 | tf_op jit(solution)/shard_map/ppermute | solution.py:304
  (25 other events, 279.2 us)
